TPU v7x, 32 devices: a whole 2x2x4 slice. The times are simulated.
32 devices in a mesh: groups: 2 (over y), space: 16 (over z, x, core).
Axes of the slice: x: 2, y: 2, z: 4, core: 2. Of those that a mesh axis runs over, the one named last changes fastest.
Arguments:
- links: float32 [3, 3, 3, 2, 1024, 32], P(None, None, None, None, 'space', 'groups'), parts along dimension 5, may hold values from -1 to 1, as said below
- sources: float32 [24, 3, 2, 1024, 32], P(None, None, None, 'space', 'groups'), parts along dimension 4, may hold values from -6 to 6
Outputs:
- filtered: float32 [24, 3, 2, 1024, 32], P(None, None, None, 'space', 'groups'), parts along dimension 4
There are 2 independent parts, one for each index of `groups`. A program takes and returns all parts, laid end to end along the dimension named above; each array names one. Nothing has to cross between parts.
Inputs may be any that keep to these rules, and one draw needn't show every extreme that they name: At every site and direction, links[mu, :, :, 0, s] + i links[mu, :, :, 1, s] is a special unitary 3 x 3 matrix.
All inputs are finite; a program needn't handle non-finite values.
Results may differ from a plain program's by a relative error of at most 0.00002.
Values sent between devices are 32-bit elements; how exact they have to be, the bound alone decides.
No kernel may reach another device: no remote copies, remote signals or barrier semaphores. Data moves between devices by JAX's collectives and lax.ppermute only.
A program may use at most 64 MiB of HBM per device.

v0:
```python
import jax
import jax.numpy as jnp
from jax import lax
from jax.sharding import PartitionSpec as P

NT = 8
LS = 32


cheb_coeffs = (0.6, -0.5, 0.35, -0.25, 0.15)


def shifted(value, axis, steps):
    count = lax.axis_size(axis)
    pairs = [(source, (source + steps) % count) for source in range(count)]
    return lax.ppermute(value, axis, pairs)


def apply_link(link, vector):
    real_part = 0.0
    imag_part = 0.0
    for column in range(3):
        link_re = link[:, column, 0][None]
        link_im = link[:, column, 1][None]
        vec_re = vector[:, column, 0][:, None]
        vec_im = vector[:, column, 1][:, None]
        real_part = real_part + link_re * vec_re - link_im * vec_im
        imag_part = imag_part + link_re * vec_im + link_im * vec_re
    return jnp.stack([real_part, imag_part], axis=2)


def apply_dagger(link, vector):
    real_part = 0.0
    imag_part = 0.0
    for column in range(3):
        link_re = link[column, :, 0][None]
        link_im = link[column, :, 1][None]
        vec_re = vector[:, column, 0][:, None]
        vec_im = vector[:, column, 1][:, None]
        real_part = real_part + link_re * vec_re + link_im * vec_im
        imag_part = imag_part + link_re * vec_im - link_im * vec_re
    return jnp.stack([real_part, imag_part], axis=2)


def z_ahead(array, extent, z_index):
    return jnp.where(
        z_index == extent - 1, jnp.roll(array, extent - 1, axis=-1), jnp.roll(array, -1, axis=-1)
    )


def z_behind(array, extent, z_index):
    return jnp.where(
        z_index == 0, jnp.roll(array, 1 - extent, axis=-1), jnp.roll(array, 1, axis=-1)
    )


def body(links, sources):
    device_count = lax.axis_size("space")
    slabs = device_count // NT
    yz_local = links.shape[4]
    planes = links.shape[5] // device_count
    plane_sites = yz_local * device_count
    vectors = sources.shape[0]
    link_parts = links.reshape(54, yz_local, NT, slabs, planes)
    source_parts = sources.reshape(vectors * 6, yz_local, NT, slabs, planes)
    link_send = jnp.transpose(link_parts, (0, 3, 2, 4, 1)).reshape(
        54, device_count, planes, yz_local
    )
    source_send = jnp.transpose(source_parts, (0, 3, 2, 4, 1)).reshape(
        vectors * 6, device_count, planes, yz_local
    )
    link_recv, source_recv = (
        lax.all_to_all(link_send, "space", split_axis=1, concat_axis=3, tiled=True),
        lax.all_to_all(source_send, "space", split_axis=1, concat_axis=3, tiled=True),
    )
    gauge_local = link_recv.reshape(3, 3, 3, 2, planes, plane_sites)
    source_field = source_recv.reshape(vectors, 3, 2, planes, plane_sites)
    z_index = jnp.arange(plane_sites, dtype=jnp.int32) % LS
    x_top = gauge_local[0]
    x_rest = gauge_local[0][:, :, :, :-1]
    y_back = jnp.roll(gauge_local[1], LS, axis=-1)
    z_back = z_behind(gauge_local[2], LS, z_index)

    def fetch_lower(vector):
        return shifted(apply_dagger(x_top, vector), "space", NT)

    def hop_sum(vector):
        upper_face = shifted(vector, "space", -NT)
        lower_face = fetch_lower(vector)
        ahead = apply_link(
            gauge_local[0], jnp.concatenate([vector[:, :, :, 1:], upper_face], axis=3)
        )
        behind = jnp.concatenate([lower_face, apply_dagger(x_rest, vector[:, :, :, :-1])], axis=3)
        summed = ahead + behind
        summed = (
            summed
            + apply_link(gauge_local[1], jnp.roll(vector, -LS, axis=-1))
            + apply_dagger(y_back, jnp.roll(vector, LS, axis=-1))
        )
        summed = (
            summed
            + apply_link(gauge_local[2], z_ahead(vector, LS, z_index))
            + apply_dagger(z_back, z_behind(vector, LS, z_index))
        )
        return summed

    def scaled(vector):
        return hop_sum(vector) * (-1.0 / 6.0)

    previous = source_field
    current = scaled(previous)
    filtered = cheb_coeffs[0] * previous + cheb_coeffs[1] * current
    for degree in range(2, 5):
        following = 2.0 * scaled(current) - previous
        filtered = filtered + cheb_coeffs[degree] * following
        previous, current = (current, following)
    outgoing = filtered.reshape(vectors * 6, 1, planes, plane_sites)
    returned = lax.all_to_all(outgoing, "space", split_axis=3, concat_axis=1, tiled=True)
    ordered = jnp.transpose(
        returned.reshape(vectors * 6, slabs, NT, planes, yz_local), (0, 4, 2, 1, 3)
    )
    return ordered.reshape(vectors, 3, 2, yz_local, NT * slabs * planes)


def solution(mesh):
    in_specs = (
        P(None, None, None, None, "space", "groups"),
        P(None, None, None, "space", "groups"),
    )
    out_specs = P(None, None, None, "space", "groups")
    return jax.shard_map(body, mesh=mesh, in_specs=in_specs, out_specs=out_specs, check_vma=False)
```

profile of v0, /device:TPU:1, one launch (start us, length us, event | category | flops | bytes accessed | tf_op | source)
XLA Modules:
  0.0 321.7 jit_solution(1192837110841796550)
XLA Ops:
  4.7 7.3 %all-to-all-start.1 = ((f32[16,1,3456]{2,1,0:T(1,128)}), f32[16,1,3456]{2,1,0:T(1,128)S(1)}, u32[]{:S(2)}, u32[]{:S(2)}) async-start(f32[16,1,3456]{2,1,0:T(1,128)} %reshape.3185), calls=%async_computation.1 | async-start | bytes 442368 | tf_op jit(solution)/shard_map/all_to_all | solution.py:73
  13.6 7.2 %all-to-all-done.1 = f32[16,1,3456]{2,1,0:T(1,128)S(1)} async-done(((f32[16,1,3456]{2,1,0:T(1,128)}), f32[16,1,3456]{2,1,0:T(1,128)S(1)}, u32[]{:S(2)}, u32[]{:S(2)}) %all-to-all-start.1) | async-done | bytes 221216 | tf_op jit(solution)/shard_map/all_to_all | solution.py:73
  20.8 4.8 %all-to-all-start = ((f32[144,16,1,64]{0,3,2,1:T(8,128)}), f32[144,16,1,64]{0,3,2,1:T(8,128)S(1)}, u32[]{:S(2)}, u32[]{:S(2)}) async-start(f32[144,16,1,64]{0,3,2,1:T(8,128)} %bitcast.2), calls=%async_computation | async-start | bytes 2097152 | tf_op jit(solution)/shard_map/all_to_all | solution.py:74
  29.1 19.6 %all-to-all-done = f32[144,16,1,64]{0,3,2,1:T(8,128)S(1)} async-done(((f32[144,16,1,64]{0,3,2,1:T(8,128)}), f32[144,16,1,64]{0,3,2,1:T(8,128)S(1)}, u32[]{:S(2)}, u32[]{:S(2)}) %all-to-all-start) | async-done | bytes 589856 | tf_op jit(solution)/shard_map/all_to_all | solution.py:74
  52.9 3.9 %collective-permute-start = (f32[24,3,2,1,1024]{4,2,1,0,3:T(2,128)S(1)}, f32[24,3,2,1,1024]{4,2,1,0,3:T(2,128)S(1)}, u32[]{:S(2)}, u32[]{:S(2)}) collective-permute-start(f32[24,3,2,1,1024]{4,2,1,0,3:T(2,128)S(1)} %reshape.3179), channel_id=1, source_target_pairs={{0,8},{1,9},{2,10},{3,11},{4,12},{5,13},{6,14},{7,15},{8,0},{9,1},... | collective-permute-start | bytes 1769480 | tf_op jit(solution)/shard_map/ppermute | solution.py:16
  59.6 1.9 multiply_add_fusion.23
  71.3 23.6 %collective-permute-done = f32[24,3,2,1,1024]{4,2,1,0,3:T(2,128)S(1)} collective-permute-done((f32[24,3,2,1,1024]{4,2,1,0,3:T(2,128)S(1)}, f32[24,3,2,1,1024]{4,2,1,0,3:T(2,128)S(1)}, u32[]{:S(2)}, u32[]{:S(2)}) %collective-permute-start) | collective-permute-done | bytes 589856 | tf_op jit(solution)/shard_map/ppermute | solution.py:16
  97.1 10.4 %collective-permute-done.1 = f32[24,3,2,1,1024]{4,2,1,0,3:T(2,128)S(1)} collective-permute-done((f32[24,3,2,1,1024]{4,2,1,0,3:T(2,128)S(1)}, f32[24,3,2,1,1024]{4,2,1,0,3:T(2,128)S(1)}, u32[]{:S(2)}, u32[]{:S(2)}) %collective-permute-start.1) | collective-permute-done | bytes 589856 | tf_op jit(solution)/shard_map/ppermute | solution.py:16
  107.5 2.9 broadcast_multiply_fusion
  120.0 2.4 collective-permute-start.3
  125.9 2.1 multiply_add_fusion.15
  130.5 24.2 %collective-permute-done.2 = f32[24,3,2,1,1024]{4,2,1,0,3:T(2,128)S(1)} collective-permute-done((f32[24,3,2,1,1024]{4,2,1,0,3:T(2,128)S(1)}, f32[24,3,2,1,1024]{4,2,1,0,3:T(2,128)S(1)}, u32[]{:S(2)}, u32[]{:S(2)}) %collective-permute-start.2) | collective-permute-done | bytes 589856 | tf_op jit(solution)/shard_map/ppermute | solution.py:16
  157.0 10.3 %collective-permute-done.3 = f32[24,3,2,1,1024]{4,2,1,0,3:T(2,128)S(1)} collective-permute-done((f32[24,3,2,1,1024]{4,2,1,0,3:T(2,128)S(1)}, f32[24,3,2,1,1024]{4,2,1,0,3:T(2,128)S(1)}, u32[]{:S(2)}, u32[]{:S(2)}) %collective-permute-start.3) | collective-permute-done | bytes 589856 | tf_op jit(solution)/shard_map/ppermute | solution.py:16
  167.3 2.6 multiply_subtract_fusion.1
  179.8 2.4 collective-permute-start.5
  189.9 23.2 %collective-permute-done.4 = f32[24,3,2,1,1024]{4,2,1,0,3:T(2,128)S(1)} collective-permute-done((f32[24,3,2,1,1024]{4,2,1,0,3:T(2,128)S(1)}, f32[24,3,2,1,1024]{4,2,1,0,3:T(2,128)S(1)}, u32[]{:S(2)}, u32[]{:S(2)}) %collective-permute-start.4) | collective-permute-done | bytes 589856 | tf_op jit(solution)/shard_map/ppermute | solution.py:16
  215.3 10.3 %collective-permute-done.5 = f32[24,3,2,1,1024]{4,2,1,0,3:T(2,128)S(1)} collective-permute-done((f32[24,3,2,1,1024]{4,2,1,0,3:T(2,128)S(1)}, f32[24,3,2,1,1024]{4,2,1,0,3:T(2,128)S(1)}, u32[]{:S(2)}, u32[]{:S(2)}) %collective-permute-start.5) | collective-permute-done | bytes 589856 | tf_op jit(solution)/shard_map/ppermute | solution.py:16
  225.7 2.9 multiply_subtract_fusion
  238.2 2.4 collective-permute-start.7
  244.1 2.0 multiply_add_fusion.3
  248.6 24.4 %collective-permute-done.6 = f32[24,3,2,1,1024]{4,2,1,0,3:T(2,128)S(1)} collective-permute-done((f32[24,3,2,1,1024]{4,2,1,0,3:T(2,128)S(1)}, f32[24,3,2,1,1024]{4,2,1,0,3:T(2,128)S(1)}, u32[]{:S(2)}, u32[]{:S(2)}) %collective-permute-start.6) | collective-permute-done | bytes 589856 | tf_op jit(solution)/shard_map/ppermute | solution.py:16
  275.2 10.3 %collective-permute-done.7 = f32[24,3,2,1,1024]{4,2,1,0,3:T(2,128)S(1)} collective-permute-done((f32[24,3,2,1,1024]{4,2,1,0,3:T(2,128)S(1)}, f32[24,3,2,1,1024]{4,2,1,0,3:T(2,128)S(1)}, u32[]{:S(2)}, u32[]{:S(2)}) %collective-permute-start.7) | collective-permute-done | bytes 589856 | tf_op jit(solution)/shard_map/ppermute | solution.py:16
  285.6 3.4 %multiply_add_fusion = f32[24,3,2,1,1024]{4,2,1,0,3:T(2,128)S(1)} fusion(f32[24,3,2,1,1024]{4,2,1,0,3:T(2,128)S(1)} %multiply_subtract_fusion.1, f32[24,3,2,1,1024]{4,2,1,0,3:T(2,128)S(1)} %multiply_subtract_fusion, f32[24,3,2,1,1024]{4,2,1,0,3:T(2,128)S(1)} %get-tuple-element.6, f32[24,3,2,1,1024]{4,2,1,0,3:T(2,128)S(1)} %reshape.3179, ...), kind=kLoop, calls=%fused_computation.72 | loop fusion | flops 3096576 | bytes 6488064 | tf_op jit(solution)/shard_map/add | solution.py:115
  290.1 28.9 %all_to_all.12 = f32[144,1,1,1024]{0,2,1,3:T(1,128)S(1)} all-to-all(f32[144,1,1,1024]{0,2,1,3:T(1,128)S(1)} %copy.25), channel_id=1, replica_groups=mesh['groups'=2,'space'=16] {'space'}, dimensions={3} | all-to-all | bytes 1179648 | tf_op jit(solution)/shard_map/all_to_all | solution.py:118
  (271 shorter events, 86.2 us)
Async XLA Ops:
  1.5 10.5 %copy-start = (f32[24,3,2,64,16]{3,4,2,1,0:T(8,128)S(1)}, f32[24,3,2,64,16]{3,4,2,1,0:T(8,128)}, u32[]{:S(2)}) copy-start(f32[24,3,2,64,16]{3,4,2,1,0:T(8,128)} %param.3) | copy-start | bytes 1769476
  4.7 16.1 %all-to-all-start.1 = ((f32[16,1,3456]{2,1,0:T(1,128)}), f32[16,1,3456]{2,1,0:T(1,128)S(1)}, u32[]{:S(2)}, u32[]{:S(2)}) async-start(f32[16,1,3456]{2,1,0:T(1,128)} %reshape.3185), calls=%async_computation.1 | async-start | bytes 442368 | tf_op jit(solution)/shard_map/all_to_all | solution.py:73
  20.8 27.9 %all-to-all-start = ((f32[144,16,1,64]{0,3,2,1:T(8,128)}), f32[144,16,1,64]{0,3,2,1:T(8,128)S(1)}, u32[]{:S(2)}, u32[]{:S(2)}) async-start(f32[144,16,1,64]{0,3,2,1:T(8,128)} %bitcast.2), calls=%async_computation | async-start | bytes 2097152 | tf_op jit(solution)/shard_map/all_to_all | solution.py:74
  52.9 42.0 %collective-permute-start = (f32[24,3,2,1,1024]{4,2,1,0,3:T(2,128)S(1)}, f32[24,3,2,1,1024]{4,2,1,0,3:T(2,128)S(1)}, u32[]{:S(2)}, u32[]{:S(2)}) collective-permute-start(f32[24,3,2,1,1024]{4,2,1,0,3:T(2,128)S(1)} %reshape.3179), channel_id=1, source_target_pairs={{0,8},{1,9},{2,10},{3,11},{4,12},{5,13},{6,14},{7,15},{8,0},{9,1},... | collective-permute-start | bytes 1769480 | tf_op jit(solution)/shard_map/ppermute | solution.py:16
  62.0 45.4 %collective-permute-start.1 = (f32[24,3,2,1,1024]{4,2,1,0,3:T(2,128)S(1)}, f32[24,3,2,1,1024]{4,2,1,0,3:T(2,128)S(1)}, u32[]{:S(2)}, u32[]{:S(2)}) collective-permute-start(f32[24,3,2,1,1024]{4,2,1,0,3:T(2,128)S(1)} %pad_maximum_fusion), channel_id=1, source_target_pairs={{0,8},{1,9},{2,10},{3,11},{4,12},{5,13},{6,14},{7,15},{8,0},{9,1},... | collective-permute-start | bytes 1769480 | tf_op jit(solution)/shard_map/ppermute | solution.py:16
  113.3 41.4 %collective-permute-start.2 = (f32[24,3,2,1,1024]{4,2,1,0,3:T(2,128)S(1)}, f32[24,3,2,1,1024]{4,2,1,0,3:T(2,128)S(1)}, u32[]{:S(2)}, u32[]{:S(2)}) collective-permute-start(f32[24,3,2,1,1024]{4,2,1,0,3:T(2,128)S(1)} %get-tuple-element.5), channel_id=1, source_target_pairs={{0,8},{1,9},{2,10},{3,11},{4,12},{5,13},{6,14},{7,15},{8,0},{9,1},... | collective-permute-start | bytes 1769480 | tf_op jit(solution)/shard_map/ppermute | solution.py:16
  120.0 47.3 %collective-permute-start.3 = (f32[24,3,2,1,1024]{4,2,1,0,3:T(2,128)S(1)}, f32[24,3,2,1,1024]{4,2,1,0,3:T(2,128)S(1)}, u32[]{:S(2)}, u32[]{:S(2)}) collective-permute-start(f32[24,3,2,1,1024]{4,2,1,0,3:T(2,128)S(1)} %pad_maximum_fusion.1), channel_id=1, source_target_pairs={{0,8},{1,9},{2,10},{3,11},{4,12},{5,13},{6,14},{7,15},{8,0},{9,1},... | collective-permute-start | bytes 1769480 | tf_op jit(solution)/shard_map/ppermute | solution.py:16
  172.9 40.1 %collective-permute-start.4 = (f32[24,3,2,1,1024]{4,2,1,0,3:T(2,128)S(1)}, f32[24,3,2,1,1024]{4,2,1,0,3:T(2,128)S(1)}, u32[]{:S(2)}, u32[]{:S(2)}) collective-permute-start(f32[24,3,2,1,1024]{4,2,1,0,3:T(2,128)S(1)} %multiply_subtract_fusion.1), channel_id=1, source_target_pairs={{0,8},{1,9},{2,10},{3,11},{4,12},{5,13},{6,14},{7,15},{8,0},{9,1},... | collective-permute-start | bytes 1769480 | tf_op jit(solution)/shard_map/ppermute | solution.py:16
  179.8 45.9 %collective-permute-start.5 = (f32[24,3,2,1,1024]{4,2,1,0,3:T(2,128)S(1)}, f32[24,3,2,1,1024]{4,2,1,0,3:T(2,128)S(1)}, u32[]{:S(2)}, u32[]{:S(2)}) collective-permute-start(f32[24,3,2,1,1024]{4,2,1,0,3:T(2,128)S(1)} %pad_maximum_fusion.2), channel_id=1, source_target_pairs={{0,8},{1,9},{2,10},{3,11},{4,12},{5,13},{6,14},{7,15},{8,0},{9,1},... | collective-permute-start | bytes 1769480 | tf_op jit(solution)/shard_map/ppermute | solution.py:16
  231.5 41.4 %collective-permute-start.6 = (f32[24,3,2,1,1024]{4,2,1,0,3:T(2,128)S(1)}, f32[24,3,2,1,1024]{4,2,1,0,3:T(2,128)S(1)}, u32[]{:S(2)}, u32[]{:S(2)}) collective-permute-start(f32[24,3,2,1,1024]{4,2,1,0,3:T(2,128)S(1)} %multiply_subtract_fusion), channel_id=1, source_target_pairs={{0,8},{1,9},{2,10},{3,11},{4,12},{5,13},{6,14},{7,15},{8,0},{9,1},... | collective-permute-start | bytes 1769480 | tf_op jit(solution)/shard_map/ppermute | solution.py:16
  238.2 47.3 %collective-permute-start.7 = (f32[24,3,2,1,1024]{4,2,1,0,3:T(2,128)S(1)}, f32[24,3,2,1,1024]{4,2,1,0,3:T(2,128)S(1)}, u32[]{:S(2)}, u32[]{:S(2)}) collective-permute-start(f32[24,3,2,1,1024]{4,2,1,0,3:T(2,128)S(1)} %pad_maximum_fusion.3), channel_id=1, source_target_pairs={{0,8},{1,9},{2,10},{3,11},{4,12},{5,13},{6,14},{7,15},{8,0},{9,1},... | collective-permute-start | bytes 1769480 | tf_op jit(solution)/shard_map/ppermute | solution.py:16
where the time goes:
time: 325 us; the launch traced here: 322 us
  waiting for transfers between devices  163 us (50%)
  other arithmetic  73.5 us (23%)
  local copies, waits for them, and re-layouts  30.4 us (9%)
  blocking collectives  28.9 us (9%)
  starting transfers between devices  23.5 us (7%)
    ppermute x8, waiting for transfers between devices, shifted(): return lax.ppermute(value, axis, pairs)  137 us
    all_to_all x1, blocking collectives, body(): lax.all_to_all(outgoing, 'space', split_axis=3, concat_axis=1, tiled=True)  28.9 us
    add x12, other arithmetic, apply_dagger(): real_part = real_part + link_re * vec_re + link_im * vec_im  21.7 us
    sub x12, other arithmetic, apply_link(): real_part = real_part + link_re * vec_re - link_im * vec_im  20.7 us
    all_to_all x1, waiting for transfers between devices, body(): lax.all_to_all(source_send, 'space', split_axis=1, concat_axis=3, tiled=T...  19.6 us
    ppermute x8, starting transfers between devices, shifted(): return lax.ppermute(value, axis, pairs)  11.4 us
    all_to_all x1, starting transfers between devices, body(): lax.all_to_all(link_send, 'space', split_axis=1, concat_axis=3, tiled=True)  7.32 us
    all_to_all x1, waiting for transfers between devices, body(): lax.all_to_all(link_send, 'space', split_axis=1, concat_axis=3, tiled=True)  7.21 us
  transfers between devices with their start and end apart: 10, of which 10 were waited for; matrix products, arithmetic and copies ran while one was open for 22% of the time, Pallas kernels for 0%

commit v1 on v0

--- a/solution.py
+++ b/solution.py
@@ -1,13 +1,267 @@
+import functools
+
 import jax
 import jax.numpy as jnp
 from jax import lax
+from jax.experimental import pallas as pl
+from jax.experimental.pallas import tpu as pltpu
 from jax.sharding import PartitionSpec as P
 
 NT = 8
 LS = 32
 
-
 cheb_coeffs = (0.6, -0.5, 0.35, -0.25, 0.15)
+
+
+def power_coeffs():
+    c0, c1, c2, c3, c4 = cheb_coeffs
+    return (c0 - c2 + c4, c1 - 3.0 * c3, 2.0 * c2 - 8.0 * c4, 4.0 * c3, 8.0 * c4)
+
+
+def lane_ids():
+    return lax.broadcasted_iota(jnp.int32, (8, 128), 1)
+
+
+def sublane_ids():
+    return lax.broadcasted_iota(jnp.int32, (8, 128), 0)
+
+
+def low_half():
+    return (lane_ids() // LS) % 2 == 0
+
+
+def first_of(p, q, low):
+    return jnp.where(low, p, pltpu.roll(q, LS, 1))
+
+
+def second_of(p, q, low):
+    return jnp.where(low, pltpu.roll(p, 128 - LS, 1), q)
+
+
+def z_next(value, z):
+    return jnp.where(z == LS - 1, pltpu.roll(value, LS - 1, 1), pltpu.roll(value, 127, 1))
+
+
+def z_prev(value, z):
+    return jnp.where(z == 0, pltpu.roll(value, 129 - LS, 1), pltpu.roll(value, 1, 1))
+
+
+def x_other(value, even):
+    return jnp.where(even, pltpu.roll(value, 7, 0), pltpu.roll(value, 1, 0))
+
+
+def pack_kernel(src, links, row0, row1, inner, edge, send):
+    low = low_half()
+    z = lane_ids() % LS
+    even = sublane_ids() % 2 == 0
+    half = src.shape[0] // 2
+
+    def tile(ref, index):
+        return jnp.concatenate([ref[index + (slice(0, 8),)], ref[index + (slice(8, 16),)]], axis=1)
+
+    for a in range(3):
+        for b in range(3):
+            for part in range(2):
+                sign = 1.0 - 2.0 * part
+                x_link = tile(links, (0, a, b, part)) * (-1.0 / 6.0)
+                y_link = tile(links, (1, a, b, part)) * (-1.0 / 6.0)
+                z_link = tile(links, (2, a, b, part)) * (-1.0 / 6.0)
+                for row, pick in enumerate((first_of, second_of)):
+                    u_x = pick(x_link, x_link, low)
+                    inner[row, 0, a, b, part] = u_x
+                    u_z = pick(z_link, z_link, low)
+                    inner[row, 1, a, b, part] = u_z
+                    inner[row, 2, b, a, part] = sign * z_prev(u_z, z)
+                u_y = first_of(y_link, y_link, low)
+                inner[0, 3, a, b, part] = u_y
+                inner[1, 3, b, a, part] = sign * u_y
+                edge[a, b, part] = second_of(y_link, y_link, low)
+            y_re = tile(links, (1, a, b, 0)) * (-1.0 / 6.0)
+            y_im = tile(links, (1, a, b, 1)) * (-1.0 / 6.0)
+            send[a, b] = second_of(y_re, y_im, low)
+    for row in range(2):
+        for part in range(2):
+            sign = 1.0 - 2.0 * part
+            own = [[inner[row, 0, a, b, part] for b in range(3)] for a in range(3)]
+            for a in range(3):
+                for b in range(3):
+                    inner[row, 0, a, b, part] = own[a][b] + sign * x_other(own[b][a], even)
+
+    def step(n, carry):
+        for k in range(6):
+            p = tile(src, (n, k))
+            q = tile(src, (n + half, k))
+            row0[n, k] = first_of(p, q, low)
+            row1[n, k] = second_of(p, q, low)
+        return carry
+
+    lax.fori_loop(0, half, step, 0)
+
+
+def mat_vec(load, vectors, sums):
+    for a in range(3):
+        for b in range(3):
+            w_re, w_im = load(a, b)
+            for vec, acc in zip(vectors, sums):
+                v_re, v_im = vec[2 * b], vec[2 * b + 1]
+                acc[2 * a] = acc[2 * a] + w_re * v_re - w_im * v_im
+                acc[2 * a + 1] = acc[2 * a + 1] + w_re * v_im + w_im * v_re
+
+
+def inner_kernel(coeff, width, y0, y1, inner, v0, v1, sum0, sum1):
+    z = lane_ids() % LS
+    even = sublane_ids() % 2 == 0
+
+    def step(i, carry):
+        pairs = [i * width + w for w in range(width)]
+        for row, (here, there, start, out) in enumerate(((y0, y1, v0, sum0), (y1, y0, v1, sum1))):
+            sums = [[coeff * start[n, k] for k in range(6)] for n in pairs]
+
+            def term(index, vectors):
+                mat_vec(
+                    lambda a, b: (inner[row, index, a, b, 0], inner[row, index, a, b, 1]),
+                    vectors,
+                    sums,
+                )
+
+            term(0, [[x_other(here[n, k], even) for k in range(6)] for n in pairs])
+            term(1, [[z_next(here[n, k], z) for k in range(6)] for n in pairs])
+            term(2, [[z_prev(here[n, k], z) for k in range(6)] for n in pairs])
+            term(3, [[there[n, k] for k in range(6)] for n in pairs])
+            for n, acc in zip(pairs, sums):
+                for k in range(6):
+                    out[n, k] = acc[k]
+        return carry
+
+    lax.fori_loop(0, y0.shape[0] // width, step, 0)
+
+
+def edge_sums(pairs, below, above, edge, links_below, sum0, sum1):
+    acc0 = [[sum0[n, k] for k in range(6)] for n in pairs]
+    mat_vec(
+        lambda a, b: (links_below[b, a, 0], links_below[b, a, 1]),
+        [[below[n, k] for k in range(6)] for n in pairs],
+        acc0,
+    )
+    acc1 = [[sum1[n, k] for k in range(6)] for n in pairs]
+    mat_vec(
+        lambda a, b: (edge[a, b, 0], edge[a, b, 1]),
+        [[above[n, k] for k in range(6)] for n in pairs],
+        acc1,
+    )
+    return acc0, acc1
+
+
+def unpack_links(received, links_below, low):
+    for a in range(3):
+        for b in range(3):
+            w = received[a, b]
+            links_below[a, b, 0] = first_of(w, w, low)
+            links_below[a, b, 1] = -second_of(w, w, low)
+
+
+def edge_kernel(width, below, above, edge, received, sum0, sum1, row0, row1, links_below):
+    unpack_links(received, links_below, low_half())
+
+    def step(i, carry):
+        pairs = [i * width + w for w in range(width)]
+        acc0, acc1 = edge_sums(pairs, below, above, edge, links_below, sum0, sum1)
+        for n, top, bottom in zip(pairs, acc0, acc1):
+            for k in range(6):
+                row0[n, k] = top[k]
+                row1[n, k] = bottom[k]
+        return carry
+
+    lax.fori_loop(0, below.shape[0] // width, step, 0)
+
+
+def last_kernel(width, lead, below, above, edge, received, sum0, sum1, out, links_below):
+    low = low_half()
+    unpack_links(received, links_below, low)
+    half = below.shape[0]
+
+    def step(i, carry):
+        pairs = [i * width + w for w in range(width)]
+        acc0, acc1 = edge_sums(pairs, below, above, edge, links_below, sum0, sum1)
+        for n, top, bottom in zip(pairs, acc0, acc1):
+            for k in range(6):
+                p = first_of(top[k], bottom[k], low) * lead
+                q = second_of(top[k], bottom[k], low) * lead
+                for m, value in ((n, p), (n + half, q)):
+                    out[m, k, 0:8] = value[:, : 2 * LS]
+                    out[m, k, 8:16] = value[:, 2 * LS :]
+        return carry
+
+    lax.fori_loop(0, half // width, step, 0)
+
+
+VMEM_LIMIT = 32 * 1024 * 1024
+
+
+def call(kernel, outs, args, flops, scratch=()):
+    moved = sum(4 * a.size for a in args) + sum(4 * o.size for o in outs)
+    return pl.pallas_call(
+        kernel,
+        out_shape=outs,
+        in_specs=[pl.BlockSpec(memory_space=pltpu.VMEM)] * len(args),
+        out_specs=[pl.BlockSpec(memory_space=pltpu.VMEM)] * len(outs),
+        scratch_shapes=list(scratch),
+        compiler_params=pltpu.CompilerParams(vmem_limit_bytes=VMEM_LIMIT),
+        cost_estimate=pl.CostEstimate(flops=flops, bytes_accessed=moved, transcendentals=0),
+    )(*args)
+
+
+def halo_body(links, sources):
+    vectors = sources.shape[0]
+    half = vectors // 2
+    width = 2
+    sites, planes = links.shape[4:]
+    f32 = functools.partial(jax.ShapeDtypeStruct, dtype=jnp.float32)
+    field = f32((half, 6, 8, 128))
+    inner_shape = f32((2, 4, 3, 3, 2, 8, 128))
+    edge_shape = f32((3, 3, 2, 8, 128))
+    send_shape = f32((3, 3, 8, 128))
+    source_view = jnp.swapaxes(sources, 3, 4).reshape(vectors, 6, planes, sites)
+    link_view = jnp.swapaxes(links, 4, 5)
+    powers = power_coeffs()
+    lead = powers[4]
+    work = 2 * half * 36 * 2 * 1024
+
+    v0, v1, inner, edge, link_send = call(
+        pack_kernel,
+        [field, field, inner_shape, edge_shape, send_shape],
+        [source_view, link_view],
+        2 * half * 6 * 1024,
+    )
+    count = lax.axis_size("space")
+    up = [(d, (d + 1) % count) for d in range(count)]
+    down = [(d, (d - 1) % count) for d in range(count)]
+    received = lax.ppermute(link_send, "space", up)
+    y0, y1 = v0, v1
+    for power in (3, 2, 1, 0):
+        below = lax.ppermute(y1, "space", up)
+        above = lax.ppermute(y0, "space", down)
+        sum0, sum1 = call(
+            functools.partial(inner_kernel, powers[power] / lead, width),
+            [field, field],
+            [y0, y1, inner, v0, v1],
+            4 * work,
+        )
+        args = [below, above, edge, received, sum0, sum1]
+        scratch = [pltpu.VMEM(edge_shape.shape, jnp.float32)]
+        if power:
+            y0, y1 = call(
+                functools.partial(edge_kernel, width), [field, field], args, work, scratch
+            )
+        else:
+            (out,) = call(
+                functools.partial(last_kernel, width, lead),
+                [f32(source_view.shape)],
+                args,
+                work,
+                scratch,
+            )
+    return jnp.swapaxes(out.reshape(vectors, 3, 2, planes, sites), 3, 4)
 
 
 def shifted(value, axis, steps):
@@ -54,7 +308,7 @@
     )
 
 
-def body(links, sources):
+def plane_body(links, sources):
     device_count = lax.axis_size("space")
     slabs = device_count // NT
     yz_local = links.shape[4]
@@ -122,6 +376,13 @@
     return ordered.reshape(vectors, 3, 2, yz_local, NT * slabs * planes)
 
 
+def body(links, sources):
+    sites, planes = sources.shape[3:]
+    if sites == 2 * LS and planes == 2 * NT and sources.shape[0] % 4 == 0:
+        return halo_body(links, sources)
+    return plane_body(links, sources)
+
+
 def solution(mesh):
     in_specs = (
         P(None, None, None, None, "space", "groups"),

time: 325 us -> 49.6 us (0.15)
  waiting for transfers between devices: 163 us -> 29.5 us
  other arithmetic: 73.5 us -> 0 us
  blocking collectives: 28.9 us -> 0 us
  local copies, waits for them, and re-layouts: 30.4 us -> 2.28 us
  starting transfers between devices: 23.5 us -> 6.07 us
  Pallas kernels: 0 us -> 11.4 us
    ppermute x8 -> x9, waiting for transfers between devices: 137 us -> 29.5 us  [the longest x4 12.8 us: halo_body(): below = lax.ppermute(y1, 'space', up)]
    all_to_all x1 -> x0, blocking collectives: 28.9 us -> none  [body(): lax.all_to_all(outgoing, 'space', split_axis=3, concat_axis=1, tiled=True)]
    all_to_all x2 -> x0, waiting for transfers between devices: 26.8 us -> none  [the longest x1 19.6 us: body(): lax.all_to_all(source_send, 'space', split_axis=1, concat_axis=3, tiled=T...]
    sub x14 -> x0, other arithmetic: 26.3 us -> none  [the longest x12 20.7 us: apply_link(): real_part = real_part + link_re * vec_re - link_im * vec_im]
    add x13 -> x0, other arithmetic: 25.1 us -> none  [the longest x12 21.7 us: apply_dagger(): real_part = real_part + link_re * vec_re + link_im * vec_im]
    slice x53 -> x0, local copies, waits for them, and re-layouts: 17 us -> none  [the longest x8 3.3 us: z_ahead(): jnp.roll(array, -1, axis=-1)]
    all_to_all x2 -> x0, starting transfers between devices: 12.1 us -> none  [the longest x1 7.32 us: body(): lax.all_to_all(link_send, 'space', split_axis=1, concat_axis=3, tiled=True)]
    pallas_call x0 -> x9, Pallas kernels: none -> 11.4 us  [call(): pl.pallas_call(kernel, out_shape=outs, in_specs=[pl.BlockSpec(memory_spac...]
  transfers between devices with their start and end apart: 10 -> 9, of which waited for: 10 -> 8; matrix products, arithmetic and copies ran while one was open for 22% -> 0% of each run, Pallas kernels for 0% -> 10%
where the time goes in v1:
time: 49.6 us; the launch traced here: 49.4 us
  waiting for transfers between devices  29.5 us (59%)
  Pallas kernels  11.4 us (23%)
  starting transfers between devices  6.07 us (12%)
  local copies, waits for them, and re-layouts  2.28 us (5%)
    ppermute x4, waiting for transfers between devices, halo_body(): below = lax.ppermute(y1, 'space', up)  12.8 us
    ppermute x4, waiting for transfers between devices, halo_body(): above = lax.ppermute(y0, 'space', down)  12.5 us
    pallas_call x9, Pallas kernels, call(): pl.pallas_call(kernel, out_shape=outs, in_specs=[pl.BlockSpec(memory_spac...  11.4 us
    ppermute x1, waiting for transfers between devices, halo_body(): received = lax.ppermute(link_send, 'space', up)  4.23 us
    ppermute x4, starting transfers between devices, halo_body(): below = lax.ppermute(y1, 'space', up)  2.83 us
    unnamed x4, local copies, waits for them, and re-layouts  2.28 us
    ppermute x1, starting transfers between devices, halo_body(): received = lax.ppermute(link_send, 'space', up)  1.74 us
    ppermute x4, starting transfers between devices, halo_body(): above = lax.ppermute(y0, 'space', down)  1.49 us
  transfers between devices with their start and end apart: 9, of which 8 were waited for; matrix products, arithmetic and copies ran while one was open for 0% of the time, Pallas kernels for 10%

profile of v1, /device:TPU:1, one launch (start us, length us, event | category | flops | bytes accessed | tf_op | source)
XLA Modules:
  0.0 49.4 jit_solution(9454367433338890048)
XLA Ops:
  0.0 1.3 %copy-done = f32[24,3,2,64,16]{3,4,2,1,0:T(8,128)S(1)} copy-done((f32[24,3,2,64,16]{3,4,2,1,0:T(8,128)S(1)}, f32[24,3,2,64,16]{3,4,2,1,0:T(8,128)}, u32[]{:S(2)}) %copy-start) | copy-done | bytes 589848
  1.3 1.0 %copy-done.1 = f32[3,3,3,2,64,16]{4,5,3,2,1,0:T(8,128)S(1)} copy-done((f32[3,3,3,2,64,16]{4,5,3,2,1,0:T(8,128)S(1)}, f32[3,3,3,2,64,16]{4,5,3,2,1,0:T(8,128)}, u32[]{:S(2)}) %copy-start.1) | copy-done | bytes 221208
  2.3 3.1 %shard_map.28 = (f32[12,6,8,128]{3,2,1,0:T(8,128)S(1)}, f32[12,6,8,128]{3,2,1,0:T(8,128)S(1)}, f32[2,4,3,3,2,8,128]{6,5,4,3,2,1,0:T(8,128)S(1)}, f32[3,3,2,8,128]{4,3,2,1,0:T(8,128)S(1)}, f32[3,3,8,128]{3,2,1,0:T(8,128)S(1)}) custom-call(f32[24,6,16,64]{3,2,1,0:T(8,128)S(1)} %bitcast.7, f32[3,3,3,2,16,64]{5,4,3,2,1,0:T(8,128)S(1)} %bitcast.8), custom_call_target="tpu_custom_call" | custom-call | flops 147456 | bytes 2101248 | tf_op jit(solution)/shard_map/pallas_call | solution.py:203
  5.4 2.7 %collective-permute-start = (f32[12,6,8,128]{3,2,1,0:T(8,128)S(1)}, f32[12,6,8,128]{3,2,1,0:T(8,128)S(1)}, u32[]{:S(2)}, u32[]{:S(2)}) collective-permute-start(f32[12,6,8,128]{3,2,1,0:T(8,128)S(1)} %get-tuple-element.24.y1.v1), channel_id=1, source_target_pairs={{0,1},{1,2},{2,3},{3,4},{4,5},{5,6},{6,7},{7,8},{8,9},{9,10},{10,1... | collective-permute-start | bytes 884744 | tf_op jit(solution)/shard_map/ppermute | solution.py:242
  8.1 1.7 %collective-permute-start.2 = (f32[3,3,8,128]{3,2,1,0:T(8,128)S(1)}, f32[3,3,8,128]{3,2,1,0:T(8,128)S(1)}, u32[]{:S(2)}, u32[]{:S(2)}) collective-permute-start(f32[3,3,8,128]{3,2,1,0:T(8,128)S(1)} %get-tuple-element.27), channel_id=1, source_target_pairs={{0,1},{1,2},{2,3},{3,4},{4,5},{5,6},{6,7},{7,8},{8,9},{9,10},{10,1... | collective-permute-start | bytes 110600 | tf_op jit(solution)/shard_map/ppermute | solution.py:239
  9.8 1.2 %shard_map.29 = (f32[12,6,8,128]{3,2,1,0:T(8,128)S(1)}, f32[12,6,8,128]{3,2,1,0:T(8,128)S(1)}) custom-call(f32[12,6,8,128]{3,2,1,0:T(8,128)S(1)} %get-tuple-element.25.y0.v0, f32[12,6,8,128]{3,2,1,0:T(8,128)S(1)} %get-tuple-element.24.y1.v1, f32[2,4,3,3,2,8,128]{6,5,4,3,2,1,0:T(8,128)S(1)} %get-tuple-element.28.inner, ...), custom_call_target="tpu_custom_call" | custom-call | flops 7077888 | bytes 2359296 | tf_op jit(solution)/shard_map/pallas_call | solution.py:203
  11.0 4.2 %collective-permute-done.2.received = f32[3,3,8,128]{3,2,1,0:T(8,128)S(1)} collective-permute-done((f32[3,3,8,128]{3,2,1,0:T(8,128)S(1)}, f32[3,3,8,128]{3,2,1,0:T(8,128)S(1)}, u32[]{:S(2)}, u32[]{:S(2)}) %collective-permute-start.2) | collective-permute-done | bytes 36896 | tf_op jit(solution)/shard_map/ppermute | solution.py:239
  15.3 2.5 %collective-permute-done.1.above = f32[12,6,8,128]{3,2,1,0:T(8,128)S(1)} collective-permute-done((f32[12,6,8,128]{3,2,1,0:T(8,128)S(1)}, f32[12,6,8,128]{3,2,1,0:T(8,128)S(1)}, u32[]{:S(2)}, u32[]{:S(2)}) %collective-permute-start.1) | collective-permute-done | bytes 294944 | tf_op jit(solution)/shard_map/ppermute | solution.py:243
  17.8 0.4 shard_map.30
  18.2 0.5 %collective-permute-start.4 = (f32[12,6,8,128]{3,2,1,0:T(8,128)S(1)}, f32[12,6,8,128]{3,2,1,0:T(8,128)S(1)}, u32[]{:S(2)}, u32[]{:S(2)}) collective-permute-start(f32[12,6,8,128]{3,2,1,0:T(8,128)S(1)} %get-tuple-element.32.y0), channel_id=1, source_target_pairs={{0,15},{1,0},{2,1},{3,2},{4,3},{5,4},{6,5},{7,6},{8,7},{9,8},{10,9... | collective-permute-start | bytes 884744 | tf_op jit(solution)/shard_map/ppermute | solution.py:243
  18.7 1.3 %shard_map.31 = (f32[12,6,8,128]{3,2,1,0:T(8,128)S(1)}, f32[12,6,8,128]{3,2,1,0:T(8,128)S(1)}) custom-call(f32[12,6,8,128]{3,2,1,0:T(8,128)S(1)} %get-tuple-element.32.y0, f32[12,6,8,128]{3,2,1,0:T(8,128)S(1)} %get-tuple-element.31.y1, f32[2,4,3,3,2,8,128]{6,5,4,3,2,1,0:T(8,128)S(1)} %get-tuple-element.28.inner, ...), custom_call_target="tpu_custom_call" | custom-call | flops 7077888 | bytes 2359296 | tf_op jit(solution)/shard_map/pallas_call | solution.py:203
  20.0 5.1 %collective-permute-done.3.below = f32[12,6,8,128]{3,2,1,0:T(8,128)S(1)} collective-permute-done((f32[12,6,8,128]{3,2,1,0:T(8,128)S(1)}, f32[12,6,8,128]{3,2,1,0:T(8,128)S(1)}, u32[]{:S(2)}, u32[]{:S(2)}) %collective-permute-start.3) | collective-permute-done | bytes 294944 | tf_op jit(solution)/shard_map/ppermute | solution.py:242
  25.0 2.5 %collective-permute-done.4.above = f32[12,6,8,128]{3,2,1,0:T(8,128)S(1)} collective-permute-done((f32[12,6,8,128]{3,2,1,0:T(8,128)S(1)}, f32[12,6,8,128]{3,2,1,0:T(8,128)S(1)}, u32[]{:S(2)}, u32[]{:S(2)}) %collective-permute-start.4) | collective-permute-done | bytes 294944 | tf_op jit(solution)/shard_map/ppermute | solution.py:243
  27.6 0.4 shard_map.32
  28.0 0.5 %collective-permute-start.6 = (f32[12,6,8,128]{3,2,1,0:T(8,128)S(1)}, f32[12,6,8,128]{3,2,1,0:T(8,128)S(1)}, u32[]{:S(2)}, u32[]{:S(2)}) collective-permute-start(f32[12,6,8,128]{3,2,1,0:T(8,128)S(1)} %get-tuple-element.36.y0), channel_id=1, source_target_pairs={{0,15},{1,0},{2,1},{3,2},{4,3},{5,4},{6,5},{7,6},{8,7},{9,8},{10,9... | collective-permute-start | bytes 884744 | tf_op jit(solution)/shard_map/ppermute | solution.py:243
  28.5 1.2 %shard_map.33 = (f32[12,6,8,128]{3,2,1,0:T(8,128)S(1)}, f32[12,6,8,128]{3,2,1,0:T(8,128)S(1)}) custom-call(f32[12,6,8,128]{3,2,1,0:T(8,128)S(1)} %get-tuple-element.36.y0, f32[12,6,8,128]{3,2,1,0:T(8,128)S(1)} %get-tuple-element.35.y1, f32[2,4,3,3,2,8,128]{6,5,4,3,2,1,0:T(8,128)S(1)} %get-tuple-element.28.inner, ...), custom_call_target="tpu_custom_call" | custom-call | flops 7077888 | bytes 2359296 | tf_op jit(solution)/shard_map/pallas_call | solution.py:203
  29.8 4.2 %collective-permute-done.5.below = f32[12,6,8,128]{3,2,1,0:T(8,128)S(1)} collective-permute-done((f32[12,6,8,128]{3,2,1,0:T(8,128)S(1)}, f32[12,6,8,128]{3,2,1,0:T(8,128)S(1)}, u32[]{:S(2)}, u32[]{:S(2)}) %collective-permute-start.5) | collective-permute-done | bytes 294944 | tf_op jit(solution)/shard_map/ppermute | solution.py:242
  34.0 3.4 %collective-permute-done.6.above = f32[12,6,8,128]{3,2,1,0:T(8,128)S(1)} collective-permute-done((f32[12,6,8,128]{3,2,1,0:T(8,128)S(1)}, f32[12,6,8,128]{3,2,1,0:T(8,128)S(1)}, u32[]{:S(2)}, u32[]{:S(2)}) %collective-permute-start.6) | collective-permute-done | bytes 294944 | tf_op jit(solution)/shard_map/ppermute | solution.py:243
  37.4 0.4 shard_map.34
  37.8 0.5 %collective-permute-start.8 = (f32[12,6,8,128]{3,2,1,0:T(8,128)S(1)}, f32[12,6,8,128]{3,2,1,0:T(8,128)S(1)}, u32[]{:S(2)}, u32[]{:S(2)}) collective-permute-start(f32[12,6,8,128]{3,2,1,0:T(8,128)S(1)} %get-tuple-element.40.y0), channel_id=1, source_target_pairs={{0,15},{1,0},{2,1},{3,2},{4,3},{5,4},{6,5},{7,6},{8,7},{9,8},{10,9... | collective-permute-start | bytes 884744 | tf_op jit(solution)/shard_map/ppermute | solution.py:243
  38.3 1.2 %shard_map.35 = (f32[12,6,8,128]{3,2,1,0:T(8,128)S(1)}, f32[12,6,8,128]{3,2,1,0:T(8,128)S(1)}) custom-call(f32[12,6,8,128]{3,2,1,0:T(8,128)S(1)} %get-tuple-element.40.y0, f32[12,6,8,128]{3,2,1,0:T(8,128)S(1)} %get-tuple-element.39.y1, f32[2,4,3,3,2,8,128]{6,5,4,3,2,1,0:T(8,128)S(1)} %get-tuple-element.28.inner, ...), custom_call_target="tpu_custom_call" | custom-call | flops 7077888 | bytes 2359296 | tf_op jit(solution)/shard_map/pallas_call | solution.py:203
  39.6 3.5 %collective-permute-done.7.below = f32[12,6,8,128]{3,2,1,0:T(8,128)S(1)} collective-permute-done((f32[12,6,8,128]{3,2,1,0:T(8,128)S(1)}, f32[12,6,8,128]{3,2,1,0:T(8,128)S(1)}, u32[]{:S(2)}, u32[]{:S(2)}) %collective-permute-start.7) | collective-permute-done | bytes 294944 | tf_op jit(solution)/shard_map/ppermute | solution.py:242
  43.1 4.1 %collective-permute-done.8.above = f32[12,6,8,128]{3,2,1,0:T(8,128)S(1)} collective-permute-done((f32[12,6,8,128]{3,2,1,0:T(8,128)S(1)}, f32[12,6,8,128]{3,2,1,0:T(8,128)S(1)}, u32[]{:S(2)}, u32[]{:S(2)}) %collective-permute-start.8) | collective-permute-done | bytes 294944 | tf_op jit(solution)/shard_map/ppermute | solution.py:243
  47.2 2.2 %shard_map.36 = f32[24,6,16,64]{3,2,1,0:T(8,128)} custom-call(f32[12,6,8,128]{3,2,1,0:T(8,128)S(1)} %collective-permute-done.7.below, f32[12,6,8,128]{3,2,1,0:T(8,128)S(1)} %collective-permute-done.8.above, f32[3,3,2,8,128]{4,3,2,1,0:T(8,128)S(1)} %get-tuple-element.26.edge, f32[3,3,8,128]{3,2,1,0:T(8,128)S(1)} %collective-permute-done.2.received, ...), custom_call_target="tpu_custom_call" | custom-call | flops 1769472 | bytes 1880064 | tf_op jit(solution)/shard_map/pallas_call | solution.py:203
  (7 shorter events, 0.2 us)
Async XLA Ops:
  0.0 1.3 %copy-start = (f32[24,3,2,64,16]{3,4,2,1,0:T(8,128)S(1)}, f32[24,3,2,64,16]{3,4,2,1,0:T(8,128)}, u32[]{:S(2)}) copy-start(f32[24,3,2,64,16]{3,4,2,1,0:T(8,128)} %param.3) | copy-start | bytes 1769476
  1.3 1.0 %copy-start.1 = (f32[3,3,3,2,64,16]{4,5,3,2,1,0:T(8,128)S(1)}, f32[3,3,3,2,64,16]{4,5,3,2,1,0:T(8,128)}, u32[]{:S(2)}) copy-start(f32[3,3,3,2,64,16]{4,5,3,2,1,0:T(8,128)} %param.2) | copy-start | bytes 663556
  5.4 9.9 %collective-permute-start = (f32[12,6,8,128]{3,2,1,0:T(8,128)S(1)}, f32[12,6,8,128]{3,2,1,0:T(8,128)S(1)}, u32[]{:S(2)}, u32[]{:S(2)}) collective-permute-start(f32[12,6,8,128]{3,2,1,0:T(8,128)S(1)} %get-tuple-element.24.y1.v1), channel_id=1, source_target_pairs={{0,1},{1,2},{2,3},{3,4},{4,5},{5,6},{6,7},{7,8},{8,9},{9,10},{10,1... | collective-permute-start | bytes 884744 | tf_op jit(solution)/shard_map/ppermute | solution.py:242
  8.0 9.7 %collective-permute-start.1 = (f32[12,6,8,128]{3,2,1,0:T(8,128)S(1)}, f32[12,6,8,128]{3,2,1,0:T(8,128)S(1)}, u32[]{:S(2)}, u32[]{:S(2)}) collective-permute-start(f32[12,6,8,128]{3,2,1,0:T(8,128)S(1)} %get-tuple-element.25.y0.v0), channel_id=1, source_target_pairs={{0,15},{1,0},{2,1},{3,2},{4,3},{5,4},{6,5},{7,6},{8,7},{9,8},{10,9... | collective-permute-start | bytes 884744 | tf_op jit(solution)/shard_map/ppermute | solution.py:243
  8.1 7.2 %collective-permute-start.2 = (f32[3,3,8,128]{3,2,1,0:T(8,128)S(1)}, f32[3,3,8,128]{3,2,1,0:T(8,128)S(1)}, u32[]{:S(2)}, u32[]{:S(2)}) collective-permute-start(f32[3,3,8,128]{3,2,1,0:T(8,128)S(1)} %get-tuple-element.27), channel_id=1, source_target_pairs={{0,1},{1,2},{2,3},{3,4},{4,5},{5,6},{6,7},{7,8},{8,9},{9,10},{10,1... | collective-permute-start | bytes 110600 | tf_op jit(solution)/shard_map/ppermute | solution.py:239
  18.1 6.9 %collective-permute-start.3 = (f32[12,6,8,128]{3,2,1,0:T(8,128)S(1)}, f32[12,6,8,128]{3,2,1,0:T(8,128)S(1)}, u32[]{:S(2)}, u32[]{:S(2)}) collective-permute-start(f32[12,6,8,128]{3,2,1,0:T(8,128)S(1)} %get-tuple-element.31.y1), channel_id=1, source_target_pairs={{0,1},{1,2},{2,3},{3,4},{4,5},{5,6},{6,7},{7,8},{8,9},{9,10},{10,1... | collective-permute-start | bytes 884744 | tf_op jit(solution)/shard_map/ppermute | solution.py:242
  18.2 9.4 %collective-permute-start.4 = (f32[12,6,8,128]{3,2,1,0:T(8,128)S(1)}, f32[12,6,8,128]{3,2,1,0:T(8,128)S(1)}, u32[]{:S(2)}, u32[]{:S(2)}) collective-permute-start(f32[12,6,8,128]{3,2,1,0:T(8,128)S(1)} %get-tuple-element.32.y0), channel_id=1, source_target_pairs={{0,15},{1,0},{2,1},{3,2},{4,3},{5,4},{6,5},{7,6},{8,7},{9,8},{10,9... | collective-permute-start | bytes 884744 | tf_op jit(solution)/shard_map/ppermute | solution.py:243
  27.9 6.1 %collective-permute-start.5 = (f32[12,6,8,128]{3,2,1,0:T(8,128)S(1)}, f32[12,6,8,128]{3,2,1,0:T(8,128)S(1)}, u32[]{:S(2)}, u32[]{:S(2)}) collective-permute-start(f32[12,6,8,128]{3,2,1,0:T(8,128)S(1)} %get-tuple-element.35.y1), channel_id=1, source_target_pairs={{0,1},{1,2},{2,3},{3,4},{4,5},{5,6},{6,7},{7,8},{8,9},{9,10},{10,1... | collective-permute-start | bytes 884744 | tf_op jit(solution)/shard_map/ppermute | solution.py:242
  28.0 9.4 %collective-permute-start.6 = (f32[12,6,8,128]{3,2,1,0:T(8,128)S(1)}, f32[12,6,8,128]{3,2,1,0:T(8,128)S(1)}, u32[]{:S(2)}, u32[]{:S(2)}) collective-permute-start(f32[12,6,8,128]{3,2,1,0:T(8,128)S(1)} %get-tuple-element.36.y0), channel_id=1, source_target_pairs={{0,15},{1,0},{2,1},{3,2},{4,3},{5,4},{6,5},{7,6},{8,7},{9,8},{10,9... | collective-permute-start | bytes 884744 | tf_op jit(solution)/shard_map/ppermute | solution.py:243
  37.7 5.3 %collective-permute-start.7 = (f32[12,6,8,128]{3,2,1,0:T(8,128)S(1)}, f32[12,6,8,128]{3,2,1,0:T(8,128)S(1)}, u32[]{:S(2)}, u32[]{:S(2)}) collective-permute-start(f32[12,6,8,128]{3,2,1,0:T(8,128)S(1)} %get-tuple-element.39.y1), channel_id=1, source_target_pairs={{0,1},{1,2},{2,3},{3,4},{4,5},{5,6},{6,7},{7,8},{8,9},{9,10},{10,1... | collective-permute-start | bytes 884744 | tf_op jit(solution)/shard_map/ppermute | solution.py:242
  37.8 9.4 %collective-permute-start.8 = (f32[12,6,8,128]{3,2,1,0:T(8,128)S(1)}, f32[12,6,8,128]{3,2,1,0:T(8,128)S(1)}, u32[]{:S(2)}, u32[]{:S(2)}) collective-permute-start(f32[12,6,8,128]{3,2,1,0:T(8,128)S(1)} %get-tuple-element.40.y0), channel_id=1, source_target_pairs={{0,15},{1,0},{2,1},{3,2},{4,3},{5,4},{6,5},{7,6},{8,7},{9,8},{10,9... | collective-permute-start | bytes 884744 | tf_op jit(solution)/shard_map/ppermute | solution.py:243

commit v2 on v1

--- a/solution.py
+++ b/solution.py
@@ -50,15 +50,91 @@
     return jnp.where(even, pltpu.roll(value, 7, 0), pltpu.roll(value, 1, 0))
 
 
-def pack_kernel(src, links, row0, row1, inner, edge, send):
+def mat_vec(load, vectors, sums, dagger=False):
+    for a in range(3):
+        for b in range(3):
+            w_re, w_im = load(b, a) if dagger else load(a, b)
+            for vec, acc in zip(vectors, sums):
+                v_re, v_im = vec[2 * b], vec[2 * b + 1]
+                if dagger:
+                    acc[2 * a] = acc[2 * a] + w_re * v_re + w_im * v_im
+                    acc[2 * a + 1] = acc[2 * a + 1] + w_re * v_im - w_im * v_re
+                else:
+                    acc[2 * a] = acc[2 * a] + w_re * v_re - w_im * v_im
+                    acc[2 * a + 1] = acc[2 * a + 1] + w_re * v_im + w_im * v_re
+
+
+def zeros(count):
+    return [[jnp.zeros((8, 128), jnp.float32) for _ in range(6)] for _ in range(count)]
+
+
+def edge_link(edge):
+    return lambda a, b: (edge[a, b, 0], edge[a, b, 1])
+
+
+def tile(ref, index):
+    return jnp.concatenate([ref[index + (slice(0, 8),)], ref[index + (slice(8, 16),)]], axis=1)
+
+
+def pack_edge(links, edge):
+    low = low_half()
+    for a in range(3):
+        for b in range(3):
+            for part in range(2):
+                y_link = tile(links, (a, b, part)) * (-1.0 / 6.0)
+                edge[a, b, part] = second_of(y_link, y_link, low)
+
+
+def pack_sources(first, src, edge, row0, row1, up, arrived, sems):
+    low = low_half()
+    pairs = row0.shape[0]
+
+    def fetch(i):
+        here = pl.ds(2 * i, 2)
+        there = pl.ds(first + 2 * i, 2)
+        return pltpu.make_async_copy(src.at[there], arrived.at[here], sems.at[i])
+
+    for i in range(pairs):
+        fetch(i).start()
+
+    def finish():
+        def step(i, carry):
+            fetch(i).wait()
+            upper = []
+            for k in range(6):
+                p = tile(arrived, (2 * i, k))
+                q = tile(arrived, (2 * i + 1, k))
+                row0[i, k] = first_of(p, q, low)
+                upper.append(second_of(p, q, low))
+                row1[i, k] = upper[k]
+            sums = zeros(1)
+            mat_vec(edge_link(edge), [upper], sums, dagger=True)
+            for k in range(6):
+                up[i, k] = sums[0][k]
+            return carry
+
+        lax.fori_loop(0, pairs, step, 0)
+
+    return finish
+
+
+def first_pack_kernel(first, src, links, edge, row0, row1, up, arrived, y_links, sems, link_sem):
+    link_copy = pltpu.make_async_copy(links.at[1], y_links, link_sem)
+    link_copy.start()
+    finish = pack_sources(first, src, edge, row0, row1, up, arrived, sems)
+    link_copy.wait()
+    pack_edge(y_links, edge)
+    finish()
+
+
+def pack_kernel(first, src, edge, row0, row1, up, arrived, sems):
+    pack_sources(first, src, edge, row0, row1, up, arrived, sems)()
+
+
+def link_kernel(links, inner):
     low = low_half()
     z = lane_ids() % LS
     even = sublane_ids() % 2 == 0
-    half = src.shape[0] // 2
-
-    def tile(ref, index):
-        return jnp.concatenate([ref[index + (slice(0, 8),)], ref[index + (slice(8, 16),)]], axis=1)
-
     for a in range(3):
         for b in range(3):
             for part in range(2):
@@ -67,18 +143,13 @@
                 y_link = tile(links, (1, a, b, part)) * (-1.0 / 6.0)
                 z_link = tile(links, (2, a, b, part)) * (-1.0 / 6.0)
                 for row, pick in enumerate((first_of, second_of)):
-                    u_x = pick(x_link, x_link, low)
-                    inner[row, 0, a, b, part] = u_x
+                    inner[row, 0, a, b, part] = pick(x_link, x_link, low)
                     u_z = pick(z_link, z_link, low)
                     inner[row, 1, a, b, part] = u_z
                     inner[row, 2, b, a, part] = sign * z_prev(u_z, z)
                 u_y = first_of(y_link, y_link, low)
                 inner[0, 3, a, b, part] = u_y
                 inner[1, 3, b, a, part] = sign * u_y
-                edge[a, b, part] = second_of(y_link, y_link, low)
-            y_re = tile(links, (1, a, b, 0)) * (-1.0 / 6.0)
-            y_im = tile(links, (1, a, b, 1)) * (-1.0 / 6.0)
-            send[a, b] = second_of(y_re, y_im, low)
     for row in range(2):
         for part in range(2):
             sign = 1.0 - 2.0 * part
@@ -86,26 +157,6 @@
             for a in range(3):
                 for b in range(3):
                     inner[row, 0, a, b, part] = own[a][b] + sign * x_other(own[b][a], even)
-
-    def step(n, carry):
-        for k in range(6):
-            p = tile(src, (n, k))
-            q = tile(src, (n + half, k))
-            row0[n, k] = first_of(p, q, low)
-            row1[n, k] = second_of(p, q, low)
-        return carry
-
-    lax.fori_loop(0, half, step, 0)
-
-
-def mat_vec(load, vectors, sums):
-    for a in range(3):
-        for b in range(3):
-            w_re, w_im = load(a, b)
-            for vec, acc in zip(vectors, sums):
-                v_re, v_im = vec[2 * b], vec[2 * b + 1]
-                acc[2 * a] = acc[2 * a] + w_re * v_re - w_im * v_im
-                acc[2 * a + 1] = acc[2 * a + 1] + w_re * v_im + w_im * v_re
 
 
 def inner_kernel(coeff, width, y0, y1, inner, v0, v1, sum0, sum1):
@@ -136,76 +187,77 @@
     lax.fori_loop(0, y0.shape[0] // width, step, 0)
 
 
-def edge_sums(pairs, below, above, edge, links_below, sum0, sum1):
-    acc0 = [[sum0[n, k] for k in range(6)] for n in pairs]
-    mat_vec(
-        lambda a, b: (links_below[b, a, 0], links_below[b, a, 1]),
-        [[below[n, k] for k in range(6)] for n in pairs],
-        acc0,
-    )
-    acc1 = [[sum1[n, k] for k in range(6)] for n in pairs]
-    mat_vec(
-        lambda a, b: (edge[a, b, 0], edge[a, b, 1]),
-        [[above[n, k] for k in range(6)] for n in pairs],
-        acc1,
-    )
-    return acc0, acc1
-
-
-def unpack_links(received, links_below, low):
-    for a in range(3):
-        for b in range(3):
-            w = received[a, b]
-            links_below[a, b, 0] = first_of(w, w, low)
-            links_below[a, b, 1] = -second_of(w, w, low)
-
-
-def edge_kernel(width, below, above, edge, received, sum0, sum1, row0, row1, links_below):
-    unpack_links(received, links_below, low_half())
-
+def edge_sums(pairs, below, above, edge, sum0, sum1):
+    lower = [[sum0[n, k] + below[n, k] for k in range(6)] for n in pairs]
+    upper = [[sum1[n, k] for k in range(6)] for n in pairs]
+    mat_vec(edge_link(edge), [[above[n, k] for k in range(6)] for n in pairs], upper)
+    return lower, upper
+
+
+def edge_kernel(width, below, above, edge, sum0, sum1, row0, row1, up):
     def step(i, carry):
         pairs = [i * width + w for w in range(width)]
-        acc0, acc1 = edge_sums(pairs, below, above, edge, links_below, sum0, sum1)
-        for n, top, bottom in zip(pairs, acc0, acc1):
+        lower, upper = edge_sums(pairs, below, above, edge, sum0, sum1)
+        back = zeros(width)
+        mat_vec(edge_link(edge), upper, back, dagger=True)
+        for n, bottom, top, product in zip(pairs, lower, upper, back):
             for k in range(6):
-                row0[n, k] = top[k]
-                row1[n, k] = bottom[k]
+                row0[n, k] = bottom[k]
+                row1[n, k] = top[k]
+                up[n, k] = product[k]
         return carry
 
     lax.fori_loop(0, below.shape[0] // width, step, 0)
 
 
-def last_kernel(width, lead, below, above, edge, received, sum0, sum1, out, links_below):
+def last_kernel(first, lead, below, above, edge, sum0, sum1, *rest):
+    out, filled, sems = rest[-3:]
     low = low_half()
-    unpack_links(received, links_below, low)
-    half = below.shape[0]
+    pairs = below.shape[0]
+
+    def store(i):
+        here = pl.ds(2 * i, 2)
+        there = pl.ds(first + 2 * i, 2)
+        return pltpu.make_async_copy(filled.at[here], out.at[there], sems.at[i])
 
     def step(i, carry):
-        pairs = [i * width + w for w in range(width)]
-        acc0, acc1 = edge_sums(pairs, below, above, edge, links_below, sum0, sum1)
-        for n, top, bottom in zip(pairs, acc0, acc1):
-            for k in range(6):
-                p = first_of(top[k], bottom[k], low) * lead
-                q = second_of(top[k], bottom[k], low) * lead
-                for m, value in ((n, p), (n + half, q)):
-                    out[m, k, 0:8] = value[:, : 2 * LS]
-                    out[m, k, 8:16] = value[:, 2 * LS :]
+        (lower,), (upper,) = edge_sums([i], below, above, edge, sum0, sum1)
+        for k in range(6):
+            p = first_of(lower[k], upper[k], low) * lead
+            q = second_of(lower[k], upper[k], low) * lead
+            for m, value in ((2 * i, p), (2 * i + 1, q)):
+                filled[m, k, 0:8] = value[:, : 2 * LS]
+                filled[m, k, 8:16] = value[:, 2 * LS :]
+        store(i).start()
         return carry
 
-    lax.fori_loop(0, half // width, step, 0)
+    def drain(i, carry):
+        store(i).wait()
+        return carry
+
+    lax.fori_loop(0, pairs, step, 0)
+    lax.fori_loop(0, pairs, drain, 0)
 
 
 VMEM_LIMIT = 32 * 1024 * 1024
-
-
-def call(kernel, outs, args, flops, scratch=()):
+CHUNKS = 2
+
+
+def call(kernel, outs, args, flops, scratch=(), in_hbm=(), out_hbm=False, aliases={}):
     moved = sum(4 * a.size for a in args) + sum(4 * o.size for o in outs)
+    args = [
+        pltpu.with_memory_space_constraint(a, pltpu.HBM) if i in in_hbm else a
+        for i, a in enumerate(args)
+    ]
+    vmem = pl.BlockSpec(memory_space=pltpu.VMEM)
+    hbm = pl.BlockSpec(memory_space=pltpu.HBM)
     return pl.pallas_call(
         kernel,
         out_shape=outs,
-        in_specs=[pl.BlockSpec(memory_space=pltpu.VMEM)] * len(args),
-        out_specs=[pl.BlockSpec(memory_space=pltpu.VMEM)] * len(outs),
+        in_specs=[hbm if i in in_hbm else vmem for i in range(len(args))],
+        out_specs=[hbm if out_hbm else vmem] * len(outs),
         scratch_shapes=list(scratch),
+        input_output_aliases=aliases,
         compiler_params=pltpu.CompilerParams(vmem_limit_bytes=VMEM_LIMIT),
         cost_estimate=pl.CostEstimate(flops=flops, bytes_accessed=moved, transcendentals=0),
     )(*args)
@@ -213,54 +265,85 @@
 
 def halo_body(links, sources):
     vectors = sources.shape[0]
-    half = vectors // 2
+    share = vectors // CHUNKS
+    pairs = share // 2
     width = 2
     sites, planes = links.shape[4:]
     f32 = functools.partial(jax.ShapeDtypeStruct, dtype=jnp.float32)
-    field = f32((half, 6, 8, 128))
+    field = f32((pairs, 6, 8, 128))
     inner_shape = f32((2, 4, 3, 3, 2, 8, 128))
     edge_shape = f32((3, 3, 2, 8, 128))
-    send_shape = f32((3, 3, 8, 128))
     source_view = jnp.swapaxes(sources, 3, 4).reshape(vectors, 6, planes, sites)
     link_view = jnp.swapaxes(links, 4, 5)
     powers = power_coeffs()
     lead = powers[4]
-    work = 2 * half * 36 * 2 * 1024
-
-    v0, v1, inner, edge, link_send = call(
-        pack_kernel,
-        [field, field, inner_shape, edge_shape, send_shape],
-        [source_view, link_view],
-        2 * half * 6 * 1024,
-    )
+    work = 2 * pairs * 36 * 2 * 1024
     count = lax.axis_size("space")
     up = [(d, (d + 1) % count) for d in range(count)]
     down = [(d, (d - 1) % count) for d in range(count)]
-    received = lax.ppermute(link_send, "space", up)
-    y0, y1 = v0, v1
-    for power in (3, 2, 1, 0):
-        below = lax.ppermute(y1, "space", up)
-        above = lax.ppermute(y0, "space", down)
-        sum0, sum1 = call(
-            functools.partial(inner_kernel, powers[power] / lead, width),
-            [field, field],
-            [y0, y1, inner, v0, v1],
-            4 * work,
-        )
-        args = [below, above, edge, received, sum0, sum1]
-        scratch = [pltpu.VMEM(edge_shape.shape, jnp.float32)]
-        if power:
-            y0, y1 = call(
-                functools.partial(edge_kernel, width), [field, field], args, work, scratch
+    arrived = pltpu.VMEM((share, 6, planes, sites), jnp.float32)
+    sems = pltpu.SemaphoreType.DMA((pairs,))
+
+    edge = None
+    start, halo = [], []
+    for chunk in range(CHUNKS):
+        if chunk == 0:
+            edge, row0, row1, product = call(
+                functools.partial(first_pack_kernel, 0),
+                [edge_shape, field, field, field],
+                [source_view, link_view],
+                work,
+                [
+                    arrived,
+                    pltpu.VMEM(link_view.shape[1:], jnp.float32),
+                    sems,
+                    pltpu.SemaphoreType.DMA,
+                ],
+                (0, 1),
             )
         else:
-            (out,) = call(
-                functools.partial(last_kernel, width, lead),
-                [f32(source_view.shape)],
-                args,
+            row0, row1, product = call(
+                functools.partial(pack_kernel, chunk * share),
+                [field, field, field],
+                [source_view, edge],
                 work,
-                scratch,
+                [arrived, sems],
+                (0,),
             )
+        start.append((row0, row1))
+        halo.append((lax.ppermute(product, "space", up), lax.ppermute(row0, "space", down)))
+    (inner,) = call(link_kernel, [inner_shape], [link_view], 8 * 18 * 1024)
+    current = list(start)
+    out = None
+    for power in (3, 2, 1, 0):
+        for chunk in range(CHUNKS):
+            sum0, sum1 = call(
+                functools.partial(inner_kernel, powers[power] / lead, width),
+                [field, field],
+                [*current[chunk], inner, *start[chunk]],
+                4 * work,
+            )
+            args = [*halo[chunk], edge, sum0, sum1]
+            if power:
+                row0, row1, product = call(
+                    functools.partial(edge_kernel, width), [field, field, field], args, work
+                )
+                current[chunk] = (row0, row1)
+                halo[chunk] = (
+                    lax.ppermute(product, "space", up),
+                    lax.ppermute(row0, "space", down),
+                )
+            else:
+                (out,) = call(
+                    functools.partial(last_kernel, chunk * share, lead),
+                    [f32(source_view.shape)],
+                    args if out is None else args + [out],
+                    work,
+                    [arrived, sems],
+                    () if out is None else (len(args),),
+                    True,
+                    {} if out is None else {len(args): 0},
+                )
     return jnp.swapaxes(out.reshape(vectors, 3, 2, planes, sites), 3, 4)
 
 
@@ -378,7 +461,7 @@
 
 def body(links, sources):
     sites, planes = sources.shape[3:]
-    if sites == 2 * LS and planes == 2 * NT and sources.shape[0] % 4 == 0:
+    if sites == 2 * LS and planes == 2 * NT and sources.shape[0] % (4 * CHUNKS) == 0:
         return halo_body(links, sources)
     return plane_body(links, sources)
 

time: 49.6 us -> 51.4 us (1.036)
  the two profiles are of different devices: /device:TPU:1 before, /device:TPU:0 now
where the time goes in v2:
time: 51.4 us; the launch traced here: 51.3 us
  starting transfers between devices  36.9 us (72%)
  Pallas kernels  14 us (27%)
    ppermute x8, starting transfers between devices, halo_body(): lax.ppermute(row0, 'space', down)  36 us
    pallas_call x19, Pallas kernels, call(): pl.pallas_call(kernel, out_shape=outs, in_specs=[hbm if i in in_hbm else...  14 us
  transfers between devices with their start and end apart: 16, of which 0 were waited for; matrix products, arithmetic and copies ran while one was open for 0% of the time, Pallas kernels for 20%

profile of v2, /device:TPU:0, one launch (start us, length us, event | category | flops | bytes accessed | tf_op | source)
XLA Modules:
  0.0 51.3 jit_solution(6210583574537444455)
XLA Ops:
  0.0 2.3 %shard_map.28 = (f32[3,3,2,8,128]{4,3,2,1,0:T(8,128)S(1)}, f32[6,6,8,128]{3,2,1,0:T(8,128)S(1)}, f32[6,6,8,128]{3,2,1,0:T(8,128)S(1)}, f32[6,6,8,128]{3,2,1,0:T(8,128)S(1)}) custom-call(f32[24,6,16,64]{3,2,1,0:T(8,128)} %bitcast.9, f32[3,3,3,2,16,64]{5,4,3,2,1,0:T(8,128)} %bitcast.7), custom_call_target="tpu_custom_call" | custom-call | flops 884736 | bytes 1327104 | tf_op jit(solution)/shard_map/pallas_call | solution.py:254
  2.3 0.5 collective-permute-start.8
  2.8 5.0 %collective-permute-start.9 = (f32[6,6,8,128]{3,2,1,0:T(8,128)S(1)}, f32[6,6,8,128]{3,2,1,0:T(8,128)S(1)}, u32[]{:S(2)}, u32[]{:S(2)}) collective-permute-start(f32[6,6,8,128]{3,2,1,0:T(8,128)S(1)} %get-tuple-element.68.y0.v0), channel_id=1, source_target_pairs={{0,15},{1,0},{2,1},{3,2},{4,3},{5,4},{6,5},{7,6},{8,7},{9,8},{10,9... | collective-permute-start | bytes 442376 | tf_op jit(solution)/shard_map/ppermute | solution.py:314
  7.9 1.9 %shard_map.29 = (f32[6,6,8,128]{3,2,1,0:T(8,128)S(1)}, f32[6,6,8,128]{3,2,1,0:T(8,128)S(1)}, f32[6,6,8,128]{3,2,1,0:T(8,128)S(1)}) custom-call(f32[24,6,16,64]{3,2,1,0:T(8,128)} %bitcast.10, f32[3,3,2,8,128]{4,3,2,1,0:T(8,128)S(1)} %get-tuple-element.46.edge), custom_call_target="tpu_custom_call" | custom-call | flops 884736 | bytes 1105920 | tf_op jit(solution)/shard_map/pallas_call | solution.py:254
  9.8 4.4 %collective-permute-start.1 = (f32[6,6,8,128]{3,2,1,0:T(8,128)S(1)}, f32[6,6,8,128]{3,2,1,0:T(8,128)S(1)}, u32[]{:S(2)}, u32[]{:S(2)}) collective-permute-start(f32[6,6,8,128]{3,2,1,0:T(8,128)S(1)} %get-tuple-element.48.y0.v0), channel_id=1, source_target_pairs={{0,15},{1,0},{2,1},{3,2},{4,3},{5,4},{6,5},{7,6},{8,7},{9,8},{10,9... | collective-permute-start | bytes 442376 | tf_op jit(solution)/shard_map/ppermute | solution.py:314
  14.2 0.7 %shard_map.30.inner = f32[2,4,3,3,2,8,128]{6,5,4,3,2,1,0:T(8,128)S(1)} custom-call(f32[3,3,3,2,16,64]{5,4,3,2,1,0:T(8,128)S(1)} %bitcast.8), custom_call_target="tpu_custom_call" | custom-call | flops 147456 | bytes 811008 | tf_op jit(solution)/shard_map/pallas_call | solution.py:254
  14.9 0.6 %shard_map.38 = (f32[6,6,8,128]{3,2,1,0:T(8,128)S(1)}, f32[6,6,8,128]{3,2,1,0:T(8,128)S(1)}) custom-call(f32[6,6,8,128]{3,2,1,0:T(8,128)S(1)} %get-tuple-element.68.y0.v0, f32[6,6,8,128]{3,2,1,0:T(8,128)S(1)} %get-tuple-element.69.y1.v1, f32[2,4,3,3,2,8,128]{6,5,4,3,2,1,0:T(8,128)S(1)} %shard_map.30.inner, f32[6,6,8,128]{3,2,1,0:T(8,128)S(1)} %get-tuple-element.68.y0.v0, ...), custom_call_target="tpu_custom_call" | custom-call | flops 3538944 | bytes 1474560 | tf_op jit(solution)/shard_map/pallas_call | solution.py:254
  15.6 0.1 shard_map.39
  15.8 4.4 %collective-permute-start.11 = (f32[6,6,8,128]{3,2,1,0:T(8,128)S(1)}, f32[6,6,8,128]{3,2,1,0:T(8,128)S(1)}, u32[]{:S(2)}, u32[]{:S(2)}) collective-permute-start(f32[6,6,8,128]{3,2,1,0:T(8,128)S(1)} %get-tuple-element.73.y0), channel_id=1, source_target_pairs={{0,15},{1,0},{2,1},{3,2},{4,3},{5,4},{6,5},{7,6},{8,7},{9,8},{10,9... | collective-permute-start | bytes 442376 | tf_op jit(solution)/shard_map/ppermute | solution.py:334
  20.2 0.6 %shard_map.31 = (f32[6,6,8,128]{3,2,1,0:T(8,128)S(1)}, f32[6,6,8,128]{3,2,1,0:T(8,128)S(1)}) custom-call(f32[6,6,8,128]{3,2,1,0:T(8,128)S(1)} %get-tuple-element.48.y0.v0, f32[6,6,8,128]{3,2,1,0:T(8,128)S(1)} %get-tuple-element.49.y1.v1, f32[2,4,3,3,2,8,128]{6,5,4,3,2,1,0:T(8,128)S(1)} %shard_map.30.inner, f32[6,6,8,128]{3,2,1,0:T(8,128)S(1)} %get-tuple-element.48.y0.v0, ...), custom_call_target="tpu_custom_call" | custom-call | flops 3538944 | bytes 1474560 | tf_op jit(solution)/shard_map/pallas_call | solution.py:254
  21.1 4.4 %collective-permute-start.3 = (f32[6,6,8,128]{3,2,1,0:T(8,128)S(1)}, f32[6,6,8,128]{3,2,1,0:T(8,128)S(1)}, u32[]{:S(2)}, u32[]{:S(2)}) collective-permute-start(f32[6,6,8,128]{3,2,1,0:T(8,128)S(1)} %get-tuple-element.53.y0), channel_id=1, source_target_pairs={{0,15},{1,0},{2,1},{3,2},{4,3},{5,4},{6,5},{7,6},{8,7},{9,8},{10,9... | collective-permute-start | bytes 442376 | tf_op jit(solution)/shard_map/ppermute | solution.py:334
  25.5 0.6 %shard_map.40 = (f32[6,6,8,128]{3,2,1,0:T(8,128)S(1)}, f32[6,6,8,128]{3,2,1,0:T(8,128)S(1)}) custom-call(f32[6,6,8,128]{3,2,1,0:T(8,128)S(1)} %get-tuple-element.73.y0, f32[6,6,8,128]{3,2,1,0:T(8,128)S(1)} %get-tuple-element.74.y1, f32[2,4,3,3,2,8,128]{6,5,4,3,2,1,0:T(8,128)S(1)} %shard_map.30.inner, f32[6,6,8,128]{3,2,1,0:T(8,128)S(1)} %get-tuple-element.68.y0.v0, ...), custom_call_target="tpu_custom_call" | custom-call | flops 3538944 | bytes 1474560 | tf_op jit(solution)/shard_map/pallas_call | solution.py:254
  26.1 0.6 %shard_map.33 = (f32[6,6,8,128]{3,2,1,0:T(8,128)S(1)}, f32[6,6,8,128]{3,2,1,0:T(8,128)S(1)}) custom-call(f32[6,6,8,128]{3,2,1,0:T(8,128)S(1)} %get-tuple-element.53.y0, f32[6,6,8,128]{3,2,1,0:T(8,128)S(1)} %get-tuple-element.54.y1, f32[2,4,3,3,2,8,128]{6,5,4,3,2,1,0:T(8,128)S(1)} %shard_map.30.inner, f32[6,6,8,128]{3,2,1,0:T(8,128)S(1)} %get-tuple-element.48.y0.v0, ...), custom_call_target="tpu_custom_call" | custom-call | flops 3538944 | bytes 1474560 | tf_op jit(solution)/shard_map/pallas_call | solution.py:254
  26.8 0.1 shard_map.41
  27.0 4.4 %collective-permute-start.13 = (f32[6,6,8,128]{3,2,1,0:T(8,128)S(1)}, f32[6,6,8,128]{3,2,1,0:T(8,128)S(1)}, u32[]{:S(2)}, u32[]{:S(2)}) collective-permute-start(f32[6,6,8,128]{3,2,1,0:T(8,128)S(1)} %get-tuple-element.78.y0), channel_id=1, source_target_pairs={{0,15},{1,0},{2,1},{3,2},{4,3},{5,4},{6,5},{7,6},{8,7},{9,8},{10,9... | collective-permute-start | bytes 442376 | tf_op jit(solution)/shard_map/ppermute | solution.py:334
  31.6 4.4 %collective-permute-start.5 = (f32[6,6,8,128]{3,2,1,0:T(8,128)S(1)}, f32[6,6,8,128]{3,2,1,0:T(8,128)S(1)}, u32[]{:S(2)}, u32[]{:S(2)}) collective-permute-start(f32[6,6,8,128]{3,2,1,0:T(8,128)S(1)} %get-tuple-element.58.y0), channel_id=1, source_target_pairs={{0,15},{1,0},{2,1},{3,2},{4,3},{5,4},{6,5},{7,6},{8,7},{9,8},{10,9... | collective-permute-start | bytes 442376 | tf_op jit(solution)/shard_map/ppermute | solution.py:334
  36.1 0.6 %shard_map.42 = (f32[6,6,8,128]{3,2,1,0:T(8,128)S(1)}, f32[6,6,8,128]{3,2,1,0:T(8,128)S(1)}) custom-call(f32[6,6,8,128]{3,2,1,0:T(8,128)S(1)} %get-tuple-element.78.y0, f32[6,6,8,128]{3,2,1,0:T(8,128)S(1)} %get-tuple-element.79.y1, f32[2,4,3,3,2,8,128]{6,5,4,3,2,1,0:T(8,128)S(1)} %shard_map.30.inner, f32[6,6,8,128]{3,2,1,0:T(8,128)S(1)} %get-tuple-element.68.y0.v0, ...), custom_call_target="tpu_custom_call" | custom-call | flops 3538944 | bytes 1474560 | tf_op jit(solution)/shard_map/pallas_call | solution.py:254
  36.7 0.6 %shard_map.35 = (f32[6,6,8,128]{3,2,1,0:T(8,128)S(1)}, f32[6,6,8,128]{3,2,1,0:T(8,128)S(1)}) custom-call(f32[6,6,8,128]{3,2,1,0:T(8,128)S(1)} %get-tuple-element.58.y0, f32[6,6,8,128]{3,2,1,0:T(8,128)S(1)} %get-tuple-element.59.y1, f32[2,4,3,3,2,8,128]{6,5,4,3,2,1,0:T(8,128)S(1)} %shard_map.30.inner, f32[6,6,8,128]{3,2,1,0:T(8,128)S(1)} %get-tuple-element.48.y0.v0, ...), custom_call_target="tpu_custom_call" | custom-call | flops 3538944 | bytes 1474560 | tf_op jit(solution)/shard_map/pallas_call | solution.py:254
  37.5 4.4 %collective-permute-start.15 = (f32[6,6,8,128]{3,2,1,0:T(8,128)S(1)}, f32[6,6,8,128]{3,2,1,0:T(8,128)S(1)}, u32[]{:S(2)}, u32[]{:S(2)}) collective-permute-start(f32[6,6,8,128]{3,2,1,0:T(8,128)S(1)} %get-tuple-element.83.y0), channel_id=1, source_target_pairs={{0,15},{1,0},{2,1},{3,2},{4,3},{5,4},{6,5},{7,6},{8,7},{9,8},{10,9... | collective-permute-start | bytes 442376 | tf_op jit(solution)/shard_map/ppermute | solution.py:334
  42.2 4.4 %collective-permute-start.7 = (f32[6,6,8,128]{3,2,1,0:T(8,128)S(1)}, f32[6,6,8,128]{3,2,1,0:T(8,128)S(1)}, u32[]{:S(2)}, u32[]{:S(2)}) collective-permute-start(f32[6,6,8,128]{3,2,1,0:T(8,128)S(1)} %get-tuple-element.63.y0), channel_id=1, source_target_pairs={{0,15},{1,0},{2,1},{3,2},{4,3},{5,4},{6,5},{7,6},{8,7},{9,8},{10,9... | collective-permute-start | bytes 442376 | tf_op jit(solution)/shard_map/ppermute | solution.py:334
  46.6 0.6 %shard_map.44 = (f32[6,6,8,128]{3,2,1,0:T(8,128)S(1)}, f32[6,6,8,128]{3,2,1,0:T(8,128)S(1)}) custom-call(f32[6,6,8,128]{3,2,1,0:T(8,128)S(1)} %get-tuple-element.83.y0, f32[6,6,8,128]{3,2,1,0:T(8,128)S(1)} %get-tuple-element.84.y1, f32[2,4,3,3,2,8,128]{6,5,4,3,2,1,0:T(8,128)S(1)} %shard_map.30.inner, f32[6,6,8,128]{3,2,1,0:T(8,128)S(1)} %get-tuple-element.68.y0.v0, ...), custom_call_target="tpu_custom_call" | custom-call | flops 3538944 | bytes 1474560 | tf_op jit(solution)/shard_map/pallas_call | solution.py:254
  47.3 0.6 %shard_map.37 = (f32[6,6,8,128]{3,2,1,0:T(8,128)S(1)}, f32[6,6,8,128]{3,2,1,0:T(8,128)S(1)}) custom-call(f32[6,6,8,128]{3,2,1,0:T(8,128)S(1)} %get-tuple-element.63.y0, f32[6,6,8,128]{3,2,1,0:T(8,128)S(1)} %get-tuple-element.64.y1, f32[2,4,3,3,2,8,128]{6,5,4,3,2,1,0:T(8,128)S(1)} %shard_map.30.inner, f32[6,6,8,128]{3,2,1,0:T(8,128)S(1)} %get-tuple-element.48.y0.v0, ...), custom_call_target="tpu_custom_call" | custom-call | flops 3538944 | bytes 1474560 | tf_op jit(solution)/shard_map/pallas_call | solution.py:254
  47.9 1.7 %shard_map.45.rest_0_ = f32[24,6,16,64]{3,2,1,0:T(8,128)} custom-call(f32[6,6,8,128]{3,2,1,0:T(8,128)S(1)} %collective-permute-done.14.below, f32[6,6,8,128]{3,2,1,0:T(8,128)S(1)} %collective-permute-done.15.above, f32[3,3,2,8,128]{4,3,2,1,0:T(8,128)S(1)} %get-tuple-element.46.edge, f32[6,6,8,128]{3,2,1,0:T(8,128)S(1)} %get-tuple-element.85.sum0, ...), custom_call_target="tpu_custom_call" | custom-call | flops 884736 | bytes 1253376 | tf_op jit(solution)/shard_map/pallas_call | solution.py:254
  49.6 1.7 %shard_map.46 = f32[24,6,16,64]{3,2,1,0:T(8,128)} custom-call(f32[6,6,8,128]{3,2,1,0:T(8,128)S(1)} %collective-permute-done.6.below, f32[6,6,8,128]{3,2,1,0:T(8,128)S(1)} %collective-permute-done.7.above, f32[3,3,2,8,128]{4,3,2,1,0:T(8,128)S(1)} %get-tuple-element.46.edge, ...), custom_call_target="tpu_custom_call", output_to_operand_aliasing={{}: (5, {})} | custom-call | flops 884736 | bytes 1843200 | tf_op jit(solution)/shard_map/pallas_call | solution.py:254
  (29 shorter events, 1.0 us)
Async XLA Ops:
  0.0 14.2 %copy-start = (f32[3,3,3,2,64,16]{4,5,3,2,1,0:T(8,128)S(1)}, f32[3,3,3,2,64,16]{4,5,3,2,1,0:T(8,128)}, u32[]{:S(2)}) copy-start(f32[3,3,3,2,64,16]{4,5,3,2,1,0:T(8,128)} %param.2) | copy-start | bytes 663556
  2.3 13.2 %collective-permute-start.8 = (f32[6,6,8,128]{3,2,1,0:T(8,128)S(1)}, f32[6,6,8,128]{3,2,1,0:T(8,128)S(1)}, u32[]{:S(2)}, u32[]{:S(2)}) collective-permute-start(f32[6,6,8,128]{3,2,1,0:T(8,128)S(1)} %get-tuple-element.67), channel_id=1, source_target_pairs={{0,1},{1,2},{2,3},{3,4},{4,5},{5,6},{6,7},{7,8},{8,9},{9,10},{10,1... | collective-permute-start | bytes 442376 | tf_op jit(solution)/shard_map/ppermute | solution.py:314
  2.8 12.7 %collective-permute-start.9 = (f32[6,6,8,128]{3,2,1,0:T(8,128)S(1)}, f32[6,6,8,128]{3,2,1,0:T(8,128)S(1)}, u32[]{:S(2)}, u32[]{:S(2)}) collective-permute-start(f32[6,6,8,128]{3,2,1,0:T(8,128)S(1)} %get-tuple-element.68.y0.v0), channel_id=1, source_target_pairs={{0,15},{1,0},{2,1},{3,2},{4,3},{5,4},{6,5},{7,6},{8,7},{9,8},{10,9... | collective-permute-start | bytes 442376 | tf_op jit(solution)/shard_map/ppermute | solution.py:314
  9.7 11.1 %collective-permute-start = (f32[6,6,8,128]{3,2,1,0:T(8,128)S(1)}, f32[6,6,8,128]{3,2,1,0:T(8,128)S(1)}, u32[]{:S(2)}, u32[]{:S(2)}) collective-permute-start(f32[6,6,8,128]{3,2,1,0:T(8,128)S(1)} %get-tuple-element.47), channel_id=1, source_target_pairs={{0,1},{1,2},{2,3},{3,4},{4,5},{5,6},{6,7},{7,8},{8,9},{9,10},{10,1... | collective-permute-start | bytes 442376 | tf_op jit(solution)/shard_map/ppermute | solution.py:314
  9.8 11.0 %collective-permute-start.1 = (f32[6,6,8,128]{3,2,1,0:T(8,128)S(1)}, f32[6,6,8,128]{3,2,1,0:T(8,128)S(1)}, u32[]{:S(2)}, u32[]{:S(2)}) collective-permute-start(f32[6,6,8,128]{3,2,1,0:T(8,128)S(1)} %get-tuple-element.48.y0.v0), channel_id=1, source_target_pairs={{0,15},{1,0},{2,1},{3,2},{4,3},{5,4},{6,5},{7,6},{8,7},{9,8},{10,9... | collective-permute-start | bytes 442376 | tf_op jit(solution)/shard_map/ppermute | solution.py:314
  15.7 11.0 %collective-permute-start.10 = (f32[6,6,8,128]{3,2,1,0:T(8,128)S(1)}, f32[6,6,8,128]{3,2,1,0:T(8,128)S(1)}, u32[]{:S(2)}, u32[]{:S(2)}) collective-permute-start(f32[6,6,8,128]{3,2,1,0:T(8,128)S(1)} %get-tuple-element.72), channel_id=1, source_target_pairs={{0,1},{1,2},{2,3},{3,4},{4,5},{5,6},{6,7},{7,8},{8,9},{9,10},{10,1... | collective-permute-start | bytes 442376 | tf_op jit(solution)/shard_map/ppermute | solution.py:333
  15.8 11.0 %collective-permute-start.11 = (f32[6,6,8,128]{3,2,1,0:T(8,128)S(1)}, f32[6,6,8,128]{3,2,1,0:T(8,128)S(1)}, u32[]{:S(2)}, u32[]{:S(2)}) collective-permute-start(f32[6,6,8,128]{3,2,1,0:T(8,128)S(1)} %get-tuple-element.73.y0), channel_id=1, source_target_pairs={{0,15},{1,0},{2,1},{3,2},{4,3},{5,4},{6,5},{7,6},{8,7},{9,8},{10,9... | collective-permute-start | bytes 442376 | tf_op jit(solution)/shard_map/ppermute | solution.py:334
  21.0 10.4 %collective-permute-start.2 = (f32[6,6,8,128]{3,2,1,0:T(8,128)S(1)}, f32[6,6,8,128]{3,2,1,0:T(8,128)S(1)}, u32[]{:S(2)}, u32[]{:S(2)}) collective-permute-start(f32[6,6,8,128]{3,2,1,0:T(8,128)S(1)} %get-tuple-element.52), channel_id=1, source_target_pairs={{0,1},{1,2},{2,3},{3,4},{4,5},{5,6},{6,7},{7,8},{8,9},{9,10},{10,1... | collective-permute-start | bytes 442376 | tf_op jit(solution)/shard_map/ppermute | solution.py:333
  21.1 10.4 %collective-permute-start.3 = (f32[6,6,8,128]{3,2,1,0:T(8,128)S(1)}, f32[6,6,8,128]{3,2,1,0:T(8,128)S(1)}, u32[]{:S(2)}, u32[]{:S(2)}) collective-permute-start(f32[6,6,8,128]{3,2,1,0:T(8,128)S(1)} %get-tuple-element.53.y0), channel_id=1, source_target_pairs={{0,15},{1,0},{2,1},{3,2},{4,3},{5,4},{6,5},{7,6},{8,7},{9,8},{10,9... | collective-permute-start | bytes 442376 | tf_op jit(solution)/shard_map/ppermute | solution.py:334
  26.9 10.4 %collective-permute-start.12 = (f32[6,6,8,128]{3,2,1,0:T(8,128)S(1)}, f32[6,6,8,128]{3,2,1,0:T(8,128)S(1)}, u32[]{:S(2)}, u32[]{:S(2)}) collective-permute-start(f32[6,6,8,128]{3,2,1,0:T(8,128)S(1)} %get-tuple-element.77), channel_id=1, source_target_pairs={{0,1},{1,2},{2,3},{3,4},{4,5},{5,6},{6,7},{7,8},{8,9},{9,10},{10,1... | collective-permute-start | bytes 442376 | tf_op jit(solution)/shard_map/ppermute | solution.py:333
  27.0 10.3 %collective-permute-start.13 = (f32[6,6,8,128]{3,2,1,0:T(8,128)S(1)}, f32[6,6,8,128]{3,2,1,0:T(8,128)S(1)}, u32[]{:S(2)}, u32[]{:S(2)}) collective-permute-start(f32[6,6,8,128]{3,2,1,0:T(8,128)S(1)} %get-tuple-element.78.y0), channel_id=1, source_target_pairs={{0,15},{1,0},{2,1},{3,2},{4,3},{5,4},{6,5},{7,6},{8,7},{9,8},{10,9... | collective-permute-start | bytes 442376 | tf_op jit(solution)/shard_map/ppermute | solution.py:334
  31.6 10.4 %collective-permute-start.4 = (f32[6,6,8,128]{3,2,1,0:T(8,128)S(1)}, f32[6,6,8,128]{3,2,1,0:T(8,128)S(1)}, u32[]{:S(2)}, u32[]{:S(2)}) collective-permute-start(f32[6,6,8,128]{3,2,1,0:T(8,128)S(1)} %get-tuple-element.57), channel_id=1, source_target_pairs={{0,1},{1,2},{2,3},{3,4},{4,5},{5,6},{6,7},{7,8},{8,9},{9,10},{10,1... | collective-permute-start | bytes 442376 | tf_op jit(solution)/shard_map/ppermute | solution.py:333
  31.6 10.4 %collective-permute-start.5 = (f32[6,6,8,128]{3,2,1,0:T(8,128)S(1)}, f32[6,6,8,128]{3,2,1,0:T(8,128)S(1)}, u32[]{:S(2)}, u32[]{:S(2)}) collective-permute-start(f32[6,6,8,128]{3,2,1,0:T(8,128)S(1)} %get-tuple-element.58.y0), channel_id=1, source_target_pairs={{0,15},{1,0},{2,1},{3,2},{4,3},{5,4},{6,5},{7,6},{8,7},{9,8},{10,9... | collective-permute-start | bytes 442376 | tf_op jit(solution)/shard_map/ppermute | solution.py:334
  37.5 10.4 %collective-permute-start.14 = (f32[6,6,8,128]{3,2,1,0:T(8,128)S(1)}, f32[6,6,8,128]{3,2,1,0:T(8,128)S(1)}, u32[]{:S(2)}, u32[]{:S(2)}) collective-permute-start(f32[6,6,8,128]{3,2,1,0:T(8,128)S(1)} %get-tuple-element.82), channel_id=1, source_target_pairs={{0,1},{1,2},{2,3},{3,4},{4,5},{5,6},{6,7},{7,8},{8,9},{9,10},{10,1... | collective-permute-start | bytes 442376 | tf_op jit(solution)/shard_map/ppermute | solution.py:333
  37.5 10.3 %collective-permute-start.15 = (f32[6,6,8,128]{3,2,1,0:T(8,128)S(1)}, f32[6,6,8,128]{3,2,1,0:T(8,128)S(1)}, u32[]{:S(2)}, u32[]{:S(2)}) collective-permute-start(f32[6,6,8,128]{3,2,1,0:T(8,128)S(1)} %get-tuple-element.83.y0), channel_id=1, source_target_pairs={{0,15},{1,0},{2,1},{3,2},{4,3},{5,4},{6,5},{7,6},{8,7},{9,8},{10,9... | collective-permute-start | bytes 442376 | tf_op jit(solution)/shard_map/ppermute | solution.py:334
  42.1 7.5 %collective-permute-start.6 = (f32[6,6,8,128]{3,2,1,0:T(8,128)S(1)}, f32[6,6,8,128]{3,2,1,0:T(8,128)S(1)}, u32[]{:S(2)}, u32[]{:S(2)}) collective-permute-start(f32[6,6,8,128]{3,2,1,0:T(8,128)S(1)} %get-tuple-element.62), channel_id=1, source_target_pairs={{0,1},{1,2},{2,3},{3,4},{4,5},{5,6},{6,7},{7,8},{8,9},{9,10},{10,1... | collective-permute-start | bytes 442376 | tf_op jit(solution)/shard_map/ppermute | solution.py:333
  42.2 7.4 %collective-permute-start.7 = (f32[6,6,8,128]{3,2,1,0:T(8,128)S(1)}, f32[6,6,8,128]{3,2,1,0:T(8,128)S(1)}, u32[]{:S(2)}, u32[]{:S(2)}) collective-permute-start(f32[6,6,8,128]{3,2,1,0:T(8,128)S(1)} %get-tuple-element.63.y0), channel_id=1, source_target_pairs={{0,15},{1,0},{2,1},{3,2},{4,3},{5,4},{6,5},{7,6},{8,7},{9,8},{10,9... | collective-permute-start | bytes 442376 | tf_op jit(solution)/shard_map/ppermute | solution.py:334

commit v3 on v2

--- a/solution.py
+++ b/solution.py
@@ -85,7 +85,19 @@
                 edge[a, b, part] = second_of(y_link, y_link, low)
 
 
-def pack_sources(first, src, edge, row0, row1, up, arrived, sems):
+def by_parity(run, pair, other):
+    odd = lax.axis_index("space") % 2 == 1
+
+    @pl.when(odd)
+    def _():
+        run(pair, other)
+
+    @pl.when(jnp.logical_not(odd))
+    def _():
+        run(other, pair)
+
+
+def pack_sources(first, src, edge, row0, row1, pair_out, other_out, arrived, sems):
     low = low_half()
     pairs = row0.shape[0]
 
@@ -97,14 +109,14 @@
     for i in range(pairs):
         fetch(i).start()
 
-    def finish():
+    def finish(down, up):
         def step(i, carry):
             fetch(i).wait()
             upper = []
             for k in range(6):
                 p = tile(arrived, (2 * i, k))
                 q = tile(arrived, (2 * i + 1, k))
-                row0[i, k] = first_of(p, q, low)
+                row0[i, k] = down[i, k] = first_of(p, q, low)
                 upper.append(second_of(p, q, low))
                 row1[i, k] = upper[k]
             sums = zeros(1)
@@ -115,20 +127,22 @@
 
         lax.fori_loop(0, pairs, step, 0)
 
-    return finish
-
-
-def first_pack_kernel(first, src, links, edge, row0, row1, up, arrived, y_links, sems, link_sem):
+    return lambda: by_parity(finish, pair_out, other_out)
+
+
+def first_pack_kernel(
+    first, src, links, edge, row0, row1, pair_out, other_out, arrived, y_links, sems, link_sem
+):
     link_copy = pltpu.make_async_copy(links.at[1], y_links, link_sem)
     link_copy.start()
-    finish = pack_sources(first, src, edge, row0, row1, up, arrived, sems)
+    finish = pack_sources(first, src, edge, row0, row1, pair_out, other_out, arrived, sems)
     link_copy.wait()
     pack_edge(y_links, edge)
     finish()
 
 
-def pack_kernel(first, src, edge, row0, row1, up, arrived, sems):
-    pack_sources(first, src, edge, row0, row1, up, arrived, sems)()
+def pack_kernel(first, src, edge, row0, row1, pair_out, other_out, arrived, sems):
+    pack_sources(first, src, edge, row0, row1, pair_out, other_out, arrived, sems)()
 
 
 def link_kernel(links, inner):
@@ -194,48 +208,59 @@
     return lower, upper
 
 
-def edge_kernel(width, below, above, edge, sum0, sum1, row0, row1, up):
-    def step(i, carry):
-        pairs = [i * width + w for w in range(width)]
-        lower, upper = edge_sums(pairs, below, above, edge, sum0, sum1)
-        back = zeros(width)
-        mat_vec(edge_link(edge), upper, back, dagger=True)
-        for n, bottom, top, product in zip(pairs, lower, upper, back):
-            for k in range(6):
-                row0[n, k] = bottom[k]
-                row1[n, k] = top[k]
-                up[n, k] = product[k]
-        return carry
-
-    lax.fori_loop(0, below.shape[0] // width, step, 0)
-
-
-def last_kernel(first, lead, below, above, edge, sum0, sum1, *rest):
+def edge_kernel(
+    width, pair_in, other_in, edge, sum0, sum1, row0, row1, pair_out, other_out
+):
+    def run(lower_side, upper_side):
+        below, down = lower_side
+        above, up = upper_side
+
+        def step(i, carry):
+            pairs = [i * width + w for w in range(width)]
+            lower, upper = edge_sums(pairs, below, above, edge, sum0, sum1)
+            back = zeros(width)
+            mat_vec(edge_link(edge), upper, back, dagger=True)
+            for n, bottom, top, product in zip(pairs, lower, upper, back):
+                for k in range(6):
+                    row0[n, k] = down[n, k] = bottom[k]
+                    row1[n, k] = top[k]
+                    up[n, k] = product[k]
+            return carry
+
+        lax.fori_loop(0, row0.shape[0] // width, step, 0)
+
+    by_parity(run, (pair_in, pair_out), (other_in, other_out))
+
+
+def last_kernel(first, lead, pair_in, other_in, edge, sum0, sum1, *rest):
     out, filled, sems = rest[-3:]
     low = low_half()
-    pairs = below.shape[0]
+    pairs = sum0.shape[0]
 
     def store(i):
         here = pl.ds(2 * i, 2)
         there = pl.ds(first + 2 * i, 2)
         return pltpu.make_async_copy(filled.at[here], out.at[there], sems.at[i])
 
-    def step(i, carry):
-        (lower,), (upper,) = edge_sums([i], below, above, edge, sum0, sum1)
-        for k in range(6):
-            p = first_of(lower[k], upper[k], low) * lead
-            q = second_of(lower[k], upper[k], low) * lead
-            for m, value in ((2 * i, p), (2 * i + 1, q)):
-                filled[m, k, 0:8] = value[:, : 2 * LS]
-                filled[m, k, 8:16] = value[:, 2 * LS :]
-        store(i).start()
-        return carry
+    def run(below, above):
+        def step(i, carry):
+            (lower,), (upper,) = edge_sums([i], below, above, edge, sum0, sum1)
+            for k in range(6):
+                p = first_of(lower[k], upper[k], low) * lead
+                q = second_of(lower[k], upper[k], low) * lead
+                for m, value in ((2 * i, p), (2 * i + 1, q)):
+                    filled[m, k, 0:8] = value[:, : 2 * LS]
+                    filled[m, k, 8:16] = value[:, 2 * LS :]
+            store(i).start()
+            return carry
+
+        lax.fori_loop(0, pairs, step, 0)
 
     def drain(i, carry):
         store(i).wait()
         return carry
 
-    lax.fori_loop(0, pairs, step, 0)
+    by_parity(run, pair_in, other_in)
     lax.fori_loop(0, pairs, drain, 0)
 
 
@@ -279,8 +304,13 @@
     lead = powers[4]
     work = 2 * pairs * 36 * 2 * 1024
     count = lax.axis_size("space")
-    up = [(d, (d + 1) % count) for d in range(count)]
-    down = [(d, (d - 1) % count) for d in range(count)]
+    pairing = [(d, d ^ 1) for d in range(count)]
+    others = [(d, (d + 1 if d % 2 else d - 1) % count) for d in range(count)]
+
+    def exchange(to_pair, to_other):
+        far = lax.ppermute(to_other, "space", others)
+        return lax.ppermute(to_pair, "space", pairing), far
+
     arrived = pltpu.VMEM((share, 6, planes, sites), jnp.float32)
     sems = pltpu.SemaphoreType.DMA((pairs,))
 
@@ -288,9 +318,9 @@
     start, halo = [], []
     for chunk in range(CHUNKS):
         if chunk == 0:
-            edge, row0, row1, product = call(
+            edge, row0, row1, *sends = call(
                 functools.partial(first_pack_kernel, 0),
-                [edge_shape, field, field, field],
+                [edge_shape, field, field, field, field],
                 [source_view, link_view],
                 work,
                 [
@@ -302,16 +332,16 @@
                 (0, 1),
             )
         else:
-            row0, row1, product = call(
+            row0, row1, *sends = call(
                 functools.partial(pack_kernel, chunk * share),
-                [field, field, field],
+                [field, field, field, field],
                 [source_view, edge],
                 work,
                 [arrived, sems],
                 (0,),
             )
         start.append((row0, row1))
-        halo.append((lax.ppermute(product, "space", up), lax.ppermute(row0, "space", down)))
+        halo.append(exchange(*sends))
     (inner,) = call(link_kernel, [inner_shape], [link_view], 8 * 18 * 1024)
     current = list(start)
     out = None
@@ -325,14 +355,11 @@
             )
             args = [*halo[chunk], edge, sum0, sum1]
             if power:
-                row0, row1, product = call(
-                    functools.partial(edge_kernel, width), [field, field, field], args, work
+                row0, row1, *sends = call(
+                    functools.partial(edge_kernel, width), [field, field, field, field], args, work
                 )
                 current[chunk] = (row0, row1)
-                halo[chunk] = (
-                    lax.ppermute(product, "space", up),
-                    lax.ppermute(row0, "space", down),
-                )
+                halo[chunk] = exchange(*sends)
             else:
                 (out,) = call(
                     functools.partial(last_kernel, chunk * share, lead),

time: 51.4 us -> 42.6 us (0.83)
  starting transfers between devices: 36.9 us -> 21.5 us
  waiting for transfers between devices: 0.04 us -> 6.68 us
    ppermute x16, starting transfers between devices: 36.9 us -> 21.5 us  [the longest x8 19.7 us: exchange(): far = lax.ppermute(to_other, 'space', others)]
    ppermute x16, waiting for transfers between devices: 0.04 us -> 6.68 us  [the longest x8 6.66 us: exchange(): far = lax.ppermute(to_other, 'space', others)]
  transfers between devices with their start and end apart: 16 -> 16, of which waited for: 0 -> 7; matrix products, arithmetic and copies ran while one was open for 0% -> 0% of each run, Pallas kernels for 20% -> 24%
where the time goes in v3:
time: 42.6 us; the launch traced here: 42.4 us
  starting transfers between devices  21.5 us (50%)
  Pallas kernels  14.1 us (33%)
  waiting for transfers between devices  6.68 us (16%)
    ppermute x8, starting transfers between devices, exchange(): far = lax.ppermute(to_other, 'space', others)  19.7 us
    pallas_call x19, Pallas kernels, call(): pl.pallas_call(kernel, out_shape=outs, in_specs=[hbm if i in in_hbm else...  14.1 us
    ppermute x8, waiting for transfers between devices, exchange(): far = lax.ppermute(to_other, 'space', others)  6.66 us
    ppermute x8, starting transfers between devices, exchange(): return (lax.ppermute(to_pair, 'space', pairing), far)  1.75 us
  transfers between devices with their start and end apart: 16, of which 7 were waited for; matrix products, arithmetic and copies ran while one was open for 0% of the time, Pallas kernels for 24%

profile of v3, /device:TPU:0, one launch (start us, length us, event | category | flops | bytes accessed | tf_op | source)
XLA Modules:
  0.0 42.4 jit_solution(16189266540749536644)
XLA Ops:
  0.0 2.3 %shard_map.28 = (f32[3,3,2,8,128]{4,3,2,1,0:T(8,128)S(1)}, f32[6,6,8,128]{3,2,1,0:T(8,128)S(1)}, f32[6,6,8,128]{3,2,1,0:T(8,128)S(1)}, f32[6,6,8,128]{3,2,1,0:T(8,128)S(1)}, f32[6,6,8,128]{3,2,1,0:T(8,128)S(1)}) custom-call(f32[24,6,16,64]{3,2,1,0:T(8,128)} %bitcast.9, f32[3,3,3,2,16,64]{5,4,3,2,1,0:T(8,128)} %bitcast.7), custom_call_target="tpu_custom_call" | custom-call | flops 884736 | bytes 1474560 | tf_op jit(solution)/shard_map/pallas_call | solution.py:279
  2.9 5.6 %collective-permute-start.9 = (f32[6,6,8,128]{3,2,1,0:T(8,128)S(1)}, f32[6,6,8,128]{3,2,1,0:T(8,128)S(1)}, u32[]{:S(2)}, u32[]{:S(2)}) collective-permute-start(f32[6,6,8,128]{3,2,1,0:T(8,128)S(1)} %get-tuple-element.80), channel_id=1, source_target_pairs={{0,15},{1,2},{2,1},{3,4},{4,3},{5,6},{6,5},{7,8},{8,7},{9,10},{10,... | collective-permute-start | bytes 442376 | tf_op jit(solution)/shard_map/ppermute | solution.py:311
  8.5 1.9 %shard_map.29 = (f32[6,6,8,128]{3,2,1,0:T(8,128)S(1)}, f32[6,6,8,128]{3,2,1,0:T(8,128)S(1)}, f32[6,6,8,128]{3,2,1,0:T(8,128)S(1)}, f32[6,6,8,128]{3,2,1,0:T(8,128)S(1)}) custom-call(f32[24,6,16,64]{3,2,1,0:T(8,128)} %bitcast.10, f32[3,3,2,8,128]{4,3,2,1,0:T(8,128)S(1)} %get-tuple-element.54.edge), custom_call_target="tpu_custom_call" | custom-call | flops 884736 | bytes 1253376 | tf_op jit(solution)/shard_map/pallas_call | solution.py:279
  10.5 0.6 %collective-permute-start.1 = (f32[6,6,8,128]{3,2,1,0:T(8,128)S(1)}, f32[6,6,8,128]{3,2,1,0:T(8,128)S(1)}, u32[]{:S(2)}, u32[]{:S(2)}) collective-permute-start(f32[6,6,8,128]{3,2,1,0:T(8,128)S(1)} %get-tuple-element.56), channel_id=1, source_target_pairs={{0,15},{1,2},{2,1},{3,4},{4,3},{5,6},{6,5},{7,8},{8,7},{9,10},{10,... | collective-permute-start | bytes 442376 | tf_op jit(solution)/shard_map/ppermute | solution.py:311
  11.1 0.7 %shard_map.30.inner = f32[2,4,3,3,2,8,128]{6,5,4,3,2,1,0:T(8,128)S(1)} custom-call(f32[3,3,3,2,16,64]{5,4,3,2,1,0:T(8,128)S(1)} %bitcast.8), custom_call_target="tpu_custom_call" | custom-call | flops 147456 | bytes 811008 | tf_op jit(solution)/shard_map/pallas_call | solution.py:279
  11.8 0.6 %shard_map.38 = (f32[6,6,8,128]{3,2,1,0:T(8,128)S(1)}, f32[6,6,8,128]{3,2,1,0:T(8,128)S(1)}) custom-call(f32[6,6,8,128]{3,2,1,0:T(8,128)S(1)} %get-tuple-element.81.y0.v0, f32[6,6,8,128]{3,2,1,0:T(8,128)S(1)} %get-tuple-element.82.y1.v1, f32[2,4,3,3,2,8,128]{6,5,4,3,2,1,0:T(8,128)S(1)} %shard_map.30.inner, f32[6,6,8,128]{3,2,1,0:T(8,128)S(1)} %get-tuple-element.81.y0.v0, ...), custom_call_target="tpu_custom_call" | custom-call | flops 3538944 | bytes 1474560 | tf_op jit(solution)/shard_map/pallas_call | solution.py:279
  12.7 3.9 %collective-permute-start.11 = (f32[6,6,8,128]{3,2,1,0:T(8,128)S(1)}, f32[6,6,8,128]{3,2,1,0:T(8,128)S(1)}, u32[]{:S(2)}, u32[]{:S(2)}) collective-permute-start(f32[6,6,8,128]{3,2,1,0:T(8,128)S(1)} %get-tuple-element.86), channel_id=1, source_target_pairs={{0,15},{1,2},{2,1},{3,4},{4,3},{5,6},{6,5},{7,8},{8,7},{9,10},{10,... | collective-permute-start | bytes 442376 | tf_op jit(solution)/shard_map/ppermute | solution.py:311
  16.6 0.6 %shard_map.31 = (f32[6,6,8,128]{3,2,1,0:T(8,128)S(1)}, f32[6,6,8,128]{3,2,1,0:T(8,128)S(1)}) custom-call(f32[6,6,8,128]{3,2,1,0:T(8,128)S(1)} %get-tuple-element.57.y0.v0, f32[6,6,8,128]{3,2,1,0:T(8,128)S(1)} %get-tuple-element.58.y1.v1, f32[2,4,3,3,2,8,128]{6,5,4,3,2,1,0:T(8,128)S(1)} %shard_map.30.inner, f32[6,6,8,128]{3,2,1,0:T(8,128)S(1)} %get-tuple-element.57.y0.v0, ...), custom_call_target="tpu_custom_call" | custom-call | flops 3538944 | bytes 1474560 | tf_op jit(solution)/shard_map/pallas_call | solution.py:279
  17.2 0.7 %collective-permute-done.1.other_in = f32[6,6,8,128]{3,2,1,0:T(8,128)S(1)} collective-permute-done((f32[6,6,8,128]{3,2,1,0:T(8,128)S(1)}, f32[6,6,8,128]{3,2,1,0:T(8,128)S(1)}, u32[]{:S(2)}, u32[]{:S(2)}) %collective-permute-start.1) | collective-permute-done | bytes 147488 | tf_op jit(solution)/shard_map/ppermute | solution.py:311
  18.7 0.6 %shard_map.33 = (f32[6,6,8,128]{3,2,1,0:T(8,128)S(1)}, f32[6,6,8,128]{3,2,1,0:T(8,128)S(1)}) custom-call(f32[6,6,8,128]{3,2,1,0:T(8,128)S(1)} %get-tuple-element.63.y0, f32[6,6,8,128]{3,2,1,0:T(8,128)S(1)} %get-tuple-element.64.y1, f32[2,4,3,3,2,8,128]{6,5,4,3,2,1,0:T(8,128)S(1)} %shard_map.30.inner, f32[6,6,8,128]{3,2,1,0:T(8,128)S(1)} %get-tuple-element.57.y0.v0, ...), custom_call_target="tpu_custom_call" | custom-call | flops 3538944 | bytes 1474560 | tf_op jit(solution)/shard_map/pallas_call | solution.py:279
  19.3 0.6 %shard_map.40 = (f32[6,6,8,128]{3,2,1,0:T(8,128)S(1)}, f32[6,6,8,128]{3,2,1,0:T(8,128)S(1)}) custom-call(f32[6,6,8,128]{3,2,1,0:T(8,128)S(1)} %get-tuple-element.87.y0, f32[6,6,8,128]{3,2,1,0:T(8,128)S(1)} %get-tuple-element.88.y1, f32[2,4,3,3,2,8,128]{6,5,4,3,2,1,0:T(8,128)S(1)} %shard_map.30.inner, f32[6,6,8,128]{3,2,1,0:T(8,128)S(1)} %get-tuple-element.81.y0.v0, ...), custom_call_target="tpu_custom_call" | custom-call | flops 3538944 | bytes 1474560 | tf_op jit(solution)/shard_map/pallas_call | solution.py:279
  20.3 0.7 %collective-permute-start.12 = (f32[6,6,8,128]{3,2,1,0:T(8,128)S(1)}, f32[6,6,8,128]{3,2,1,0:T(8,128)S(1)}, u32[]{:S(2)}, u32[]{:S(2)}) collective-permute-start(f32[6,6,8,128]{3,2,1,0:T(8,128)S(1)} %get-tuple-element.91), channel_id=1, source_target_pairs={{0,1},{1,0},{2,3},{3,2},{4,5},{5,4},{6,7},{7,6},{8,9},{9,8},{10,11... | collective-permute-start | bytes 442376 | tf_op jit(solution)/shard_map/ppermute | solution.py:312
  21.0 3.3 %collective-permute-start.13 = (f32[6,6,8,128]{3,2,1,0:T(8,128)S(1)}, f32[6,6,8,128]{3,2,1,0:T(8,128)S(1)}, u32[]{:S(2)}, u32[]{:S(2)}) collective-permute-start(f32[6,6,8,128]{3,2,1,0:T(8,128)S(1)} %get-tuple-element.92), channel_id=1, source_target_pairs={{0,15},{1,2},{2,1},{3,4},{4,3},{5,6},{6,5},{7,8},{8,7},{9,10},{10,... | collective-permute-start | bytes 442376 | tf_op jit(solution)/shard_map/ppermute | solution.py:311
  24.3 1.3 %collective-permute-done.3.other_in = f32[6,6,8,128]{3,2,1,0:T(8,128)S(1)} collective-permute-done((f32[6,6,8,128]{3,2,1,0:T(8,128)S(1)}, f32[6,6,8,128]{3,2,1,0:T(8,128)S(1)}, u32[]{:S(2)}, u32[]{:S(2)}) %collective-permute-start.3) | collective-permute-done | bytes 147488 | tf_op jit(solution)/shard_map/ppermute | solution.py:311
  25.8 1.2 %collective-permute-start.5 = (f32[6,6,8,128]{3,2,1,0:T(8,128)S(1)}, f32[6,6,8,128]{3,2,1,0:T(8,128)S(1)}, u32[]{:S(2)}, u32[]{:S(2)}) collective-permute-start(f32[6,6,8,128]{3,2,1,0:T(8,128)S(1)} %get-tuple-element.68), channel_id=1, source_target_pairs={{0,15},{1,2},{2,1},{3,4},{4,3},{5,6},{6,5},{7,8},{8,7},{9,10},{10,... | collective-permute-start | bytes 442376 | tf_op jit(solution)/shard_map/ppermute | solution.py:311
  27.0 0.6 %shard_map.35 = (f32[6,6,8,128]{3,2,1,0:T(8,128)S(1)}, f32[6,6,8,128]{3,2,1,0:T(8,128)S(1)}) custom-call(f32[6,6,8,128]{3,2,1,0:T(8,128)S(1)} %get-tuple-element.69.y0, f32[6,6,8,128]{3,2,1,0:T(8,128)S(1)} %get-tuple-element.70.y1, f32[2,4,3,3,2,8,128]{6,5,4,3,2,1,0:T(8,128)S(1)} %shard_map.30.inner, f32[6,6,8,128]{3,2,1,0:T(8,128)S(1)} %get-tuple-element.57.y0.v0, ...), custom_call_target="tpu_custom_call" | custom-call | flops 3538944 | bytes 1474560 | tf_op jit(solution)/shard_map/pallas_call | solution.py:279
  27.7 0.6 %shard_map.42 = (f32[6,6,8,128]{3,2,1,0:T(8,128)S(1)}, f32[6,6,8,128]{3,2,1,0:T(8,128)S(1)}) custom-call(f32[6,6,8,128]{3,2,1,0:T(8,128)S(1)} %get-tuple-element.93.y0, f32[6,6,8,128]{3,2,1,0:T(8,128)S(1)} %get-tuple-element.94.y1, f32[2,4,3,3,2,8,128]{6,5,4,3,2,1,0:T(8,128)S(1)} %shard_map.30.inner, f32[6,6,8,128]{3,2,1,0:T(8,128)S(1)} %get-tuple-element.81.y0.v0, ...), custom_call_target="tpu_custom_call" | custom-call | flops 3538944 | bytes 1474560 | tf_op jit(solution)/shard_map/pallas_call | solution.py:279
  28.7 3.3 %collective-permute-start.15 = (f32[6,6,8,128]{3,2,1,0:T(8,128)S(1)}, f32[6,6,8,128]{3,2,1,0:T(8,128)S(1)}, u32[]{:S(2)}, u32[]{:S(2)}) collective-permute-start(f32[6,6,8,128]{3,2,1,0:T(8,128)S(1)} %get-tuple-element.98), channel_id=1, source_target_pairs={{0,15},{1,2},{2,1},{3,4},{4,3},{5,6},{6,5},{7,8},{8,7},{9,10},{10,... | collective-permute-start | bytes 442376 | tf_op jit(solution)/shard_map/ppermute | solution.py:311
  31.9 1.3 %collective-permute-done.5.other_in = f32[6,6,8,128]{3,2,1,0:T(8,128)S(1)} collective-permute-done((f32[6,6,8,128]{3,2,1,0:T(8,128)S(1)}, f32[6,6,8,128]{3,2,1,0:T(8,128)S(1)}, u32[]{:S(2)}, u32[]{:S(2)}) %collective-permute-start.5) | collective-permute-done | bytes 147488 | tf_op jit(solution)/shard_map/ppermute | solution.py:311
  33.4 1.2 %collective-permute-start.7 = (f32[6,6,8,128]{3,2,1,0:T(8,128)S(1)}, f32[6,6,8,128]{3,2,1,0:T(8,128)S(1)}, u32[]{:S(2)}, u32[]{:S(2)}) collective-permute-start(f32[6,6,8,128]{3,2,1,0:T(8,128)S(1)} %get-tuple-element.74), channel_id=1, source_target_pairs={{0,15},{1,2},{2,1},{3,4},{4,3},{5,6},{6,5},{7,8},{8,7},{9,10},{10,... | collective-permute-start | bytes 442376 | tf_op jit(solution)/shard_map/ppermute | solution.py:311
  35.2 0.6 %shard_map.44 = (f32[6,6,8,128]{3,2,1,0:T(8,128)S(1)}, f32[6,6,8,128]{3,2,1,0:T(8,128)S(1)}) custom-call(f32[6,6,8,128]{3,2,1,0:T(8,128)S(1)} %get-tuple-element.99.y0, f32[6,6,8,128]{3,2,1,0:T(8,128)S(1)} %get-tuple-element.100.y1, f32[2,4,3,3,2,8,128]{6,5,4,3,2,1,0:T(8,128)S(1)} %shard_map.30.inner, f32[6,6,8,128]{3,2,1,0:T(8,128)S(1)} %get-tuple-element.81.y0.v0, ...), custom_call_target="tpu_custom_call" | custom-call | flops 3538944 | bytes 1474560 | tf_op jit(solution)/shard_map/pallas_call | solution.py:279
  36.0 1.7 %shard_map.45.rest_0_ = f32[24,6,16,64]{3,2,1,0:T(8,128)} custom-call(f32[6,6,8,128]{3,2,1,0:T(8,128)S(1)} %collective-permute-done.14.pair_in, f32[6,6,8,128]{3,2,1,0:T(8,128)S(1)} %collective-permute-done.15.other_in, f32[3,3,2,8,128]{4,3,2,1,0:T(8,128)S(1)} %get-tuple-element.54.edge, f32[6,6,8,128]{3,2,1,0:T(8,128)S(1)} %get-tuple-element.101.sum0, ...), custom_call_target="tpu_custom_call" | custom-call | flops 884736 | bytes 1253376 | tf_op jit(solution)/shard_map/pallas_call | solution.py:279
  37.7 3.0 %collective-permute-done.7.other_in = f32[6,6,8,128]{3,2,1,0:T(8,128)S(1)} collective-permute-done((f32[6,6,8,128]{3,2,1,0:T(8,128)S(1)}, f32[6,6,8,128]{3,2,1,0:T(8,128)S(1)}, u32[]{:S(2)}, u32[]{:S(2)}) %collective-permute-start.7) | collective-permute-done | bytes 147488 | tf_op jit(solution)/shard_map/ppermute | solution.py:311
  40.8 1.7 %shard_map.46 = f32[24,6,16,64]{3,2,1,0:T(8,128)} custom-call(f32[6,6,8,128]{3,2,1,0:T(8,128)S(1)} %collective-permute-done.6.pair_in, f32[6,6,8,128]{3,2,1,0:T(8,128)S(1)} %collective-permute-done.7.other_in, f32[3,3,2,8,128]{4,3,2,1,0:T(8,128)S(1)} %get-tuple-element.54.edge, ...), custom_call_target="tpu_custom_call", output_to_operand_aliasing={{}: (5, {})} | custom-call | flops 884736 | bytes 1843200 | tf_op jit(solution)/shard_map/pallas_call | solution.py:279
  (29 shorter events, 3.5 us)
Async XLA Ops:
  0.0 11.1 %copy-start = (f32[3,3,3,2,64,16]{4,5,3,2,1,0:T(8,128)S(1)}, f32[3,3,3,2,64,16]{4,5,3,2,1,0:T(8,128)}, u32[]{:S(2)}) copy-start(f32[3,3,3,2,64,16]{4,5,3,2,1,0:T(8,128)} %param.2) | copy-start | bytes 663556
  2.4 10.0 %collective-permute-start.8 = (f32[6,6,8,128]{3,2,1,0:T(8,128)S(1)}, f32[6,6,8,128]{3,2,1,0:T(8,128)S(1)}, u32[]{:S(2)}, u32[]{:S(2)}) collective-permute-start(f32[6,6,8,128]{3,2,1,0:T(8,128)S(1)} %get-tuple-element.79), channel_id=1, source_target_pairs={{0,1},{1,0},{2,3},{3,2},{4,5},{5,4},{6,7},{7,6},{8,9},{9,8},{10,11... | collective-permute-start | bytes 442376 | tf_op jit(solution)/shard_map/ppermute | solution.py:312
  2.9 9.5 %collective-permute-start.9 = (f32[6,6,8,128]{3,2,1,0:T(8,128)S(1)}, f32[6,6,8,128]{3,2,1,0:T(8,128)S(1)}, u32[]{:S(2)}, u32[]{:S(2)}) collective-permute-start(f32[6,6,8,128]{3,2,1,0:T(8,128)S(1)} %get-tuple-element.80), channel_id=1, source_target_pairs={{0,15},{1,2},{2,1},{3,4},{4,3},{5,6},{6,5},{7,8},{8,7},{9,10},{10,... | collective-permute-start | bytes 442376 | tf_op jit(solution)/shard_map/ppermute | solution.py:311
  10.4 6.8 %collective-permute-start = (f32[6,6,8,128]{3,2,1,0:T(8,128)S(1)}, f32[6,6,8,128]{3,2,1,0:T(8,128)S(1)}, u32[]{:S(2)}, u32[]{:S(2)}) collective-permute-start(f32[6,6,8,128]{3,2,1,0:T(8,128)S(1)} %get-tuple-element.55), channel_id=1, source_target_pairs={{0,1},{1,0},{2,3},{3,2},{4,5},{5,4},{6,7},{7,6},{8,9},{9,8},{10,11... | collective-permute-start | bytes 442376 | tf_op jit(solution)/shard_map/ppermute | solution.py:312
  10.5 7.4 %collective-permute-start.1 = (f32[6,6,8,128]{3,2,1,0:T(8,128)S(1)}, f32[6,6,8,128]{3,2,1,0:T(8,128)S(1)}, u32[]{:S(2)}, u32[]{:S(2)}) collective-permute-start(f32[6,6,8,128]{3,2,1,0:T(8,128)S(1)} %get-tuple-element.56), channel_id=1, source_target_pairs={{0,15},{1,2},{2,1},{3,4},{4,3},{5,6},{6,5},{7,8},{8,7},{9,10},{10,... | collective-permute-start | bytes 442376 | tf_op jit(solution)/shard_map/ppermute | solution.py:311
  12.6 7.3 %collective-permute-start.10 = (f32[6,6,8,128]{3,2,1,0:T(8,128)S(1)}, f32[6,6,8,128]{3,2,1,0:T(8,128)S(1)}, u32[]{:S(2)}, u32[]{:S(2)}) collective-permute-start(f32[6,6,8,128]{3,2,1,0:T(8,128)S(1)} %get-tuple-element.85), channel_id=1, source_target_pairs={{0,1},{1,0},{2,3},{3,2},{4,5},{5,4},{6,7},{7,6},{8,9},{9,8},{10,11... | collective-permute-start | bytes 442376 | tf_op jit(solution)/shard_map/ppermute | solution.py:312
  12.7 7.4 %collective-permute-start.11 = (f32[6,6,8,128]{3,2,1,0:T(8,128)S(1)}, f32[6,6,8,128]{3,2,1,0:T(8,128)S(1)}, u32[]{:S(2)}, u32[]{:S(2)}) collective-permute-start(f32[6,6,8,128]{3,2,1,0:T(8,128)S(1)} %get-tuple-element.86), channel_id=1, source_target_pairs={{0,15},{1,2},{2,1},{3,4},{4,3},{5,6},{6,5},{7,8},{8,7},{9,10},{10,... | collective-permute-start | bytes 442376 | tf_op jit(solution)/shard_map/ppermute | solution.py:311
  18.0 6.2 %collective-permute-start.2 = (f32[6,6,8,128]{3,2,1,0:T(8,128)S(1)}, f32[6,6,8,128]{3,2,1,0:T(8,128)S(1)}, u32[]{:S(2)}, u32[]{:S(2)}) collective-permute-start(f32[6,6,8,128]{3,2,1,0:T(8,128)S(1)} %get-tuple-element.61), channel_id=1, source_target_pairs={{0,1},{1,0},{2,3},{3,2},{4,5},{5,4},{6,7},{7,6},{8,9},{9,8},{10,11... | collective-permute-start | bytes 442376 | tf_op jit(solution)/shard_map/ppermute | solution.py:312
  18.1 7.4 %collective-permute-start.3 = (f32[6,6,8,128]{3,2,1,0:T(8,128)S(1)}, f32[6,6,8,128]{3,2,1,0:T(8,128)S(1)}, u32[]{:S(2)}, u32[]{:S(2)}) collective-permute-start(f32[6,6,8,128]{3,2,1,0:T(8,128)S(1)} %get-tuple-element.62), channel_id=1, source_target_pairs={{0,15},{1,2},{2,1},{3,4},{4,3},{5,6},{6,5},{7,8},{8,7},{9,10},{10,... | collective-permute-start | bytes 442376 | tf_op jit(solution)/shard_map/ppermute | solution.py:311
  20.3 8.0 %collective-permute-start.12 = (f32[6,6,8,128]{3,2,1,0:T(8,128)S(1)}, f32[6,6,8,128]{3,2,1,0:T(8,128)S(1)}, u32[]{:S(2)}, u32[]{:S(2)}) collective-permute-start(f32[6,6,8,128]{3,2,1,0:T(8,128)S(1)} %get-tuple-element.91), channel_id=1, source_target_pairs={{0,1},{1,0},{2,3},{3,2},{4,5},{5,4},{6,7},{7,6},{8,9},{9,8},{10,11... | collective-permute-start | bytes 442376 | tf_op jit(solution)/shard_map/ppermute | solution.py:312
  21.0 7.4 %collective-permute-start.13 = (f32[6,6,8,128]{3,2,1,0:T(8,128)S(1)}, f32[6,6,8,128]{3,2,1,0:T(8,128)S(1)}, u32[]{:S(2)}, u32[]{:S(2)}) collective-permute-start(f32[6,6,8,128]{3,2,1,0:T(8,128)S(1)} %get-tuple-element.92), channel_id=1, source_target_pairs={{0,15},{1,2},{2,1},{3,4},{4,3},{5,6},{6,5},{7,8},{8,7},{9,10},{10,... | collective-permute-start | bytes 442376 | tf_op jit(solution)/shard_map/ppermute | solution.py:311
  25.7 6.2 %collective-permute-start.4 = (f32[6,6,8,128]{3,2,1,0:T(8,128)S(1)}, f32[6,6,8,128]{3,2,1,0:T(8,128)S(1)}, u32[]{:S(2)}, u32[]{:S(2)}) collective-permute-start(f32[6,6,8,128]{3,2,1,0:T(8,128)S(1)} %get-tuple-element.67), channel_id=1, source_target_pairs={{0,1},{1,0},{2,3},{3,2},{4,5},{5,4},{6,7},{7,6},{8,9},{9,8},{10,11... | collective-permute-start | bytes 442376 | tf_op jit(solution)/shard_map/ppermute | solution.py:312
  25.8 7.4 %collective-permute-start.5 = (f32[6,6,8,128]{3,2,1,0:T(8,128)S(1)}, f32[6,6,8,128]{3,2,1,0:T(8,128)S(1)}, u32[]{:S(2)}, u32[]{:S(2)}) collective-permute-start(f32[6,6,8,128]{3,2,1,0:T(8,128)S(1)} %get-tuple-element.68), channel_id=1, source_target_pairs={{0,15},{1,2},{2,1},{3,4},{4,3},{5,6},{6,5},{7,8},{8,7},{9,10},{10,... | collective-permute-start | bytes 442376 | tf_op jit(solution)/shard_map/ppermute | solution.py:311
  28.5 7.3 %collective-permute-start.14 = (f32[6,6,8,128]{3,2,1,0:T(8,128)S(1)}, f32[6,6,8,128]{3,2,1,0:T(8,128)S(1)}, u32[]{:S(2)}, u32[]{:S(2)}) collective-permute-start(f32[6,6,8,128]{3,2,1,0:T(8,128)S(1)} %get-tuple-element.97), channel_id=1, source_target_pairs={{0,1},{1,0},{2,3},{3,2},{4,5},{5,4},{6,7},{7,6},{8,9},{9,8},{10,11... | collective-permute-start | bytes 442376 | tf_op jit(solution)/shard_map/ppermute | solution.py:312
  28.7 7.4 %collective-permute-start.15 = (f32[6,6,8,128]{3,2,1,0:T(8,128)S(1)}, f32[6,6,8,128]{3,2,1,0:T(8,128)S(1)}, u32[]{:S(2)}, u32[]{:S(2)}) collective-permute-start(f32[6,6,8,128]{3,2,1,0:T(8,128)S(1)} %get-tuple-element.98), channel_id=1, source_target_pairs={{0,15},{1,2},{2,1},{3,4},{4,3},{5,6},{6,5},{7,8},{8,7},{9,10},{10,... | collective-permute-start | bytes 442376 | tf_op jit(solution)/shard_map/ppermute | solution.py:311
  33.4 4.4 %collective-permute-start.6 = (f32[6,6,8,128]{3,2,1,0:T(8,128)S(1)}, f32[6,6,8,128]{3,2,1,0:T(8,128)S(1)}, u32[]{:S(2)}, u32[]{:S(2)}) collective-permute-start(f32[6,6,8,128]{3,2,1,0:T(8,128)S(1)} %get-tuple-element.73), channel_id=1, source_target_pairs={{0,1},{1,0},{2,3},{3,2},{4,5},{5,4},{6,7},{7,6},{8,9},{9,8},{10,11... | collective-permute-start | bytes 442376 | tf_op jit(solution)/shard_map/ppermute | solution.py:312
  33.4 7.3 %collective-permute-start.7 = (f32[6,6,8,128]{3,2,1,0:T(8,128)S(1)}, f32[6,6,8,128]{3,2,1,0:T(8,128)S(1)}, u32[]{:S(2)}, u32[]{:S(2)}) collective-permute-start(f32[6,6,8,128]{3,2,1,0:T(8,128)S(1)} %get-tuple-element.74), channel_id=1, source_target_pairs={{0,15},{1,2},{2,1},{3,4},{4,3},{5,6},{6,5},{7,8},{8,7},{9,10},{10,... | collective-permute-start | bytes 442376 | tf_op jit(solution)/shard_map/ppermute | solution.py:311

commit v4 on v3

--- a/solution.py
+++ b/solution.py
@@ -97,52 +97,43 @@
         run(other, pair)
 
 
-def pack_sources(first, src, edge, row0, row1, pair_out, other_out, arrived, sems):
+def pack_sources(source, edge, row0, row1, pair_out, other_out):
     low = low_half()
-    pairs = row0.shape[0]
-
-    def fetch(i):
-        here = pl.ds(2 * i, 2)
-        there = pl.ds(first + 2 * i, 2)
-        return pltpu.make_async_copy(src.at[there], arrived.at[here], sems.at[i])
-
-    for i in range(pairs):
-        fetch(i).start()
-
-    def finish(down, up):
-        def step(i, carry):
-            fetch(i).wait()
+
+    def run(down, up):
+        for n in range(row0.shape[0]):
             upper = []
             for k in range(6):
-                p = tile(arrived, (2 * i, k))
-                q = tile(arrived, (2 * i + 1, k))
-                row0[i, k] = down[i, k] = first_of(p, q, low)
+                p, q = source(2 * n, k), source(2 * n + 1, k)
+                row0[n, k] = down[n, k] = first_of(p, q, low)
                 upper.append(second_of(p, q, low))
-                row1[i, k] = upper[k]
+                row1[n, k] = upper[k]
             sums = zeros(1)
             mat_vec(edge_link(edge), [upper], sums, dagger=True)
             for k in range(6):
-                up[i, k] = sums[0][k]
-            return carry
-
-        lax.fori_loop(0, pairs, step, 0)
-
-    return lambda: by_parity(finish, pair_out, other_out)
-
-
-def first_pack_kernel(
-    first, src, links, edge, row0, row1, pair_out, other_out, arrived, y_links, sems, link_sem
-):
-    link_copy = pltpu.make_async_copy(links.at[1], y_links, link_sem)
-    link_copy.start()
-    finish = pack_sources(first, src, edge, row0, row1, pair_out, other_out, arrived, sems)
-    link_copy.wait()
+                up[n, k] = sums[0][k]
+
+    by_parity(run, pair_out, other_out)
+
+
+def first_pack_kernel(src, links, edge, row0, row1, other_out, pair_out, later, now, y_links, sems):
+    count = now.shape[0]
+    copies = [
+        pltpu.make_async_copy(links.at[1], y_links, sems.at[0]),
+        pltpu.make_async_copy(src.at[pl.ds(0, count)], now, sems.at[1]),
+        pltpu.make_async_copy(src.at[pl.ds(count, later.shape[0])], later, sems.at[2]),
+    ]
+    for copy in copies:
+        copy.start()
+    copies[0].wait()
     pack_edge(y_links, edge)
-    finish()
-
-
-def pack_kernel(first, src, edge, row0, row1, pair_out, other_out, arrived, sems):
-    pack_sources(first, src, edge, row0, row1, pair_out, other_out, arrived, sems)()
+    copies[1].wait()
+    pack_sources(lambda n, k: tile(now, (n, k)), edge, row0, row1, pair_out, other_out)
+    copies[2].wait()
+
+
+def pack_kernel(first, later, edge, row0, row1, other_out, pair_out):
+    pack_sources(lambda n, k: tile(later, (first + n, k)), edge, row0, row1, pair_out, other_out)
 
 
 def link_kernel(links, inner):
@@ -177,7 +168,7 @@
     z = lane_ids() % LS
     even = sublane_ids() % 2 == 0
 
-    def step(i, carry):
+    for i in range(y0.shape[0] // width):
         pairs = [i * width + w for w in range(width)]
         for row, (here, there, start, out) in enumerate(((y0, y1, v0, sum0), (y1, y0, v1, sum1))):
             sums = [[coeff * start[n, k] for k in range(6)] for n in pairs]
@@ -196,9 +187,6 @@
             for n, acc in zip(pairs, sums):
                 for k in range(6):
                     out[n, k] = acc[k]
-        return carry
-
-    lax.fori_loop(0, y0.shape[0] // width, step, 0)
 
 
 def edge_sums(pairs, below, above, edge, sum0, sum1):
@@ -209,13 +197,13 @@
 
 
 def edge_kernel(
-    width, pair_in, other_in, edge, sum0, sum1, row0, row1, pair_out, other_out
+    width, other_in, pair_in, edge, sum0, sum1, row0, row1, other_out, pair_out
 ):
     def run(lower_side, upper_side):
         below, down = lower_side
         above, up = upper_side
 
-        def step(i, carry):
+        for i in range(row0.shape[0] // width):
             pairs = [i * width + w for w in range(width)]
             lower, upper = edge_sums(pairs, below, above, edge, sum0, sum1)
             back = zeros(width)
@@ -225,14 +213,11 @@
                     row0[n, k] = down[n, k] = bottom[k]
                     row1[n, k] = top[k]
                     up[n, k] = product[k]
-            return carry
-
-        lax.fori_loop(0, row0.shape[0] // width, step, 0)
 
     by_parity(run, (pair_in, pair_out), (other_in, other_out))
 
 
-def last_kernel(first, lead, pair_in, other_in, edge, sum0, sum1, *rest):
+def last_kernel(first, lead, other_in, pair_in, edge, sum0, sum1, *rest):
     out, filled, sems = rest[-3:]
     low = low_half()
     pairs = sum0.shape[0]
@@ -243,7 +228,7 @@
         return pltpu.make_async_copy(filled.at[here], out.at[there], sems.at[i])
 
     def run(below, above):
-        def step(i, carry):
+        for i in range(pairs):
             (lower,), (upper,) = edge_sums([i], below, above, edge, sum0, sum1)
             for k in range(6):
                 p = first_of(lower[k], upper[k], low) * lead
@@ -252,16 +237,10 @@
                     filled[m, k, 0:8] = value[:, : 2 * LS]
                     filled[m, k, 8:16] = value[:, 2 * LS :]
             store(i).start()
-            return carry
-
-        lax.fori_loop(0, pairs, step, 0)
-
-    def drain(i, carry):
+
+    by_parity(run, pair_in, other_in)
+    for i in range(pairs):
         store(i).wait()
-        return carry
-
-    by_parity(run, pair_in, other_in)
-    lax.fori_loop(0, pairs, drain, 0)
 
 
 VMEM_LIMIT = 32 * 1024 * 1024
@@ -307,39 +286,32 @@
     pairing = [(d, d ^ 1) for d in range(count)]
     others = [(d, (d + 1 if d % 2 else d - 1) % count) for d in range(count)]
 
-    def exchange(to_pair, to_other):
+    def exchange(to_other, to_pair):
         far = lax.ppermute(to_other, "space", others)
-        return lax.ppermute(to_pair, "space", pairing), far
-
-    arrived = pltpu.VMEM((share, 6, planes, sites), jnp.float32)
-    sems = pltpu.SemaphoreType.DMA((pairs,))
-
-    edge = None
-    start, halo = [], []
-    for chunk in range(CHUNKS):
-        if chunk == 0:
-            edge, row0, row1, *sends = call(
-                functools.partial(first_pack_kernel, 0),
-                [edge_shape, field, field, field, field],
-                [source_view, link_view],
-                work,
-                [
-                    arrived,
-                    pltpu.VMEM(link_view.shape[1:], jnp.float32),
-                    sems,
-                    pltpu.SemaphoreType.DMA,
-                ],
-                (0, 1),
-            )
-        else:
-            row0, row1, *sends = call(
-                functools.partial(pack_kernel, chunk * share),
-                [field, field, field, field],
-                [source_view, edge],
-                work,
-                [arrived, sems],
-                (0,),
-            )
+        return far, lax.ppermute(to_pair, "space", pairing)
+
+    chunk_shape = (share, 6, planes, sites)
+
+    edge, row0, row1, *sends, later = call(
+        first_pack_kernel,
+        [edge_shape, field, field, field, field, f32((vectors - share, 6, planes, sites))],
+        [source_view, link_view],
+        work,
+        [
+            pltpu.VMEM(chunk_shape, jnp.float32),
+            pltpu.VMEM(link_view.shape[1:], jnp.float32),
+            pltpu.SemaphoreType.DMA((3,)),
+        ],
+        (0, 1),
+    )
+    start, halo = [(row0, row1)], [exchange(*sends)]
+    for chunk in range(1, CHUNKS):
+        row0, row1, *sends = call(
+            functools.partial(pack_kernel, (chunk - 1) * share),
+            [field, field, field, field],
+            [later, edge],
+            work,
+        )
         start.append((row0, row1))
         halo.append(exchange(*sends))
     (inner,) = call(link_kernel, [inner_shape], [link_view], 8 * 18 * 1024)
@@ -366,7 +338,7 @@
                     [f32(source_view.shape)],
                     args if out is None else args + [out],
                     work,
-                    [arrived, sems],
+                    [pltpu.VMEM(chunk_shape, jnp.float32), pltpu.SemaphoreType.DMA((pairs,))],
                     () if out is None else (len(args),),
                     True,
                     {} if out is None else {len(args): 0},

time: 42.6 us -> 39.2 us (0.920)
  Pallas kernels: 14.1 us -> 10.4 us
  starting transfers between devices: 21.5 us -> 22.8 us
  waiting for transfers between devices: 6.68 us -> 5.67 us
    pallas_call x19, Pallas kernels: 14.1 us -> 10.4 us  [call(): pl.pallas_call(kernel, out_shape=outs, in_specs=[hbm if i in in_hbm else...]
    ppermute x8, starting transfers between devices: 19.7 us -> 22.8 us  [exchange(): far = lax.ppermute(to_other, 'space', others)]
    ppermute x8, starting transfers between devices: 1.75 us -> 0.02 us  [exchange(): return (far, lax.ppermute(to_pair, 'space', pairing))]
    ppermute x8, waiting for transfers between devices: 6.66 us -> 5.65 us  [exchange(): far = lax.ppermute(to_other, 'space', others)]
  transfers between devices with their start and end apart: 16 -> 16, of which waited for: 7 -> 6; matrix products, arithmetic and copies ran while one was open for 0% -> 0% of each run, Pallas kernels for 24% -> 20%
where the time goes in v4:
time: 39.2 us; the launch traced here: 39 us
  starting transfers between devices  22.8 us (58%)
  Pallas kernels  10.4 us (27%)
  waiting for transfers between devices  5.67 us (14%)
    ppermute x8, starting transfers between devices, exchange(): far = lax.ppermute(to_other, 'space', others)  22.8 us
    pallas_call x19, Pallas kernels, call(): pl.pallas_call(kernel, out_shape=outs, in_specs=[hbm if i in in_hbm else...  10.4 us
    ppermute x8, waiting for transfers between devices, exchange(): far = lax.ppermute(to_other, 'space', others)  5.65 us
  transfers between devices with their start and end apart: 16, of which 6 were waited for; matrix products, arithmetic and copies ran while one was open for 0% of the time, Pallas kernels for 20%

profile of v4, /device:TPU:0, one launch (start us, length us, event | category | flops | bytes accessed | tf_op | source)
XLA Modules:
  0.0 39.0 jit_solution(14067709914984677874)
XLA Ops:
  0.0 1.6 %shard_map.28 = (f32[3,3,2,8,128]{4,3,2,1,0:T(8,128)S(1)}, f32[6,6,8,128]{3,2,1,0:T(8,128)S(1)}, f32[6,6,8,128]{3,2,1,0:T(8,128)S(1)}, f32[6,6,8,128]{3,2,1,0:T(...) custom-call(f32[24,6,16,64]{3,2,1,0:T(8,128)} %bitcast.9, f32[3,3,3,2,16,64]{5,4,3,2,1,0:T(8,128)} %bitcast.7), custom_call_target="tpu_custom_call" | custom-call | flops 884736 | bytes 1769472 | tf_op jit(solution)/shard_map/pallas_call | solution.py:258
  1.6 5.5 %collective-permute-start.8 = (f32[6,6,8,128]{3,2,1,0:T(8,128)S(1)}, f32[6,6,8,128]{3,2,1,0:T(8,128)S(1)}, u32[]{:S(2)}, u32[]{:S(2)}) collective-permute-start(f32[6,6,8,128]{3,2,1,0:T(8,128)S(1)} %get-tuple-element.81), channel_id=1, source_target_pairs={{0,15},{1,2},{2,1},{3,4},{4,3},{5,6},{6,5},{7,8},{8,7},{9,10},{10,... | collective-permute-start | bytes 442376 | tf_op jit(solution)/shard_map/ppermute | solution.py:290
  7.4 0.8 %collective-permute-start = (f32[6,6,8,128]{3,2,1,0:T(8,128)S(1)}, f32[6,6,8,128]{3,2,1,0:T(8,128)S(1)}, u32[]{:S(2)}, u32[]{:S(2)}) collective-permute-start(f32[6,6,8,128]{3,2,1,0:T(8,128)S(1)} %get-tuple-element.57), channel_id=1, source_target_pairs={{0,15},{1,2},{2,1},{3,4},{4,3},{5,6},{6,5},{7,8},{8,7},{9,10},{10,... | collective-permute-start | bytes 442376 | tf_op jit(solution)/shard_map/ppermute | solution.py:290
  8.3 0.7 %shard_map.30.inner = f32[2,4,3,3,2,8,128]{6,5,4,3,2,1,0:T(8,128)S(1)} custom-call(f32[3,3,3,2,16,64]{5,4,3,2,1,0:T(8,128)S(1)} %bitcast.8), custom_call_target="tpu_custom_call" | custom-call | flops 147456 | bytes 811008 | tf_op jit(solution)/shard_map/pallas_call | solution.py:258
  8.9 0.6 %shard_map.38 = (f32[6,6,8,128]{3,2,1,0:T(8,128)S(1)}, f32[6,6,8,128]{3,2,1,0:T(8,128)S(1)}) custom-call(f32[6,6,8,128]{3,2,1,0:T(8,128)S(1)} %get-tuple-element.83.y0.v0, f32[6,6,8,128]{3,2,1,0:T(8,128)S(1)} %get-tuple-element.84.y1.v1, f32[2,4,3,3,2,8,128]{6,5,4,3,2,1,0:T(8,128)S(1)} %shard_map.30.inner, f32[6,6,8,128]{3,2,1,0:T(8,128)S(1)} %get-tuple-element.83.y0.v0, ...), custom_call_target="tpu_custom_call" | custom-call | flops 3538944 | bytes 1474560 | tf_op jit(solution)/shard_map/pallas_call | solution.py:258
  9.5 0.4 collective-permute-done.8.other_in
  10.0 4.6 %collective-permute-start.10 = (f32[6,6,8,128]{3,2,1,0:T(8,128)S(1)}, f32[6,6,8,128]{3,2,1,0:T(8,128)S(1)}, u32[]{:S(2)}, u32[]{:S(2)}) collective-permute-start(f32[6,6,8,128]{3,2,1,0:T(8,128)S(1)} %get-tuple-element.87), channel_id=1, source_target_pairs={{0,15},{1,2},{2,1},{3,4},{4,3},{5,6},{6,5},{7,8},{8,7},{9,10},{10,... | collective-permute-start | bytes 442376 | tf_op jit(solution)/shard_map/ppermute | solution.py:290
  14.6 0.6 %shard_map.31 = (f32[6,6,8,128]{3,2,1,0:T(8,128)S(1)}, f32[6,6,8,128]{3,2,1,0:T(8,128)S(1)}) custom-call(f32[6,6,8,128]{3,2,1,0:T(8,128)S(1)} %get-tuple-element.59.y0.v0, f32[6,6,8,128]{3,2,1,0:T(8,128)S(1)} %get-tuple-element.60.y1.v1, f32[2,4,3,3,2,8,128]{6,5,4,3,2,1,0:T(8,128)S(1)} %shard_map.30.inner, f32[6,6,8,128]{3,2,1,0:T(8,128)S(1)} %get-tuple-element.59.y0.v0, ...), custom_call_target="tpu_custom_call" | custom-call | flops 3538944 | bytes 1474560 | tf_op jit(solution)/shard_map/pallas_call | solution.py:258
  15.4 1.1 %collective-permute-start.2 = (f32[6,6,8,128]{3,2,1,0:T(8,128)S(1)}, f32[6,6,8,128]{3,2,1,0:T(8,128)S(1)}, u32[]{:S(2)}, u32[]{:S(2)}) collective-permute-start(f32[6,6,8,128]{3,2,1,0:T(8,128)S(1)} %get-tuple-element.63), channel_id=1, source_target_pairs={{0,15},{1,2},{2,1},{3,4},{4,3},{5,6},{6,5},{7,8},{8,7},{9,10},{10,... | collective-permute-start | bytes 442376 | tf_op jit(solution)/shard_map/ppermute | solution.py:290
  16.5 0.6 %shard_map.33 = (f32[6,6,8,128]{3,2,1,0:T(8,128)S(1)}, f32[6,6,8,128]{3,2,1,0:T(8,128)S(1)}) custom-call(f32[6,6,8,128]{3,2,1,0:T(8,128)S(1)} %get-tuple-element.65.y0, f32[6,6,8,128]{3,2,1,0:T(8,128)S(1)} %get-tuple-element.66.y1, f32[2,4,3,3,2,8,128]{6,5,4,3,2,1,0:T(8,128)S(1)} %shard_map.30.inner, f32[6,6,8,128]{3,2,1,0:T(8,128)S(1)} %get-tuple-element.59.y0.v0, ...), custom_call_target="tpu_custom_call" | custom-call | flops 3538944 | bytes 1474560 | tf_op jit(solution)/shard_map/pallas_call | solution.py:258
  17.1 0.6 %shard_map.40 = (f32[6,6,8,128]{3,2,1,0:T(8,128)S(1)}, f32[6,6,8,128]{3,2,1,0:T(8,128)S(1)}) custom-call(f32[6,6,8,128]{3,2,1,0:T(8,128)S(1)} %get-tuple-element.89.y0, f32[6,6,8,128]{3,2,1,0:T(8,128)S(1)} %get-tuple-element.90.y1, f32[2,4,3,3,2,8,128]{6,5,4,3,2,1,0:T(8,128)S(1)} %shard_map.30.inner, f32[6,6,8,128]{3,2,1,0:T(8,128)S(1)} %get-tuple-element.83.y0.v0, ...), custom_call_target="tpu_custom_call" | custom-call | flops 3538944 | bytes 1474560 | tf_op jit(solution)/shard_map/pallas_call | solution.py:258
  17.9 4.3 %collective-permute-start.12 = (f32[6,6,8,128]{3,2,1,0:T(8,128)S(1)}, f32[6,6,8,128]{3,2,1,0:T(8,128)S(1)}, u32[]{:S(2)}, u32[]{:S(2)}) collective-permute-start(f32[6,6,8,128]{3,2,1,0:T(8,128)S(1)} %get-tuple-element.93), channel_id=1, source_target_pairs={{0,15},{1,2},{2,1},{3,4},{4,3},{5,6},{6,5},{7,8},{8,7},{9,10},{10,... | collective-permute-start | bytes 442376 | tf_op jit(solution)/shard_map/ppermute | solution.py:290
  22.2 0.6 %collective-permute-done.2.other_in = f32[6,6,8,128]{3,2,1,0:T(8,128)S(1)} collective-permute-done((f32[6,6,8,128]{3,2,1,0:T(8,128)S(1)}, f32[6,6,8,128]{3,2,1,0:T(8,128)S(1)}, u32[]{:S(2)}, u32[]{:S(2)}) %collective-permute-start.2) | collective-permute-done | bytes 147488 | tf_op jit(solution)/shard_map/ppermute | solution.py:290
  23.0 1.1 %collective-permute-start.4 = (f32[6,6,8,128]{3,2,1,0:T(8,128)S(1)}, f32[6,6,8,128]{3,2,1,0:T(8,128)S(1)}, u32[]{:S(2)}, u32[]{:S(2)}) collective-permute-start(f32[6,6,8,128]{3,2,1,0:T(8,128)S(1)} %get-tuple-element.69), channel_id=1, source_target_pairs={{0,15},{1,2},{2,1},{3,4},{4,3},{5,6},{6,5},{7,8},{8,7},{9,10},{10,... | collective-permute-start | bytes 442376 | tf_op jit(solution)/shard_map/ppermute | solution.py:290
  24.1 0.6 %shard_map.35 = (f32[6,6,8,128]{3,2,1,0:T(8,128)S(1)}, f32[6,6,8,128]{3,2,1,0:T(8,128)S(1)}) custom-call(f32[6,6,8,128]{3,2,1,0:T(8,128)S(1)} %get-tuple-element.71.y0, f32[6,6,8,128]{3,2,1,0:T(8,128)S(1)} %get-tuple-element.72.y1, f32[2,4,3,3,2,8,128]{6,5,4,3,2,1,0:T(8,128)S(1)} %shard_map.30.inner, f32[6,6,8,128]{3,2,1,0:T(8,128)S(1)} %get-tuple-element.59.y0.v0, ...), custom_call_target="tpu_custom_call" | custom-call | flops 3538944 | bytes 1474560 | tf_op jit(solution)/shard_map/pallas_call | solution.py:258
  24.7 0.6 %shard_map.42 = (f32[6,6,8,128]{3,2,1,0:T(8,128)S(1)}, f32[6,6,8,128]{3,2,1,0:T(8,128)S(1)}) custom-call(f32[6,6,8,128]{3,2,1,0:T(8,128)S(1)} %get-tuple-element.95.y0, f32[6,6,8,128]{3,2,1,0:T(8,128)S(1)} %get-tuple-element.96.y1, f32[2,4,3,3,2,8,128]{6,5,4,3,2,1,0:T(8,128)S(1)} %shard_map.30.inner, f32[6,6,8,128]{3,2,1,0:T(8,128)S(1)} %get-tuple-element.83.y0.v0, ...), custom_call_target="tpu_custom_call" | custom-call | flops 3538944 | bytes 1474560 | tf_op jit(solution)/shard_map/pallas_call | solution.py:258
  25.5 4.3 %collective-permute-start.14 = (f32[6,6,8,128]{3,2,1,0:T(8,128)S(1)}, f32[6,6,8,128]{3,2,1,0:T(8,128)S(1)}, u32[]{:S(2)}, u32[]{:S(2)}) collective-permute-start(f32[6,6,8,128]{3,2,1,0:T(8,128)S(1)} %get-tuple-element.99), channel_id=1, source_target_pairs={{0,15},{1,2},{2,1},{3,4},{4,3},{5,6},{6,5},{7,8},{8,7},{9,10},{10,... | collective-permute-start | bytes 442376 | tf_op jit(solution)/shard_map/ppermute | solution.py:290
  29.8 0.6 %collective-permute-done.4.other_in = f32[6,6,8,128]{3,2,1,0:T(8,128)S(1)} collective-permute-done((f32[6,6,8,128]{3,2,1,0:T(8,128)S(1)}, f32[6,6,8,128]{3,2,1,0:T(8,128)S(1)}, u32[]{:S(2)}, u32[]{:S(2)}) %collective-permute-start.4) | collective-permute-done | bytes 147488 | tf_op jit(solution)/shard_map/ppermute | solution.py:290
  30.6 1.0 %collective-permute-start.6 = (f32[6,6,8,128]{3,2,1,0:T(8,128)S(1)}, f32[6,6,8,128]{3,2,1,0:T(8,128)S(1)}, u32[]{:S(2)}, u32[]{:S(2)}) collective-permute-start(f32[6,6,8,128]{3,2,1,0:T(8,128)S(1)} %get-tuple-element.75), channel_id=1, source_target_pairs={{0,15},{1,2},{2,1},{3,4},{4,3},{5,6},{6,5},{7,8},{8,7},{9,10},{10,... | collective-permute-start | bytes 442376 | tf_op jit(solution)/shard_map/ppermute | solution.py:290
  31.6 0.6 %shard_map.37 = (f32[6,6,8,128]{3,2,1,0:T(8,128)S(1)}, f32[6,6,8,128]{3,2,1,0:T(8,128)S(1)}) custom-call(f32[6,6,8,128]{3,2,1,0:T(8,128)S(1)} %get-tuple-element.77.y0, f32[6,6,8,128]{3,2,1,0:T(8,128)S(1)} %get-tuple-element.78.y1, f32[2,4,3,3,2,8,128]{6,5,4,3,2,1,0:T(8,128)S(1)} %shard_map.30.inner, f32[6,6,8,128]{3,2,1,0:T(8,128)S(1)} %get-tuple-element.59.y0.v0, ...), custom_call_target="tpu_custom_call" | custom-call | flops 3538944 | bytes 1474560 | tf_op jit(solution)/shard_map/pallas_call | solution.py:258
  32.2 0.6 %shard_map.44 = (f32[6,6,8,128]{3,2,1,0:T(8,128)S(1)}, f32[6,6,8,128]{3,2,1,0:T(8,128)S(1)}) custom-call(f32[6,6,8,128]{3,2,1,0:T(8,128)S(1)} %get-tuple-element.101.y0, f32[6,6,8,128]{3,2,1,0:T(8,128)S(1)} %get-tuple-element.102.y1, f32[2,4,3,3,2,8,128]{6,5,4,3,2,1,0:T(8,128)S(1)} %shard_map.30.inner, f32[6,6,8,128]{3,2,1,0:T(8,128)S(1)} %get-tuple-element.83.y0.v0, ...), custom_call_target="tpu_custom_call" | custom-call | flops 3538944 | bytes 1474560 | tf_op jit(solution)/shard_map/pallas_call | solution.py:258
  32.9 1.1 %shard_map.45.rest_0_ = f32[24,6,16,64]{3,2,1,0:T(8,128)} custom-call(f32[6,6,8,128]{3,2,1,0:T(8,128)S(1)} %collective-permute-done.14.other_in, f32[6,6,8,128]{3,2,1,0:T(8,128)S(1)} %collective-permute-done.15.pair_in, f32[3,3,2,8,128]{4,3,2,1,0:T(8,128)S(1)} %get-tuple-element.56.edge, f32[6,6,8,128]{3,2,1,0:T(8,128)S(1)} %get-tuple-element.103.sum0, ...), custom_call_target="tpu_custom_call" | custom-call | flops 884736 | bytes 1253376 | tf_op jit(solution)/shard_map/pallas_call | solution.py:258
  34.1 3.8 %collective-permute-done.6.other_in = f32[6,6,8,128]{3,2,1,0:T(8,128)S(1)} collective-permute-done((f32[6,6,8,128]{3,2,1,0:T(8,128)S(1)}, f32[6,6,8,128]{3,2,1,0:T(8,128)S(1)}, u32[]{:S(2)}, u32[]{:S(2)}) %collective-permute-start.6) | collective-permute-done | bytes 147488 | tf_op jit(solution)/shard_map/ppermute | solution.py:290
  37.9 1.1 %shard_map.46 = f32[24,6,16,64]{3,2,1,0:T(8,128)} custom-call(f32[6,6,8,128]{3,2,1,0:T(8,128)S(1)} %collective-permute-done.6.other_in, f32[6,6,8,128]{3,2,1,0:T(8,128)S(1)} %collective-permute-done.7.pair_in, f32[3,3,2,8,128]{4,3,2,1,0:T(8,128)S(1)} %get-tuple-element.56.edge, ...), custom_call_target="tpu_custom_call", output_to_operand_aliasing={{}: (5, {})} | custom-call | flops 884736 | bytes 1843200 | tf_op jit(solution)/shard_map/pallas_call | solution.py:258
  (29 shorter events, 1.4 us)
Async XLA Ops:
  0.0 8.3 %copy-start = (f32[3,3,3,2,64,16]{4,5,3,2,1,0:T(8,128)S(1)}, f32[3,3,3,2,64,16]{4,5,3,2,1,0:T(8,128)}, u32[]{:S(2)}) copy-start(f32[3,3,3,2,64,16]{4,5,3,2,1,0:T(8,128)} %param.2) | copy-start | bytes 663556
  1.6 8.3 %collective-permute-start.8 = (f32[6,6,8,128]{3,2,1,0:T(8,128)S(1)}, f32[6,6,8,128]{3,2,1,0:T(8,128)S(1)}, u32[]{:S(2)}, u32[]{:S(2)}) collective-permute-start(f32[6,6,8,128]{3,2,1,0:T(8,128)S(1)} %get-tuple-element.81), channel_id=1, source_target_pairs={{0,15},{1,2},{2,1},{3,4},{4,3},{5,6},{6,5},{7,8},{8,7},{9,10},{10,... | collective-permute-start | bytes 442376 | tf_op jit(solution)/shard_map/ppermute | solution.py:290
  7.1 2.8 %collective-permute-start.9 = (f32[6,6,8,128]{3,2,1,0:T(8,128)S(1)}, f32[6,6,8,128]{3,2,1,0:T(8,128)S(1)}, u32[]{:S(2)}, u32[]{:S(2)}) collective-permute-start(f32[6,6,8,128]{3,2,1,0:T(8,128)S(1)} %get-tuple-element.82), channel_id=1, source_target_pairs={{0,1},{1,0},{2,3},{3,2},{4,5},{5,4},{6,7},{7,6},{8,9},{9,8},{10,11... | collective-permute-start | bytes 442376 | tf_op jit(solution)/shard_map/ppermute | solution.py:291
  7.4 7.8 %collective-permute-start = (f32[6,6,8,128]{3,2,1,0:T(8,128)S(1)}, f32[6,6,8,128]{3,2,1,0:T(8,128)S(1)}, u32[]{:S(2)}, u32[]{:S(2)}) collective-permute-start(f32[6,6,8,128]{3,2,1,0:T(8,128)S(1)} %get-tuple-element.57), channel_id=1, source_target_pairs={{0,15},{1,2},{2,1},{3,4},{4,3},{5,6},{6,5},{7,8},{8,7},{9,10},{10,... | collective-permute-start | bytes 442376 | tf_op jit(solution)/shard_map/ppermute | solution.py:290
  8.3 7.0 %collective-permute-start.1 = (f32[6,6,8,128]{3,2,1,0:T(8,128)S(1)}, f32[6,6,8,128]{3,2,1,0:T(8,128)S(1)}, u32[]{:S(2)}, u32[]{:S(2)}) collective-permute-start(f32[6,6,8,128]{3,2,1,0:T(8,128)S(1)} %get-tuple-element.58), channel_id=1, source_target_pairs={{0,1},{1,0},{2,3},{3,2},{4,5},{5,4},{6,7},{7,6},{8,9},{9,8},{10,11... | collective-permute-start | bytes 442376 | tf_op jit(solution)/shard_map/ppermute | solution.py:291
  10.0 7.7 %collective-permute-start.10 = (f32[6,6,8,128]{3,2,1,0:T(8,128)S(1)}, f32[6,6,8,128]{3,2,1,0:T(8,128)S(1)}, u32[]{:S(2)}, u32[]{:S(2)}) collective-permute-start(f32[6,6,8,128]{3,2,1,0:T(8,128)S(1)} %get-tuple-element.87), channel_id=1, source_target_pairs={{0,15},{1,2},{2,1},{3,4},{4,3},{5,6},{6,5},{7,8},{8,7},{9,10},{10,... | collective-permute-start | bytes 442376 | tf_op jit(solution)/shard_map/ppermute | solution.py:290
  14.6 3.1 %collective-permute-start.11 = (f32[6,6,8,128]{3,2,1,0:T(8,128)S(1)}, f32[6,6,8,128]{3,2,1,0:T(8,128)S(1)}, u32[]{:S(2)}, u32[]{:S(2)}) collective-permute-start(f32[6,6,8,128]{3,2,1,0:T(8,128)S(1)} %get-tuple-element.88), channel_id=1, source_target_pairs={{0,1},{1,0},{2,3},{3,2},{4,5},{5,4},{6,7},{7,6},{8,9},{9,8},{10,11... | collective-permute-start | bytes 442376 | tf_op jit(solution)/shard_map/ppermute | solution.py:291
  15.4 7.4 %collective-permute-start.2 = (f32[6,6,8,128]{3,2,1,0:T(8,128)S(1)}, f32[6,6,8,128]{3,2,1,0:T(8,128)S(1)}, u32[]{:S(2)}, u32[]{:S(2)}) collective-permute-start(f32[6,6,8,128]{3,2,1,0:T(8,128)S(1)} %get-tuple-element.63), channel_id=1, source_target_pairs={{0,15},{1,2},{2,1},{3,4},{4,3},{5,6},{6,5},{7,8},{8,7},{9,10},{10,... | collective-permute-start | bytes 442376 | tf_op jit(solution)/shard_map/ppermute | solution.py:290
  16.5 6.3 %collective-permute-start.3 = (f32[6,6,8,128]{3,2,1,0:T(8,128)S(1)}, f32[6,6,8,128]{3,2,1,0:T(8,128)S(1)}, u32[]{:S(2)}, u32[]{:S(2)}) collective-permute-start(f32[6,6,8,128]{3,2,1,0:T(8,128)S(1)} %get-tuple-element.64), channel_id=1, source_target_pairs={{0,1},{1,0},{2,3},{3,2},{4,5},{5,4},{6,7},{7,6},{8,9},{9,8},{10,11... | collective-permute-start | bytes 442376 | tf_op jit(solution)/shard_map/ppermute | solution.py:291
  17.9 7.4 %collective-permute-start.12 = (f32[6,6,8,128]{3,2,1,0:T(8,128)S(1)}, f32[6,6,8,128]{3,2,1,0:T(8,128)S(1)}, u32[]{:S(2)}, u32[]{:S(2)}) collective-permute-start(f32[6,6,8,128]{3,2,1,0:T(8,128)S(1)} %get-tuple-element.93), channel_id=1, source_target_pairs={{0,15},{1,2},{2,1},{3,4},{4,3},{5,6},{6,5},{7,8},{8,7},{9,10},{10,... | collective-permute-start | bytes 442376 | tf_op jit(solution)/shard_map/ppermute | solution.py:290
  22.2 3.1 %collective-permute-start.13 = (f32[6,6,8,128]{3,2,1,0:T(8,128)S(1)}, f32[6,6,8,128]{3,2,1,0:T(8,128)S(1)}, u32[]{:S(2)}, u32[]{:S(2)}) collective-permute-start(f32[6,6,8,128]{3,2,1,0:T(8,128)S(1)} %get-tuple-element.94), channel_id=1, source_target_pairs={{0,1},{1,0},{2,3},{3,2},{4,5},{5,4},{6,7},{7,6},{8,9},{9,8},{10,11... | collective-permute-start | bytes 442376 | tf_op jit(solution)/shard_map/ppermute | solution.py:291
  23.0 7.4 %collective-permute-start.4 = (f32[6,6,8,128]{3,2,1,0:T(8,128)S(1)}, f32[6,6,8,128]{3,2,1,0:T(8,128)S(1)}, u32[]{:S(2)}, u32[]{:S(2)}) collective-permute-start(f32[6,6,8,128]{3,2,1,0:T(8,128)S(1)} %get-tuple-element.69), channel_id=1, source_target_pairs={{0,15},{1,2},{2,1},{3,4},{4,3},{5,6},{6,5},{7,8},{8,7},{9,10},{10,... | collective-permute-start | bytes 442376 | tf_op jit(solution)/shard_map/ppermute | solution.py:290
  24.1 6.3 %collective-permute-start.5 = (f32[6,6,8,128]{3,2,1,0:T(8,128)S(1)}, f32[6,6,8,128]{3,2,1,0:T(8,128)S(1)}, u32[]{:S(2)}, u32[]{:S(2)}) collective-permute-start(f32[6,6,8,128]{3,2,1,0:T(8,128)S(1)} %get-tuple-element.70), channel_id=1, source_target_pairs={{0,1},{1,0},{2,3},{3,2},{4,5},{5,4},{6,7},{7,6},{8,9},{9,8},{10,11... | collective-permute-start | bytes 442376 | tf_op jit(solution)/shard_map/ppermute | solution.py:291
  25.5 7.4 %collective-permute-start.14 = (f32[6,6,8,128]{3,2,1,0:T(8,128)S(1)}, f32[6,6,8,128]{3,2,1,0:T(8,128)S(1)}, u32[]{:S(2)}, u32[]{:S(2)}) collective-permute-start(f32[6,6,8,128]{3,2,1,0:T(8,128)S(1)} %get-tuple-element.99), channel_id=1, source_target_pairs={{0,15},{1,2},{2,1},{3,4},{4,3},{5,6},{6,5},{7,8},{8,7},{9,10},{10,... | collective-permute-start | bytes 442376 | tf_op jit(solution)/shard_map/ppermute | solution.py:290
  29.8 3.1 %collective-permute-start.15 = (f32[6,6,8,128]{3,2,1,0:T(8,128)S(1)}, f32[6,6,8,128]{3,2,1,0:T(8,128)S(1)}, u32[]{:S(2)}, u32[]{:S(2)}) collective-permute-start(f32[6,6,8,128]{3,2,1,0:T(8,128)S(1)} %get-tuple-element.100), channel_id=1, source_target_pairs={{0,1},{1,0},{2,3},{3,2},{4,5},{5,4},{6,7},{7,6},{8,9},{9,8},{10,11... | collective-permute-start | bytes 442376 | tf_op jit(solution)/shard_map/ppermute | solution.py:291
  30.6 7.3 %collective-permute-start.6 = (f32[6,6,8,128]{3,2,1,0:T(8,128)S(1)}, f32[6,6,8,128]{3,2,1,0:T(8,128)S(1)}, u32[]{:S(2)}, u32[]{:S(2)}) collective-permute-start(f32[6,6,8,128]{3,2,1,0:T(8,128)S(1)} %get-tuple-element.75), channel_id=1, source_target_pairs={{0,15},{1,2},{2,1},{3,4},{4,3},{5,6},{6,5},{7,8},{8,7},{9,10},{10,... | collective-permute-start | bytes 442376 | tf_op jit(solution)/shard_map/ppermute | solution.py:290
  31.6 6.3 %collective-permute-start.7 = (f32[6,6,8,128]{3,2,1,0:T(8,128)S(1)}, f32[6,6,8,128]{3,2,1,0:T(8,128)S(1)}, u32[]{:S(2)}, u32[]{:S(2)}) collective-permute-start(f32[6,6,8,128]{3,2,1,0:T(8,128)S(1)} %get-tuple-element.76), channel_id=1, source_target_pairs={{0,1},{1,0},{2,3},{3,2},{4,5},{5,4},{6,7},{7,6},{8,9},{9,8},{10,11... | collective-permute-start | bytes 442376 | tf_op jit(solution)/shard_map/ppermute | solution.py:291

commit v5 on v0

--- a/solution.py
+++ b/solution.py
@@ -1,13 +1,390 @@
+import functools
+
 import jax
 import jax.numpy as jnp
 from jax import lax
+from jax.experimental import pallas as pl
+from jax.experimental.pallas import tpu as pltpu
 from jax.sharding import PartitionSpec as P
 
 NT = 8
 LS = 32
 
-
 cheb_coeffs = (0.6, -0.5, 0.35, -0.25, 0.15)
+
+
+def power_coeffs():
+    c0, c1, c2, c3, c4 = cheb_coeffs
+    return (c0 - c2 + c4, c1 - 3.0 * c3, 2.0 * c2 - 8.0 * c4, 4.0 * c3, 8.0 * c4)
+
+
+def lane_ids():
+    return lax.broadcasted_iota(jnp.int32, (8, 128), 1)
+
+
+def sublane_ids():
+    return lax.broadcasted_iota(jnp.int32, (8, 128), 0)
+
+
+def low_half():
+    return (lane_ids() // LS) % 2 == 0
+
+
+def first_of(p, q, low):
+    return jnp.where(low, p, pltpu.roll(q, LS, 1))
+
+
+def second_of(p, q, low):
+    return jnp.where(low, pltpu.roll(p, 128 - LS, 1), q)
+
+
+def z_next(value, z):
+    return jnp.where(z == LS - 1, pltpu.roll(value, LS - 1, 1), pltpu.roll(value, 127, 1))
+
+
+def z_prev(value, z):
+    return jnp.where(z == 0, pltpu.roll(value, 129 - LS, 1), pltpu.roll(value, 1, 1))
+
+
+def x_other(value, even):
+    return jnp.where(even, pltpu.roll(value, 7, 0), pltpu.roll(value, 1, 0))
+
+
+def mat_vec(load, vectors, sums, dagger=False):
+    for a in range(3):
+        for b in range(3):
+            w_re, w_im = load(b, a) if dagger else load(a, b)
+            for vec, acc in zip(vectors, sums):
+                v_re, v_im = vec[2 * b], vec[2 * b + 1]
+                if dagger:
+                    acc[2 * a] = acc[2 * a] + w_re * v_re + w_im * v_im
+                    acc[2 * a + 1] = acc[2 * a + 1] + w_re * v_im - w_im * v_re
+                else:
+                    acc[2 * a] = acc[2 * a] + w_re * v_re - w_im * v_im
+                    acc[2 * a + 1] = acc[2 * a + 1] + w_re * v_im + w_im * v_re
+
+
+def zeros(count):
+    return [[jnp.zeros((8, 128), jnp.float32) for _ in range(6)] for _ in range(count)]
+
+
+def link_at(ref, *index):
+    return lambda a, b: (ref[index + (a, b, 0)], ref[index + (a, b, 1)])
+
+
+def tile(ref, index):
+    return jnp.concatenate([ref[index + (slice(0, 8),)], ref[index + (slice(8, 16),)]], axis=1)
+
+
+def by_parity(run, near, far):
+    odd = lax.axis_index("space") % 2 == 1
+
+    @pl.when(odd)
+    def _():
+        run(near, far)
+
+    @pl.when(jnp.logical_not(odd))
+    def _():
+        run(far, near)
+
+
+def groups(ref):
+    width = 2 if ref.shape[1] % 2 == 0 else 1
+    return [range(i, i + width) for i in range(0, ref.shape[1], width)]
+
+
+def take(ref, row, pairs):
+    return [[ref[row, n, k] for k in range(6)] for n in pairs]
+
+
+def put(ref, row, pairs, vectors):
+    for n, vec in zip(pairs, vectors):
+        for k in range(6):
+            ref[row, n, k] = vec[k]
+
+
+def pack_links(links, inner, edge):
+    low = low_half()
+    z = lane_ids() % LS
+    even = sublane_ids() % 2 == 0
+    for a in range(3):
+        for b in range(3):
+            for part in range(2):
+                sign = 1.0 - 2.0 * part
+                x_link, y_link, z_link = (
+                    tile(links, (mu, a, b, part)) * (-1.0 / 6.0) for mu in range(3)
+                )
+                for row, pick in enumerate((first_of, second_of)):
+                    inner[row, 0, a, b, part] = pick(x_link, x_link, low)
+                    u_z = pick(z_link, z_link, low)
+                    inner[row, 1, a, b, part] = u_z
+                    inner[row, 2, b, a, part] = sign * z_prev(u_z, z)
+                u_y = first_of(y_link, y_link, low)
+                inner[0, 3, a, b, part] = u_y
+                inner[1, 3, b, a, part] = sign * u_y
+                edge[a, b, part] = second_of(y_link, y_link, low)
+    for row in range(2):
+        for part in range(2):
+            sign = 1.0 - 2.0 * part
+            own = [[inner[row, 0, a, b, part] for b in range(3)] for a in range(3)]
+            for a in range(3):
+                for b in range(3):
+                    inner[row, 0, a, b, part] = own[a][b] + sign * x_other(own[b][a], even)
+
+
+def add_inner(inner, row, pairs, field, sums):
+    z = lane_ids() % LS
+    even = sublane_ids() % 2 == 0
+    here = take(field, row, pairs)
+    mat_vec(link_at(inner, row, 0), [[x_other(c, even) for c in vec] for vec in here], sums)
+    mat_vec(link_at(inner, row, 1), [[z_next(c, z) for c in vec] for vec in here], sums)
+    mat_vec(link_at(inner, row, 2), [[z_prev(c, z) for c in vec] for vec in here], sums)
+    mat_vec(link_at(inner, row, 3), take(field, 1 - row, pairs), sums)
+
+
+def scaled_rows(coeff, start, row, pairs):
+    return [[coeff * c for c in vec] for vec in take(start, row, pairs)]
+
+
+def open_round(coeff, pairs, rows, start, inner, edge, sums_out, down, up):
+    for row in range(2):
+        sums = scaled_rows(coeff, start, row, pairs)
+        add_inner(inner, row, pairs, rows, sums)
+        put(sums_out, row, pairs, sums)
+        if row == 0:
+            put(down, 0, pairs, take(rows, 0, pairs))
+            put(down, 1, pairs, sums)
+        else:
+            for i, vectors in enumerate((take(rows, 1, pairs), sums)):
+                back = zeros(len(pairs))
+                mat_vec(link_at(edge), vectors, back, dagger=True)
+                put(up, i, pairs, back)
+
+
+def close_round(coeff, pairs, below, above, rows, sums_in, start, inner, edge, middle):
+    lower = [
+        [s + u for s, u in zip(*both)]
+        for both in zip(take(sums_in, 0, pairs), take(below, 0, pairs))
+    ]
+    put(middle, 0, pairs, lower)
+    upper = take(sums_in, 1, pairs)
+    mat_vec(link_at(edge), take(above, 0, pairs), upper)
+    put(middle, 1, pairs, upper)
+    result = []
+    for row in range(2):
+        sums = [
+            [c + (1.0 / 36.0) * r for c, r in zip(*both)]
+            for both in zip(scaled_rows(coeff, start, row, pairs), take(rows, row, pairs))
+        ]
+        add_inner(inner, row, pairs, middle, sums)
+        if row == 0:
+            sums = [
+                [s + u for s, u in zip(*both)] for both in zip(sums, take(below, 1, pairs))
+            ]
+        else:
+            mat_vec(link_at(edge), take(above, 1, pairs), sums)
+        result.append(sums)
+    return result
+
+
+def pack_rows(source, rows):
+    low = low_half()
+    for n in range(rows.shape[1]):
+        for k in range(6):
+            p, q = source(2 * n, k), source(2 * n + 1, k)
+            rows[0, n, k] = first_of(p, q, low)
+            rows[1, n, k] = second_of(p, q, low)
+
+
+def start_chunk(coeff, rows, inner, edge, sums, far_out, near_out):
+    def run(down, up):
+        for pairs in groups(rows):
+            open_round(coeff, pairs, rows, rows, inner, edge, sums, down, up)
+
+    by_parity(run, near_out, far_out)
+
+
+def first_kernel(
+    coeff, src, links, inner, edge, rows, sums, far_out, near_out, later, now, held, sems
+):
+    count = now.shape[0]
+    copies = [
+        pltpu.make_async_copy(links, held, sems.at[0]),
+        pltpu.make_async_copy(src.at[pl.ds(0, count)], now, sems.at[1]),
+        pltpu.make_async_copy(src.at[pl.ds(count, later.shape[0])], later, sems.at[2]),
+    ]
+    for copy in copies:
+        copy.start()
+    copies[0].wait()
+    pack_links(held, inner, edge)
+    copies[1].wait()
+    pack_rows(lambda n, k: tile(now, (n, k)), rows)
+    start_chunk(coeff, rows, inner, edge, sums, far_out, near_out)
+    copies[2].wait()
+
+
+def start_kernel(coeff, first, later, inner, edge, rows, sums, far_out, near_out):
+    pack_rows(lambda n, k: tile(later, (first + n, k)), rows)
+    start_chunk(coeff, rows, inner, edge, sums, far_out, near_out)
+
+
+def round_kernel(
+    coeff,
+    next_coeff,
+    far_in,
+    near_in,
+    rows,
+    sums_in,
+    start,
+    inner,
+    edge,
+    rows_out,
+    sums_out,
+    far_out,
+    near_out,
+    middle,
+):
+    def run(lower_side, upper_side):
+        below, down = lower_side
+        above, up = upper_side
+        for pairs in groups(rows):
+            result = close_round(
+                coeff, pairs, below, above, rows, sums_in, start, inner, edge, middle
+            )
+            for row in range(2):
+                put(rows_out, row, pairs, result[row])
+            open_round(next_coeff, pairs, rows_out, start, inner, edge, sums_out, down, up)
+
+    by_parity(run, (near_in, near_out), (far_in, far_out))
+
+
+def last_kernel(coeff, first, lead, far_in, near_in, rows, sums_in, start, inner, edge, *rest):
+    out, middle, filled, sems = rest[-4:]
+    low = low_half()
+
+    def store(n):
+        here = pl.ds(2 * n, 2)
+        there = pl.ds(first + 2 * n, 2)
+        return pltpu.make_async_copy(filled.at[here], out.at[there], sems.at[n])
+
+    def run(below, above):
+        for pairs in groups(rows):
+            lower, upper = close_round(
+                coeff, pairs, below, above, rows, sums_in, start, inner, edge, middle
+            )
+            for n, bottom, top in zip(pairs, lower, upper):
+                for k in range(6):
+                    p = first_of(bottom[k], top[k], low) * lead
+                    q = second_of(bottom[k], top[k], low) * lead
+                    for m, value in ((2 * n, p), (2 * n + 1, q)):
+                        filled[m, k, 0:8] = value[:, : 2 * LS]
+                        filled[m, k, 8:16] = value[:, 2 * LS :]
+                store(n).start()
+
+    by_parity(run, near_in, far_in)
+    for n in range(rows.shape[1]):
+        store(n).wait()
+
+
+VMEM_LIMIT = 32 * 1024 * 1024
+CHUNKS = 2
+
+
+def call(kernel, outs, args, flops, scratch=(), in_hbm=(), out_hbm=False, aliases={}):
+    moved = sum(4 * a.size for a in args) + sum(4 * o.size for o in outs)
+    args = [
+        pltpu.with_memory_space_constraint(a, pltpu.HBM) if i in in_hbm else a
+        for i, a in enumerate(args)
+    ]
+    vmem = pl.BlockSpec(memory_space=pltpu.VMEM)
+    hbm = pl.BlockSpec(memory_space=pltpu.HBM)
+    return pl.pallas_call(
+        kernel,
+        out_shape=outs,
+        in_specs=[hbm if i in in_hbm else vmem for i in range(len(args))],
+        out_specs=[hbm if out_hbm else vmem] * len(outs),
+        scratch_shapes=list(scratch),
+        input_output_aliases=aliases,
+        compiler_params=pltpu.CompilerParams(vmem_limit_bytes=VMEM_LIMIT),
+        cost_estimate=pl.CostEstimate(flops=flops, bytes_accessed=moved, transcendentals=0),
+    )(*args)
+
+
+def halo_body(links, sources):
+    vectors = sources.shape[0]
+    share = vectors // CHUNKS
+    pairs = share // 2
+    sites, planes = links.shape[4:]
+    f32 = functools.partial(jax.ShapeDtypeStruct, dtype=jnp.float32)
+    both = f32((2, pairs, 6, 8, 128))
+    middle = pltpu.VMEM(both.shape, jnp.float32)
+    source_view = jnp.swapaxes(sources, 3, 4).reshape(vectors, 6, planes, sites)
+    link_view = jnp.swapaxes(links, 4, 5)
+    chunk_shape = (share, 6, planes, sites)
+    powers = power_coeffs()
+    lead = powers[4]
+    steps = [powers[power] / lead for power in (3, 2, 1, 0)]
+    work = 2 * pairs * 36 * 2 * 1024
+    count = lax.axis_size("space")
+    near_pairs = [(d, d ^ 1) for d in range(count)]
+    far_pairs = [(d, (d + 1 if d % 2 else d - 1) % count) for d in range(count)]
+
+    def exchange(far_out, near_out):
+        far = lax.ppermute(far_out, "space", far_pairs)
+        return far, lax.ppermute(near_out, "space", near_pairs)
+
+    inner, edge, rows, sums, *sends, later = call(
+        functools.partial(first_kernel, steps[0]),
+        [
+            f32((2, 4, 3, 3, 2, 8, 128)),
+            f32((3, 3, 2, 8, 128)),
+            *[both] * 4,
+            f32((vectors - share, 6, planes, sites)),
+        ],
+        [source_view, link_view],
+        6 * work,
+        [
+            pltpu.VMEM(chunk_shape, jnp.float32),
+            pltpu.VMEM(link_view.shape, jnp.float32),
+            pltpu.SemaphoreType.DMA((3,)),
+        ],
+        (0, 1),
+    )
+    start, fields, halos = [rows], [(rows, sums)], [exchange(*sends)]
+    for chunk in range(1, CHUNKS):
+        rows, sums, *sends = call(
+            functools.partial(start_kernel, steps[0], (chunk - 1) * share),
+            [both] * 4,
+            [later, inner, edge],
+            6 * work,
+        )
+        start.append(rows)
+        fields.append((rows, sums))
+        halos.append(exchange(*sends))
+    for chunk in range(CHUNKS):
+        rows, sums, *sends = call(
+            functools.partial(round_kernel, steps[1], steps[2]),
+            [both] * 4,
+            [*halos[chunk], *fields[chunk], start[chunk], inner, edge],
+            12 * work,
+            [middle],
+        )
+        fields[chunk] = (rows, sums)
+        halos[chunk] = exchange(*sends)
+    out = None
+    for chunk in range(CHUNKS):
+        args = [*halos[chunk], *fields[chunk], start[chunk], inner, edge]
+        (out,) = call(
+            functools.partial(last_kernel, steps[3], chunk * share, lead),
+            [f32(source_view.shape)],
+            args if out is None else args + [out],
+            6 * work,
+            [middle, pltpu.VMEM(chunk_shape, jnp.float32), pltpu.SemaphoreType.DMA((pairs,))],
+            () if out is None else (len(args),),
+            True,
+            {} if out is None else {len(args): 0},
+        )
+    return jnp.swapaxes(out.reshape(vectors, 3, 2, planes, sites), 3, 4)
 
 
 def shifted(value, axis, steps):
@@ -54,7 +431,7 @@
     )
 
 
-def body(links, sources):
+def plane_body(links, sources):
     device_count = lax.axis_size("space")
     slabs = device_count // NT
     yz_local = links.shape[4]
@@ -122,6 +499,13 @@
     return ordered.reshape(vectors, 3, 2, yz_local, NT * slabs * planes)
 
 
+def body(links, sources):
+    sites, planes = sources.shape[3:]
+    if sites == 2 * LS and planes == 2 * NT and sources.shape[0] % (2 * CHUNKS) == 0:
+        return halo_body(links, sources)
+    return plane_body(links, sources)
+
+
 def solution(mesh):
     in_specs = (
         P(None, None, None, None, "space", "groups"),

time: 325 us -> 35.8 us (0.11)
  waiting for transfers between devices: 163 us -> 12 us
  other arithmetic: 73.5 us -> 0 us
  local copies, waits for them, and re-layouts: 30.4 us -> 0 us
  blocking collectives: 28.9 us -> 0 us
  starting transfers between devices: 23.5 us -> 11.4 us
  Pallas kernels: 0 us -> 12 us
    ppermute x8, waiting for transfers between devices: 137 us -> 12 us  [the longest x4 12 us: exchange(): far = lax.ppermute(far_out, 'space', far_pairs)]
    all_to_all x1 -> x0, blocking collectives: 28.9 us -> none  [body(): lax.all_to_all(outgoing, 'space', split_axis=3, concat_axis=1, tiled=True)]
    all_to_all x2 -> x0, waiting for transfers between devices: 26.8 us -> none  [the longest x1 19.6 us: body(): lax.all_to_all(source_send, 'space', split_axis=1, concat_axis=3, tiled=T...]
    sub x14 -> x0, other arithmetic: 26.3 us -> none  [the longest x12 20.7 us: apply_link(): real_part = real_part + link_re * vec_re - link_im * vec_im]
    add x13 -> x0, other arithmetic: 25.1 us -> none  [the longest x12 21.7 us: apply_dagger(): real_part = real_part + link_re * vec_re + link_im * vec_im]
    slice x53 -> x0, local copies, waits for them, and re-layouts: 17 us -> none  [the longest x8 3.3 us: z_ahead(): jnp.roll(array, -1, axis=-1)]
    all_to_all x2 -> x0, starting transfers between devices: 12.1 us -> none  [the longest x1 7.32 us: body(): lax.all_to_all(link_send, 'space', split_axis=1, concat_axis=3, tiled=True)]
    pallas_call x0 -> x6, Pallas kernels: none -> 12 us  [call(): pl.pallas_call(kernel, out_shape=outs, in_specs=[hbm if i in in_hbm else...]
  transfers between devices with their start and end apart: 10 -> 8, of which waited for: 10 -> 4; matrix products, arithmetic and copies ran while one was open for 22% -> 0% of each run, Pallas kernels for 0% -> 18%
where the time goes in v5:
time: 35.8 us; the launch traced here: 35.7 us
  Pallas kernels  12 us (34%)
  waiting for transfers between devices  12 us (34%)
  starting transfers between devices  11.4 us (32%)
    ppermute x4, waiting for transfers between devices, exchange(): far = lax.ppermute(far_out, 'space', far_pairs)  12 us
    pallas_call x6, Pallas kernels, call(): pl.pallas_call(kernel, out_shape=outs, in_specs=[hbm if i in in_hbm else...  12 us
    ppermute x4, starting transfers between devices, exchange(): far = lax.ppermute(far_out, 'space', far_pairs)  7.83 us
    ppermute x4, starting transfers between devices, exchange(): return (far, lax.ppermute(near_out, 'space', near_pairs))  3.62 us
  transfers between devices with their start and end apart: 8, of which 4 were waited for; matrix products, arithmetic and copies ran while one was open for 0% of the time, Pallas kernels for 18%

profile of v5, /device:TPU:1, one launch (start us, length us, event | category | flops | bytes accessed | tf_op | source)
XLA Modules:
  0.0 35.7 jit_solution(7453802459757444513)
XLA Ops:
  0.0 3.0 %shard_map.28 = (f32[2,4,3,3,2,8,128]{6,5,4,3,2,1,0:T(8,128)S(1)}, f32[3,3,2,8,128]{4,3,2,1,0:T(8,128)S(1)}, f32[2,6,6,8,128]{4,3,2,1,0:T(8,128)S(1)}, f32[2,6,6...) custom-call(f32[24,6,16,64]{3,2,1,0:T(8,128)} %bitcast.7, ...), custom_call_target="tpu_custom_call" | custom-call | flops 5308416 | bytes 2949120 | tf_op jit(solution)/shard_map/pallas_call | solution.py:301
  3.0 2.7 %collective-permute-start.4 = (f32[2,6,6,8,128]{4,3,2,1,0:T(8,128)S(1)}, f32[2,6,6,8,128]{4,3,2,1,0:T(8,128)S(1)}, u32[]{:S(2)}, u32[]{:S(2)}) collective-permute-start(f32[2,6,6,8,128]{4,3,2,1,0:T(8,128)S(1)} %get-tuple-element.35), channel_id=1, source_target_pairs={{0,15},{1,2},{2,1},{3,4},{4,3},{5,6},{6,5},{7,8},{8,7},{9,10},{10,... | collective-permute-start | bytes 884744 | tf_op jit(solution)/shard_map/ppermute | solution.py:333
  5.6 2.9 %collective-permute-start.5 = (f32[2,6,6,8,128]{4,3,2,1,0:T(8,128)S(1)}, f32[2,6,6,8,128]{4,3,2,1,0:T(8,128)S(1)}, u32[]{:S(2)}, u32[]{:S(2)}) collective-permute-start(f32[2,6,6,8,128]{4,3,2,1,0:T(8,128)S(1)} %get-tuple-element.36), channel_id=1, source_target_pairs={{0,1},{1,0},{2,3},{3,2},{4,5},{5,4},{6,7},{7,6},{8,9},{9,8},{10,11... | collective-permute-start | bytes 884744 | tf_op jit(solution)/shard_map/ppermute | solution.py:334
  8.5 1.2 %shard_map.29 = (f32[2,6,6,8,128]{4,3,2,1,0:T(8,128)S(1)}, f32[2,6,6,8,128]{4,3,2,1,0:T(8,128)S(1)}, f32[2,6,6,8,128]{4,3,2,1,0:T(8,128)S(1)}, f32[2,6,6,8,128]{4,3,2,1,0:T(8,128)S(1)}) custom-call(f32[12,6,16,64]{3,2,1,0:T(8,128)S(1)} %get-tuple-element.24.later, f32[2,4,3,3,2,8,128]{6,5,4,3,2,1,0:T(8,128)S(1)} %get-tuple-element.25.inner, ...), custom_call_target="tpu_custom_call" | custom-call | flops 5308416 | bytes 2138112 | tf_op jit(solution)/shard_map/pallas_call | solution.py:301
  9.7 0.1 collective-permute-start
  9.7 0.7 %collective-permute-start.1 = (f32[2,6,6,8,128]{4,3,2,1,0:T(8,128)S(1)}, f32[2,6,6,8,128]{4,3,2,1,0:T(8,128)S(1)}, u32[]{:S(2)}, u32[]{:S(2)}) collective-permute-start(f32[2,6,6,8,128]{4,3,2,1,0:T(8,128)S(1)} %get-tuple-element.28), channel_id=1, source_target_pairs={{0,1},{1,0},{2,3},{3,2},{4,5},{5,4},{6,7},{7,6},{8,9},{9,8},{10,11... | collective-permute-start | bytes 884744 | tf_op jit(solution)/shard_map/ppermute | solution.py:334
  10.5 5.1 %collective-permute-done.4.far_in = f32[2,6,6,8,128]{4,3,2,1,0:T(8,128)S(1)} collective-permute-done((f32[2,6,6,8,128]{4,3,2,1,0:T(8,128)S(1)}, f32[2,6,6,8,128]{4,3,2,1,0:T(8,128)S(1)}, u32[]{:S(2)}, u32[]{:S(2)}) %collective-permute-start.4) | collective-permute-done | bytes 294944 | tf_op jit(solution)/shard_map/ppermute | solution.py:333
  15.6 0.0 collective-permute-done.5.near_in
  15.6 1.5 %shard_map.31 = (f32[2,6,6,8,128]{4,3,2,1,0:T(8,128)S(1)}, f32[2,6,6,8,128]{4,3,2,1,0:T(8,128)S(1)}, f32[2,6,6,8,128]{4,3,2,1,0:T(8,128)S(1)}, f32[2,6,6,8,128]{4,3,2,1,0:T(8,128)S(1)}) custom-call(f32[2,6,6,8,128]{4,3,2,1,0:T(8,128)S(1)} %collective-permute-done.4.far_in, f32[2,6,6,8,128]{4,3,2,1,0:T(8,128)S(1)} %collective-permute-done.5.near_in, ...), custom_call_target="tpu_custom_call" | custom-call | flops 10616832 | bytes 3317760 | tf_op jit(solution)/shard_map/pallas_call | solution.py:301
  17.1 2.5 %collective-permute-start.6 = (f32[2,6,6,8,128]{4,3,2,1,0:T(8,128)S(1)}, f32[2,6,6,8,128]{4,3,2,1,0:T(8,128)S(1)}, u32[]{:S(2)}, u32[]{:S(2)}) collective-permute-start(f32[2,6,6,8,128]{4,3,2,1,0:T(8,128)S(1)} %get-tuple-element.39), channel_id=1, source_target_pairs={{0,15},{1,2},{2,1},{3,4},{4,3},{5,6},{6,5},{7,8},{8,7},{9,10},{10,... | collective-permute-start | bytes 884744 | tf_op jit(solution)/shard_map/ppermute | solution.py:333
  19.7 0.0 collective-permute-start.7
  19.7 2.3 %collective-permute-done.far_in = f32[2,6,6,8,128]{4,3,2,1,0:T(8,128)S(1)} collective-permute-done((f32[2,6,6,8,128]{4,3,2,1,0:T(8,128)S(1)}, f32[2,6,6,8,128]{4,3,2,1,0:T(8,128)S(1)}, u32[]{:S(2)}, u32[]{:S(2)}) %collective-permute-start) | collective-permute-done | bytes 294944 | tf_op jit(solution)/shard_map/ppermute | solution.py:333
  21.9 0.0 collective-permute-done.1.near_in
  21.9 1.5 %shard_map.30 = (f32[2,6,6,8,128]{4,3,2,1,0:T(8,128)S(1)}, f32[2,6,6,8,128]{4,3,2,1,0:T(8,128)S(1)}, f32[2,6,6,8,128]{4,3,2,1,0:T(8,128)S(1)}, f32[2,6,6,8,128]{4,3,2,1,0:T(8,128)S(1)}) custom-call(f32[2,6,6,8,128]{4,3,2,1,0:T(8,128)S(1)} %collective-permute-done.far_in, f32[2,6,6,8,128]{4,3,2,1,0:T(8,128)S(1)} %collective-permute-done.1.near_in, ...), custom_call_target="tpu_custom_call" | custom-call | flops 10616832 | bytes 3317760 | tf_op jit(solution)/shard_map/pallas_call | solution.py:301
  23.4 2.5 %collective-permute-start.2 = (f32[2,6,6,8,128]{4,3,2,1,0:T(8,128)S(1)}, f32[2,6,6,8,128]{4,3,2,1,0:T(8,128)S(1)}, u32[]{:S(2)}, u32[]{:S(2)}) collective-permute-start(f32[2,6,6,8,128]{4,3,2,1,0:T(8,128)S(1)} %get-tuple-element.31), channel_id=1, source_target_pairs={{0,15},{1,2},{2,1},{3,4},{4,3},{5,6},{6,5},{7,8},{8,7},{9,10},{10,... | collective-permute-start | bytes 884744 | tf_op jit(solution)/shard_map/ppermute | solution.py:333
  26.0 0.0 collective-permute-start.3
  26.0 2.3 %collective-permute-done.6.far_in = f32[2,6,6,8,128]{4,3,2,1,0:T(8,128)S(1)} collective-permute-done((f32[2,6,6,8,128]{4,3,2,1,0:T(8,128)S(1)}, f32[2,6,6,8,128]{4,3,2,1,0:T(8,128)S(1)}, u32[]{:S(2)}, u32[]{:S(2)}) %collective-permute-start.6) | collective-permute-done | bytes 294944 | tf_op jit(solution)/shard_map/ppermute | solution.py:333
  28.3 0.0 collective-permute-done.7.near_in
  28.3 2.5 %shard_map.32.rest_0_ = f32[24,6,16,64]{3,2,1,0:T(8,128)} custom-call(f32[2,6,6,8,128]{4,3,2,1,0:T(8,128)S(1)} %collective-permute-done.6.far_in, f32[2,6,6,8,128]{4,3,2,1,0:T(8,128)S(1)} %collective-permute-done.7.near_in, f32[2,6,6,8,128]{4,3,2,1,0:T(8,128)S(1)} %get-tuple-element.41.rows, f32[2,6,6,8,128]{4,3,2,1,0:T(8,128)S(1)} %get-tuple-element.42.sums_in, ...), custom_call_target="tpu_custom_call" | custom-call | flops 5308416 | bytes 2727936 | tf_op jit(solution)/shard_map/pallas_call | solution.py:301
  30.7 2.3 %collective-permute-done.2.far_in = f32[2,6,6,8,128]{4,3,2,1,0:T(8,128)S(1)} collective-permute-done((f32[2,6,6,8,128]{4,3,2,1,0:T(8,128)S(1)}, f32[2,6,6,8,128]{4,3,2,1,0:T(8,128)S(1)}, u32[]{:S(2)}, u32[]{:S(2)}) %collective-permute-start.2) | collective-permute-done | bytes 294944 | tf_op jit(solution)/shard_map/ppermute | solution.py:333
  33.1 0.0 collective-permute-done.3.near_in
  33.1 2.5 %shard_map.33 = f32[24,6,16,64]{3,2,1,0:T(8,128)} custom-call(f32[2,6,6,8,128]{4,3,2,1,0:T(8,128)S(1)} %collective-permute-done.2.far_in, f32[2,6,6,8,128]{4,3,2,1,0:T(8,128)S(1)} %collective-permute-done.3.near_in, f32[2,6,6,8,128]{4,3,2,1,0:T(8,128)S(1)} %get-tuple-element.33.rows, ...), custom_call_target="tpu_custom_call", output_to_operand_aliasing={{}: (7, {})} | custom-call | flops 5308416 | bytes 3317760 | tf_op jit(solution)/shard_map/pallas_call | solution.py:301
Async XLA Ops:
  3.0 12.7 %collective-permute-start.4 = (f32[2,6,6,8,128]{4,3,2,1,0:T(8,128)S(1)}, f32[2,6,6,8,128]{4,3,2,1,0:T(8,128)S(1)}, u32[]{:S(2)}, u32[]{:S(2)}) collective-permute-start(f32[2,6,6,8,128]{4,3,2,1,0:T(8,128)S(1)} %get-tuple-element.35), channel_id=1, source_target_pairs={{0,15},{1,2},{2,1},{3,4},{4,3},{5,6},{6,5},{7,8},{8,7},{9,10},{10,... | collective-permute-start | bytes 884744 | tf_op jit(solution)/shard_map/ppermute | solution.py:333
  5.6 10.0 %collective-permute-start.5 = (f32[2,6,6,8,128]{4,3,2,1,0:T(8,128)S(1)}, f32[2,6,6,8,128]{4,3,2,1,0:T(8,128)S(1)}, u32[]{:S(2)}, u32[]{:S(2)}) collective-permute-start(f32[2,6,6,8,128]{4,3,2,1,0:T(8,128)S(1)} %get-tuple-element.36), channel_id=1, source_target_pairs={{0,1},{1,0},{2,3},{3,2},{4,5},{5,4},{6,7},{7,6},{8,9},{9,8},{10,11... | collective-permute-start | bytes 884744 | tf_op jit(solution)/shard_map/ppermute | solution.py:334
  9.7 12.3 %collective-permute-start = (f32[2,6,6,8,128]{4,3,2,1,0:T(8,128)S(1)}, f32[2,6,6,8,128]{4,3,2,1,0:T(8,128)S(1)}, u32[]{:S(2)}, u32[]{:S(2)}) collective-permute-start(f32[2,6,6,8,128]{4,3,2,1,0:T(8,128)S(1)} %get-tuple-element.27), channel_id=1, source_target_pairs={{0,15},{1,2},{2,1},{3,4},{4,3},{5,6},{6,5},{7,8},{8,7},{9,10},{10,... | collective-permute-start | bytes 884744 | tf_op jit(solution)/shard_map/ppermute | solution.py:333
  9.7 12.2 %collective-permute-start.1 = (f32[2,6,6,8,128]{4,3,2,1,0:T(8,128)S(1)}, f32[2,6,6,8,128]{4,3,2,1,0:T(8,128)S(1)}, u32[]{:S(2)}, u32[]{:S(2)}) collective-permute-start(f32[2,6,6,8,128]{4,3,2,1,0:T(8,128)S(1)} %get-tuple-element.28), channel_id=1, source_target_pairs={{0,1},{1,0},{2,3},{3,2},{4,5},{5,4},{6,7},{7,6},{8,9},{9,8},{10,11... | collective-permute-start | bytes 884744 | tf_op jit(solution)/shard_map/ppermute | solution.py:334
  17.1 11.1 %collective-permute-start.6 = (f32[2,6,6,8,128]{4,3,2,1,0:T(8,128)S(1)}, f32[2,6,6,8,128]{4,3,2,1,0:T(8,128)S(1)}, u32[]{:S(2)}, u32[]{:S(2)}) collective-permute-start(f32[2,6,6,8,128]{4,3,2,1,0:T(8,128)S(1)} %get-tuple-element.39), channel_id=1, source_target_pairs={{0,15},{1,2},{2,1},{3,4},{4,3},{5,6},{6,5},{7,8},{8,7},{9,10},{10,... | collective-permute-start | bytes 884744 | tf_op jit(solution)/shard_map/ppermute | solution.py:333
  19.7 8.6 %collective-permute-start.7 = (f32[2,6,6,8,128]{4,3,2,1,0:T(8,128)S(1)}, f32[2,6,6,8,128]{4,3,2,1,0:T(8,128)S(1)}, u32[]{:S(2)}, u32[]{:S(2)}) collective-permute-start(f32[2,6,6,8,128]{4,3,2,1,0:T(8,128)S(1)} %get-tuple-element.40), channel_id=1, source_target_pairs={{0,1},{1,0},{2,3},{3,2},{4,5},{5,4},{6,7},{7,6},{8,9},{9,8},{10,11... | collective-permute-start | bytes 884744 | tf_op jit(solution)/shard_map/ppermute | solution.py:334
  23.4 9.6 %collective-permute-start.2 = (f32[2,6,6,8,128]{4,3,2,1,0:T(8,128)S(1)}, f32[2,6,6,8,128]{4,3,2,1,0:T(8,128)S(1)}, u32[]{:S(2)}, u32[]{:S(2)}) collective-permute-start(f32[2,6,6,8,128]{4,3,2,1,0:T(8,128)S(1)} %get-tuple-element.31), channel_id=1, source_target_pairs={{0,15},{1,2},{2,1},{3,4},{4,3},{5,6},{6,5},{7,8},{8,7},{9,10},{10,... | collective-permute-start | bytes 884744 | tf_op jit(solution)/shard_map/ppermute | solution.py:333
  26.0 7.1 %collective-permute-start.3 = (f32[2,6,6,8,128]{4,3,2,1,0:T(8,128)S(1)}, f32[2,6,6,8,128]{4,3,2,1,0:T(8,128)S(1)}, u32[]{:S(2)}, u32[]{:S(2)}) collective-permute-start(f32[2,6,6,8,128]{4,3,2,1,0:T(8,128)S(1)} %get-tuple-element.32), channel_id=1, source_target_pairs={{0,1},{1,0},{2,3},{3,2},{4,5},{5,4},{6,7},{7,6},{8,9},{9,8},{10,11... | collective-permute-start | bytes 884744 | tf_op jit(solution)/shard_map/ppermute | solution.py:334

commit v6 on v5

--- a/solution.py
+++ b/solution.py
@@ -287,7 +287,7 @@
 
 
 VMEM_LIMIT = 32 * 1024 * 1024
-CHUNKS = 2
+CHUNKS = 3
 
 
 def call(kernel, outs, args, flops, scratch=(), in_hbm=(), out_hbm=False, aliases={}):

time: 35.8 us -> 34.6 us (0.966)
  waiting for transfers between devices: 12 us -> 7.97 us
  starting transfers between devices: 11.4 us -> 14.9 us
  Pallas kernels: 12 us -> 11.3 us
    ppermute x4 -> x6, starting transfers between devices: 3.62 us -> 10.1 us  [exchange(): return (far, lax.ppermute(near_out, 'space', near_pairs))]
    ppermute x4 -> x6, waiting for transfers between devices: 12 us -> 7.95 us  [exchange(): far = lax.ppermute(far_out, 'space', far_pairs)]
    ppermute x4 -> x6, starting transfers between devices: 7.83 us -> 4.89 us  [exchange(): far = lax.ppermute(far_out, 'space', far_pairs)]
    pallas_call x6 -> x9, Pallas kernels: 12 us -> 11.3 us  [call(): pl.pallas_call(kernel, out_shape=outs, in_specs=[hbm if i in in_hbm else...]
  transfers between devices with their start and end apart: 8 -> 12, of which waited for: 4 -> 6; matrix products, arithmetic and copies ran while one was open for 0% -> 0% of each run, Pallas kernels for 18% -> 21%
where the time goes in v6:
time: 34.6 us; the launch traced here: 34.5 us
  starting transfers between devices  14.9 us (43%)
  Pallas kernels  11.3 us (33%)
  waiting for transfers between devices  7.97 us (23%)
    pallas_call x9, Pallas kernels, call(): pl.pallas_call(kernel, out_shape=outs, in_specs=[hbm if i in in_hbm else...  11.3 us
    ppermute x6, starting transfers between devices, exchange(): return (far, lax.ppermute(near_out, 'space', near_pairs))  10.1 us
    ppermute x6, waiting for transfers between devices, exchange(): far = lax.ppermute(far_out, 'space', far_pairs)  7.95 us
    ppermute x6, starting transfers between devices, exchange(): far = lax.ppermute(far_out, 'space', far_pairs)  4.89 us
  transfers between devices with their start and end apart: 12, of which 6 were waited for; matrix products, arithmetic and copies ran while one was open for 0% of the time, Pallas kernels for 21%

profile of v6, /device:TPU:1, one launch (start us, length us, event | category | flops | bytes accessed | tf_op | source)
XLA Modules:
  0.0 34.5 jit_solution(9444190440080238698)
XLA Ops:
  0.0 2.6 %shard_map.28 = (f32[2,4,3,3,2,8,128]{6,5,4,3,2,1,0:T(8,128)S(1)}, f32[3,3,2,8,128]{4,3,2,1,0:T(8,128)S(1)}, f32[2,4,6,8,128]{4,3,2,1,0:T(8,128)S(1)}, f32[2,4,6...) custom-call(f32[24,6,16,64]{3,2,1,0:T(8,128)} %bitcast.7, ...), custom_call_target="tpu_custom_call" | custom-call | flops 3538944 | bytes 2654208 | tf_op jit(solution)/shard_map/pallas_call | solution.py:301
  2.6 2.7 %collective-permute-start.8 = (f32[2,4,6,8,128]{4,3,2,1,0:T(8,128)S(1)}, f32[2,4,6,8,128]{4,3,2,1,0:T(8,128)S(1)}, u32[]{:S(2)}, u32[]{:S(2)}) collective-permute-start(f32[2,4,6,8,128]{4,3,2,1,0:T(8,128)S(1)} %get-tuple-element.51), channel_id=1, source_target_pairs={{0,15},{1,2},{2,1},{3,4},{4,3},{5,6},{6,5},{7,8},{8,7},{9,10},{10,... | collective-permute-start | bytes 589832 | tf_op jit(solution)/shard_map/ppermute | solution.py:333
  5.2 2.9 %collective-permute-start.9 = (f32[2,4,6,8,128]{4,3,2,1,0:T(8,128)S(1)}, f32[2,4,6,8,128]{4,3,2,1,0:T(8,128)S(1)}, u32[]{:S(2)}, u32[]{:S(2)}) collective-permute-start(f32[2,4,6,8,128]{4,3,2,1,0:T(8,128)S(1)} %get-tuple-element.52), channel_id=1, source_target_pairs={{0,1},{1,0},{2,3},{3,2},{4,5},{5,4},{6,7},{7,6},{8,9},{9,8},{10,11... | collective-permute-start | bytes 589832 | tf_op jit(solution)/shard_map/ppermute | solution.py:334
  8.1 0.7 %shard_map.31 = (f32[2,4,6,8,128]{4,3,2,1,0:T(8,128)S(1)}, f32[2,4,6,8,128]{4,3,2,1,0:T(8,128)S(1)}, f32[2,4,6,8,128]{4,3,2,1,0:T(8,128)S(1)}, f32[2,4,6,8,128]{4,3,2,1,0:T(8,128)S(1)}) custom-call(f32[16,6,16,64]{3,2,1,0:T(8,128)S(1)} %get-tuple-element.32.later, f32[2,4,3,3,2,8,128]{6,5,4,3,2,1,0:T(8,128)S(1)} %get-tuple-element.33.inner, ...), custom_call_target="tpu_custom_call" | custom-call | flops 3538944 | bytes 1843200 | tf_op jit(solution)/shard_map/pallas_call | solution.py:301
  8.9 0.7 %collective-permute-start.5 = (f32[2,4,6,8,128]{4,3,2,1,0:T(8,128)S(1)}, f32[2,4,6,8,128]{4,3,2,1,0:T(8,128)S(1)}, u32[]{:S(2)}, u32[]{:S(2)}) collective-permute-start(f32[2,4,6,8,128]{4,3,2,1,0:T(8,128)S(1)} %get-tuple-element.44), channel_id=1, source_target_pairs={{0,1},{1,0},{2,3},{3,2},{4,5},{5,4},{6,7},{7,6},{8,9},{9,8},{10,11... | collective-permute-start | bytes 589832 | tf_op jit(solution)/shard_map/ppermute | solution.py:334
  9.6 0.7 %shard_map.29 = (f32[2,4,6,8,128]{4,3,2,1,0:T(8,128)S(1)}, f32[2,4,6,8,128]{4,3,2,1,0:T(8,128)S(1)}, f32[2,4,6,8,128]{4,3,2,1,0:T(8,128)S(1)}, f32[2,4,6,8,128]{4,3,2,1,0:T(8,128)S(1)}) custom-call(f32[16,6,16,64]{3,2,1,0:T(8,128)S(1)} %get-tuple-element.32.later, f32[2,4,3,3,2,8,128]{6,5,4,3,2,1,0:T(8,128)S(1)} %get-tuple-element.33.inner, ...), custom_call_target="tpu_custom_call" | custom-call | flops 3538944 | bytes 1843200 | tf_op jit(solution)/shard_map/pallas_call | solution.py:301
  10.3 1.1 %collective-permute-start = (f32[2,4,6,8,128]{4,3,2,1,0:T(8,128)S(1)}, f32[2,4,6,8,128]{4,3,2,1,0:T(8,128)S(1)}, u32[]{:S(2)}, u32[]{:S(2)}) collective-permute-start(f32[2,4,6,8,128]{4,3,2,1,0:T(8,128)S(1)} %get-tuple-element.35), channel_id=1, source_target_pairs={{0,15},{1,2},{2,1},{3,4},{4,3},{5,6},{6,5},{7,8},{8,7},{9,10},{10,... | collective-permute-start | bytes 589832 | tf_op jit(solution)/shard_map/ppermute | solution.py:333
  11.3 0.7 %collective-permute-done.8.far_in = f32[2,4,6,8,128]{4,3,2,1,0:T(8,128)S(1)} collective-permute-done((f32[2,4,6,8,128]{4,3,2,1,0:T(8,128)S(1)}, f32[2,4,6,8,128]{4,3,2,1,0:T(8,128)S(1)}, u32[]{:S(2)}, u32[]{:S(2)}) %collective-permute-start.8) | collective-permute-done | bytes 196640 | tf_op jit(solution)/shard_map/ppermute | solution.py:333
  12.1 2.0 %collective-permute-start.1 = (f32[2,4,6,8,128]{4,3,2,1,0:T(8,128)S(1)}, f32[2,4,6,8,128]{4,3,2,1,0:T(8,128)S(1)}, u32[]{:S(2)}, u32[]{:S(2)}) collective-permute-start(f32[2,4,6,8,128]{4,3,2,1,0:T(8,128)S(1)} %get-tuple-element.36), channel_id=1, source_target_pairs={{0,1},{1,0},{2,3},{3,2},{4,5},{5,4},{6,7},{7,6},{8,9},{9,8},{10,11... | collective-permute-start | bytes 589832 | tf_op jit(solution)/shard_map/ppermute | solution.py:334
  14.1 1.0 %shard_map.33 = (f32[2,4,6,8,128]{4,3,2,1,0:T(8,128)S(1)}, f32[2,4,6,8,128]{4,3,2,1,0:T(8,128)S(1)}, f32[2,4,6,8,128]{4,3,2,1,0:T(8,128)S(1)}, f32[2,4,6,8,128]{4,3,2,1,0:T(8,128)S(1)}) custom-call(f32[2,4,6,8,128]{4,3,2,1,0:T(8,128)S(1)} %collective-permute-done.8.far_in, f32[2,4,6,8,128]{4,3,2,1,0:T(8,128)S(1)} %collective-permute-done.9.near_in, ...), custom_call_target="tpu_custom_call" | custom-call | flops 7077888 | bytes 2433024 | tf_op jit(solution)/shard_map/pallas_call | solution.py:301
  15.1 0.6 %collective-permute-start.10 = (f32[2,4,6,8,128]{4,3,2,1,0:T(8,128)S(1)}, f32[2,4,6,8,128]{4,3,2,1,0:T(8,128)S(1)}, u32[]{:S(2)}, u32[]{:S(2)}) collective-permute-start(f32[2,4,6,8,128]{4,3,2,1,0:T(8,128)S(1)} %get-tuple-element.55), channel_id=1, source_target_pairs={{0,15},{1,2},{2,1},{3,4},{4,3},{5,6},{6,5},{7,8},{8,7},{9,10},{10,... | collective-permute-start | bytes 589832 | tf_op jit(solution)/shard_map/ppermute | solution.py:333
  15.6 0.7 %collective-permute-done.4.far_in = f32[2,4,6,8,128]{4,3,2,1,0:T(8,128)S(1)} collective-permute-done((f32[2,4,6,8,128]{4,3,2,1,0:T(8,128)S(1)}, f32[2,4,6,8,128]{4,3,2,1,0:T(8,128)S(1)}, u32[]{:S(2)}, u32[]{:S(2)}) %collective-permute-start.4) | collective-permute-done | bytes 196640 | tf_op jit(solution)/shard_map/ppermute | solution.py:333
  16.3 3.1 %collective-permute-start.11 = (f32[2,4,6,8,128]{4,3,2,1,0:T(8,128)S(1)}, f32[2,4,6,8,128]{4,3,2,1,0:T(8,128)S(1)}, u32[]{:S(2)}, u32[]{:S(2)}) collective-permute-start(f32[2,4,6,8,128]{4,3,2,1,0:T(8,128)S(1)} %get-tuple-element.56), channel_id=1, source_target_pairs={{0,1},{1,0},{2,3},{3,2},{4,5},{5,4},{6,7},{7,6},{8,9},{9,8},{10,11... | collective-permute-start | bytes 589832 | tf_op jit(solution)/shard_map/ppermute | solution.py:334
  19.4 1.0 %shard_map.32 = (f32[2,4,6,8,128]{4,3,2,1,0:T(8,128)S(1)}, f32[2,4,6,8,128]{4,3,2,1,0:T(8,128)S(1)}, f32[2,4,6,8,128]{4,3,2,1,0:T(8,128)S(1)}, f32[2,4,6,8,128]{4,3,2,1,0:T(8,128)S(1)}) custom-call(f32[2,4,6,8,128]{4,3,2,1,0:T(8,128)S(1)} %collective-permute-done.4.far_in, f32[2,4,6,8,128]{4,3,2,1,0:T(8,128)S(1)} %collective-permute-done.5.near_in, ...), custom_call_target="tpu_custom_call" | custom-call | flops 7077888 | bytes 2433024 | tf_op jit(solution)/shard_map/pallas_call | solution.py:301
  20.5 2.1 %collective-permute-done.far_in = f32[2,4,6,8,128]{4,3,2,1,0:T(8,128)S(1)} collective-permute-done((f32[2,4,6,8,128]{4,3,2,1,0:T(8,128)S(1)}, f32[2,4,6,8,128]{4,3,2,1,0:T(8,128)S(1)}, u32[]{:S(2)}, u32[]{:S(2)}) %collective-permute-start) | collective-permute-done | bytes 196640 | tf_op jit(solution)/shard_map/ppermute | solution.py:333
  22.6 1.0 %shard_map.30 = (f32[2,4,6,8,128]{4,3,2,1,0:T(8,128)S(1)}, f32[2,4,6,8,128]{4,3,2,1,0:T(8,128)S(1)}, f32[2,4,6,8,128]{4,3,2,1,0:T(8,128)S(1)}, f32[2,4,6,8,128]{4,3,2,1,0:T(8,128)S(1)}) custom-call(f32[2,4,6,8,128]{4,3,2,1,0:T(8,128)S(1)} %collective-permute-done.far_in, f32[2,4,6,8,128]{4,3,2,1,0:T(8,128)S(1)} %collective-permute-done.1.near_in, ...), custom_call_target="tpu_custom_call" | custom-call | flops 7077888 | bytes 2433024 | tf_op jit(solution)/shard_map/pallas_call | solution.py:301
  23.6 0.5 %collective-permute-start.2 = (f32[2,4,6,8,128]{4,3,2,1,0:T(8,128)S(1)}, f32[2,4,6,8,128]{4,3,2,1,0:T(8,128)S(1)}, u32[]{:S(2)}, u32[]{:S(2)}) collective-permute-start(f32[2,4,6,8,128]{4,3,2,1,0:T(8,128)S(1)} %get-tuple-element.39), channel_id=1, source_target_pairs={{0,15},{1,2},{2,1},{3,4},{4,3},{5,6},{6,5},{7,8},{8,7},{9,10},{10,... | collective-permute-start | bytes 589832 | tf_op jit(solution)/shard_map/ppermute | solution.py:333
  24.0 0.7 %collective-permute-done.10.far_in = f32[2,4,6,8,128]{4,3,2,1,0:T(8,128)S(1)} collective-permute-done((f32[2,4,6,8,128]{4,3,2,1,0:T(8,128)S(1)}, f32[2,4,6,8,128]{4,3,2,1,0:T(8,128)S(1)}, u32[]{:S(2)}, u32[]{:S(2)}) %collective-permute-start.10) | collective-permute-done | bytes 196640 | tf_op jit(solution)/shard_map/ppermute | solution.py:333
  24.7 1.3 %collective-permute-start.3 = (f32[2,4,6,8,128]{4,3,2,1,0:T(8,128)S(1)}, f32[2,4,6,8,128]{4,3,2,1,0:T(8,128)S(1)}, u32[]{:S(2)}, u32[]{:S(2)}) collective-permute-start(f32[2,4,6,8,128]{4,3,2,1,0:T(8,128)S(1)} %get-tuple-element.40), channel_id=1, source_target_pairs={{0,1},{1,0},{2,3},{3,2},{4,5},{5,4},{6,7},{7,6},{8,9},{9,8},{10,11... | collective-permute-start | bytes 589832 | tf_op jit(solution)/shard_map/ppermute | solution.py:334
  26.0 1.4 %shard_map.34.rest_0_ = f32[24,6,16,64]{3,2,1,0:T(8,128)} custom-call(f32[2,4,6,8,128]{4,3,2,1,0:T(8,128)S(1)} %collective-permute-done.10.far_in, f32[2,4,6,8,128]{4,3,2,1,0:T(8,128)S(1)} %collective-permute-done.11.near_in, f32[2,4,6,8,128]{4,3,2,1,0:T(8,128)S(1)} %get-tuple-element.57.rows, f32[2,4,6,8,128]{4,3,2,1,0:T(8,128)S(1)} %get-tuple-element.58.sums_in, ...), custom_call_target="tpu_custom_call" | custom-call | flops 3538944 | bytes 2236416 | tf_op jit(solution)/shard_map/pallas_call | solution.py:301
  27.4 1.5 %collective-permute-done.6.far_in = f32[2,4,6,8,128]{4,3,2,1,0:T(8,128)S(1)} collective-permute-done((f32[2,4,6,8,128]{4,3,2,1,0:T(8,128)S(1)}, f32[2,4,6,8,128]{4,3,2,1,0:T(8,128)S(1)}, u32[]{:S(2)}, u32[]{:S(2)}) %collective-permute-start.6) | collective-permute-done | bytes 196640 | tf_op jit(solution)/shard_map/ppermute | solution.py:333
  28.9 1.6 %shard_map.35.rest_0_ = f32[24,6,16,64]{3,2,1,0:T(8,128)} custom-call(f32[2,4,6,8,128]{4,3,2,1,0:T(8,128)S(1)} %collective-permute-done.6.far_in, f32[2,4,6,8,128]{4,3,2,1,0:T(8,128)S(1)} %collective-permute-done.7.near_in, f32[2,4,6,8,128]{4,3,2,1,0:T(8,128)S(1)} %get-tuple-element.49.rows, ...), custom_call_target="tpu_custom_call", output_to_operand_aliasing={{}: (7, {})} | custom-call | flops 3538944 | bytes 2826240 | tf_op jit(solution)/shard_map/pallas_call | solution.py:301
  30.5 2.4 %collective-permute-done.2.far_in = f32[2,4,6,8,128]{4,3,2,1,0:T(8,128)S(1)} collective-permute-done((f32[2,4,6,8,128]{4,3,2,1,0:T(8,128)S(1)}, f32[2,4,6,8,128]{4,3,2,1,0:T(8,128)S(1)}, u32[]{:S(2)}, u32[]{:S(2)}) %collective-permute-start.2) | collective-permute-done | bytes 196640 | tf_op jit(solution)/shard_map/ppermute | solution.py:333
  32.9 1.4 %shard_map.36 = f32[24,6,16,64]{3,2,1,0:T(8,128)} custom-call(f32[2,4,6,8,128]{4,3,2,1,0:T(8,128)S(1)} %collective-permute-done.2.far_in, f32[2,4,6,8,128]{4,3,2,1,0:T(8,128)S(1)} %collective-permute-done.3.near_in, f32[2,4,6,8,128]{4,3,2,1,0:T(8,128)S(1)} %get-tuple-element.41.rows, ...), custom_call_target="tpu_custom_call", output_to_operand_aliasing={{}: (7, {})} | custom-call | flops 3538944 | bytes 2826240 | tf_op jit(solution)/shard_map/pallas_call | solution.py:301
  (9 shorter events, 0.2 us)
Async XLA Ops:
  2.6 9.5 %collective-permute-start.8 = (f32[2,4,6,8,128]{4,3,2,1,0:T(8,128)S(1)}, f32[2,4,6,8,128]{4,3,2,1,0:T(8,128)S(1)}, u32[]{:S(2)}, u32[]{:S(2)}) collective-permute-start(f32[2,4,6,8,128]{4,3,2,1,0:T(8,128)S(1)} %get-tuple-element.51), channel_id=1, source_target_pairs={{0,15},{1,2},{2,1},{3,4},{4,3},{5,6},{6,5},{7,8},{8,7},{9,10},{10,... | collective-permute-start | bytes 589832 | tf_op jit(solution)/shard_map/ppermute | solution.py:333
  5.2 8.8 %collective-permute-start.9 = (f32[2,4,6,8,128]{4,3,2,1,0:T(8,128)S(1)}, f32[2,4,6,8,128]{4,3,2,1,0:T(8,128)S(1)}, u32[]{:S(2)}, u32[]{:S(2)}) collective-permute-start(f32[2,4,6,8,128]{4,3,2,1,0:T(8,128)S(1)} %get-tuple-element.52), channel_id=1, source_target_pairs={{0,1},{1,0},{2,3},{3,2},{4,5},{5,4},{6,7},{7,6},{8,9},{9,8},{10,11... | collective-permute-start | bytes 589832 | tf_op jit(solution)/shard_map/ppermute | solution.py:334
  8.8 7.5 %collective-permute-start.4 = (f32[2,4,6,8,128]{4,3,2,1,0:T(8,128)S(1)}, f32[2,4,6,8,128]{4,3,2,1,0:T(8,128)S(1)}, u32[]{:S(2)}, u32[]{:S(2)}) collective-permute-start(f32[2,4,6,8,128]{4,3,2,1,0:T(8,128)S(1)} %get-tuple-element.43), channel_id=1, source_target_pairs={{0,15},{1,2},{2,1},{3,4},{4,3},{5,6},{6,5},{7,8},{8,7},{9,10},{10,... | collective-permute-start | bytes 589832 | tf_op jit(solution)/shard_map/ppermute | solution.py:333
  8.9 10.5 %collective-permute-start.5 = (f32[2,4,6,8,128]{4,3,2,1,0:T(8,128)S(1)}, f32[2,4,6,8,128]{4,3,2,1,0:T(8,128)S(1)}, u32[]{:S(2)}, u32[]{:S(2)}) collective-permute-start(f32[2,4,6,8,128]{4,3,2,1,0:T(8,128)S(1)} %get-tuple-element.44), channel_id=1, source_target_pairs={{0,1},{1,0},{2,3},{3,2},{4,5},{5,4},{6,7},{7,6},{8,9},{9,8},{10,11... | collective-permute-start | bytes 589832 | tf_op jit(solution)/shard_map/ppermute | solution.py:334
  10.3 12.3 %collective-permute-start = (f32[2,4,6,8,128]{4,3,2,1,0:T(8,128)S(1)}, f32[2,4,6,8,128]{4,3,2,1,0:T(8,128)S(1)}, u32[]{:S(2)}, u32[]{:S(2)}) collective-permute-start(f32[2,4,6,8,128]{4,3,2,1,0:T(8,128)S(1)} %get-tuple-element.35), channel_id=1, source_target_pairs={{0,15},{1,2},{2,1},{3,4},{4,3},{5,6},{6,5},{7,8},{8,7},{9,10},{10,... | collective-permute-start | bytes 589832 | tf_op jit(solution)/shard_map/ppermute | solution.py:333
  12.1 10.5 %collective-permute-start.1 = (f32[2,4,6,8,128]{4,3,2,1,0:T(8,128)S(1)}, f32[2,4,6,8,128]{4,3,2,1,0:T(8,128)S(1)}, u32[]{:S(2)}, u32[]{:S(2)}) collective-permute-start(f32[2,4,6,8,128]{4,3,2,1,0:T(8,128)S(1)} %get-tuple-element.36), channel_id=1, source_target_pairs={{0,1},{1,0},{2,3},{3,2},{4,5},{5,4},{6,7},{7,6},{8,9},{9,8},{10,11... | collective-permute-start | bytes 589832 | tf_op jit(solution)/shard_map/ppermute | solution.py:334
  15.1 9.6 %collective-permute-start.10 = (f32[2,4,6,8,128]{4,3,2,1,0:T(8,128)S(1)}, f32[2,4,6,8,128]{4,3,2,1,0:T(8,128)S(1)}, u32[]{:S(2)}, u32[]{:S(2)}) collective-permute-start(f32[2,4,6,8,128]{4,3,2,1,0:T(8,128)S(1)} %get-tuple-element.55), channel_id=1, source_target_pairs={{0,15},{1,2},{2,1},{3,4},{4,3},{5,6},{6,5},{7,8},{8,7},{9,10},{10,... | collective-permute-start | bytes 589832 | tf_op jit(solution)/shard_map/ppermute | solution.py:333
  16.3 9.8 %collective-permute-start.11 = (f32[2,4,6,8,128]{4,3,2,1,0:T(8,128)S(1)}, f32[2,4,6,8,128]{4,3,2,1,0:T(8,128)S(1)}, u32[]{:S(2)}, u32[]{:S(2)}) collective-permute-start(f32[2,4,6,8,128]{4,3,2,1,0:T(8,128)S(1)} %get-tuple-element.56), channel_id=1, source_target_pairs={{0,1},{1,0},{2,3},{3,2},{4,5},{5,4},{6,7},{7,6},{8,9},{9,8},{10,11... | collective-permute-start | bytes 589832 | tf_op jit(solution)/shard_map/ppermute | solution.py:334
  20.4 8.5 %collective-permute-start.6 = (f32[2,4,6,8,128]{4,3,2,1,0:T(8,128)S(1)}, f32[2,4,6,8,128]{4,3,2,1,0:T(8,128)S(1)}, u32[]{:S(2)}, u32[]{:S(2)}) collective-permute-start(f32[2,4,6,8,128]{4,3,2,1,0:T(8,128)S(1)} %get-tuple-element.47), channel_id=1, source_target_pairs={{0,15},{1,2},{2,1},{3,4},{4,3},{5,6},{6,5},{7,8},{8,7},{9,10},{10,... | collective-permute-start | bytes 589832 | tf_op jit(solution)/shard_map/ppermute | solution.py:333
  22.5 6.4 %collective-permute-start.7 = (f32[2,4,6,8,128]{4,3,2,1,0:T(8,128)S(1)}, f32[2,4,6,8,128]{4,3,2,1,0:T(8,128)S(1)}, u32[]{:S(2)}, u32[]{:S(2)}) collective-permute-start(f32[2,4,6,8,128]{4,3,2,1,0:T(8,128)S(1)} %get-tuple-element.48), channel_id=1, source_target_pairs={{0,1},{1,0},{2,3},{3,2},{4,5},{5,4},{6,7},{7,6},{8,9},{9,8},{10,11... | collective-permute-start | bytes 589832 | tf_op jit(solution)/shard_map/ppermute | solution.py:334
  23.6 9.3 %collective-permute-start.2 = (f32[2,4,6,8,128]{4,3,2,1,0:T(8,128)S(1)}, f32[2,4,6,8,128]{4,3,2,1,0:T(8,128)S(1)}, u32[]{:S(2)}, u32[]{:S(2)}) collective-permute-start(f32[2,4,6,8,128]{4,3,2,1,0:T(8,128)S(1)} %get-tuple-element.39), channel_id=1, source_target_pairs={{0,15},{1,2},{2,1},{3,4},{4,3},{5,6},{6,5},{7,8},{8,7},{9,10},{10,... | collective-permute-start | bytes 589832 | tf_op jit(solution)/shard_map/ppermute | solution.py:333
  24.7 8.2 %collective-permute-start.3 = (f32[2,4,6,8,128]{4,3,2,1,0:T(8,128)S(1)}, f32[2,4,6,8,128]{4,3,2,1,0:T(8,128)S(1)}, u32[]{:S(2)}, u32[]{:S(2)}) collective-permute-start(f32[2,4,6,8,128]{4,3,2,1,0:T(8,128)S(1)} %get-tuple-element.40), channel_id=1, source_target_pairs={{0,1},{1,0},{2,3},{3,2},{4,5},{5,4},{6,7},{7,6},{8,9},{9,8},{10,11... | collective-permute-start | bytes 589832 | tf_op jit(solution)/shard_map/ppermute | solution.py:334

commit v7 on v6

--- a/solution.py
+++ b/solution.py
@@ -89,8 +89,8 @@
 
 
 def groups(ref):
-    width = 2 if ref.shape[1] % 2 == 0 else 1
-    return [range(i, i + width) for i in range(0, ref.shape[1], width)]
+    count = ref.shape[1]
+    return [range(i, min(i + 2, count)) for i in range(0, count, 2)]
 
 
 def take(ref, row, pairs):
@@ -103,33 +103,39 @@
             ref[row, n, k] = vec[k]
 
 
-def pack_links(links, inner, edge):
+def pack_links(links, inner, edge, arrive):
     low = low_half()
     z = lane_ids() % LS
     even = sublane_ids() % 2 == 0
-    for a in range(3):
-        for b in range(3):
-            for part in range(2):
-                sign = 1.0 - 2.0 * part
-                x_link, y_link, z_link = (
-                    tile(links, (mu, a, b, part)) * (-1.0 / 6.0) for mu in range(3)
-                )
-                for row, pick in enumerate((first_of, second_of)):
-                    inner[row, 0, a, b, part] = pick(x_link, x_link, low)
-                    u_z = pick(z_link, z_link, low)
-                    inner[row, 1, a, b, part] = u_z
-                    inner[row, 2, b, a, part] = sign * z_prev(u_z, z)
-                u_y = first_of(y_link, y_link, low)
-                inner[0, 3, a, b, part] = u_y
-                inner[1, 3, b, a, part] = sign * u_y
-                edge[a, b, part] = second_of(y_link, y_link, low)
-    for row in range(2):
-        for part in range(2):
-            sign = 1.0 - 2.0 * part
-            own = [[inner[row, 0, a, b, part] for b in range(3)] for a in range(3)]
+    entries = [(a, b, part) for a in range(3) for b in range(3) for part in range(2)]
+    rows = tuple(enumerate((first_of, second_of)))
+
+    arrive(1)
+    for a, b, part in entries:
+        y_link = tile(links, (1, a, b, part)) * (-1.0 / 6.0)
+        u_y = first_of(y_link, y_link, low)
+        inner[0, 3, a, b, part] = u_y
+        inner[1, 3, b, a, part] = u_y if part == 0 else -u_y
+        edge[a, b, part] = second_of(y_link, y_link, low)
+    arrive(2)
+    for a, b, part in entries:
+        z_link = tile(links, (2, a, b, part)) * (-1.0 / 6.0)
+        for row, pick in rows:
+            u_z = pick(z_link, z_link, low)
+            inner[row, 1, a, b, part] = u_z
+            u_z = z_prev(u_z, z)
+            inner[row, 2, b, a, part] = u_z if part == 0 else -u_z
+    arrive(0)
+    for part in range(2):
+        x_link = [
+            [tile(links, (0, a, b, part)) * (-1.0 / 6.0) for b in range(3)] for a in range(3)
+        ]
+        for row, pick in rows:
+            own = [[pick(entry, entry, low) for entry in line] for line in x_link]
             for a in range(3):
                 for b in range(3):
-                    inner[row, 0, a, b, part] = own[a][b] + sign * x_other(own[b][a], even)
+                    other = x_other(own[b][a], even)
+                    inner[row, 0, a, b, part] = own[a][b] + (other if part == 0 else -other)
 
 
 def add_inner(inner, row, pairs, field, sums):
@@ -208,19 +214,22 @@
     coeff, src, links, inner, edge, rows, sums, far_out, near_out, later, now, held, sems
 ):
     count = now.shape[0]
-    copies = [
-        pltpu.make_async_copy(links, held, sems.at[0]),
-        pltpu.make_async_copy(src.at[pl.ds(0, count)], now, sems.at[1]),
-        pltpu.make_async_copy(src.at[pl.ds(count, later.shape[0])], later, sems.at[2]),
+    link_copies = [
+        pltpu.make_async_copy(links.at[mu], held.at[mu], sems.at[mu]) for mu in range(3)
     ]
-    for copy in copies:
-        copy.start()
-    copies[0].wait()
-    pack_links(held, inner, edge)
-    copies[1].wait()
+    first_copy = pltpu.make_async_copy(src.at[pl.ds(0, count)], now, sems.at[3])
+    rest = src.at[pl.ds(count, later.shape[0])]
+    later_copy = pltpu.make_async_copy(rest, later, sems.at[4])
+    link_copies[1].start()
+    first_copy.start()
+    link_copies[2].start()
+    link_copies[0].start()
+    later_copy.start()
+    pack_links(held, inner, edge, lambda mu: link_copies[mu].wait())
+    first_copy.wait()
     pack_rows(lambda n, k: tile(now, (n, k)), rows)
     start_chunk(coeff, rows, inner, edge, sums, far_out, near_out)
-    copies[2].wait()
+    later_copy.wait()
 
 
 def start_kernel(coeff, first, later, inner, edge, rows, sums, far_out, near_out):
@@ -238,12 +247,15 @@
     start,
     inner,
     edge,
+    all_started,
     rows_out,
     sums_out,
     far_out,
     near_out,
     middle,
 ):
+    del all_started
+
     def run(lower_side, upper_side):
         below, down = lower_side
         above, up = upper_side
@@ -287,10 +299,11 @@
 
 
 VMEM_LIMIT = 32 * 1024 * 1024
-CHUNKS = 3
-
-
-def call(kernel, outs, args, flops, scratch=(), in_hbm=(), out_hbm=False, aliases={}):
+
+
+def call(
+    kernel, outs, args, flops, scratch=(), in_hbm=(), out_hbm=False, aliases={}, unread=()
+):
     moved = sum(4 * a.size for a in args) + sum(4 * o.size for o in outs)
     args = [
         pltpu.with_memory_space_constraint(a, pltpu.HBM) if i in in_hbm else a
@@ -298,10 +311,13 @@
     ]
     vmem = pl.BlockSpec(memory_space=pltpu.VMEM)
     hbm = pl.BlockSpec(memory_space=pltpu.HBM)
+    anywhere = pl.BlockSpec(memory_space=pl.ANY)
     return pl.pallas_call(
         kernel,
         out_shape=outs,
-        in_specs=[hbm if i in in_hbm else vmem for i in range(len(args))],
+        in_specs=[
+            hbm if i in in_hbm else anywhere if i in unread else vmem for i in range(len(args))
+        ],
         out_specs=[hbm if out_hbm else vmem] * len(outs),
         scratch_shapes=list(scratch),
         input_output_aliases=aliases,
@@ -310,21 +326,28 @@
     )(*args)
 
 
+def chunk_sizes(pairs):
+    last = pairs // 4
+    second = pairs // 3
+    return (pairs - second - last, second, last)
+
+
 def halo_body(links, sources):
     vectors = sources.shape[0]
-    share = vectors // CHUNKS
-    pairs = share // 2
+    sizes = chunk_sizes(vectors // 2)
+    chunks = range(len(sizes))
+    first = [2 * sum(sizes[:chunk]) for chunk in chunks]
     sites, planes = links.shape[4:]
     f32 = functools.partial(jax.ShapeDtypeStruct, dtype=jnp.float32)
-    both = f32((2, pairs, 6, 8, 128))
-    middle = pltpu.VMEM(both.shape, jnp.float32)
+    both = [f32((2, pairs, 6, 8, 128)) for pairs in sizes]
+    middle = [pltpu.VMEM(shape.shape, jnp.float32) for shape in both]
+    raw = [(2 * pairs, 6, planes, sites) for pairs in sizes]
     source_view = jnp.swapaxes(sources, 3, 4).reshape(vectors, 6, planes, sites)
     link_view = jnp.swapaxes(links, 4, 5)
-    chunk_shape = (share, 6, planes, sites)
     powers = power_coeffs()
     lead = powers[4]
     steps = [powers[power] / lead for power in (3, 2, 1, 0)]
-    work = 2 * pairs * 36 * 2 * 1024
+    work = [2 * pairs * 36 * 2 * 1024 for pairs in sizes]
     count = lax.axis_size("space")
     near_pairs = [(d, d ^ 1) for d in range(count)]
     far_pairs = [(d, (d + 1 if d % 2 else d - 1) % count) for d in range(count)]
@@ -338,48 +361,53 @@
         [
             f32((2, 4, 3, 3, 2, 8, 128)),
             f32((3, 3, 2, 8, 128)),
-            *[both] * 4,
-            f32((vectors - share, 6, planes, sites)),
+            *[both[0]] * 4,
+            f32((vectors - first[1], 6, planes, sites)),
         ],
         [source_view, link_view],
-        6 * work,
+        6 * work[0],
         [
-            pltpu.VMEM(chunk_shape, jnp.float32),
+            pltpu.VMEM(raw[0], jnp.float32),
             pltpu.VMEM(link_view.shape, jnp.float32),
-            pltpu.SemaphoreType.DMA((3,)),
+            pltpu.SemaphoreType.DMA((5,)),
         ],
         (0, 1),
     )
     start, fields, halos = [rows], [(rows, sums)], [exchange(*sends)]
-    for chunk in range(1, CHUNKS):
+    for chunk in chunks[1:]:
         rows, sums, *sends = call(
-            functools.partial(start_kernel, steps[0], (chunk - 1) * share),
-            [both] * 4,
+            functools.partial(start_kernel, steps[0], first[chunk] - first[1]),
+            [both[chunk]] * 4,
             [later, inner, edge],
-            6 * work,
+            6 * work[chunk],
         )
         start.append(rows)
         fields.append((rows, sums))
         halos.append(exchange(*sends))
-    for chunk in range(CHUNKS):
+    for chunk in chunks:
         rows, sums, *sends = call(
             functools.partial(round_kernel, steps[1], steps[2]),
-            [both] * 4,
-            [*halos[chunk], *fields[chunk], start[chunk], inner, edge],
-            12 * work,
-            [middle],
+            [both[chunk]] * 4,
+            [*halos[chunk], *fields[chunk], start[chunk], inner, edge, start[-1]],
+            12 * work[chunk],
+            [middle[chunk]],
+            unread=(7,),
         )
         fields[chunk] = (rows, sums)
         halos[chunk] = exchange(*sends)
     out = None
-    for chunk in range(CHUNKS):
+    for chunk in chunks:
         args = [*halos[chunk], *fields[chunk], start[chunk], inner, edge]
         (out,) = call(
-            functools.partial(last_kernel, steps[3], chunk * share, lead),
+            functools.partial(last_kernel, steps[3], first[chunk], lead),
             [f32(source_view.shape)],
             args if out is None else args + [out],
-            6 * work,
-            [middle, pltpu.VMEM(chunk_shape, jnp.float32), pltpu.SemaphoreType.DMA((pairs,))],
+            6 * work[chunk],
+            [
+                middle[chunk],
+                pltpu.VMEM(raw[chunk], jnp.float32),
+                pltpu.SemaphoreType.DMA((sizes[chunk],)),
+            ],
             () if out is None else (len(args),),
             True,
             {} if out is None else {len(args): 0},
@@ -501,7 +529,7 @@
 
 def body(links, sources):
     sites, planes = sources.shape[3:]
-    if sites == 2 * LS and planes == 2 * NT and sources.shape[0] % (2 * CHUNKS) == 0:
+    if sites == 2 * LS and planes == 2 * NT and sources.shape[0] % 8 == 0:
         return halo_body(links, sources)
     return plane_body(links, sources)
 

time: 34.6 us -> 38.7 us (1.12)
  the two profiles are of different devices: /device:TPU:1 before, /device:TPU:0 now
where the time goes in v7:
time: 38.7 us; the launch traced here: 38.6 us
  starting transfers between devices  21.6 us (56%)
  Pallas kernels  11.1 us (29%)
  waiting for transfers between devices  5.59 us (14%)
    ppermute x6, starting transfers between devices, exchange(): far = lax.ppermute(far_out, 'space', far_pairs)  15.6 us
    pallas_call x9, Pallas kernels, call(): pl.pallas_call(kernel, out_shape=outs, in_specs=[hbm if i in in_hbm else...  11.1 us
    ppermute x6, starting transfers between devices, exchange(): return (far, lax.ppermute(near_out, 'space', near_pairs))  6.01 us
    ppermute x6, waiting for transfers between devices, exchange(): far = lax.ppermute(far_out, 'space', far_pairs)  5.57 us
  transfers between devices with their start and end apart: 12, of which 3 were waited for; matrix products, arithmetic and copies ran while one was open for 0% of the time, Pallas kernels for 19%

profile of v7, /device:TPU:0, one launch (start us, length us, event | category | flops | bytes accessed | tf_op | source)
XLA Modules:
  0.0 38.6 jit_solution(7177292002763841155)
XLA Ops:
  0.0 2.5 %shard_map.28 = (f32[2,4,3,3,2,8,128]{6,5,4,3,2,1,0:T(8,128)S(1)}, f32[3,3,2,8,128]{4,3,2,1,0:T(8,128)S(1)}, f32[2,5,6,8,128]{4,3,2,1,0:T(8,128)S(1)}, f32[2,5,6...) custom-call(f32[24,6,16,64]{3,2,1,0:T(8,128)} %bitcast.7, ...), custom_call_target="tpu_custom_call" | custom-call | flops 4423680 | bytes 2801664 | tf_op jit(solution)/shard_map/pallas_call | solution.py:315
  2.5 5.5 %collective-permute-start.8 = (f32[2,5,6,8,128]{4,3,2,1,0:T(8,128)S(1)}, f32[2,5,6,8,128]{4,3,2,1,0:T(8,128)S(1)}, u32[]{:S(2)}, u32[]{:S(2)}) collective-permute-start(f32[2,5,6,8,128]{4,3,2,1,0:T(8,128)S(1)} %get-tuple-element.51), channel_id=1, source_target_pairs={{0,15},{1,2},{2,1},{3,4},{4,3},{5,6},{6,5},{7,8},{8,7},{9,10},{10,... | collective-permute-start | bytes 737288 | tf_op jit(solution)/shard_map/ppermute | solution.py:356
  8.0 0.7 %shard_map.31 = (f32[2,4,6,8,128]{4,3,2,1,0:T(8,128)S(1)}, f32[2,4,6,8,128]{4,3,2,1,0:T(8,128)S(1)}, f32[2,4,6,8,128]{4,3,2,1,0:T(8,128)S(1)}, f32[2,4,6,8,128]{4,3,2,1,0:T(8,128)S(1)}) custom-call(f32[14,6,16,64]{3,2,1,0:T(8,128)S(1)} %get-tuple-element.32.later, f32[2,4,3,3,2,8,128]{6,5,4,3,2,1,0:T(8,128)S(1)} %get-tuple-element.33.inner, ...), custom_call_target="tpu_custom_call" | custom-call | flops 3538944 | bytes 1794048 | tf_op jit(solution)/shard_map/pallas_call | solution.py:315
  8.7 0.8 %collective-permute-start.4 = (f32[2,4,6,8,128]{4,3,2,1,0:T(8,128)S(1)}, f32[2,4,6,8,128]{4,3,2,1,0:T(8,128)S(1)}, u32[]{:S(2)}, u32[]{:S(2)}) collective-permute-start(f32[2,4,6,8,128]{4,3,2,1,0:T(8,128)S(1)} %get-tuple-element.43), channel_id=1, source_target_pairs={{0,15},{1,2},{2,1},{3,4},{4,3},{5,6},{6,5},{7,8},{8,7},{9,10},{10,... | collective-permute-start | bytes 589832 | tf_op jit(solution)/shard_map/ppermute | solution.py:356
  9.5 0.0 collective-permute-start.5
  9.5 0.5 %shard_map.29 = (f32[2,3,6,8,128]{4,3,2,1,0:T(8,128)S(1)}, f32[2,3,6,8,128]{4,3,2,1,0:T(8,128)S(1)}, f32[2,3,6,8,128]{4,3,2,1,0:T(8,128)S(1)}, f32[2,3,6,8,128]{4,3,2,1,0:T(8,128)S(1)}) custom-call(f32[14,6,16,64]{3,2,1,0:T(8,128)S(1)} %get-tuple-element.32.later, f32[2,4,3,3,2,8,128]{6,5,4,3,2,1,0:T(8,128)S(1)} %get-tuple-element.33.inner, ...), custom_call_target="tpu_custom_call" | custom-call | flops 2654208 | bytes 1597440 | tf_op jit(solution)/shard_map/pallas_call | solution.py:315
  10.1 1.9 %collective-permute-done.8.far_in = f32[2,5,6,8,128]{4,3,2,1,0:T(8,128)S(1)} collective-permute-done((f32[2,5,6,8,128]{4,3,2,1,0:T(8,128)S(1)}, f32[2,5,6,8,128]{4,3,2,1,0:T(8,128)S(1)}, u32[]{:S(2)}, u32[]{:S(2)}) %collective-permute-start.8) | collective-permute-done | bytes 245792 | tf_op jit(solution)/shard_map/ppermute | solution.py:356
  12.0 1.2 %shard_map.33 = (f32[2,5,6,8,128]{4,3,2,1,0:T(8,128)S(1)}, f32[2,5,6,8,128]{4,3,2,1,0:T(8,128)S(1)}, f32[2,5,6,8,128]{4,3,2,1,0:T(8,128)S(1)}, f32[2,5,6,8,128]{4,3,2,1,0:T(8,128)S(1)}) custom-call(f32[2,5,6,8,128]{4,3,2,1,0:T(8,128)S(1)} %collective-permute-done.8.far_in, f32[2,5,6,8,128]{4,3,2,1,0:T(8,128)S(1)} %collective-permute-done.9.near_in, ...), custom_call_target="tpu_custom_call" | custom-call | flops 8847360 | bytes 3022848 | tf_op jit(solution)/shard_map/pallas_call | solution.py:315
  13.2 4.5 %collective-permute-start.10 = (f32[2,5,6,8,128]{4,3,2,1,0:T(8,128)S(1)}, f32[2,5,6,8,128]{4,3,2,1,0:T(8,128)S(1)}, u32[]{:S(2)}, u32[]{:S(2)}) collective-permute-start(f32[2,5,6,8,128]{4,3,2,1,0:T(8,128)S(1)} %get-tuple-element.55), channel_id=1, source_target_pairs={{0,15},{1,2},{2,1},{3,4},{4,3},{5,6},{6,5},{7,8},{8,7},{9,10},{10,... | collective-permute-start | bytes 737288 | tf_op jit(solution)/shard_map/ppermute | solution.py:356
  17.7 0.1 collective-permute-start
  17.8 2.0 %collective-permute-start.11 = (f32[2,5,6,8,128]{4,3,2,1,0:T(8,128)S(1)}, f32[2,5,6,8,128]{4,3,2,1,0:T(8,128)S(1)}, u32[]{:S(2)}, u32[]{:S(2)}) collective-permute-start(f32[2,5,6,8,128]{4,3,2,1,0:T(8,128)S(1)} %get-tuple-element.56), channel_id=1, source_target_pairs={{0,1},{1,0},{2,3},{3,2},{4,5},{5,4},{6,7},{7,6},{8,9},{9,8},{10,11... | collective-permute-start | bytes 737288 | tf_op jit(solution)/shard_map/ppermute | solution.py:357
  19.8 1.0 %shard_map.32 = (f32[2,4,6,8,128]{4,3,2,1,0:T(8,128)S(1)}, f32[2,4,6,8,128]{4,3,2,1,0:T(8,128)S(1)}, f32[2,4,6,8,128]{4,3,2,1,0:T(8,128)S(1)}, f32[2,4,6,8,128]{4,3,2,1,0:T(8,128)S(1)}) custom-call(f32[2,4,6,8,128]{4,3,2,1,0:T(8,128)S(1)} %collective-permute-done.4.far_in, f32[2,4,6,8,128]{4,3,2,1,0:T(8,128)S(1)} %collective-permute-done.5.near_in, ...), custom_call_target="tpu_custom_call" | custom-call | flops 7077888 | bytes 2580480 | tf_op jit(solution)/shard_map/pallas_call | solution.py:315
  20.8 3.7 %collective-permute-start.6 = (f32[2,4,6,8,128]{4,3,2,1,0:T(8,128)S(1)}, f32[2,4,6,8,128]{4,3,2,1,0:T(8,128)S(1)}, u32[]{:S(2)}, u32[]{:S(2)}) collective-permute-start(f32[2,4,6,8,128]{4,3,2,1,0:T(8,128)S(1)} %get-tuple-element.47), channel_id=1, source_target_pairs={{0,15},{1,2},{2,1},{3,4},{4,3},{5,6},{6,5},{7,8},{8,7},{9,10},{10,... | collective-permute-start | bytes 589832 | tf_op jit(solution)/shard_map/ppermute | solution.py:356
  24.6 0.5 %collective-permute-done.far_in = f32[2,3,6,8,128]{4,3,2,1,0:T(8,128)S(1)} collective-permute-done((f32[2,3,6,8,128]{4,3,2,1,0:T(8,128)S(1)}, f32[2,3,6,8,128]{4,3,2,1,0:T(8,128)S(1)}, u32[]{:S(2)}, u32[]{:S(2)}) %collective-permute-start) | collective-permute-done | bytes 147488 | tf_op jit(solution)/shard_map/ppermute | solution.py:356
  25.1 4.0 %collective-permute-start.7 = (f32[2,4,6,8,128]{4,3,2,1,0:T(8,128)S(1)}, f32[2,4,6,8,128]{4,3,2,1,0:T(8,128)S(1)}, u32[]{:S(2)}, u32[]{:S(2)}) collective-permute-start(f32[2,4,6,8,128]{4,3,2,1,0:T(8,128)S(1)} %get-tuple-element.48), channel_id=1, source_target_pairs={{0,1},{1,0},{2,3},{3,2},{4,5},{5,4},{6,7},{7,6},{8,9},{9,8},{10,11... | collective-permute-start | bytes 589832 | tf_op jit(solution)/shard_map/ppermute | solution.py:357
  29.1 0.7 %shard_map.30 = (f32[2,3,6,8,128]{4,3,2,1,0:T(8,128)S(1)}, f32[2,3,6,8,128]{4,3,2,1,0:T(8,128)S(1)}, f32[2,3,6,8,128]{4,3,2,1,0:T(8,128)S(1)}, f32[2,3,6,8,128]{4,3,2,1,0:T(8,128)S(1)}) custom-call(f32[2,3,6,8,128]{4,3,2,1,0:T(8,128)S(1)} %collective-permute-done.far_in, f32[2,3,6,8,128]{4,3,2,1,0:T(8,128)S(1)} %collective-permute-done.1.near_in, ...), custom_call_target="tpu_custom_call" | custom-call | flops 5308416 | bytes 2138112 | tf_op jit(solution)/shard_map/pallas_call | solution.py:315
  29.8 1.0 %collective-permute-start.2 = (f32[2,3,6,8,128]{4,3,2,1,0:T(8,128)S(1)}, f32[2,3,6,8,128]{4,3,2,1,0:T(8,128)S(1)}, u32[]{:S(2)}, u32[]{:S(2)}) collective-permute-start(f32[2,3,6,8,128]{4,3,2,1,0:T(8,128)S(1)} %get-tuple-element.39), channel_id=1, source_target_pairs={{0,15},{1,2},{2,1},{3,4},{4,3},{5,6},{6,5},{7,8},{8,7},{9,10},{10,... | collective-permute-start | bytes 442376 | tf_op jit(solution)/shard_map/ppermute | solution.py:356
  30.8 0.0 collective-permute-done.10.far_in
  30.8 0.0 collective-permute-start.3
  30.8 0.0 collective-permute-done.11.near_in
  30.9 1.7 %shard_map.34.rest_0_ = f32[24,6,16,64]{3,2,1,0:T(8,128)} custom-call(f32[2,5,6,8,128]{4,3,2,1,0:T(8,128)S(1)} %collective-permute-done.10.far_in, f32[2,5,6,8,128]{4,3,2,1,0:T(8,128)S(1)} %collective-permute-done.11.near_in, f32[2,5,6,8,128]{4,3,2,1,0:T(8,128)S(1)} %get-tuple-element.57.rows, f32[2,5,6,8,128]{4,3,2,1,0:T(8,128)S(1)} %get-tuple-element.58.sums_in, ...), custom_call_target="tpu_custom_call" | custom-call | flops 4423680 | bytes 2482176 | tf_op jit(solution)/shard_map/pallas_call | solution.py:315
  32.6 1.4 %shard_map.35.rest_0_ = f32[24,6,16,64]{3,2,1,0:T(8,128)} custom-call(f32[2,4,6,8,128]{4,3,2,1,0:T(8,128)S(1)} %collective-permute-done.6.far_in, f32[2,4,6,8,128]{4,3,2,1,0:T(8,128)S(1)} %collective-permute-done.7.near_in, f32[2,4,6,8,128]{4,3,2,1,0:T(8,128)S(1)} %get-tuple-element.49.rows, ...), custom_call_target="tpu_custom_call", output_to_operand_aliasing={{}: (7, {})} | custom-call | flops 3538944 | bytes 2826240 | tf_op jit(solution)/shard_map/pallas_call | solution.py:315
  34.1 3.1 %collective-permute-done.2.far_in = f32[2,3,6,8,128]{4,3,2,1,0:T(8,128)S(1)} collective-permute-done((f32[2,3,6,8,128]{4,3,2,1,0:T(8,128)S(1)}, f32[2,3,6,8,128]{4,3,2,1,0:T(8,128)S(1)}, u32[]{:S(2)}, u32[]{:S(2)}) %collective-permute-start.2) | collective-permute-done | bytes 147488 | tf_op jit(solution)/shard_map/ppermute | solution.py:356
  37.2 1.2 %shard_map.36 = f32[24,6,16,64]{3,2,1,0:T(8,128)} custom-call(f32[2,3,6,8,128]{4,3,2,1,0:T(8,128)S(1)} %collective-permute-done.2.far_in, f32[2,3,6,8,128]{4,3,2,1,0:T(8,128)S(1)} %collective-permute-done.3.near_in, f32[2,3,6,8,128]{4,3,2,1,0:T(8,128)S(1)} %get-tuple-element.41.rows, ...), custom_call_target="tpu_custom_call", output_to_operand_aliasing={{}: (7, {})} | custom-call | flops 2654208 | bytes 2580480 | tf_op jit(solution)/shard_map/pallas_call | solution.py:315
  (9 shorter events, 0.0 us)
Async XLA Ops:
  2.5 9.5 %collective-permute-start.8 = (f32[2,5,6,8,128]{4,3,2,1,0:T(8,128)S(1)}, f32[2,5,6,8,128]{4,3,2,1,0:T(8,128)S(1)}, u32[]{:S(2)}, u32[]{:S(2)}) collective-permute-start(f32[2,5,6,8,128]{4,3,2,1,0:T(8,128)S(1)} %get-tuple-element.51), channel_id=1, source_target_pairs={{0,15},{1,2},{2,1},{3,4},{4,3},{5,6},{6,5},{7,8},{8,7},{9,10},{10,... | collective-permute-start | bytes 737288 | tf_op jit(solution)/shard_map/ppermute | solution.py:356
  8.0 4.0 %collective-permute-start.9 = (f32[2,5,6,8,128]{4,3,2,1,0:T(8,128)S(1)}, f32[2,5,6,8,128]{4,3,2,1,0:T(8,128)S(1)}, u32[]{:S(2)}, u32[]{:S(2)}) collective-permute-start(f32[2,5,6,8,128]{4,3,2,1,0:T(8,128)S(1)} %get-tuple-element.52), channel_id=1, source_target_pairs={{0,1},{1,0},{2,3},{3,2},{4,5},{5,4},{6,7},{7,6},{8,9},{9,8},{10,11... | collective-permute-start | bytes 737288 | tf_op jit(solution)/shard_map/ppermute | solution.py:357
  8.7 9.1 %collective-permute-start.4 = (f32[2,4,6,8,128]{4,3,2,1,0:T(8,128)S(1)}, f32[2,4,6,8,128]{4,3,2,1,0:T(8,128)S(1)}, u32[]{:S(2)}, u32[]{:S(2)}) collective-permute-start(f32[2,4,6,8,128]{4,3,2,1,0:T(8,128)S(1)} %get-tuple-element.43), channel_id=1, source_target_pairs={{0,15},{1,2},{2,1},{3,4},{4,3},{5,6},{6,5},{7,8},{8,7},{9,10},{10,... | collective-permute-start | bytes 589832 | tf_op jit(solution)/shard_map/ppermute | solution.py:356
  9.5 10.3 %collective-permute-start.5 = (f32[2,4,6,8,128]{4,3,2,1,0:T(8,128)S(1)}, f32[2,4,6,8,128]{4,3,2,1,0:T(8,128)S(1)}, u32[]{:S(2)}, u32[]{:S(2)}) collective-permute-start(f32[2,4,6,8,128]{4,3,2,1,0:T(8,128)S(1)} %get-tuple-element.44), channel_id=1, source_target_pairs={{0,1},{1,0},{2,3},{3,2},{4,5},{5,4},{6,7},{7,6},{8,9},{9,8},{10,11... | collective-permute-start | bytes 589832 | tf_op jit(solution)/shard_map/ppermute | solution.py:357
  13.2 17.6 %collective-permute-start.10 = (f32[2,5,6,8,128]{4,3,2,1,0:T(8,128)S(1)}, f32[2,5,6,8,128]{4,3,2,1,0:T(8,128)S(1)}, u32[]{:S(2)}, u32[]{:S(2)}) collective-permute-start(f32[2,5,6,8,128]{4,3,2,1,0:T(8,128)S(1)} %get-tuple-element.55), channel_id=1, source_target_pairs={{0,15},{1,2},{2,1},{3,4},{4,3},{5,6},{6,5},{7,8},{8,7},{9,10},{10,... | collective-permute-start | bytes 737288 | tf_op jit(solution)/shard_map/ppermute | solution.py:356
  17.7 7.4 %collective-permute-start = (f32[2,3,6,8,128]{4,3,2,1,0:T(8,128)S(1)}, f32[2,3,6,8,128]{4,3,2,1,0:T(8,128)S(1)}, u32[]{:S(2)}, u32[]{:S(2)}) collective-permute-start(f32[2,3,6,8,128]{4,3,2,1,0:T(8,128)S(1)} %get-tuple-element.35), channel_id=1, source_target_pairs={{0,15},{1,2},{2,1},{3,4},{4,3},{5,6},{6,5},{7,8},{8,7},{9,10},{10,... | collective-permute-start | bytes 442376 | tf_op jit(solution)/shard_map/ppermute | solution.py:356
  17.8 11.3 %collective-permute-start.1 = (f32[2,3,6,8,128]{4,3,2,1,0:T(8,128)S(1)}, f32[2,3,6,8,128]{4,3,2,1,0:T(8,128)S(1)}, u32[]{:S(2)}, u32[]{:S(2)}) collective-permute-start(f32[2,3,6,8,128]{4,3,2,1,0:T(8,128)S(1)} %get-tuple-element.36), channel_id=1, source_target_pairs={{0,1},{1,0},{2,3},{3,2},{4,5},{5,4},{6,7},{7,6},{8,9},{9,8},{10,11... | collective-permute-start | bytes 442376 | tf_op jit(solution)/shard_map/ppermute | solution.py:357
  17.8 13.0 %collective-permute-start.11 = (f32[2,5,6,8,128]{4,3,2,1,0:T(8,128)S(1)}, f32[2,5,6,8,128]{4,3,2,1,0:T(8,128)S(1)}, u32[]{:S(2)}, u32[]{:S(2)}) collective-permute-start(f32[2,5,6,8,128]{4,3,2,1,0:T(8,128)S(1)} %get-tuple-element.56), channel_id=1, source_target_pairs={{0,1},{1,0},{2,3},{3,2},{4,5},{5,4},{6,7},{7,6},{8,9},{9,8},{10,11... | collective-permute-start | bytes 737288 | tf_op jit(solution)/shard_map/ppermute | solution.py:357
  20.8 11.8 %collective-permute-start.6 = (f32[2,4,6,8,128]{4,3,2,1,0:T(8,128)S(1)}, f32[2,4,6,8,128]{4,3,2,1,0:T(8,128)S(1)}, u32[]{:S(2)}, u32[]{:S(2)}) collective-permute-start(f32[2,4,6,8,128]{4,3,2,1,0:T(8,128)S(1)} %get-tuple-element.47), channel_id=1, source_target_pairs={{0,15},{1,2},{2,1},{3,4},{4,3},{5,6},{6,5},{7,8},{8,7},{9,10},{10,... | collective-permute-start | bytes 589832 | tf_op jit(solution)/shard_map/ppermute | solution.py:356
  25.1 7.5 %collective-permute-start.7 = (f32[2,4,6,8,128]{4,3,2,1,0:T(8,128)S(1)}, f32[2,4,6,8,128]{4,3,2,1,0:T(8,128)S(1)}, u32[]{:S(2)}, u32[]{:S(2)}) collective-permute-start(f32[2,4,6,8,128]{4,3,2,1,0:T(8,128)S(1)} %get-tuple-element.48), channel_id=1, source_target_pairs={{0,1},{1,0},{2,3},{3,2},{4,5},{5,4},{6,7},{7,6},{8,9},{9,8},{10,11... | collective-permute-start | bytes 589832 | tf_op jit(solution)/shard_map/ppermute | solution.py:357
  29.8 7.3 %collective-permute-start.2 = (f32[2,3,6,8,128]{4,3,2,1,0:T(8,128)S(1)}, f32[2,3,6,8,128]{4,3,2,1,0:T(8,128)S(1)}, u32[]{:S(2)}, u32[]{:S(2)}) collective-permute-start(f32[2,3,6,8,128]{4,3,2,1,0:T(8,128)S(1)} %get-tuple-element.39), channel_id=1, source_target_pairs={{0,15},{1,2},{2,1},{3,4},{4,3},{5,6},{6,5},{7,8},{8,7},{9,10},{10,... | collective-permute-start | bytes 442376 | tf_op jit(solution)/shard_map/ppermute | solution.py:356
  30.8 6.3 %collective-permute-start.3 = (f32[2,3,6,8,128]{4,3,2,1,0:T(8,128)S(1)}, f32[2,3,6,8,128]{4,3,2,1,0:T(8,128)S(1)}, u32[]{:S(2)}, u32[]{:S(2)}) collective-permute-start(f32[2,3,6,8,128]{4,3,2,1,0:T(8,128)S(1)} %get-tuple-element.40), channel_id=1, source_target_pairs={{0,1},{1,0},{2,3},{3,2},{4,5},{5,4},{6,7},{7,6},{8,9},{9,8},{10,11... | collective-permute-start | bytes 442376 | tf_op jit(solution)/shard_map/ppermute | solution.py:357

commit v8 on v7

--- a/solution.py
+++ b/solution.py
@@ -130,12 +130,12 @@
         x_link = [
             [tile(links, (0, a, b, part)) * (-1.0 / 6.0) for b in range(3)] for a in range(3)
         ]
-        for row, pick in rows:
-            own = [[pick(entry, entry, low) for entry in line] for line in x_link]
-            for a in range(3):
-                for b in range(3):
-                    other = x_other(own[b][a], even)
-                    inner[row, 0, a, b, part] = own[a][b] + (other if part == 0 else -other)
+        for a in range(3):
+            for b in range(3):
+                other = x_other(x_link[b][a], even)
+                both = x_link[a][b] + (other if part == 0 else -other)
+                for row, pick in rows:
+                    inner[row, 0, a, b, part] = pick(both, both, low)
 
 
 def add_inner(inner, row, pairs, field, sums):
@@ -247,15 +247,12 @@
     start,
     inner,
     edge,
-    all_started,
     rows_out,
     sums_out,
     far_out,
     near_out,
     middle,
 ):
-    del all_started
-
     def run(lower_side, upper_side):
         below, down = lower_side
         above, up = upper_side
@@ -299,11 +296,10 @@
 
 
 VMEM_LIMIT = 32 * 1024 * 1024
-
-
-def call(
-    kernel, outs, args, flops, scratch=(), in_hbm=(), out_hbm=False, aliases={}, unread=()
-):
+CHUNKS = 3
+
+
+def call(kernel, outs, args, flops, scratch=(), in_hbm=(), out_hbm=False, aliases={}):
     moved = sum(4 * a.size for a in args) + sum(4 * o.size for o in outs)
     args = [
         pltpu.with_memory_space_constraint(a, pltpu.HBM) if i in in_hbm else a
@@ -311,13 +307,10 @@
     ]
     vmem = pl.BlockSpec(memory_space=pltpu.VMEM)
     hbm = pl.BlockSpec(memory_space=pltpu.HBM)
-    anywhere = pl.BlockSpec(memory_space=pl.ANY)
     return pl.pallas_call(
         kernel,
         out_shape=outs,
-        in_specs=[
-            hbm if i in in_hbm else anywhere if i in unread else vmem for i in range(len(args))
-        ],
+        in_specs=[hbm if i in in_hbm else vmem for i in range(len(args))],
         out_specs=[hbm if out_hbm else vmem] * len(outs),
         scratch_shapes=list(scratch),
         input_output_aliases=aliases,
@@ -326,28 +319,21 @@
     )(*args)
 
 
-def chunk_sizes(pairs):
-    last = pairs // 4
-    second = pairs // 3
-    return (pairs - second - last, second, last)
-
-
 def halo_body(links, sources):
     vectors = sources.shape[0]
-    sizes = chunk_sizes(vectors // 2)
-    chunks = range(len(sizes))
-    first = [2 * sum(sizes[:chunk]) for chunk in chunks]
+    share = vectors // CHUNKS
+    pairs = share // 2
     sites, planes = links.shape[4:]
     f32 = functools.partial(jax.ShapeDtypeStruct, dtype=jnp.float32)
-    both = [f32((2, pairs, 6, 8, 128)) for pairs in sizes]
-    middle = [pltpu.VMEM(shape.shape, jnp.float32) for shape in both]
-    raw = [(2 * pairs, 6, planes, sites) for pairs in sizes]
+    both = f32((2, pairs, 6, 8, 128))
+    middle = pltpu.VMEM(both.shape, jnp.float32)
     source_view = jnp.swapaxes(sources, 3, 4).reshape(vectors, 6, planes, sites)
     link_view = jnp.swapaxes(links, 4, 5)
+    chunk_shape = (share, 6, planes, sites)
     powers = power_coeffs()
     lead = powers[4]
     steps = [powers[power] / lead for power in (3, 2, 1, 0)]
-    work = [2 * pairs * 36 * 2 * 1024 for pairs in sizes]
+    work = 2 * pairs * 36 * 2 * 1024
     count = lax.axis_size("space")
     near_pairs = [(d, d ^ 1) for d in range(count)]
     far_pairs = [(d, (d + 1 if d % 2 else d - 1) % count) for d in range(count)]
@@ -361,53 +347,48 @@
         [
             f32((2, 4, 3, 3, 2, 8, 128)),
             f32((3, 3, 2, 8, 128)),
-            *[both[0]] * 4,
-            f32((vectors - first[1], 6, planes, sites)),
+            *[both] * 4,
+            f32((vectors - share, 6, planes, sites)),
         ],
         [source_view, link_view],
-        6 * work[0],
+        6 * work,
         [
-            pltpu.VMEM(raw[0], jnp.float32),
+            pltpu.VMEM(chunk_shape, jnp.float32),
             pltpu.VMEM(link_view.shape, jnp.float32),
             pltpu.SemaphoreType.DMA((5,)),
         ],
         (0, 1),
     )
     start, fields, halos = [rows], [(rows, sums)], [exchange(*sends)]
-    for chunk in chunks[1:]:
+    for chunk in range(1, CHUNKS):
         rows, sums, *sends = call(
-            functools.partial(start_kernel, steps[0], first[chunk] - first[1]),
-            [both[chunk]] * 4,
+            functools.partial(start_kernel, steps[0], (chunk - 1) * share),
+            [both] * 4,
             [later, inner, edge],
-            6 * work[chunk],
+            6 * work,
         )
         start.append(rows)
         fields.append((rows, sums))
         halos.append(exchange(*sends))
-    for chunk in chunks:
+    for chunk in range(CHUNKS):
         rows, sums, *sends = call(
             functools.partial(round_kernel, steps[1], steps[2]),
-            [both[chunk]] * 4,
-            [*halos[chunk], *fields[chunk], start[chunk], inner, edge, start[-1]],
-            12 * work[chunk],
-            [middle[chunk]],
-            unread=(7,),
+            [both] * 4,
+            [*halos[chunk], *fields[chunk], start[chunk], inner, edge],
+            12 * work,
+            [middle],
         )
         fields[chunk] = (rows, sums)
         halos[chunk] = exchange(*sends)
     out = None
-    for chunk in chunks:
+    for chunk in range(CHUNKS):
         args = [*halos[chunk], *fields[chunk], start[chunk], inner, edge]
         (out,) = call(
-            functools.partial(last_kernel, steps[3], first[chunk], lead),
+            functools.partial(last_kernel, steps[3], chunk * share, lead),
             [f32(source_view.shape)],
             args if out is None else args + [out],
-            6 * work[chunk],
-            [
-                middle[chunk],
-                pltpu.VMEM(raw[chunk], jnp.float32),
-                pltpu.SemaphoreType.DMA((sizes[chunk],)),
-            ],
+            6 * work,
+            [middle, pltpu.VMEM(chunk_shape, jnp.float32), pltpu.SemaphoreType.DMA((pairs,))],
             () if out is None else (len(args),),
             True,
             {} if out is None else {len(args): 0},
@@ -529,7 +510,7 @@
 
 def body(links, sources):
     sites, planes = sources.shape[3:]
-    if sites == 2 * LS and planes == 2 * NT and sources.shape[0] % 8 == 0:
+    if sites == 2 * LS and planes == 2 * NT and sources.shape[0] % (2 * CHUNKS) == 0:
         return halo_body(links, sources)
     return plane_body(links, sources)
 

time: 38.7 us -> 34.4 us (0.89)
  the two profiles are of different devices: /device:TPU:0 before, /device:TPU:1 now
where the time goes in v8:
time: 34.4 us; the launch traced here: 34.2 us
  starting transfers between devices  14.9 us (43%)
  Pallas kernels  11.1 us (32%)
  waiting for transfers between devices  7.97 us (23%)
    pallas_call x9, Pallas kernels, call(): pl.pallas_call(kernel, out_shape=outs, in_specs=[hbm if i in in_hbm else...  11.1 us
    ppermute x6, starting transfers between devices, exchange(): return (far, lax.ppermute(near_out, 'space', near_pairs))  10.1 us
    ppermute x6, waiting for transfers between devices, exchange(): far = lax.ppermute(far_out, 'space', far_pairs)  7.95 us
    ppermute x6, starting transfers between devices, exchange(): far = lax.ppermute(far_out, 'space', far_pairs)  4.89 us
  transfers between devices with their start and end apart: 12, of which 6 were waited for; matrix products, arithmetic and copies ran while one was open for 0% of the time, Pallas kernels for 22%

profile of v8, /device:TPU:1, one launch (start us, length us, event | category | flops | bytes accessed | tf_op | source)
XLA Modules:
  0.0 34.2 jit_solution(13609262914014645820)
XLA Ops:
  0.0 2.3 %shard_map.28 = (f32[2,4,3,3,2,8,128]{6,5,4,3,2,1,0:T(8,128)S(1)}, f32[3,3,2,8,128]{4,3,2,1,0:T(8,128)S(1)}, f32[2,4,6,8,128]{4,3,2,1,0:T(8,128)S(1)}, f32[2,4,6...) custom-call(f32[24,6,16,64]{3,2,1,0:T(8,128)} %bitcast.7, ...), custom_call_target="tpu_custom_call" | custom-call | flops 3538944 | bytes 2654208 | tf_op jit(solution)/shard_map/pallas_call | solution.py:310
  2.3 2.7 %collective-permute-start.8 = (f32[2,4,6,8,128]{4,3,2,1,0:T(8,128)S(1)}, f32[2,4,6,8,128]{4,3,2,1,0:T(8,128)S(1)}, u32[]{:S(2)}, u32[]{:S(2)}) collective-permute-start(f32[2,4,6,8,128]{4,3,2,1,0:T(8,128)S(1)} %get-tuple-element.51), channel_id=1, source_target_pairs={{0,15},{1,2},{2,1},{3,4},{4,3},{5,6},{6,5},{7,8},{8,7},{9,10},{10,... | collective-permute-start | bytes 589832 | tf_op jit(solution)/shard_map/ppermute | solution.py:342
  5.0 2.9 %collective-permute-start.9 = (f32[2,4,6,8,128]{4,3,2,1,0:T(8,128)S(1)}, f32[2,4,6,8,128]{4,3,2,1,0:T(8,128)S(1)}, u32[]{:S(2)}, u32[]{:S(2)}) collective-permute-start(f32[2,4,6,8,128]{4,3,2,1,0:T(8,128)S(1)} %get-tuple-element.52), channel_id=1, source_target_pairs={{0,1},{1,0},{2,3},{3,2},{4,5},{5,4},{6,7},{7,6},{8,9},{9,8},{10,11... | collective-permute-start | bytes 589832 | tf_op jit(solution)/shard_map/ppermute | solution.py:343
  7.8 0.7 %shard_map.31 = (f32[2,4,6,8,128]{4,3,2,1,0:T(8,128)S(1)}, f32[2,4,6,8,128]{4,3,2,1,0:T(8,128)S(1)}, f32[2,4,6,8,128]{4,3,2,1,0:T(8,128)S(1)}, f32[2,4,6,8,128]{4,3,2,1,0:T(8,128)S(1)}) custom-call(f32[16,6,16,64]{3,2,1,0:T(8,128)S(1)} %get-tuple-element.32.later, f32[2,4,3,3,2,8,128]{6,5,4,3,2,1,0:T(8,128)S(1)} %get-tuple-element.33.inner, ...), custom_call_target="tpu_custom_call" | custom-call | flops 3538944 | bytes 1843200 | tf_op jit(solution)/shard_map/pallas_call | solution.py:310
  8.6 0.7 %collective-permute-start.5 = (f32[2,4,6,8,128]{4,3,2,1,0:T(8,128)S(1)}, f32[2,4,6,8,128]{4,3,2,1,0:T(8,128)S(1)}, u32[]{:S(2)}, u32[]{:S(2)}) collective-permute-start(f32[2,4,6,8,128]{4,3,2,1,0:T(8,128)S(1)} %get-tuple-element.44), channel_id=1, source_target_pairs={{0,1},{1,0},{2,3},{3,2},{4,5},{5,4},{6,7},{7,6},{8,9},{9,8},{10,11... | collective-permute-start | bytes 589832 | tf_op jit(solution)/shard_map/ppermute | solution.py:343
  9.4 0.7 %shard_map.29 = (f32[2,4,6,8,128]{4,3,2,1,0:T(8,128)S(1)}, f32[2,4,6,8,128]{4,3,2,1,0:T(8,128)S(1)}, f32[2,4,6,8,128]{4,3,2,1,0:T(8,128)S(1)}, f32[2,4,6,8,128]{4,3,2,1,0:T(8,128)S(1)}) custom-call(f32[16,6,16,64]{3,2,1,0:T(8,128)S(1)} %get-tuple-element.32.later, f32[2,4,3,3,2,8,128]{6,5,4,3,2,1,0:T(8,128)S(1)} %get-tuple-element.33.inner, ...), custom_call_target="tpu_custom_call" | custom-call | flops 3538944 | bytes 1843200 | tf_op jit(solution)/shard_map/pallas_call | solution.py:310
  10.0 1.1 %collective-permute-start = (f32[2,4,6,8,128]{4,3,2,1,0:T(8,128)S(1)}, f32[2,4,6,8,128]{4,3,2,1,0:T(8,128)S(1)}, u32[]{:S(2)}, u32[]{:S(2)}) collective-permute-start(f32[2,4,6,8,128]{4,3,2,1,0:T(8,128)S(1)} %get-tuple-element.35), channel_id=1, source_target_pairs={{0,15},{1,2},{2,1},{3,4},{4,3},{5,6},{6,5},{7,8},{8,7},{9,10},{10,... | collective-permute-start | bytes 589832 | tf_op jit(solution)/shard_map/ppermute | solution.py:342
  11.1 0.7 %collective-permute-done.8.far_in = f32[2,4,6,8,128]{4,3,2,1,0:T(8,128)S(1)} collective-permute-done((f32[2,4,6,8,128]{4,3,2,1,0:T(8,128)S(1)}, f32[2,4,6,8,128]{4,3,2,1,0:T(8,128)S(1)}, u32[]{:S(2)}, u32[]{:S(2)}) %collective-permute-start.8) | collective-permute-done | bytes 196640 | tf_op jit(solution)/shard_map/ppermute | solution.py:342
  11.8 2.0 %collective-permute-start.1 = (f32[2,4,6,8,128]{4,3,2,1,0:T(8,128)S(1)}, f32[2,4,6,8,128]{4,3,2,1,0:T(8,128)S(1)}, u32[]{:S(2)}, u32[]{:S(2)}) collective-permute-start(f32[2,4,6,8,128]{4,3,2,1,0:T(8,128)S(1)} %get-tuple-element.36), channel_id=1, source_target_pairs={{0,1},{1,0},{2,3},{3,2},{4,5},{5,4},{6,7},{7,6},{8,9},{9,8},{10,11... | collective-permute-start | bytes 589832 | tf_op jit(solution)/shard_map/ppermute | solution.py:343
  13.8 1.0 %shard_map.33 = (f32[2,4,6,8,128]{4,3,2,1,0:T(8,128)S(1)}, f32[2,4,6,8,128]{4,3,2,1,0:T(8,128)S(1)}, f32[2,4,6,8,128]{4,3,2,1,0:T(8,128)S(1)}, f32[2,4,6,8,128]{4,3,2,1,0:T(8,128)S(1)}) custom-call(f32[2,4,6,8,128]{4,3,2,1,0:T(8,128)S(1)} %collective-permute-done.8.far_in, f32[2,4,6,8,128]{4,3,2,1,0:T(8,128)S(1)} %collective-permute-done.9.near_in, ...), custom_call_target="tpu_custom_call" | custom-call | flops 7077888 | bytes 2433024 | tf_op jit(solution)/shard_map/pallas_call | solution.py:310
  14.8 0.6 %collective-permute-start.10 = (f32[2,4,6,8,128]{4,3,2,1,0:T(8,128)S(1)}, f32[2,4,6,8,128]{4,3,2,1,0:T(8,128)S(1)}, u32[]{:S(2)}, u32[]{:S(2)}) collective-permute-start(f32[2,4,6,8,128]{4,3,2,1,0:T(8,128)S(1)} %get-tuple-element.55), channel_id=1, source_target_pairs={{0,15},{1,2},{2,1},{3,4},{4,3},{5,6},{6,5},{7,8},{8,7},{9,10},{10,... | collective-permute-start | bytes 589832 | tf_op jit(solution)/shard_map/ppermute | solution.py:342
  15.4 0.7 %collective-permute-done.4.far_in = f32[2,4,6,8,128]{4,3,2,1,0:T(8,128)S(1)} collective-permute-done((f32[2,4,6,8,128]{4,3,2,1,0:T(8,128)S(1)}, f32[2,4,6,8,128]{4,3,2,1,0:T(8,128)S(1)}, u32[]{:S(2)}, u32[]{:S(2)}) %collective-permute-start.4) | collective-permute-done | bytes 196640 | tf_op jit(solution)/shard_map/ppermute | solution.py:342
  16.0 3.1 %collective-permute-start.11 = (f32[2,4,6,8,128]{4,3,2,1,0:T(8,128)S(1)}, f32[2,4,6,8,128]{4,3,2,1,0:T(8,128)S(1)}, u32[]{:S(2)}, u32[]{:S(2)}) collective-permute-start(f32[2,4,6,8,128]{4,3,2,1,0:T(8,128)S(1)} %get-tuple-element.56), channel_id=1, source_target_pairs={{0,1},{1,0},{2,3},{3,2},{4,5},{5,4},{6,7},{7,6},{8,9},{9,8},{10,11... | collective-permute-start | bytes 589832 | tf_op jit(solution)/shard_map/ppermute | solution.py:343
  19.1 1.0 %shard_map.32 = (f32[2,4,6,8,128]{4,3,2,1,0:T(8,128)S(1)}, f32[2,4,6,8,128]{4,3,2,1,0:T(8,128)S(1)}, f32[2,4,6,8,128]{4,3,2,1,0:T(8,128)S(1)}, f32[2,4,6,8,128]{4,3,2,1,0:T(8,128)S(1)}) custom-call(f32[2,4,6,8,128]{4,3,2,1,0:T(8,128)S(1)} %collective-permute-done.4.far_in, f32[2,4,6,8,128]{4,3,2,1,0:T(8,128)S(1)} %collective-permute-done.5.near_in, ...), custom_call_target="tpu_custom_call" | custom-call | flops 7077888 | bytes 2433024 | tf_op jit(solution)/shard_map/pallas_call | solution.py:310
  20.2 2.1 %collective-permute-done.far_in = f32[2,4,6,8,128]{4,3,2,1,0:T(8,128)S(1)} collective-permute-done((f32[2,4,6,8,128]{4,3,2,1,0:T(8,128)S(1)}, f32[2,4,6,8,128]{4,3,2,1,0:T(8,128)S(1)}, u32[]{:S(2)}, u32[]{:S(2)}) %collective-permute-start) | collective-permute-done | bytes 196640 | tf_op jit(solution)/shard_map/ppermute | solution.py:342
  22.3 1.0 %shard_map.30 = (f32[2,4,6,8,128]{4,3,2,1,0:T(8,128)S(1)}, f32[2,4,6,8,128]{4,3,2,1,0:T(8,128)S(1)}, f32[2,4,6,8,128]{4,3,2,1,0:T(8,128)S(1)}, f32[2,4,6,8,128]{4,3,2,1,0:T(8,128)S(1)}) custom-call(f32[2,4,6,8,128]{4,3,2,1,0:T(8,128)S(1)} %collective-permute-done.far_in, f32[2,4,6,8,128]{4,3,2,1,0:T(8,128)S(1)} %collective-permute-done.1.near_in, ...), custom_call_target="tpu_custom_call" | custom-call | flops 7077888 | bytes 2433024 | tf_op jit(solution)/shard_map/pallas_call | solution.py:310
  23.3 0.5 %collective-permute-start.2 = (f32[2,4,6,8,128]{4,3,2,1,0:T(8,128)S(1)}, f32[2,4,6,8,128]{4,3,2,1,0:T(8,128)S(1)}, u32[]{:S(2)}, u32[]{:S(2)}) collective-permute-start(f32[2,4,6,8,128]{4,3,2,1,0:T(8,128)S(1)} %get-tuple-element.39), channel_id=1, source_target_pairs={{0,15},{1,2},{2,1},{3,4},{4,3},{5,6},{6,5},{7,8},{8,7},{9,10},{10,... | collective-permute-start | bytes 589832 | tf_op jit(solution)/shard_map/ppermute | solution.py:342
  23.8 0.7 %collective-permute-done.10.far_in = f32[2,4,6,8,128]{4,3,2,1,0:T(8,128)S(1)} collective-permute-done((f32[2,4,6,8,128]{4,3,2,1,0:T(8,128)S(1)}, f32[2,4,6,8,128]{4,3,2,1,0:T(8,128)S(1)}, u32[]{:S(2)}, u32[]{:S(2)}) %collective-permute-start.10) | collective-permute-done | bytes 196640 | tf_op jit(solution)/shard_map/ppermute | solution.py:342
  24.4 1.3 %collective-permute-start.3 = (f32[2,4,6,8,128]{4,3,2,1,0:T(8,128)S(1)}, f32[2,4,6,8,128]{4,3,2,1,0:T(8,128)S(1)}, u32[]{:S(2)}, u32[]{:S(2)}) collective-permute-start(f32[2,4,6,8,128]{4,3,2,1,0:T(8,128)S(1)} %get-tuple-element.40), channel_id=1, source_target_pairs={{0,1},{1,0},{2,3},{3,2},{4,5},{5,4},{6,7},{7,6},{8,9},{9,8},{10,11... | collective-permute-start | bytes 589832 | tf_op jit(solution)/shard_map/ppermute | solution.py:343
  25.8 1.4 %shard_map.34.rest_0_ = f32[24,6,16,64]{3,2,1,0:T(8,128)} custom-call(f32[2,4,6,8,128]{4,3,2,1,0:T(8,128)S(1)} %collective-permute-done.10.far_in, f32[2,4,6,8,128]{4,3,2,1,0:T(8,128)S(1)} %collective-permute-done.11.near_in, f32[2,4,6,8,128]{4,3,2,1,0:T(8,128)S(1)} %get-tuple-element.57.rows, f32[2,4,6,8,128]{4,3,2,1,0:T(8,128)S(1)} %get-tuple-element.58.sums_in, ...), custom_call_target="tpu_custom_call" | custom-call | flops 3538944 | bytes 2236416 | tf_op jit(solution)/shard_map/pallas_call | solution.py:310
  27.2 1.5 %collective-permute-done.6.far_in = f32[2,4,6,8,128]{4,3,2,1,0:T(8,128)S(1)} collective-permute-done((f32[2,4,6,8,128]{4,3,2,1,0:T(8,128)S(1)}, f32[2,4,6,8,128]{4,3,2,1,0:T(8,128)S(1)}, u32[]{:S(2)}, u32[]{:S(2)}) %collective-permute-start.6) | collective-permute-done | bytes 196640 | tf_op jit(solution)/shard_map/ppermute | solution.py:342
  28.7 1.6 %shard_map.35.rest_0_ = f32[24,6,16,64]{3,2,1,0:T(8,128)} custom-call(f32[2,4,6,8,128]{4,3,2,1,0:T(8,128)S(1)} %collective-permute-done.6.far_in, f32[2,4,6,8,128]{4,3,2,1,0:T(8,128)S(1)} %collective-permute-done.7.near_in, f32[2,4,6,8,128]{4,3,2,1,0:T(8,128)S(1)} %get-tuple-element.49.rows, ...), custom_call_target="tpu_custom_call", output_to_operand_aliasing={{}: (7, {})} | custom-call | flops 3538944 | bytes 2826240 | tf_op jit(solution)/shard_map/pallas_call | solution.py:310
  30.2 2.4 %collective-permute-done.2.far_in = f32[2,4,6,8,128]{4,3,2,1,0:T(8,128)S(1)} collective-permute-done((f32[2,4,6,8,128]{4,3,2,1,0:T(8,128)S(1)}, f32[2,4,6,8,128]{4,3,2,1,0:T(8,128)S(1)}, u32[]{:S(2)}, u32[]{:S(2)}) %collective-permute-start.2) | collective-permute-done | bytes 196640 | tf_op jit(solution)/shard_map/ppermute | solution.py:342
  32.7 1.4 %shard_map.36 = f32[24,6,16,64]{3,2,1,0:T(8,128)} custom-call(f32[2,4,6,8,128]{4,3,2,1,0:T(8,128)S(1)} %collective-permute-done.2.far_in, f32[2,4,6,8,128]{4,3,2,1,0:T(8,128)S(1)} %collective-permute-done.3.near_in, f32[2,4,6,8,128]{4,3,2,1,0:T(8,128)S(1)} %get-tuple-element.41.rows, ...), custom_call_target="tpu_custom_call", output_to_operand_aliasing={{}: (7, {})} | custom-call | flops 3538944 | bytes 2826240 | tf_op jit(solution)/shard_map/pallas_call | solution.py:310
  (9 shorter events, 0.2 us)
Async XLA Ops:
  2.3 9.5 %collective-permute-start.8 = (f32[2,4,6,8,128]{4,3,2,1,0:T(8,128)S(1)}, f32[2,4,6,8,128]{4,3,2,1,0:T(8,128)S(1)}, u32[]{:S(2)}, u32[]{:S(2)}) collective-permute-start(f32[2,4,6,8,128]{4,3,2,1,0:T(8,128)S(1)} %get-tuple-element.51), channel_id=1, source_target_pairs={{0,15},{1,2},{2,1},{3,4},{4,3},{5,6},{6,5},{7,8},{8,7},{9,10},{10,... | collective-permute-start | bytes 589832 | tf_op jit(solution)/shard_map/ppermute | solution.py:342
  5.0 8.8 %collective-permute-start.9 = (f32[2,4,6,8,128]{4,3,2,1,0:T(8,128)S(1)}, f32[2,4,6,8,128]{4,3,2,1,0:T(8,128)S(1)}, u32[]{:S(2)}, u32[]{:S(2)}) collective-permute-start(f32[2,4,6,8,128]{4,3,2,1,0:T(8,128)S(1)} %get-tuple-element.52), channel_id=1, source_target_pairs={{0,1},{1,0},{2,3},{3,2},{4,5},{5,4},{6,7},{7,6},{8,9},{9,8},{10,11... | collective-permute-start | bytes 589832 | tf_op jit(solution)/shard_map/ppermute | solution.py:343
  8.5 7.5 %collective-permute-start.4 = (f32[2,4,6,8,128]{4,3,2,1,0:T(8,128)S(1)}, f32[2,4,6,8,128]{4,3,2,1,0:T(8,128)S(1)}, u32[]{:S(2)}, u32[]{:S(2)}) collective-permute-start(f32[2,4,6,8,128]{4,3,2,1,0:T(8,128)S(1)} %get-tuple-element.43), channel_id=1, source_target_pairs={{0,15},{1,2},{2,1},{3,4},{4,3},{5,6},{6,5},{7,8},{8,7},{9,10},{10,... | collective-permute-start | bytes 589832 | tf_op jit(solution)/shard_map/ppermute | solution.py:342
  8.6 10.5 %collective-permute-start.5 = (f32[2,4,6,8,128]{4,3,2,1,0:T(8,128)S(1)}, f32[2,4,6,8,128]{4,3,2,1,0:T(8,128)S(1)}, u32[]{:S(2)}, u32[]{:S(2)}) collective-permute-start(f32[2,4,6,8,128]{4,3,2,1,0:T(8,128)S(1)} %get-tuple-element.44), channel_id=1, source_target_pairs={{0,1},{1,0},{2,3},{3,2},{4,5},{5,4},{6,7},{7,6},{8,9},{9,8},{10,11... | collective-permute-start | bytes 589832 | tf_op jit(solution)/shard_map/ppermute | solution.py:343
  10.0 12.3 %collective-permute-start = (f32[2,4,6,8,128]{4,3,2,1,0:T(8,128)S(1)}, f32[2,4,6,8,128]{4,3,2,1,0:T(8,128)S(1)}, u32[]{:S(2)}, u32[]{:S(2)}) collective-permute-start(f32[2,4,6,8,128]{4,3,2,1,0:T(8,128)S(1)} %get-tuple-element.35), channel_id=1, source_target_pairs={{0,15},{1,2},{2,1},{3,4},{4,3},{5,6},{6,5},{7,8},{8,7},{9,10},{10,... | collective-permute-start | bytes 589832 | tf_op jit(solution)/shard_map/ppermute | solution.py:342
  11.8 10.5 %collective-permute-start.1 = (f32[2,4,6,8,128]{4,3,2,1,0:T(8,128)S(1)}, f32[2,4,6,8,128]{4,3,2,1,0:T(8,128)S(1)}, u32[]{:S(2)}, u32[]{:S(2)}) collective-permute-start(f32[2,4,6,8,128]{4,3,2,1,0:T(8,128)S(1)} %get-tuple-element.36), channel_id=1, source_target_pairs={{0,1},{1,0},{2,3},{3,2},{4,5},{5,4},{6,7},{7,6},{8,9},{9,8},{10,11... | collective-permute-start | bytes 589832 | tf_op jit(solution)/shard_map/ppermute | solution.py:343
  14.8 9.6 %collective-permute-start.10 = (f32[2,4,6,8,128]{4,3,2,1,0:T(8,128)S(1)}, f32[2,4,6,8,128]{4,3,2,1,0:T(8,128)S(1)}, u32[]{:S(2)}, u32[]{:S(2)}) collective-permute-start(f32[2,4,6,8,128]{4,3,2,1,0:T(8,128)S(1)} %get-tuple-element.55), channel_id=1, source_target_pairs={{0,15},{1,2},{2,1},{3,4},{4,3},{5,6},{6,5},{7,8},{8,7},{9,10},{10,... | collective-permute-start | bytes 589832 | tf_op jit(solution)/shard_map/ppermute | solution.py:342
  16.0 9.8 %collective-permute-start.11 = (f32[2,4,6,8,128]{4,3,2,1,0:T(8,128)S(1)}, f32[2,4,6,8,128]{4,3,2,1,0:T(8,128)S(1)}, u32[]{:S(2)}, u32[]{:S(2)}) collective-permute-start(f32[2,4,6,8,128]{4,3,2,1,0:T(8,128)S(1)} %get-tuple-element.56), channel_id=1, source_target_pairs={{0,1},{1,0},{2,3},{3,2},{4,5},{5,4},{6,7},{7,6},{8,9},{9,8},{10,11... | collective-permute-start | bytes 589832 | tf_op jit(solution)/shard_map/ppermute | solution.py:343
  20.1 8.5 %collective-permute-start.6 = (f32[2,4,6,8,128]{4,3,2,1,0:T(8,128)S(1)}, f32[2,4,6,8,128]{4,3,2,1,0:T(8,128)S(1)}, u32[]{:S(2)}, u32[]{:S(2)}) collective-permute-start(f32[2,4,6,8,128]{4,3,2,1,0:T(8,128)S(1)} %get-tuple-element.47), channel_id=1, source_target_pairs={{0,15},{1,2},{2,1},{3,4},{4,3},{5,6},{6,5},{7,8},{8,7},{9,10},{10,... | collective-permute-start | bytes 589832 | tf_op jit(solution)/shard_map/ppermute | solution.py:342
  22.3 6.4 %collective-permute-start.7 = (f32[2,4,6,8,128]{4,3,2,1,0:T(8,128)S(1)}, f32[2,4,6,8,128]{4,3,2,1,0:T(8,128)S(1)}, u32[]{:S(2)}, u32[]{:S(2)}) collective-permute-start(f32[2,4,6,8,128]{4,3,2,1,0:T(8,128)S(1)} %get-tuple-element.48), channel_id=1, source_target_pairs={{0,1},{1,0},{2,3},{3,2},{4,5},{5,4},{6,7},{7,6},{8,9},{9,8},{10,11... | collective-permute-start | bytes 589832 | tf_op jit(solution)/shard_map/ppermute | solution.py:343
  23.3 9.3 %collective-permute-start.2 = (f32[2,4,6,8,128]{4,3,2,1,0:T(8,128)S(1)}, f32[2,4,6,8,128]{4,3,2,1,0:T(8,128)S(1)}, u32[]{:S(2)}, u32[]{:S(2)}) collective-permute-start(f32[2,4,6,8,128]{4,3,2,1,0:T(8,128)S(1)} %get-tuple-element.39), channel_id=1, source_target_pairs={{0,15},{1,2},{2,1},{3,4},{4,3},{5,6},{6,5},{7,8},{8,7},{9,10},{10,... | collective-permute-start | bytes 589832 | tf_op jit(solution)/shard_map/ppermute | solution.py:342
  24.4 8.2 %collective-permute-start.3 = (f32[2,4,6,8,128]{4,3,2,1,0:T(8,128)S(1)}, f32[2,4,6,8,128]{4,3,2,1,0:T(8,128)S(1)}, u32[]{:S(2)}, u32[]{:S(2)}) collective-permute-start(f32[2,4,6,8,128]{4,3,2,1,0:T(8,128)S(1)} %get-tuple-element.40), channel_id=1, source_target_pairs={{0,1},{1,0},{2,3},{3,2},{4,5},{5,4},{6,7},{7,6},{8,9},{9,8},{10,11... | collective-permute-start | bytes 589832 | tf_op jit(solution)/shard_map/ppermute | solution.py:343

commit v9 on v7

--- a/solution.py
+++ b/solution.py
@@ -130,12 +130,12 @@
         x_link = [
             [tile(links, (0, a, b, part)) * (-1.0 / 6.0) for b in range(3)] for a in range(3)
         ]
-        for row, pick in rows:
-            own = [[pick(entry, entry, low) for entry in line] for line in x_link]
-            for a in range(3):
-                for b in range(3):
-                    other = x_other(own[b][a], even)
-                    inner[row, 0, a, b, part] = own[a][b] + (other if part == 0 else -other)
+        for a in range(3):
+            for b in range(3):
+                other = x_other(x_link[b][a], even)
+                both = x_link[a][b] + (other if part == 0 else -other)
+                for row, pick in rows:
+                    inner[row, 0, a, b, part] = pick(both, both, low)
 
 
 def add_inner(inner, row, pairs, field, sums):
@@ -232,14 +232,23 @@
     later_copy.wait()
 
 
-def start_kernel(coeff, first, later, inner, edge, rows, sums, far_out, near_out):
+def start_kernel(coeff, first, later, inner, edge, *refs):
+    before, (rows, sums, far_out, near_out) = refs[:-4], refs[-4:]
     pack_rows(lambda n, k: tile(later, (first + n, k)), rows)
-    start_chunk(coeff, rows, inner, edge, sums, far_out, near_out)
+    held = 0
+    for ref in before:
+        held = ref.shape[1]
+        for row in range(2):
+            for n in range(held):
+                put(near_out, row, [n], take(ref, row, [n]))
+    own = near_out.at[:, pl.ds(held, rows.shape[1])]
+    start_chunk(coeff, rows, inner, edge, sums, far_out, own)
 
 
 def round_kernel(
     coeff,
     next_coeff,
+    place,
     far_in,
     near_in,
     rows,
@@ -247,14 +256,13 @@
     start,
     inner,
     edge,
-    all_started,
     rows_out,
     sums_out,
     far_out,
     near_out,
     middle,
 ):
-    del all_started
+    near_in = near_in.at[:, pl.ds(place, rows.shape[1])]
 
     def run(lower_side, upper_side):
         below, down = lower_side
@@ -327,9 +335,7 @@
 
 
 def chunk_sizes(pairs):
-    last = pairs // 4
-    second = pairs // 3
-    return (pairs - second - last, second, last)
+    return tuple(pairs * part // 12 for part in (6, 4, 2))
 
 
 def halo_body(links, sources):
@@ -374,24 +380,29 @@
         (0, 1),
     )
     start, fields, halos = [rows], [(rows, sums)], [exchange(*sends)]
+    fars, before, places = [], [], [0, 0]
     for chunk in chunks[1:]:
-        rows, sums, *sends = call(
+        near_shape = f32((2, places[-1] + sizes[chunk], *both[chunk].shape[2:]))
+        rows, sums, far_out, near_out = call(
             functools.partial(start_kernel, steps[0], first[chunk] - first[1]),
-            [both[chunk]] * 4,
-            [later, inner, edge],
+            [both[chunk]] * 3 + [near_shape],
+            [later, inner, edge, *before],
             6 * work[chunk],
         )
         start.append(rows)
         fields.append((rows, sums))
-        halos.append(exchange(*sends))
+        fars.append(lax.ppermute(far_out, "space", far_pairs))
+        before = [near_out]
+        places.append(places[-1] + sizes[chunk])
+    near = lax.ppermute(near_out, "space", near_pairs)
+    halos += [(far, near) for far in fars]
     for chunk in chunks:
         rows, sums, *sends = call(
-            functools.partial(round_kernel, steps[1], steps[2]),
+            functools.partial(round_kernel, steps[1], steps[2], places[chunk]),
             [both[chunk]] * 4,
-            [*halos[chunk], *fields[chunk], start[chunk], inner, edge, start[-1]],
+            [*halos[chunk], *fields[chunk], start[chunk], inner, edge],
             12 * work[chunk],
             [middle[chunk]],
-            unread=(7,),
         )
         fields[chunk] = (rows, sums)
         halos[chunk] = exchange(*sends)

time: 38.7 us -> 37.1 us (0.959)
  waiting for transfers between devices: 5.59 us -> 3.85 us
  Pallas kernels: 11.1 us -> 12 us
  starting transfers between devices: 21.6 us -> 20.8 us
    ppermute x0 -> x3, starting transfers between devices: none -> 4.02 us  [the longest x2 3.44 us: halo_body(): fars.append(lax.ppermute(far_out, 'space', far_pairs))]
    ppermute x6 -> x4, starting transfers between devices: 6.01 us -> 2.31 us  [exchange(): return (far, lax.ppermute(near_out, 'space', near_pairs))]
    ppermute x6 -> x4, waiting for transfers between devices: 5.57 us -> 2.52 us  [exchange(): far = lax.ppermute(far_out, 'space', far_pairs)]
    ppermute x0 -> x3, waiting for transfers between devices: none -> 1.32 us  [the longest x2 1.32 us: halo_body(): fars.append(lax.ppermute(far_out, 'space', far_pairs))]
    ppermute x6 -> x4, starting transfers between devices: 15.6 us -> 14.5 us  [exchange(): far = lax.ppermute(far_out, 'space', far_pairs)]
    pallas_call x9, Pallas kernels: 11.1 us -> 12 us  [call(): pl.pallas_call(kernel, out_shape=outs, in_specs=[hbm if i in in_hbm else...]
  transfers between devices with their start and end apart: 12 -> 11, of which waited for: 3 -> 2; matrix products, arithmetic and copies ran while one was open for 0% -> 0% of each run, Pallas kernels for 19% -> 22%
where the time goes in v9:
time: 37.1 us; the launch traced here: 36.9 us
  starting transfers between devices  20.8 us (56%)
  Pallas kernels  12 us (32%)
  waiting for transfers between devices  3.85 us (10%)
    ppermute x4, starting transfers between devices, exchange(): far = lax.ppermute(far_out, 'space', far_pairs)  14.5 us
    pallas_call x9, Pallas kernels, call(): pl.pallas_call(kernel, out_shape=outs, in_specs=[hbm if i in in_hbm else...  12 us
    ppermute x2, starting transfers between devices, halo_body(): fars.append(lax.ppermute(far_out, 'space', far_pairs))  3.44 us
    ppermute x4, waiting for transfers between devices, exchange(): far = lax.ppermute(far_out, 'space', far_pairs)  2.52 us
    ppermute x4, starting transfers between devices, exchange(): return (far, lax.ppermute(near_out, 'space', near_pairs))  2.31 us
    ppermute x2, waiting for transfers between devices, halo_body(): fars.append(lax.ppermute(far_out, 'space', far_pairs))  1.32 us
  transfers between devices with their start and end apart: 11, of which 2 were waited for; matrix products, arithmetic and copies ran while one was open for 0% of the time, Pallas kernels for 22%

profile of v9, /device:TPU:0, one launch (start us, length us, event | category | flops | bytes accessed | tf_op | source)
XLA Modules:
  0.0 36.9 jit_solution(12441430636685690010)
XLA Ops:
  0.0 2.8 %shard_map.28 = (f32[2,4,3,3,2,8,128]{6,5,4,3,2,1,0:T(8,128)S(1)}, f32[3,3,2,8,128]{4,3,2,1,0:T(8,128)S(1)}, f32[2,6,6,8,128]{4,3,2,1,0:T(8,128)S(1)}, f32[2,6,6...) custom-call(f32[24,6,16,64]{3,2,1,0:T(8,128)} %bitcast.7, ...), custom_call_target="tpu_custom_call" | custom-call | flops 5308416 | bytes 2949120 | tf_op jit(solution)/shard_map/pallas_call | solution.py:323
  2.8 5.5 %collective-permute-start.7 = (f32[2,6,6,8,128]{4,3,2,1,0:T(8,128)S(1)}, f32[2,6,6,8,128]{4,3,2,1,0:T(8,128)S(1)}, u32[]{:S(2)}, u32[]{:S(2)}) collective-permute-start(f32[2,6,6,8,128]{4,3,2,1,0:T(8,128)S(1)} %get-tuple-element.51), channel_id=1, source_target_pairs={{0,15},{1,2},{2,1},{3,4},{4,3},{5,6},{6,5},{7,8},{8,7},{9,10},{10,... | collective-permute-start | bytes 884744 | tf_op jit(solution)/shard_map/ppermute | solution.py:362
  8.3 0.7 %shard_map.29 = (f32[2,4,6,8,128]{4,3,2,1,0:T(8,128)S(1)}, f32[2,4,6,8,128]{4,3,2,1,0:T(8,128)S(1)}, f32[2,4,6,8,128]{4,3,2,1,0:T(8,128)S(1)}, f32[2,4,6,8,128]{4,3,2,1,0:T(8,128)S(1)}) custom-call(f32[12,6,16,64]{3,2,1,0:T(8,128)S(1)} %get-tuple-element.32.later, f32[2,4,3,3,2,8,128]{6,5,4,3,2,1,0:T(8,128)S(1)} %get-tuple-element.33.inner, ...), custom_call_target="tpu_custom_call" | custom-call | flops 3538944 | bytes 1744896 | tf_op jit(solution)/shard_map/pallas_call | solution.py:323
  8.9 0.4 %shard_map.30 = (f32[2,2,6,8,128]{4,3,2,1,0:T(8,128)S(1)}, f32[2,2,6,8,128]{4,3,2,1,0:T(8,128)S(1)}, f32[2,2,6,8,128]{4,3,2,1,0:T(8,128)S(1)}, f32[2,6,6,8,128]{4,3,2,1,0:T(8,128)S(1)}) custom-call(f32[12,6,16,64]{3,2,1,0:T(8,128)S(1)} %get-tuple-element.32.later, f32[2,4,3,3,2,8,128]{6,5,4,3,2,1,0:T(8,128)S(1)} %get-tuple-element.33.inner, ...), custom_call_target="tpu_custom_call" | custom-call | flops 1769472 | bytes 1744896 | tf_op jit(solution)/shard_map/pallas_call | solution.py:323
  9.3 0.6 %collective-permute-start.1 = (f32[2,6,6,8,128]{4,3,2,1,0:T(8,128)S(1)}, f32[2,6,6,8,128]{4,3,2,1,0:T(8,128)S(1)}, u32[]{:S(2)}, u32[]{:S(2)}) collective-permute-start(f32[2,6,6,8,128]{4,3,2,1,0:T(8,128)S(1)} %get-tuple-element.37), channel_id=1, source_target_pairs={{0,1},{1,0},{2,3},{3,2},{4,5},{5,4},{6,7},{7,6},{8,9},{9,8},{10,11... | collective-permute-start | bytes 884744 | tf_op jit(solution)/shard_map/ppermute | solution.py:397
  9.9 0.3 collective-permute-start.4
  10.3 2.5 %collective-permute-done.7.far_in = f32[2,6,6,8,128]{4,3,2,1,0:T(8,128)S(1)} collective-permute-done((f32[2,6,6,8,128]{4,3,2,1,0:T(8,128)S(1)}, f32[2,6,6,8,128]{4,3,2,1,0:T(8,128)S(1)}, u32[]{:S(2)}, u32[]{:S(2)}) %collective-permute-start.7) | collective-permute-done | bytes 294944 | tf_op jit(solution)/shard_map/ppermute | solution.py:362
  12.8 0.0 collective-permute-done.8.near_in
  12.8 1.5 %shard_map.33 = (f32[2,6,6,8,128]{4,3,2,1,0:T(8,128)S(1)}, f32[2,6,6,8,128]{4,3,2,1,0:T(8,128)S(1)}, f32[2,6,6,8,128]{4,3,2,1,0:T(8,128)S(1)}, f32[2,6,6,8,128]{4,3,2,1,0:T(8,128)S(1)}) custom-call(f32[2,6,6,8,128]{4,3,2,1,0:T(8,128)S(1)} %collective-permute-done.7.far_in, f32[2,6,6,8,128]{4,3,2,1,0:T(8,128)S(1)} %collective-permute-done.8.near_in, ...), custom_call_target="tpu_custom_call" | custom-call | flops 10616832 | bytes 3317760 | tf_op jit(solution)/shard_map/pallas_call | solution.py:323
  14.3 4.5 %collective-permute-start.9 = (f32[2,6,6,8,128]{4,3,2,1,0:T(8,128)S(1)}, f32[2,6,6,8,128]{4,3,2,1,0:T(8,128)S(1)}, u32[]{:S(2)}, u32[]{:S(2)}) collective-permute-start(f32[2,6,6,8,128]{4,3,2,1,0:T(8,128)S(1)} %get-tuple-element.55), channel_id=1, source_target_pairs={{0,15},{1,2},{2,1},{3,4},{4,3},{5,6},{6,5},{7,8},{8,7},{9,10},{10,... | collective-permute-start | bytes 884744 | tf_op jit(solution)/shard_map/ppermute | solution.py:362
  18.8 0.1 collective-permute-start.10
  18.9 3.1 %collective-permute-start = (f32[2,2,6,8,128]{4,3,2,1,0:T(8,128)S(1)}, f32[2,2,6,8,128]{4,3,2,1,0:T(8,128)S(1)}, u32[]{:S(2)}, u32[]{:S(2)}) collective-permute-start(f32[2,2,6,8,128]{4,3,2,1,0:T(8,128)S(1)} %get-tuple-element.36), channel_id=1, source_target_pairs={{0,15},{1,2},{2,1},{3,4},{4,3},{5,6},{6,5},{7,8},{8,7},{9,10},{10,... | collective-permute-start | bytes 294920 | tf_op jit(solution)/shard_map/ppermute | solution.py:394
  22.0 0.0 collective-permute-done.4.far_in
  22.0 0.0 collective-permute-done.1.near_in
  22.0 1.0 %shard_map.32 = (f32[2,4,6,8,128]{4,3,2,1,0:T(8,128)S(1)}, f32[2,4,6,8,128]{4,3,2,1,0:T(8,128)S(1)}, f32[2,4,6,8,128]{4,3,2,1,0:T(8,128)S(1)}, f32[2,4,6,8,128]{4,3,2,1,0:T(8,128)S(1)}) custom-call(f32[2,4,6,8,128]{4,3,2,1,0:T(8,128)S(1)} %collective-permute-done.4.far_in, f32[2,6,6,8,128]{4,3,2,1,0:T(8,128)S(1)} %collective-permute-done.1.near_in, ...), custom_call_target="tpu_custom_call" | custom-call | flops 7077888 | bytes 2531328 | tf_op jit(solution)/shard_map/pallas_call | solution.py:323
  23.0 1.4 %collective-permute-start.5 = (f32[2,4,6,8,128]{4,3,2,1,0:T(8,128)S(1)}, f32[2,4,6,8,128]{4,3,2,1,0:T(8,128)S(1)}, u32[]{:S(2)}, u32[]{:S(2)}) collective-permute-start(f32[2,4,6,8,128]{4,3,2,1,0:T(8,128)S(1)} %get-tuple-element.47), channel_id=1, source_target_pairs={{0,15},{1,2},{2,1},{3,4},{4,3},{5,6},{6,5},{7,8},{8,7},{9,10},{10,... | collective-permute-start | bytes 589832 | tf_op jit(solution)/shard_map/ppermute | solution.py:362
  24.4 0.0 collective-permute-start.6
  24.4 1.3 %collective-permute-done.far_in = f32[2,2,6,8,128]{4,3,2,1,0:T(8,128)S(1)} collective-permute-done((f32[2,2,6,8,128]{4,3,2,1,0:T(8,128)S(1)}, f32[2,2,6,8,128]{4,3,2,1,0:T(8,128)S(1)}, u32[]{:S(2)}, u32[]{:S(2)}) %collective-permute-start) | collective-permute-done | bytes 98336 | tf_op jit(solution)/shard_map/ppermute | solution.py:394
  25.7 0.5 %shard_map.31 = (f32[2,2,6,8,128]{4,3,2,1,0:T(8,128)S(1)}, f32[2,2,6,8,128]{4,3,2,1,0:T(8,128)S(1)}, f32[2,2,6,8,128]{4,3,2,1,0:T(8,128)S(1)}, f32[2,2,6,8,128]{4,3,2,1,0:T(8,128)S(1)}) custom-call(f32[2,2,6,8,128]{4,3,2,1,0:T(8,128)S(1)} %collective-permute-done.far_in, f32[2,6,6,8,128]{4,3,2,1,0:T(8,128)S(1)} %collective-permute-done.1.near_in, ...), custom_call_target="tpu_custom_call" | custom-call | flops 3538944 | bytes 1744896 | tf_op jit(solution)/shard_map/pallas_call | solution.py:323
  26.2 3.1 %collective-permute-start.2 = (f32[2,2,6,8,128]{4,3,2,1,0:T(8,128)S(1)}, f32[2,2,6,8,128]{4,3,2,1,0:T(8,128)S(1)}, u32[]{:S(2)}, u32[]{:S(2)}) collective-permute-start(f32[2,2,6,8,128]{4,3,2,1,0:T(8,128)S(1)} %get-tuple-element.40), channel_id=1, source_target_pairs={{0,15},{1,2},{2,1},{3,4},{4,3},{5,6},{6,5},{7,8},{8,7},{9,10},{10,... | collective-permute-start | bytes 294920 | tf_op jit(solution)/shard_map/ppermute | solution.py:362
  29.4 2.2 %collective-permute-start.3 = (f32[2,2,6,8,128]{4,3,2,1,0:T(8,128)S(1)}, f32[2,2,6,8,128]{4,3,2,1,0:T(8,128)S(1)}, u32[]{:S(2)}, u32[]{:S(2)}) collective-permute-start(f32[2,2,6,8,128]{4,3,2,1,0:T(8,128)S(1)} %get-tuple-element.41), channel_id=1, source_target_pairs={{0,1},{1,0},{2,3},{3,2},{4,5},{5,4},{6,7},{7,6},{8,9},{9,8},{10,11... | collective-permute-start | bytes 294920 | tf_op jit(solution)/shard_map/ppermute | solution.py:363
  31.6 2.6 %shard_map.34.rest_0_ = f32[24,6,16,64]{3,2,1,0:T(8,128)} custom-call(f32[2,6,6,8,128]{4,3,2,1,0:T(8,128)S(1)} %collective-permute-done.9.far_in, f32[2,6,6,8,128]{4,3,2,1,0:T(8,128)S(1)} %collective-permute-done.10.near_in, f32[2,6,6,8,128]{4,3,2,1,0:T(8,128)S(1)} %get-tuple-element.57.rows, f32[2,6,6,8,128]{4,3,2,1,0:T(8,128)S(1)} %get-tuple-element.58.sums_in, ...), custom_call_target="tpu_custom_call" | custom-call | flops 5308416 | bytes 2727936 | tf_op jit(solution)/shard_map/pallas_call | solution.py:323
  34.2 1.4 %shard_map.35.rest_0_ = f32[24,6,16,64]{3,2,1,0:T(8,128)} custom-call(f32[2,4,6,8,128]{4,3,2,1,0:T(8,128)S(1)} %collective-permute-done.5.far_in, f32[2,4,6,8,128]{4,3,2,1,0:T(8,128)S(1)} %collective-permute-done.6.near_in, f32[2,4,6,8,128]{4,3,2,1,0:T(8,128)S(1)} %get-tuple-element.49.rows, ...), custom_call_target="tpu_custom_call", output_to_operand_aliasing={{}: (7, {})} | custom-call | flops 3538944 | bytes 2826240 | tf_op jit(solution)/shard_map/pallas_call | solution.py:323
  35.7 1.1 %shard_map.36 = f32[24,6,16,64]{3,2,1,0:T(8,128)} custom-call(f32[2,2,6,8,128]{4,3,2,1,0:T(8,128)S(1)} %collective-permute-done.2.far_in, f32[2,2,6,8,128]{4,3,2,1,0:T(8,128)S(1)} %collective-permute-done.3.near_in, f32[2,2,6,8,128]{4,3,2,1,0:T(8,128)S(1)} %get-tuple-element.42.rows, ...), custom_call_target="tpu_custom_call", output_to_operand_aliasing={{}: (7, {})} | custom-call | flops 1769472 | bytes 2334720 | tf_op jit(solution)/shard_map/pallas_call | solution.py:323
  (7 shorter events, 0.0 us)
Async XLA Ops:
  2.8 10.0 %collective-permute-start.7 = (f32[2,6,6,8,128]{4,3,2,1,0:T(8,128)S(1)}, f32[2,6,6,8,128]{4,3,2,1,0:T(8,128)S(1)}, u32[]{:S(2)}, u32[]{:S(2)}) collective-permute-start(f32[2,6,6,8,128]{4,3,2,1,0:T(8,128)S(1)} %get-tuple-element.51), channel_id=1, source_target_pairs={{0,15},{1,2},{2,1},{3,4},{4,3},{5,6},{6,5},{7,8},{8,7},{9,10},{10,... | collective-permute-start | bytes 884744 | tf_op jit(solution)/shard_map/ppermute | solution.py:362
  8.3 4.5 %collective-permute-start.8 = (f32[2,6,6,8,128]{4,3,2,1,0:T(8,128)S(1)}, f32[2,6,6,8,128]{4,3,2,1,0:T(8,128)S(1)}, u32[]{:S(2)}, u32[]{:S(2)}) collective-permute-start(f32[2,6,6,8,128]{4,3,2,1,0:T(8,128)S(1)} %get-tuple-element.52), channel_id=1, source_target_pairs={{0,1},{1,0},{2,3},{3,2},{4,5},{5,4},{6,7},{7,6},{8,9},{9,8},{10,11... | collective-permute-start | bytes 884744 | tf_op jit(solution)/shard_map/ppermute | solution.py:363
  9.3 12.7 %collective-permute-start.1 = (f32[2,6,6,8,128]{4,3,2,1,0:T(8,128)S(1)}, f32[2,6,6,8,128]{4,3,2,1,0:T(8,128)S(1)}, u32[]{:S(2)}, u32[]{:S(2)}) collective-permute-start(f32[2,6,6,8,128]{4,3,2,1,0:T(8,128)S(1)} %get-tuple-element.37), channel_id=1, source_target_pairs={{0,1},{1,0},{2,3},{3,2},{4,5},{5,4},{6,7},{7,6},{8,9},{9,8},{10,11... | collective-permute-start | bytes 884744 | tf_op jit(solution)/shard_map/ppermute | solution.py:397
  9.9 12.1 %collective-permute-start.4 = (f32[2,4,6,8,128]{4,3,2,1,0:T(8,128)S(1)}, f32[2,4,6,8,128]{4,3,2,1,0:T(8,128)S(1)}, u32[]{:S(2)}, u32[]{:S(2)}) collective-permute-start(f32[2,4,6,8,128]{4,3,2,1,0:T(8,128)S(1)} %get-tuple-element.44), channel_id=1, source_target_pairs={{0,15},{1,2},{2,1},{3,4},{4,3},{5,6},{6,5},{7,8},{8,7},{9,10},{10,... | collective-permute-start | bytes 589832 | tf_op jit(solution)/shard_map/ppermute | solution.py:394
  14.3 15.1 %collective-permute-start.9 = (f32[2,6,6,8,128]{4,3,2,1,0:T(8,128)S(1)}, f32[2,6,6,8,128]{4,3,2,1,0:T(8,128)S(1)}, u32[]{:S(2)}, u32[]{:S(2)}) collective-permute-start(f32[2,6,6,8,128]{4,3,2,1,0:T(8,128)S(1)} %get-tuple-element.55), channel_id=1, source_target_pairs={{0,15},{1,2},{2,1},{3,4},{4,3},{5,6},{6,5},{7,8},{8,7},{9,10},{10,... | collective-permute-start | bytes 884744 | tf_op jit(solution)/shard_map/ppermute | solution.py:362
  18.8 12.8 %collective-permute-start.10 = (f32[2,6,6,8,128]{4,3,2,1,0:T(8,128)S(1)}, f32[2,6,6,8,128]{4,3,2,1,0:T(8,128)S(1)}, u32[]{:S(2)}, u32[]{:S(2)}) collective-permute-start(f32[2,6,6,8,128]{4,3,2,1,0:T(8,128)S(1)} %get-tuple-element.56), channel_id=1, source_target_pairs={{0,1},{1,0},{2,3},{3,2},{4,5},{5,4},{6,7},{7,6},{8,9},{9,8},{10,11... | collective-permute-start | bytes 884744 | tf_op jit(solution)/shard_map/ppermute | solution.py:363
  18.9 6.8 %collective-permute-start = (f32[2,2,6,8,128]{4,3,2,1,0:T(8,128)S(1)}, f32[2,2,6,8,128]{4,3,2,1,0:T(8,128)S(1)}, u32[]{:S(2)}, u32[]{:S(2)}) collective-permute-start(f32[2,2,6,8,128]{4,3,2,1,0:T(8,128)S(1)} %get-tuple-element.36), channel_id=1, source_target_pairs={{0,15},{1,2},{2,1},{3,4},{4,3},{5,6},{6,5},{7,8},{8,7},{9,10},{10,... | collective-permute-start | bytes 294920 | tf_op jit(solution)/shard_map/ppermute | solution.py:394
  23.0 11.2 %collective-permute-start.5 = (f32[2,4,6,8,128]{4,3,2,1,0:T(8,128)S(1)}, f32[2,4,6,8,128]{4,3,2,1,0:T(8,128)S(1)}, u32[]{:S(2)}, u32[]{:S(2)}) collective-permute-start(f32[2,4,6,8,128]{4,3,2,1,0:T(8,128)S(1)} %get-tuple-element.47), channel_id=1, source_target_pairs={{0,15},{1,2},{2,1},{3,4},{4,3},{5,6},{6,5},{7,8},{8,7},{9,10},{10,... | collective-permute-start | bytes 589832 | tf_op jit(solution)/shard_map/ppermute | solution.py:362
  24.4 9.8 %collective-permute-start.6 = (f32[2,4,6,8,128]{4,3,2,1,0:T(8,128)S(1)}, f32[2,4,6,8,128]{4,3,2,1,0:T(8,128)S(1)}, u32[]{:S(2)}, u32[]{:S(2)}) collective-permute-start(f32[2,4,6,8,128]{4,3,2,1,0:T(8,128)S(1)} %get-tuple-element.48), channel_id=1, source_target_pairs={{0,1},{1,0},{2,3},{3,2},{4,5},{5,4},{6,7},{7,6},{8,9},{9,8},{10,11... | collective-permute-start | bytes 589832 | tf_op jit(solution)/shard_map/ppermute | solution.py:363
  26.2 9.4 %collective-permute-start.2 = (f32[2,2,6,8,128]{4,3,2,1,0:T(8,128)S(1)}, f32[2,2,6,8,128]{4,3,2,1,0:T(8,128)S(1)}, u32[]{:S(2)}, u32[]{:S(2)}) collective-permute-start(f32[2,2,6,8,128]{4,3,2,1,0:T(8,128)S(1)} %get-tuple-element.40), channel_id=1, source_target_pairs={{0,15},{1,2},{2,1},{3,4},{4,3},{5,6},{6,5},{7,8},{8,7},{9,10},{10,... | collective-permute-start | bytes 294920 | tf_op jit(solution)/shard_map/ppermute | solution.py:362
  29.4 6.3 %collective-permute-start.3 = (f32[2,2,6,8,128]{4,3,2,1,0:T(8,128)S(1)}, f32[2,2,6,8,128]{4,3,2,1,0:T(8,128)S(1)}, u32[]{:S(2)}, u32[]{:S(2)}) collective-permute-start(f32[2,2,6,8,128]{4,3,2,1,0:T(8,128)S(1)} %get-tuple-element.41), channel_id=1, source_target_pairs={{0,1},{1,0},{2,3},{3,2},{4,5},{5,4},{6,7},{7,6},{8,9},{9,8},{10,11... | collective-permute-start | bytes 294920 | tf_op jit(solution)/shard_map/ppermute | solution.py:363

commit v10 on v9

--- a/solution.py
+++ b/solution.py
@@ -335,7 +335,7 @@
 
 
 def chunk_sizes(pairs):
-    return tuple(pairs * part // 12 for part in (6, 4, 2))
+    return tuple(pairs * part // 12 for part in (7, 5))
 
 
 def halo_body(links, sources):

time: 37.1 us -> 35.2 us (0.949)
  the two profiles are of different devices: /device:TPU:0 before, /device:TPU:1 now
where the time goes in v10:
time: 35.2 us; the launch traced here: 35.1 us
  waiting for transfers between devices  12.1 us (34%)
  Pallas kernels  11.4 us (32%)
  starting transfers between devices  11.4 us (32%)
    pallas_call x6, Pallas kernels, call(): pl.pallas_call(kernel, out_shape=outs, in_specs=[hbm if i in in_hbm else...  11.4 us
    ppermute x3, waiting for transfers between devices, exchange(): far = lax.ppermute(far_out, 'space', far_pairs)  10 us
    ppermute x3, starting transfers between devices, exchange(): far = lax.ppermute(far_out, 'space', far_pairs)  7.75 us
    ppermute x3, starting transfers between devices, exchange(): return (far, lax.ppermute(near_out, 'space', near_pairs))  2.88 us
    ppermute x1, waiting for transfers between devices, halo_body(): fars.append(lax.ppermute(far_out, 'space', far_pairs))  2.03 us
    ppermute x1, starting transfers between devices, halo_body(): near = lax.ppermute(near_out, 'space', near_pairs)  0.74 us
  transfers between devices with their start and end apart: 8, of which 3 were waited for; matrix products, arithmetic and copies ran while one was open for 0% of the time, Pallas kernels for 18%

profile of v10, /device:TPU:1, one launch (start us, length us, event | category | flops | bytes accessed | tf_op | source)
XLA Modules:
  0.0 35.1 jit_solution(289802666134373689)
XLA Ops:
  0.0 3.3 %shard_map.28 = (f32[2,4,3,3,2,8,128]{6,5,4,3,2,1,0:T(8,128)S(1)}, f32[3,3,2,8,128]{4,3,2,1,0:T(8,128)S(1)}, f32[2,7,6,8,128]{4,3,2,1,0:T(8,128)S(1)}, f32[2,7,6...) custom-call(f32[24,6,16,64]{3,2,1,0:T(8,128)} %bitcast.7, ...), custom_call_target="tpu_custom_call" | custom-call | flops 6193152 | bytes 3096576 | tf_op jit(solution)/shard_map/pallas_call | solution.py:323
  3.3 2.7 %collective-permute-start.4 = (f32[2,7,6,8,128]{4,3,2,1,0:T(8,128)S(1)}, f32[2,7,6,8,128]{4,3,2,1,0:T(8,128)S(1)}, u32[]{:S(2)}, u32[]{:S(2)}) collective-permute-start(f32[2,7,6,8,128]{4,3,2,1,0:T(8,128)S(1)} %get-tuple-element.35), channel_id=1, source_target_pairs={{0,15},{1,2},{2,1},{3,4},{4,3},{5,6},{6,5},{7,8},{8,7},{9,10},{10,... | collective-permute-start | bytes 1032200 | tf_op jit(solution)/shard_map/ppermute | solution.py:362
  6.0 2.9 %collective-permute-start.5 = (f32[2,7,6,8,128]{4,3,2,1,0:T(8,128)S(1)}, f32[2,7,6,8,128]{4,3,2,1,0:T(8,128)S(1)}, u32[]{:S(2)}, u32[]{:S(2)}) collective-permute-start(f32[2,7,6,8,128]{4,3,2,1,0:T(8,128)S(1)} %get-tuple-element.36), channel_id=1, source_target_pairs={{0,1},{1,0},{2,3},{3,2},{4,5},{5,4},{6,7},{7,6},{8,9},{9,8},{10,11... | collective-permute-start | bytes 1032200 | tf_op jit(solution)/shard_map/ppermute | solution.py:363
  8.9 0.9 %shard_map.29 = (f32[2,5,6,8,128]{4,3,2,1,0:T(8,128)S(1)}, f32[2,5,6,8,128]{4,3,2,1,0:T(8,128)S(1)}, f32[2,5,6,8,128]{4,3,2,1,0:T(8,128)S(1)}, f32[2,5,6,8,128]{4,3,2,1,0:T(8,128)S(1)}) custom-call(f32[10,6,16,64]{3,2,1,0:T(8,128)S(1)} %get-tuple-element.24.later, f32[2,4,3,3,2,8,128]{6,5,4,3,2,1,0:T(8,128)S(1)} %get-tuple-element.25.inner, ...), custom_call_target="tpu_custom_call" | custom-call | flops 4423680 | bytes 1892352 | tf_op jit(solution)/shard_map/pallas_call | solution.py:323
  9.8 0.1 collective-permute-start
  9.8 0.7 %collective-permute-start.1 = (f32[2,5,6,8,128]{4,3,2,1,0:T(8,128)S(1)}, f32[2,5,6,8,128]{4,3,2,1,0:T(8,128)S(1)}, u32[]{:S(2)}, u32[]{:S(2)}) collective-permute-start(f32[2,5,6,8,128]{4,3,2,1,0:T(8,128)S(1)} %get-tuple-element.28), channel_id=1, source_target_pairs={{0,1},{1,0},{2,3},{3,2},{4,5},{5,4},{6,7},{7,6},{8,9},{9,8},{10,11... | collective-permute-start | bytes 737288 | tf_op jit(solution)/shard_map/ppermute | solution.py:397
  10.6 5.9 %collective-permute-done.4.far_in = f32[2,7,6,8,128]{4,3,2,1,0:T(8,128)S(1)} collective-permute-done((f32[2,7,6,8,128]{4,3,2,1,0:T(8,128)S(1)}, f32[2,7,6,8,128]{4,3,2,1,0:T(8,128)S(1)}, u32[]{:S(2)}, u32[]{:S(2)}) %collective-permute-start.4) | collective-permute-done | bytes 344096 | tf_op jit(solution)/shard_map/ppermute | solution.py:362
  16.5 0.0 collective-permute-done.5.near_in
  16.5 1.7 %shard_map.31 = (f32[2,7,6,8,128]{4,3,2,1,0:T(8,128)S(1)}, f32[2,7,6,8,128]{4,3,2,1,0:T(8,128)S(1)}, f32[2,7,6,8,128]{4,3,2,1,0:T(8,128)S(1)}, f32[2,7,6,8,128]{4,3,2,1,0:T(8,128)S(1)}) custom-call(f32[2,7,6,8,128]{4,3,2,1,0:T(8,128)S(1)} %collective-permute-done.4.far_in, f32[2,7,6,8,128]{4,3,2,1,0:T(8,128)S(1)} %collective-permute-done.5.near_in, ...), custom_call_target="tpu_custom_call" | custom-call | flops 12386304 | bytes 3760128 | tf_op jit(solution)/shard_map/pallas_call | solution.py:323
  18.3 2.5 %collective-permute-start.6 = (f32[2,7,6,8,128]{4,3,2,1,0:T(8,128)S(1)}, f32[2,7,6,8,128]{4,3,2,1,0:T(8,128)S(1)}, u32[]{:S(2)}, u32[]{:S(2)}) collective-permute-start(f32[2,7,6,8,128]{4,3,2,1,0:T(8,128)S(1)} %get-tuple-element.39), channel_id=1, source_target_pairs={{0,15},{1,2},{2,1},{3,4},{4,3},{5,6},{6,5},{7,8},{8,7},{9,10},{10,... | collective-permute-start | bytes 1032200 | tf_op jit(solution)/shard_map/ppermute | solution.py:362
  20.8 0.0 collective-permute-start.7
  20.8 2.0 %collective-permute-done.far_in = f32[2,5,6,8,128]{4,3,2,1,0:T(8,128)S(1)} collective-permute-done((f32[2,5,6,8,128]{4,3,2,1,0:T(8,128)S(1)}, f32[2,5,6,8,128]{4,3,2,1,0:T(8,128)S(1)}, u32[]{:S(2)}, u32[]{:S(2)}) %collective-permute-start) | collective-permute-done | bytes 245792 | tf_op jit(solution)/shard_map/ppermute | solution.py:394
  22.8 0.0 collective-permute-done.1.near_in
  22.8 1.2 %shard_map.30 = (f32[2,5,6,8,128]{4,3,2,1,0:T(8,128)S(1)}, f32[2,5,6,8,128]{4,3,2,1,0:T(8,128)S(1)}, f32[2,5,6,8,128]{4,3,2,1,0:T(8,128)S(1)}, f32[2,5,6,8,128]{4,3,2,1,0:T(8,128)S(1)}) custom-call(f32[2,5,6,8,128]{4,3,2,1,0:T(8,128)S(1)} %collective-permute-done.far_in, f32[2,5,6,8,128]{4,3,2,1,0:T(8,128)S(1)} %collective-permute-done.1.near_in, ...), custom_call_target="tpu_custom_call" | custom-call | flops 8847360 | bytes 2875392 | tf_op jit(solution)/shard_map/pallas_call | solution.py:323
  24.1 2.5 %collective-permute-start.2 = (f32[2,5,6,8,128]{4,3,2,1,0:T(8,128)S(1)}, f32[2,5,6,8,128]{4,3,2,1,0:T(8,128)S(1)}, u32[]{:S(2)}, u32[]{:S(2)}) collective-permute-start(f32[2,5,6,8,128]{4,3,2,1,0:T(8,128)S(1)} %get-tuple-element.31), channel_id=1, source_target_pairs={{0,15},{1,2},{2,1},{3,4},{4,3},{5,6},{6,5},{7,8},{8,7},{9,10},{10,... | collective-permute-start | bytes 737288 | tf_op jit(solution)/shard_map/ppermute | solution.py:362
  26.6 0.0 collective-permute-start.3
  26.6 4.1 %collective-permute-done.6.far_in = f32[2,7,6,8,128]{4,3,2,1,0:T(8,128)S(1)} collective-permute-done((f32[2,7,6,8,128]{4,3,2,1,0:T(8,128)S(1)}, f32[2,7,6,8,128]{4,3,2,1,0:T(8,128)S(1)}, u32[]{:S(2)}, u32[]{:S(2)}) %collective-permute-start.6) | collective-permute-done | bytes 344096 | tf_op jit(solution)/shard_map/ppermute | solution.py:362
  30.7 0.0 collective-permute-done.7.near_in
  30.7 2.6 %shard_map.32.rest_0_ = f32[24,6,16,64]{3,2,1,0:T(8,128)} custom-call(f32[2,7,6,8,128]{4,3,2,1,0:T(8,128)S(1)} %collective-permute-done.6.far_in, f32[2,7,6,8,128]{4,3,2,1,0:T(8,128)S(1)} %collective-permute-done.7.near_in, f32[2,7,6,8,128]{4,3,2,1,0:T(8,128)S(1)} %get-tuple-element.41.rows, f32[2,7,6,8,128]{4,3,2,1,0:T(8,128)S(1)} %get-tuple-element.42.sums_in, ...), custom_call_target="tpu_custom_call" | custom-call | flops 6193152 | bytes 2973696 | tf_op jit(solution)/shard_map/pallas_call | solution.py:323
  33.4 0.0 collective-permute-done.2.far_in
  33.4 0.0 collective-permute-done.3.near_in
  33.4 1.6 %shard_map.33 = f32[24,6,16,64]{3,2,1,0:T(8,128)} custom-call(f32[2,5,6,8,128]{4,3,2,1,0:T(8,128)S(1)} %collective-permute-done.2.far_in, f32[2,5,6,8,128]{4,3,2,1,0:T(8,128)S(1)} %collective-permute-done.3.near_in, f32[2,5,6,8,128]{4,3,2,1,0:T(8,128)S(1)} %get-tuple-element.33.rows, ...), custom_call_target="tpu_custom_call", output_to_operand_aliasing={{}: (7, {})} | custom-call | flops 4423680 | bytes 3072000 | tf_op jit(solution)/shard_map/pallas_call | solution.py:323
Async XLA Ops:
  3.3 13.2 %collective-permute-start.4 = (f32[2,7,6,8,128]{4,3,2,1,0:T(8,128)S(1)}, f32[2,7,6,8,128]{4,3,2,1,0:T(8,128)S(1)}, u32[]{:S(2)}, u32[]{:S(2)}) collective-permute-start(f32[2,7,6,8,128]{4,3,2,1,0:T(8,128)S(1)} %get-tuple-element.35), channel_id=1, source_target_pairs={{0,15},{1,2},{2,1},{3,4},{4,3},{5,6},{6,5},{7,8},{8,7},{9,10},{10,... | collective-permute-start | bytes 1032200 | tf_op jit(solution)/shard_map/ppermute | solution.py:362
  6.0 10.5 %collective-permute-start.5 = (f32[2,7,6,8,128]{4,3,2,1,0:T(8,128)S(1)}, f32[2,7,6,8,128]{4,3,2,1,0:T(8,128)S(1)}, u32[]{:S(2)}, u32[]{:S(2)}) collective-permute-start(f32[2,7,6,8,128]{4,3,2,1,0:T(8,128)S(1)} %get-tuple-element.36), channel_id=1, source_target_pairs={{0,1},{1,0},{2,3},{3,2},{4,5},{5,4},{6,7},{7,6},{8,9},{9,8},{10,11... | collective-permute-start | bytes 1032200 | tf_op jit(solution)/shard_map/ppermute | solution.py:363
  9.8 13.1 %collective-permute-start = (f32[2,5,6,8,128]{4,3,2,1,0:T(8,128)S(1)}, f32[2,5,6,8,128]{4,3,2,1,0:T(8,128)S(1)}, u32[]{:S(2)}, u32[]{:S(2)}) collective-permute-start(f32[2,5,6,8,128]{4,3,2,1,0:T(8,128)S(1)} %get-tuple-element.27), channel_id=1, source_target_pairs={{0,15},{1,2},{2,1},{3,4},{4,3},{5,6},{6,5},{7,8},{8,7},{9,10},{10,... | collective-permute-start | bytes 737288 | tf_op jit(solution)/shard_map/ppermute | solution.py:394
  9.8 13.0 %collective-permute-start.1 = (f32[2,5,6,8,128]{4,3,2,1,0:T(8,128)S(1)}, f32[2,5,6,8,128]{4,3,2,1,0:T(8,128)S(1)}, u32[]{:S(2)}, u32[]{:S(2)}) collective-permute-start(f32[2,5,6,8,128]{4,3,2,1,0:T(8,128)S(1)} %get-tuple-element.28), channel_id=1, source_target_pairs={{0,1},{1,0},{2,3},{3,2},{4,5},{5,4},{6,7},{7,6},{8,9},{9,8},{10,11... | collective-permute-start | bytes 737288 | tf_op jit(solution)/shard_map/ppermute | solution.py:397
  18.3 12.5 %collective-permute-start.6 = (f32[2,7,6,8,128]{4,3,2,1,0:T(8,128)S(1)}, f32[2,7,6,8,128]{4,3,2,1,0:T(8,128)S(1)}, u32[]{:S(2)}, u32[]{:S(2)}) collective-permute-start(f32[2,7,6,8,128]{4,3,2,1,0:T(8,128)S(1)} %get-tuple-element.39), channel_id=1, source_target_pairs={{0,15},{1,2},{2,1},{3,4},{4,3},{5,6},{6,5},{7,8},{8,7},{9,10},{10,... | collective-permute-start | bytes 1032200 | tf_op jit(solution)/shard_map/ppermute | solution.py:362
  20.8 9.9 %collective-permute-start.7 = (f32[2,7,6,8,128]{4,3,2,1,0:T(8,128)S(1)}, f32[2,7,6,8,128]{4,3,2,1,0:T(8,128)S(1)}, u32[]{:S(2)}, u32[]{:S(2)}) collective-permute-start(f32[2,7,6,8,128]{4,3,2,1,0:T(8,128)S(1)} %get-tuple-element.40), channel_id=1, source_target_pairs={{0,1},{1,0},{2,3},{3,2},{4,5},{5,4},{6,7},{7,6},{8,9},{9,8},{10,11... | collective-permute-start | bytes 1032200 | tf_op jit(solution)/shard_map/ppermute | solution.py:363
  24.1 9.3 %collective-permute-start.2 = (f32[2,5,6,8,128]{4,3,2,1,0:T(8,128)S(1)}, f32[2,5,6,8,128]{4,3,2,1,0:T(8,128)S(1)}, u32[]{:S(2)}, u32[]{:S(2)}) collective-permute-start(f32[2,5,6,8,128]{4,3,2,1,0:T(8,128)S(1)} %get-tuple-element.31), channel_id=1, source_target_pairs={{0,15},{1,2},{2,1},{3,4},{4,3},{5,6},{6,5},{7,8},{8,7},{9,10},{10,... | collective-permute-start | bytes 737288 | tf_op jit(solution)/shard_map/ppermute | solution.py:362
  26.6 6.7 %collective-permute-start.3 = (f32[2,5,6,8,128]{4,3,2,1,0:T(8,128)S(1)}, f32[2,5,6,8,128]{4,3,2,1,0:T(8,128)S(1)}, u32[]{:S(2)}, u32[]{:S(2)}) collective-permute-start(f32[2,5,6,8,128]{4,3,2,1,0:T(8,128)S(1)} %get-tuple-element.32), channel_id=1, source_target_pairs={{0,1},{1,0},{2,3},{3,2},{4,5},{5,4},{6,7},{7,6},{8,9},{9,8},{10,11... | collective-permute-start | bytes 737288 | tf_op jit(solution)/shard_map/ppermute | solution.py:363

commit v11 on v10

--- a/solution.py
+++ b/solution.py
@@ -88,9 +88,16 @@
         run(far, near)
 
 
-def groups(ref):
+def each_group(ref, body):
     count = ref.shape[1]
-    return [range(i, min(i + 2, count)) for i in range(0, count, 2)]
+
+    def step(i, carry):
+        body([2 * i, 2 * i + 1])
+        return carry
+
+    lax.fori_loop(0, count // 2, step, 0)
+    if count % 2:
+        body([count - 1])
 
 
 def take(ref, row, pairs):
@@ -193,19 +200,27 @@
     return result
 
 
-def pack_rows(source, rows):
+def pack_rows(source, rows, arrive=lambda n: None):
     low = low_half()
-    for n in range(rows.shape[1]):
-        for k in range(6):
-            p, q = source(2 * n, k), source(2 * n + 1, k)
-            rows[0, n, k] = first_of(p, q, low)
-            rows[1, n, k] = second_of(p, q, low)
+
+    def body(pairs):
+        for n in pairs:
+            arrive(n)
+        for n in pairs:
+            for k in range(6):
+                p, q = source(2 * n, k), source(2 * n + 1, k)
+                rows[0, n, k] = first_of(p, q, low)
+                rows[1, n, k] = second_of(p, q, low)
+
+    each_group(rows, body)
 
 
 def start_chunk(coeff, rows, inner, edge, sums, far_out, near_out):
     def run(down, up):
-        for pairs in groups(rows):
-            open_round(coeff, pairs, rows, rows, inner, edge, sums, down, up)
+        each_group(
+            rows,
+            lambda pairs: open_round(coeff, pairs, rows, rows, inner, edge, sums, down, up),
+        )
 
     by_parity(run, near_out, far_out)
 
@@ -217,17 +232,20 @@
     link_copies = [
         pltpu.make_async_copy(links.at[mu], held.at[mu], sems.at[mu]) for mu in range(3)
     ]
-    first_copy = pltpu.make_async_copy(src.at[pl.ds(0, count)], now, sems.at[3])
+
+    def first_copy(n):
+        here = pl.ds(2 * n, 2)
+        return pltpu.make_async_copy(src.at[here], now.at[here], sems.at[4 + n])
+
     rest = src.at[pl.ds(count, later.shape[0])]
-    later_copy = pltpu.make_async_copy(rest, later, sems.at[4])
-    link_copies[1].start()
-    first_copy.start()
-    link_copies[2].start()
-    link_copies[0].start()
+    later_copy = pltpu.make_async_copy(rest, later, sems.at[3])
+    for mu in (1, 2, 0):
+        link_copies[mu].start()
+    for n in range(count // 2):
+        first_copy(n).start()
     later_copy.start()
     pack_links(held, inner, edge, lambda mu: link_copies[mu].wait())
-    first_copy.wait()
-    pack_rows(lambda n, k: tile(now, (n, k)), rows)
+    pack_rows(lambda n, k: tile(now, (n, k)), rows, lambda n: first_copy(n).wait())
     start_chunk(coeff, rows, inner, edge, sums, far_out, near_out)
     later_copy.wait()
 
@@ -267,7 +285,8 @@
     def run(lower_side, upper_side):
         below, down = lower_side
         above, up = upper_side
-        for pairs in groups(rows):
+
+        def body(pairs):
             result = close_round(
                 coeff, pairs, below, above, rows, sums_in, start, inner, edge, middle
             )
@@ -275,6 +294,8 @@
                 put(rows_out, row, pairs, result[row])
             open_round(next_coeff, pairs, rows_out, start, inner, edge, sums_out, down, up)
 
+        each_group(rows, body)
+
     by_parity(run, (near_in, near_out), (far_in, far_out))
 
 
@@ -288,7 +309,7 @@
         return pltpu.make_async_copy(filled.at[here], out.at[there], sems.at[n])
 
     def run(below, above):
-        for pairs in groups(rows):
+        def body(pairs):
             lower, upper = close_round(
                 coeff, pairs, below, above, rows, sums_in, start, inner, edge, middle
             )
@@ -300,6 +321,8 @@
                         filled[m, k, 0:8] = value[:, : 2 * LS]
                         filled[m, k, 8:16] = value[:, 2 * LS :]
                 store(n).start()
+
+        each_group(rows, body)
 
     by_parity(run, near_in, far_in)
     for n in range(rows.shape[1]):
@@ -335,7 +358,8 @@
 
 
 def chunk_sizes(pairs):
-    return tuple(pairs * part // 12 for part in (7, 5))
+    first = pairs * 7 // 12
+    return (first, pairs - first)
 
 
 def halo_body(links, sources):
@@ -375,7 +399,7 @@
         [
             pltpu.VMEM(raw[0], jnp.float32),
             pltpu.VMEM(link_view.shape, jnp.float32),
-            pltpu.SemaphoreType.DMA((5,)),
+            pltpu.SemaphoreType.DMA((4 + sizes[0],)),
         ],
         (0, 1),
     )

time: 35.2 us -> 35.2 us (level)
  transfers between devices with their start and end apart: 8 -> 8, of which waited for: 3 -> 4; matrix products, arithmetic and copies ran while one was open for 0% -> 0% of each run, Pallas kernels for 18% -> 18%
where the time goes in v11:
time: 35.2 us; the launch traced here: 35.1 us
  waiting for transfers between devices  12.2 us (35%)
  Pallas kernels  11.4 us (32%)
  starting transfers between devices  11.4 us (32%)
    pallas_call x6, Pallas kernels, call(): pl.pallas_call(kernel, out_shape=outs, in_specs=[hbm if i in in_hbm else...  11.4 us
    ppermute x3, waiting for transfers between devices, exchange(): far = lax.ppermute(far_out, 'space', far_pairs)  10.2 us
    ppermute x3, starting transfers between devices, exchange(): far = lax.ppermute(far_out, 'space', far_pairs)  7.76 us
    ppermute x3, starting transfers between devices, exchange(): return (far, lax.ppermute(near_out, 'space', near_pairs))  2.88 us
    ppermute x1, waiting for transfers between devices, halo_body(): fars.append(lax.ppermute(far_out, 'space', far_pairs))  1.95 us
    ppermute x1, starting transfers between devices, halo_body(): near = lax.ppermute(near_out, 'space', near_pairs)  0.74 us
  transfers between devices with their start and end apart: 8, of which 4 were waited for; matrix products, arithmetic and copies ran while one was open for 0% of the time, Pallas kernels for 18%

profile of v11, /device:TPU:1, one launch (start us, length us, event | category | flops | bytes accessed | tf_op | source)
XLA Modules:
  0.0 35.1 jit_solution(1903533957337443449)
XLA Ops:
  0.0 3.2 %shard_map.28 = (f32[2,4,3,3,2,8,128]{6,5,4,3,2,1,0:T(8,128)S(1)}, f32[3,3,2,8,128]{4,3,2,1,0:T(8,128)S(1)}, f32[2,7,6,8,128]{4,3,2,1,0:T(8,128)S(1)}, f32[2,7,6...) custom-call(f32[24,6,16,64]{3,2,1,0:T(8,128)} %bitcast.7, ...), custom_call_target="tpu_custom_call" | custom-call | flops 6193152 | bytes 3096576 | tf_op jit(solution)/shard_map/pallas_call | solution.py:346
  3.2 2.7 %collective-permute-start.4 = (f32[2,7,6,8,128]{4,3,2,1,0:T(8,128)S(1)}, f32[2,7,6,8,128]{4,3,2,1,0:T(8,128)S(1)}, u32[]{:S(2)}, u32[]{:S(2)}) collective-permute-start(f32[2,7,6,8,128]{4,3,2,1,0:T(8,128)S(1)} %get-tuple-element.35), channel_id=1, source_target_pairs={{0,15},{1,2},{2,1},{3,4},{4,3},{5,6},{6,5},{7,8},{8,7},{9,10},{10,... | collective-permute-start | bytes 1032200 | tf_op jit(solution)/shard_map/ppermute | solution.py:386
  5.9 2.9 %collective-permute-start.5 = (f32[2,7,6,8,128]{4,3,2,1,0:T(8,128)S(1)}, f32[2,7,6,8,128]{4,3,2,1,0:T(8,128)S(1)}, u32[]{:S(2)}, u32[]{:S(2)}) collective-permute-start(f32[2,7,6,8,128]{4,3,2,1,0:T(8,128)S(1)} %get-tuple-element.36), channel_id=1, source_target_pairs={{0,1},{1,0},{2,3},{3,2},{4,5},{5,4},{6,7},{7,6},{8,9},{9,8},{10,11... | collective-permute-start | bytes 1032200 | tf_op jit(solution)/shard_map/ppermute | solution.py:387
  8.7 1.1 %shard_map.29 = (f32[2,5,6,8,128]{4,3,2,1,0:T(8,128)S(1)}, f32[2,5,6,8,128]{4,3,2,1,0:T(8,128)S(1)}, f32[2,5,6,8,128]{4,3,2,1,0:T(8,128)S(1)}, f32[2,5,6,8,128]{4,3,2,1,0:T(8,128)S(1)}) custom-call(f32[10,6,16,64]{3,2,1,0:T(8,128)S(1)} %get-tuple-element.24.later, f32[2,4,3,3,2,8,128]{6,5,4,3,2,1,0:T(8,128)S(1)} %get-tuple-element.25.inner, ...), custom_call_target="tpu_custom_call" | custom-call | flops 4423680 | bytes 1892352 | tf_op jit(solution)/shard_map/pallas_call | solution.py:346
  9.9 0.1 collective-permute-start
  9.9 0.7 %collective-permute-start.1 = (f32[2,5,6,8,128]{4,3,2,1,0:T(8,128)S(1)}, f32[2,5,6,8,128]{4,3,2,1,0:T(8,128)S(1)}, u32[]{:S(2)}, u32[]{:S(2)}) collective-permute-start(f32[2,5,6,8,128]{4,3,2,1,0:T(8,128)S(1)} %get-tuple-element.28), channel_id=1, source_target_pairs={{0,1},{1,0},{2,3},{3,2},{4,5},{5,4},{6,7},{7,6},{8,9},{9,8},{10,11... | collective-permute-start | bytes 737288 | tf_op jit(solution)/shard_map/ppermute | solution.py:421
  10.7 5.7 %collective-permute-done.4.far_in = f32[2,7,6,8,128]{4,3,2,1,0:T(8,128)S(1)} collective-permute-done((f32[2,7,6,8,128]{4,3,2,1,0:T(8,128)S(1)}, f32[2,7,6,8,128]{4,3,2,1,0:T(8,128)S(1)}, u32[]{:S(2)}, u32[]{:S(2)}) %collective-permute-start.4) | collective-permute-done | bytes 344096 | tf_op jit(solution)/shard_map/ppermute | solution.py:386
  16.4 0.0 collective-permute-done.5.near_in
  16.4 1.8 %shard_map.31 = (f32[2,7,6,8,128]{4,3,2,1,0:T(8,128)S(1)}, f32[2,7,6,8,128]{4,3,2,1,0:T(8,128)S(1)}, f32[2,7,6,8,128]{4,3,2,1,0:T(8,128)S(1)}, f32[2,7,6,8,128]{4,3,2,1,0:T(8,128)S(1)}) custom-call(f32[2,7,6,8,128]{4,3,2,1,0:T(8,128)S(1)} %collective-permute-done.4.far_in, f32[2,7,6,8,128]{4,3,2,1,0:T(8,128)S(1)} %collective-permute-done.5.near_in, ...), custom_call_target="tpu_custom_call" | custom-call | flops 12386304 | bytes 3760128 | tf_op jit(solution)/shard_map/pallas_call | solution.py:346
  18.2 2.5 %collective-permute-start.6 = (f32[2,7,6,8,128]{4,3,2,1,0:T(8,128)S(1)}, f32[2,7,6,8,128]{4,3,2,1,0:T(8,128)S(1)}, u32[]{:S(2)}, u32[]{:S(2)}) collective-permute-start(f32[2,7,6,8,128]{4,3,2,1,0:T(8,128)S(1)} %get-tuple-element.39), channel_id=1, source_target_pairs={{0,15},{1,2},{2,1},{3,4},{4,3},{5,6},{6,5},{7,8},{8,7},{9,10},{10,... | collective-permute-start | bytes 1032200 | tf_op jit(solution)/shard_map/ppermute | solution.py:386
  20.7 0.0 collective-permute-start.7
  20.7 2.0 %collective-permute-done.far_in = f32[2,5,6,8,128]{4,3,2,1,0:T(8,128)S(1)} collective-permute-done((f32[2,5,6,8,128]{4,3,2,1,0:T(8,128)S(1)}, f32[2,5,6,8,128]{4,3,2,1,0:T(8,128)S(1)}, u32[]{:S(2)}, u32[]{:S(2)}) %collective-permute-start) | collective-permute-done | bytes 245792 | tf_op jit(solution)/shard_map/ppermute | solution.py:418
  22.7 0.0 collective-permute-done.1.near_in
  22.7 1.3 %shard_map.30 = (f32[2,5,6,8,128]{4,3,2,1,0:T(8,128)S(1)}, f32[2,5,6,8,128]{4,3,2,1,0:T(8,128)S(1)}, f32[2,5,6,8,128]{4,3,2,1,0:T(8,128)S(1)}, f32[2,5,6,8,128]{4,3,2,1,0:T(8,128)S(1)}) custom-call(f32[2,5,6,8,128]{4,3,2,1,0:T(8,128)S(1)} %collective-permute-done.far_in, f32[2,5,6,8,128]{4,3,2,1,0:T(8,128)S(1)} %collective-permute-done.1.near_in, ...), custom_call_target="tpu_custom_call" | custom-call | flops 8847360 | bytes 2875392 | tf_op jit(solution)/shard_map/pallas_call | solution.py:346
  24.0 2.6 %collective-permute-start.2 = (f32[2,5,6,8,128]{4,3,2,1,0:T(8,128)S(1)}, f32[2,5,6,8,128]{4,3,2,1,0:T(8,128)S(1)}, u32[]{:S(2)}, u32[]{:S(2)}) collective-permute-start(f32[2,5,6,8,128]{4,3,2,1,0:T(8,128)S(1)} %get-tuple-element.31), channel_id=1, source_target_pairs={{0,15},{1,2},{2,1},{3,4},{4,3},{5,6},{6,5},{7,8},{8,7},{9,10},{10,... | collective-permute-start | bytes 737288 | tf_op jit(solution)/shard_map/ppermute | solution.py:386
  26.6 0.0 collective-permute-start.3
  26.6 4.1 %collective-permute-done.6.far_in = f32[2,7,6,8,128]{4,3,2,1,0:T(8,128)S(1)} collective-permute-done((f32[2,7,6,8,128]{4,3,2,1,0:T(8,128)S(1)}, f32[2,7,6,8,128]{4,3,2,1,0:T(8,128)S(1)}, u32[]{:S(2)}, u32[]{:S(2)}) %collective-permute-start.6) | collective-permute-done | bytes 344096 | tf_op jit(solution)/shard_map/ppermute | solution.py:386
  30.7 0.0 collective-permute-done.7.near_in
  30.7 2.2 %shard_map.32.rest_0_ = f32[24,6,16,64]{3,2,1,0:T(8,128)} custom-call(f32[2,7,6,8,128]{4,3,2,1,0:T(8,128)S(1)} %collective-permute-done.6.far_in, f32[2,7,6,8,128]{4,3,2,1,0:T(8,128)S(1)} %collective-permute-done.7.near_in, f32[2,7,6,8,128]{4,3,2,1,0:T(8,128)S(1)} %get-tuple-element.41.rows, f32[2,7,6,8,128]{4,3,2,1,0:T(8,128)S(1)} %get-tuple-element.42.sums_in, ...), custom_call_target="tpu_custom_call" | custom-call | flops 6193152 | bytes 2973696 | tf_op jit(solution)/shard_map/pallas_call | solution.py:346
  32.9 0.4 %collective-permute-done.2.far_in = f32[2,5,6,8,128]{4,3,2,1,0:T(8,128)S(1)} collective-permute-done((f32[2,5,6,8,128]{4,3,2,1,0:T(8,128)S(1)}, f32[2,5,6,8,128]{4,3,2,1,0:T(8,128)S(1)}, u32[]{:S(2)}, u32[]{:S(2)}) %collective-permute-start.2) | collective-permute-done | bytes 245792 | tf_op jit(solution)/shard_map/ppermute | solution.py:386
  33.3 0.0 collective-permute-done.3.near_in
  33.3 1.8 %shard_map.33 = f32[24,6,16,64]{3,2,1,0:T(8,128)} custom-call(f32[2,5,6,8,128]{4,3,2,1,0:T(8,128)S(1)} %collective-permute-done.2.far_in, f32[2,5,6,8,128]{4,3,2,1,0:T(8,128)S(1)} %collective-permute-done.3.near_in, f32[2,5,6,8,128]{4,3,2,1,0:T(8,128)S(1)} %get-tuple-element.33.rows, ...), custom_call_target="tpu_custom_call", output_to_operand_aliasing={{}: (7, {})} | custom-call | flops 4423680 | bytes 3072000 | tf_op jit(solution)/shard_map/pallas_call | solution.py:346
Async XLA Ops:
  3.2 13.2 %collective-permute-start.4 = (f32[2,7,6,8,128]{4,3,2,1,0:T(8,128)S(1)}, f32[2,7,6,8,128]{4,3,2,1,0:T(8,128)S(1)}, u32[]{:S(2)}, u32[]{:S(2)}) collective-permute-start(f32[2,7,6,8,128]{4,3,2,1,0:T(8,128)S(1)} %get-tuple-element.35), channel_id=1, source_target_pairs={{0,15},{1,2},{2,1},{3,4},{4,3},{5,6},{6,5},{7,8},{8,7},{9,10},{10,... | collective-permute-start | bytes 1032200 | tf_op jit(solution)/shard_map/ppermute | solution.py:386
  5.9 10.5 %collective-permute-start.5 = (f32[2,7,6,8,128]{4,3,2,1,0:T(8,128)S(1)}, f32[2,7,6,8,128]{4,3,2,1,0:T(8,128)S(1)}, u32[]{:S(2)}, u32[]{:S(2)}) collective-permute-start(f32[2,7,6,8,128]{4,3,2,1,0:T(8,128)S(1)} %get-tuple-element.36), channel_id=1, source_target_pairs={{0,1},{1,0},{2,3},{3,2},{4,5},{5,4},{6,7},{7,6},{8,9},{9,8},{10,11... | collective-permute-start | bytes 1032200 | tf_op jit(solution)/shard_map/ppermute | solution.py:387
  9.9 12.8 %collective-permute-start = (f32[2,5,6,8,128]{4,3,2,1,0:T(8,128)S(1)}, f32[2,5,6,8,128]{4,3,2,1,0:T(8,128)S(1)}, u32[]{:S(2)}, u32[]{:S(2)}) collective-permute-start(f32[2,5,6,8,128]{4,3,2,1,0:T(8,128)S(1)} %get-tuple-element.27), channel_id=1, source_target_pairs={{0,15},{1,2},{2,1},{3,4},{4,3},{5,6},{6,5},{7,8},{8,7},{9,10},{10,... | collective-permute-start | bytes 737288 | tf_op jit(solution)/shard_map/ppermute | solution.py:418
  9.9 12.8 %collective-permute-start.1 = (f32[2,5,6,8,128]{4,3,2,1,0:T(8,128)S(1)}, f32[2,5,6,8,128]{4,3,2,1,0:T(8,128)S(1)}, u32[]{:S(2)}, u32[]{:S(2)}) collective-permute-start(f32[2,5,6,8,128]{4,3,2,1,0:T(8,128)S(1)} %get-tuple-element.28), channel_id=1, source_target_pairs={{0,1},{1,0},{2,3},{3,2},{4,5},{5,4},{6,7},{7,6},{8,9},{9,8},{10,11... | collective-permute-start | bytes 737288 | tf_op jit(solution)/shard_map/ppermute | solution.py:421
  18.2 12.5 %collective-permute-start.6 = (f32[2,7,6,8,128]{4,3,2,1,0:T(8,128)S(1)}, f32[2,7,6,8,128]{4,3,2,1,0:T(8,128)S(1)}, u32[]{:S(2)}, u32[]{:S(2)}) collective-permute-start(f32[2,7,6,8,128]{4,3,2,1,0:T(8,128)S(1)} %get-tuple-element.39), channel_id=1, source_target_pairs={{0,15},{1,2},{2,1},{3,4},{4,3},{5,6},{6,5},{7,8},{8,7},{9,10},{10,... | collective-permute-start | bytes 1032200 | tf_op jit(solution)/shard_map/ppermute | solution.py:386
  20.7 9.9 %collective-permute-start.7 = (f32[2,7,6,8,128]{4,3,2,1,0:T(8,128)S(1)}, f32[2,7,6,8,128]{4,3,2,1,0:T(8,128)S(1)}, u32[]{:S(2)}, u32[]{:S(2)}) collective-permute-start(f32[2,7,6,8,128]{4,3,2,1,0:T(8,128)S(1)} %get-tuple-element.40), channel_id=1, source_target_pairs={{0,1},{1,0},{2,3},{3,2},{4,5},{5,4},{6,7},{7,6},{8,9},{9,8},{10,11... | collective-permute-start | bytes 1032200 | tf_op jit(solution)/shard_map/ppermute | solution.py:387
  24.0 9.3 %collective-permute-start.2 = (f32[2,5,6,8,128]{4,3,2,1,0:T(8,128)S(1)}, f32[2,5,6,8,128]{4,3,2,1,0:T(8,128)S(1)}, u32[]{:S(2)}, u32[]{:S(2)}) collective-permute-start(f32[2,5,6,8,128]{4,3,2,1,0:T(8,128)S(1)} %get-tuple-element.31), channel_id=1, source_target_pairs={{0,15},{1,2},{2,1},{3,4},{4,3},{5,6},{6,5},{7,8},{8,7},{9,10},{10,... | collective-permute-start | bytes 737288 | tf_op jit(solution)/shard_map/ppermute | solution.py:386
  26.6 6.7 %collective-permute-start.3 = (f32[2,5,6,8,128]{4,3,2,1,0:T(8,128)S(1)}, f32[2,5,6,8,128]{4,3,2,1,0:T(8,128)S(1)}, u32[]{:S(2)}, u32[]{:S(2)}) collective-permute-start(f32[2,5,6,8,128]{4,3,2,1,0:T(8,128)S(1)} %get-tuple-element.32), channel_id=1, source_target_pairs={{0,1},{1,0},{2,3},{3,2},{4,5},{5,4},{6,7},{7,6},{8,9},{9,8},{10,11... | collective-permute-start | bytes 737288 | tf_op jit(solution)/shard_map/ppermute | solution.py:387

commit v12 on v11

--- a/solution.py
+++ b/solution.py
@@ -76,6 +76,10 @@
     return jnp.concatenate([ref[index + (slice(0, 8),)], ref[index + (slice(8, 16),)]], axis=1)
 
 
+def parts(*refs):
+    return [(refs[0], 0), (refs[0], 1)] if len(refs) == 1 else [(ref, 0) for ref in refs]
+
+
 def by_parity(run, near, far):
     odd = lax.axis_index("space") % 2 == 1
 
@@ -95,7 +99,7 @@
         body([2 * i, 2 * i + 1])
         return carry
 
-    lax.fori_loop(0, count // 2, step, 0)
+    lax.fori_loop(0, count // 2, step, 0, unroll=count <= 5)
     if count % 2:
         body([count - 1])
 
@@ -159,29 +163,35 @@
     return [[coeff * c for c in vec] for vec in take(start, row, pairs)]
 
 
+def send(edge, pairs, part, row, vectors, out):
+    if row == 1:
+        field, vectors = vectors, zeros(len(pairs))
+        mat_vec(link_at(edge), field, vectors, dagger=True)
+    put(*out[part], pairs, vectors)
+
+
+def local_sums(coeff, pairs, row, rows, start, inner):
+    sums = scaled_rows(coeff, start, row, pairs)
+    add_inner(inner, row, pairs, rows, sums)
+    return sums
+
+
 def open_round(coeff, pairs, rows, start, inner, edge, sums_out, down, up):
-    for row in range(2):
-        sums = scaled_rows(coeff, start, row, pairs)
-        add_inner(inner, row, pairs, rows, sums)
+    for row, out in enumerate((down, up)):
+        sums = local_sums(coeff, pairs, row, rows, start, inner)
         put(sums_out, row, pairs, sums)
-        if row == 0:
-            put(down, 0, pairs, take(rows, 0, pairs))
-            put(down, 1, pairs, sums)
-        else:
-            for i, vectors in enumerate((take(rows, 1, pairs), sums)):
-                back = zeros(len(pairs))
-                mat_vec(link_at(edge), vectors, back, dagger=True)
-                put(up, i, pairs, back)
+        send(edge, pairs, 0, row, take(rows, row, pairs), out)
+        send(edge, pairs, 1, row, sums, out)
 
 
 def close_round(coeff, pairs, below, above, rows, sums_in, start, inner, edge, middle):
     lower = [
         [s + u for s, u in zip(*both)]
-        for both in zip(take(sums_in, 0, pairs), take(below, 0, pairs))
+        for both in zip(take(sums_in, 0, pairs), take(*below[0], pairs))
     ]
     put(middle, 0, pairs, lower)
     upper = take(sums_in, 1, pairs)
-    mat_vec(link_at(edge), take(above, 0, pairs), upper)
+    mat_vec(link_at(edge), take(*above[0], pairs), upper)
     put(middle, 1, pairs, upper)
     result = []
     for row in range(2):
@@ -192,10 +202,10 @@
         add_inner(inner, row, pairs, middle, sums)
         if row == 0:
             sums = [
-                [s + u for s, u in zip(*both)] for both in zip(sums, take(below, 1, pairs))
+                [s + u for s, u in zip(*both)] for both in zip(sums, take(*below[1], pairs))
             ]
         else:
-            mat_vec(link_at(edge), take(above, 1, pairs), sums)
+            mat_vec(link_at(edge), take(*above[1], pairs), sums)
         result.append(sums)
     return result
 
@@ -222,12 +232,10 @@
             lambda pairs: open_round(coeff, pairs, rows, rows, inner, edge, sums, down, up),
         )
 
-    by_parity(run, near_out, far_out)
-
-
-def first_kernel(
-    coeff, src, links, inner, edge, rows, sums, far_out, near_out, later, now, held, sems
-):
+    by_parity(run, parts(near_out), parts(far_out))
+
+
+def first_kernel(coeff, src, links, inner, edge, rows, far_sums, far_out, later, now, held, sems):
     count = now.shape[0]
     link_copies = [
         pltpu.make_async_copy(links.at[mu], held.at[mu], sems.at[mu]) for mu in range(3)
@@ -246,41 +254,45 @@
     later_copy.start()
     pack_links(held, inner, edge, lambda mu: link_copies[mu].wait())
     pack_rows(lambda n, k: tile(now, (n, k)), rows, lambda n: first_copy(n).wait())
+
+    def run(down, up):
+        row, out = (0, down) if up is None else (1, up)
+
+        def body(pairs):
+            sums = local_sums(coeff, pairs, row, rows, rows, inner)
+            put(far_sums, 0, pairs, sums)
+            send(edge, pairs, 0, row, take(rows, row, pairs), out)
+            send(edge, pairs, 1, row, sums, out)
+
+        each_group(rows, body)
+
+    by_parity(run, None, parts(far_out))
+    later_copy.wait()
+
+
+def start_kernel(coeff, later, inner, edge, first_rows, far_sums, *refs):
+    first_sums, *first_near, rows, sums, far_out, near_out = refs
+
+    def run(down, up):
+        row, out = (0, down) if up is None else (1, up)
+
+        def body(pairs):
+            ends = local_sums(coeff, pairs, row, first_rows, first_rows, inner)
+            put(first_sums, row, pairs, ends)
+            put(first_sums, 1 - row, pairs, take(far_sums, 0, pairs))
+            send(edge, pairs, 0, row, take(first_rows, row, pairs), out)
+            send(edge, pairs, 1, row, ends, out)
+
+        each_group(first_rows, body)
+
+    by_parity(run, parts(*first_near), None)
+    pack_rows(lambda n, k: tile(later, (n, k)), rows)
     start_chunk(coeff, rows, inner, edge, sums, far_out, near_out)
-    later_copy.wait()
-
-
-def start_kernel(coeff, first, later, inner, edge, *refs):
-    before, (rows, sums, far_out, near_out) = refs[:-4], refs[-4:]
-    pack_rows(lambda n, k: tile(later, (first + n, k)), rows)
-    held = 0
-    for ref in before:
-        held = ref.shape[1]
-        for row in range(2):
-            for n in range(held):
-                put(near_out, row, [n], take(ref, row, [n]))
-    own = near_out.at[:, pl.ds(held, rows.shape[1])]
-    start_chunk(coeff, rows, inner, edge, sums, far_out, own)
-
-
-def round_kernel(
-    coeff,
-    next_coeff,
-    place,
-    far_in,
-    near_in,
-    rows,
-    sums_in,
-    start,
-    inner,
-    edge,
-    rows_out,
-    sums_out,
-    far_out,
-    near_out,
-    middle,
-):
-    near_in = near_in.at[:, pl.ds(place, rows.shape[1])]
+
+
+def round_kernel(coeff, next_coeff, far_in, *refs):
+    *near_in, rows, sums_in, start, inner, edge = refs[:-5]
+    rows_out, sums_out, far_out, near_out, middle = refs[-5:]
 
     def run(lower_side, upper_side):
         below, down = lower_side
@@ -296,7 +308,8 @@
 
         each_group(rows, body)
 
-    by_parity(run, (near_in, near_out), (far_in, far_out))
+    near_side = parts(*near_in), parts(near_out)
+    by_parity(run, near_side, (parts(far_in), parts(far_out)))
 
 
 def last_kernel(coeff, first, lead, far_in, near_in, rows, sums_in, start, inner, edge, *rest):
@@ -324,7 +337,7 @@
 
         each_group(rows, body)
 
-    by_parity(run, near_in, far_in)
+    by_parity(run, parts(near_in), parts(far_in))
     for n in range(rows.shape[1]):
         store(n).wait()
 
@@ -382,16 +395,20 @@
     near_pairs = [(d, d ^ 1) for d in range(count)]
     far_pairs = [(d, (d + 1 if d % 2 else d - 1) % count) for d in range(count)]
 
-    def exchange(far_out, near_out):
-        far = lax.ppermute(far_out, "space", far_pairs)
-        return far, lax.ppermute(near_out, "space", near_pairs)
-
-    inner, edge, rows, sums, *sends, later = call(
+    def to_far(value):
+        return lax.ppermute(value, "space", far_pairs)
+
+    def to_near(value):
+        return lax.ppermute(value, "space", near_pairs)
+
+    inner, edge, rows, far_sums, far_out, later = call(
         functools.partial(first_kernel, steps[0]),
         [
             f32((2, 4, 3, 3, 2, 8, 128)),
             f32((3, 3, 2, 8, 128)),
-            *[both[0]] * 4,
+            both[0],
+            f32((1, *both[0].shape[1:])),
+            both[0],
             f32((vectors - first[1], 6, planes, sites)),
         ],
         [source_view, link_view],
@@ -403,33 +420,27 @@
         ],
         (0, 1),
     )
-    start, fields, halos = [rows], [(rows, sums)], [exchange(*sends)]
-    fars, before, places = [], [], [0, 0]
-    for chunk in chunks[1:]:
-        near_shape = f32((2, places[-1] + sizes[chunk], *both[chunk].shape[2:]))
-        rows, sums, far_out, near_out = call(
-            functools.partial(start_kernel, steps[0], first[chunk] - first[1]),
-            [both[chunk]] * 3 + [near_shape],
-            [later, inner, edge, *before],
-            6 * work[chunk],
-        )
-        start.append(rows)
-        fields.append((rows, sums))
-        fars.append(lax.ppermute(far_out, "space", far_pairs))
-        before = [near_out]
-        places.append(places[-1] + sizes[chunk])
-    near = lax.ppermute(near_out, "space", near_pairs)
-    halos += [(far, near) for far in fars]
+    far = to_far(far_out)
+    half = f32((1, *both[0].shape[1:]))
+    first_sums, *first_near, second_rows, second_sums, far_out, near_out = call(
+        functools.partial(start_kernel, steps[0]),
+        [both[0], half, half] + [both[1]] * 4,
+        [later, inner, edge, rows, far_sums],
+        6 * work[1],
+    )
+    start = [rows, second_rows]
+    fields = [(rows, first_sums), (second_rows, second_sums)]
+    halos = [(far, *map(to_near, first_near)), (to_far(far_out), to_near(near_out))]
     for chunk in chunks:
         rows, sums, *sends = call(
-            functools.partial(round_kernel, steps[1], steps[2], places[chunk]),
+            functools.partial(round_kernel, steps[1], steps[2]),
             [both[chunk]] * 4,
             [*halos[chunk], *fields[chunk], start[chunk], inner, edge],
             12 * work[chunk],
             [middle[chunk]],
         )
         fields[chunk] = (rows, sums)
-        halos[chunk] = exchange(*sends)
+        halos[chunk] = (to_far(sends[0]), to_near(sends[1]))
     out = None
     for chunk in chunks:
         args = [*halos[chunk], *fields[chunk], start[chunk], inner, edge]

time: 35.2 us -> 34.7 us (0.986)
    ppermute x8 -> x9, waiting for transfers between devices: 12.2 us -> 11.9 us  [the longest x4 11.3 us: to_far(): return lax.ppermute(value, 'space', far_pairs)]
    ppermute x8 -> x9, starting transfers between devices: 11.4 us -> 11.5 us  [the longest x4 7.69 us: to_far(): return lax.ppermute(value, 'space', far_pairs)]
  transfers between devices with their start and end apart: 8 -> 9, of which waited for: 4 -> 6; matrix products, arithmetic and copies ran while one was open for 0% -> 0% of each run, Pallas kernels for 18% -> 19%
where the time goes in v12:
time: 34.7 us; the launch traced here: 34.6 us
  waiting for transfers between devices  11.9 us (34%)
  starting transfers between devices  11.5 us (33%)
  Pallas kernels  11.1 us (32%)
    ppermute x4, waiting for transfers between devices, to_far(): return lax.ppermute(value, 'space', far_pairs)  11.3 us
    pallas_call x6, Pallas kernels, call(): pl.pallas_call(kernel, out_shape=outs, in_specs=[hbm if i in in_hbm else...  11.1 us
    ppermute x4, starting transfers between devices, to_far(): return lax.ppermute(value, 'space', far_pairs)  7.69 us
    ppermute x5, starting transfers between devices, to_near(): return lax.ppermute(value, 'space', near_pairs)  3.79 us
  transfers between devices with their start and end apart: 9, of which 6 were waited for; matrix products, arithmetic and copies ran while one was open for 0% of the time, Pallas kernels for 19%

profile of v12, /device:TPU:1, one launch (start us, length us, event | category | flops | bytes accessed | tf_op | source)
XLA Modules:
  0.0 34.6 jit_solution(14257425453103296487)
XLA Ops:
  0.0 2.9 %shard_map.28 = (f32[2,4,3,3,2,8,128]{6,5,4,3,2,1,0:T(8,128)S(1)}, f32[3,3,2,8,128]{4,3,2,1,0:T(8,128)S(1)}, f32[2,7,6,8,128]{4,3,2,1,0:T(8,128)S(1)}, f32[1,7,6...) custom-call(f32[24,6,16,64]{3,2,1,0:T(8,128)} %bitcast.7, ...), custom_call_target="tpu_custom_call" | custom-call | flops 6193152 | bytes 2580480 | tf_op jit(solution)/shard_map/pallas_call | solution.py:359
  2.9 2.6 %collective-permute-start.4 = (f32[2,7,6,8,128]{4,3,2,1,0:T(8,128)S(1)}, f32[2,7,6,8,128]{4,3,2,1,0:T(8,128)S(1)}, u32[]{:S(2)}, u32[]{:S(2)}) collective-permute-start(f32[2,7,6,8,128]{4,3,2,1,0:T(8,128)S(1)} %get-tuple-element.39), channel_id=1, source_target_pairs={{0,15},{1,2},{2,1},{3,4},{4,3},{5,6},{6,5},{7,8},{8,7},{9,10},{10,... | collective-permute-start | bytes 1032200 | tf_op jit(solution)/shard_map/ppermute | solution.py:399
  5.5 1.4 %shard_map.29 = (f32[2,7,6,8,128]{4,3,2,1,0:T(8,128)S(1)}, f32[1,7,6,8,128]{4,3,2,1,0:T(8,128)S(1)}, f32[1,7,6,8,128]{4,3,2,1,0:T(8,128)S(1)}, f32[2,5,6,8,128]{...) custom-call(f32[10,6,16,64]{3,2,1,0:T(8,128)S(1)} %get-tuple-element, ...), custom_call_target="tpu_custom_call" | custom-call | flops 4423680 | bytes 3096576 | tf_op jit(solution)/shard_map/pallas_call | solution.py:359
  6.9 3.1 %collective-permute-start.5 = (f32[1,7,6,8,128]{4,3,2,1,0:T(8,128)S(1)}, f32[1,7,6,8,128]{4,3,2,1,0:T(8,128)S(1)}, u32[]{:S(2)}, u32[]{:S(2)}) collective-permute-start(f32[1,7,6,8,128]{4,3,2,1,0:T(8,128)S(1)} %get-tuple-element.40), channel_id=1, source_target_pairs={{0,1},{1,0},{2,3},{3,2},{4,5},{5,4},{6,7},{7,6},{8,9},{9,8},{10,11... | collective-permute-start | bytes 516104 | tf_op jit(solution)/shard_map/ppermute | solution.py:402
  10.0 0.1 collective-permute-start.6
  10.1 0.0 collective-permute-start
  10.1 0.6 %collective-permute-start.1 = (f32[2,5,6,8,128]{4,3,2,1,0:T(8,128)S(1)}, f32[2,5,6,8,128]{4,3,2,1,0:T(8,128)S(1)}, u32[]{:S(2)}, u32[]{:S(2)}) collective-permute-start(f32[2,5,6,8,128]{4,3,2,1,0:T(8,128)S(1)} %get-tuple-element.32), channel_id=1, source_target_pairs={{0,1},{1,0},{2,3},{3,2},{4,5},{5,4},{6,7},{7,6},{8,9},{9,8},{10,11... | collective-permute-start | bytes 737288 | tf_op jit(solution)/shard_map/ppermute | solution.py:402
  10.7 0.3 collective-permute-done.5.refs_0_
  11.0 0.4 %collective-permute-done.6.refs_1_ = f32[1,7,6,8,128]{4,3,2,1,0:T(8,128)S(1)} collective-permute-done((f32[1,7,6,8,128]{4,3,2,1,0:T(8,128)S(1)}, f32[1,7,6,8,128]{4,3,2,1,0:T(8,128)S(1)}, u32[]{:S(2)}, u32[]{:S(2)}) %collective-permute-start.6) | collective-permute-done | bytes 172064 | tf_op jit(solution)/shard_map/ppermute | solution.py:402
  11.4 4.6 %collective-permute-done.4.far_in = f32[2,7,6,8,128]{4,3,2,1,0:T(8,128)S(1)} collective-permute-done((f32[2,7,6,8,128]{4,3,2,1,0:T(8,128)S(1)}, f32[2,7,6,8,128]{4,3,2,1,0:T(8,128)S(1)}, u32[]{:S(2)}, u32[]{:S(2)}) %collective-permute-start.4) | collective-permute-done | bytes 344096 | tf_op jit(solution)/shard_map/ppermute | solution.py:399
  16.0 1.8 %shard_map.31 = (f32[2,7,6,8,128]{4,3,2,1,0:T(8,128)S(1)}, f32[2,7,6,8,128]{4,3,2,1,0:T(8,128)S(1)}, f32[2,7,6,8,128]{4,3,2,1,0:T(8,128)S(1)}, f32[2,7,6,8,128]{4,3,2,1,0:T(8,128)S(1)}) custom-call(f32[2,7,6,8,128]{4,3,2,1,0:T(8,128)S(1)} %collective-permute-done.4.far_in, f32[1,7,6,8,128]{4,3,2,1,0:T(8,128)S(1)} %collective-permute-done.5.refs_0_, ...), custom_call_target="tpu_custom_call" | custom-call | flops 12386304 | bytes 3760128 | tf_op jit(solution)/shard_map/pallas_call | solution.py:359
  17.8 2.5 %collective-permute-start.7 = (f32[2,7,6,8,128]{4,3,2,1,0:T(8,128)S(1)}, f32[2,7,6,8,128]{4,3,2,1,0:T(8,128)S(1)}, u32[]{:S(2)}, u32[]{:S(2)}) collective-permute-start(f32[2,7,6,8,128]{4,3,2,1,0:T(8,128)S(1)} %get-tuple-element.43), channel_id=1, source_target_pairs={{0,15},{1,2},{2,1},{3,4},{4,3},{5,6},{6,5},{7,8},{8,7},{9,10},{10,... | collective-permute-start | bytes 1032200 | tf_op jit(solution)/shard_map/ppermute | solution.py:399
  20.4 0.0 collective-permute-start.8
  20.4 2.0 %collective-permute-done.far_in = f32[2,5,6,8,128]{4,3,2,1,0:T(8,128)S(1)} collective-permute-done((f32[2,5,6,8,128]{4,3,2,1,0:T(8,128)S(1)}, f32[2,5,6,8,128]{4,3,2,1,0:T(8,128)S(1)}, u32[]{:S(2)}, u32[]{:S(2)}) %collective-permute-start) | collective-permute-done | bytes 245792 | tf_op jit(solution)/shard_map/ppermute | solution.py:399
  22.3 0.0 collective-permute-done.1.refs_0_
  22.3 1.2 %shard_map.30 = (f32[2,5,6,8,128]{4,3,2,1,0:T(8,128)S(1)}, f32[2,5,6,8,128]{4,3,2,1,0:T(8,128)S(1)}, f32[2,5,6,8,128]{4,3,2,1,0:T(8,128)S(1)}, f32[2,5,6,8,128]{4,3,2,1,0:T(8,128)S(1)}) custom-call(f32[2,5,6,8,128]{4,3,2,1,0:T(8,128)S(1)} %collective-permute-done.far_in, f32[2,5,6,8,128]{4,3,2,1,0:T(8,128)S(1)} %collective-permute-done.1.refs_0_, ...), custom_call_target="tpu_custom_call" | custom-call | flops 8847360 | bytes 2875392 | tf_op jit(solution)/shard_map/pallas_call | solution.py:359
  23.6 2.5 %collective-permute-start.2 = (f32[2,5,6,8,128]{4,3,2,1,0:T(8,128)S(1)}, f32[2,5,6,8,128]{4,3,2,1,0:T(8,128)S(1)}, u32[]{:S(2)}, u32[]{:S(2)}) collective-permute-start(f32[2,5,6,8,128]{4,3,2,1,0:T(8,128)S(1)} %get-tuple-element.35), channel_id=1, source_target_pairs={{0,15},{1,2},{2,1},{3,4},{4,3},{5,6},{6,5},{7,8},{8,7},{9,10},{10,... | collective-permute-start | bytes 737288 | tf_op jit(solution)/shard_map/ppermute | solution.py:399
  26.1 0.0 collective-permute-start.3
  26.1 4.2 %collective-permute-done.7.far_in = f32[2,7,6,8,128]{4,3,2,1,0:T(8,128)S(1)} collective-permute-done((f32[2,7,6,8,128]{4,3,2,1,0:T(8,128)S(1)}, f32[2,7,6,8,128]{4,3,2,1,0:T(8,128)S(1)}, u32[]{:S(2)}, u32[]{:S(2)}) %collective-permute-start.7) | collective-permute-done | bytes 344096 | tf_op jit(solution)/shard_map/ppermute | solution.py:399
  30.4 0.0 collective-permute-done.8.near_in
  30.4 2.2 %shard_map.32.rest_0_ = f32[24,6,16,64]{3,2,1,0:T(8,128)} custom-call(f32[2,7,6,8,128]{4,3,2,1,0:T(8,128)S(1)} %collective-permute-done.7.far_in, f32[2,7,6,8,128]{4,3,2,1,0:T(8,128)S(1)} %collective-permute-done.8.near_in, f32[2,7,6,8,128]{4,3,2,1,0:T(8,128)S(1)} %get-tuple-element.45.rows, f32[2,7,6,8,128]{4,3,2,1,0:T(8,128)S(1)} %get-tuple-element.46.sums_in, ...), custom_call_target="tpu_custom_call" | custom-call | flops 6193152 | bytes 2973696 | tf_op jit(solution)/shard_map/pallas_call | solution.py:359
  32.6 0.4 %collective-permute-done.2.far_in = f32[2,5,6,8,128]{4,3,2,1,0:T(8,128)S(1)} collective-permute-done((f32[2,5,6,8,128]{4,3,2,1,0:T(8,128)S(1)}, f32[2,5,6,8,128]{4,3,2,1,0:T(8,128)S(1)}, u32[]{:S(2)}, u32[]{:S(2)}) %collective-permute-start.2) | collective-permute-done | bytes 245792 | tf_op jit(solution)/shard_map/ppermute | solution.py:399
  33.0 0.0 collective-permute-done.3.near_in
  33.0 1.6 %shard_map.33 = f32[24,6,16,64]{3,2,1,0:T(8,128)} custom-call(f32[2,5,6,8,128]{4,3,2,1,0:T(8,128)S(1)} %collective-permute-done.2.far_in, f32[2,5,6,8,128]{4,3,2,1,0:T(8,128)S(1)} %collective-permute-done.3.near_in, f32[2,5,6,8,128]{4,3,2,1,0:T(8,128)S(1)} %get-tuple-element.37.rows, ...), custom_call_target="tpu_custom_call", output_to_operand_aliasing={{}: (7, {})} | custom-call | flops 4423680 | bytes 3072000 | tf_op jit(solution)/shard_map/pallas_call | solution.py:359
Async XLA Ops:
  2.9 13.1 %collective-permute-start.4 = (f32[2,7,6,8,128]{4,3,2,1,0:T(8,128)S(1)}, f32[2,7,6,8,128]{4,3,2,1,0:T(8,128)S(1)}, u32[]{:S(2)}, u32[]{:S(2)}) collective-permute-start(f32[2,7,6,8,128]{4,3,2,1,0:T(8,128)S(1)} %get-tuple-element.39), channel_id=1, source_target_pairs={{0,15},{1,2},{2,1},{3,4},{4,3},{5,6},{6,5},{7,8},{8,7},{9,10},{10,... | collective-permute-start | bytes 1032200 | tf_op jit(solution)/shard_map/ppermute | solution.py:399
  6.9 4.1 %collective-permute-start.5 = (f32[1,7,6,8,128]{4,3,2,1,0:T(8,128)S(1)}, f32[1,7,6,8,128]{4,3,2,1,0:T(8,128)S(1)}, u32[]{:S(2)}, u32[]{:S(2)}) collective-permute-start(f32[1,7,6,8,128]{4,3,2,1,0:T(8,128)S(1)} %get-tuple-element.40), channel_id=1, source_target_pairs={{0,1},{1,0},{2,3},{3,2},{4,5},{5,4},{6,7},{7,6},{8,9},{9,8},{10,11... | collective-permute-start | bytes 516104 | tf_op jit(solution)/shard_map/ppermute | solution.py:402
  10.0 1.4 %collective-permute-start.6 = (f32[1,7,6,8,128]{4,3,2,1,0:T(8,128)S(1)}, f32[1,7,6,8,128]{4,3,2,1,0:T(8,128)S(1)}, u32[]{:S(2)}, u32[]{:S(2)}) collective-permute-start(f32[1,7,6,8,128]{4,3,2,1,0:T(8,128)S(1)} %get-tuple-element.41), channel_id=1, source_target_pairs={{0,1},{1,0},{2,3},{3,2},{4,5},{5,4},{6,7},{7,6},{8,9},{9,8},{10,11... | collective-permute-start | bytes 516104 | tf_op jit(solution)/shard_map/ppermute | solution.py:402
  10.1 12.3 %collective-permute-start = (f32[2,5,6,8,128]{4,3,2,1,0:T(8,128)S(1)}, f32[2,5,6,8,128]{4,3,2,1,0:T(8,128)S(1)}, u32[]{:S(2)}, u32[]{:S(2)}) collective-permute-start(f32[2,5,6,8,128]{4,3,2,1,0:T(8,128)S(1)} %get-tuple-element.31), channel_id=1, source_target_pairs={{0,15},{1,2},{2,1},{3,4},{4,3},{5,6},{6,5},{7,8},{8,7},{9,10},{10,... | collective-permute-start | bytes 737288 | tf_op jit(solution)/shard_map/ppermute | solution.py:399
  10.1 12.3 %collective-permute-start.1 = (f32[2,5,6,8,128]{4,3,2,1,0:T(8,128)S(1)}, f32[2,5,6,8,128]{4,3,2,1,0:T(8,128)S(1)}, u32[]{:S(2)}, u32[]{:S(2)}) collective-permute-start(f32[2,5,6,8,128]{4,3,2,1,0:T(8,128)S(1)} %get-tuple-element.32), channel_id=1, source_target_pairs={{0,1},{1,0},{2,3},{3,2},{4,5},{5,4},{6,7},{7,6},{8,9},{9,8},{10,11... | collective-permute-start | bytes 737288 | tf_op jit(solution)/shard_map/ppermute | solution.py:402
  17.8 12.5 %collective-permute-start.7 = (f32[2,7,6,8,128]{4,3,2,1,0:T(8,128)S(1)}, f32[2,7,6,8,128]{4,3,2,1,0:T(8,128)S(1)}, u32[]{:S(2)}, u32[]{:S(2)}) collective-permute-start(f32[2,7,6,8,128]{4,3,2,1,0:T(8,128)S(1)} %get-tuple-element.43), channel_id=1, source_target_pairs={{0,15},{1,2},{2,1},{3,4},{4,3},{5,6},{6,5},{7,8},{8,7},{9,10},{10,... | collective-permute-start | bytes 1032200 | tf_op jit(solution)/shard_map/ppermute | solution.py:399
  20.4 10.0 %collective-permute-start.8 = (f32[2,7,6,8,128]{4,3,2,1,0:T(8,128)S(1)}, f32[2,7,6,8,128]{4,3,2,1,0:T(8,128)S(1)}, u32[]{:S(2)}, u32[]{:S(2)}) collective-permute-start(f32[2,7,6,8,128]{4,3,2,1,0:T(8,128)S(1)} %get-tuple-element.44), channel_id=1, source_target_pairs={{0,1},{1,0},{2,3},{3,2},{4,5},{5,4},{6,7},{7,6},{8,9},{9,8},{10,11... | collective-permute-start | bytes 1032200 | tf_op jit(solution)/shard_map/ppermute | solution.py:402
  23.6 9.4 %collective-permute-start.2 = (f32[2,5,6,8,128]{4,3,2,1,0:T(8,128)S(1)}, f32[2,5,6,8,128]{4,3,2,1,0:T(8,128)S(1)}, u32[]{:S(2)}, u32[]{:S(2)}) collective-permute-start(f32[2,5,6,8,128]{4,3,2,1,0:T(8,128)S(1)} %get-tuple-element.35), channel_id=1, source_target_pairs={{0,15},{1,2},{2,1},{3,4},{4,3},{5,6},{6,5},{7,8},{8,7},{9,10},{10,... | collective-permute-start | bytes 737288 | tf_op jit(solution)/shard_map/ppermute | solution.py:399
  26.1 6.9 %collective-permute-start.3 = (f32[2,5,6,8,128]{4,3,2,1,0:T(8,128)S(1)}, f32[2,5,6,8,128]{4,3,2,1,0:T(8,128)S(1)}, u32[]{:S(2)}, u32[]{:S(2)}) collective-permute-start(f32[2,5,6,8,128]{4,3,2,1,0:T(8,128)S(1)} %get-tuple-element.36), channel_id=1, source_target_pairs={{0,1},{1,0},{2,3},{3,2},{4,5},{5,4},{6,7},{7,6},{8,9},{9,8},{10,11... | collective-permute-start | bytes 737288 | tf_op jit(solution)/shard_map/ppermute | solution.py:402

commit v13 on v12

--- a/solution.py
+++ b/solution.py
@@ -114,49 +114,55 @@
             ref[row, n, k] = vec[k]
 
 
-def pack_links(links, inner, edge, arrive):
+def pack_edge(links, edge):
+    low = low_half()
+    for a in range(3):
+        for b in range(3):
+            for part in range(2):
+                y_link = tile(links, (1, a, b, part)) * (-1.0 / 6.0)
+                edge[a, b, part] = second_of(y_link, y_link, low)
+
+
+def pack_links(links, inner, slot, row):
     low = low_half()
     z = lane_ids() % LS
     even = sublane_ids() % 2 == 0
-    entries = [(a, b, part) for a in range(3) for b in range(3) for part in range(2)]
-    rows = tuple(enumerate((first_of, second_of)))
-
-    arrive(1)
-    for a, b, part in entries:
-        y_link = tile(links, (1, a, b, part)) * (-1.0 / 6.0)
-        u_y = first_of(y_link, y_link, low)
-        inner[0, 3, a, b, part] = u_y
-        inner[1, 3, b, a, part] = u_y if part == 0 else -u_y
-        edge[a, b, part] = second_of(y_link, y_link, low)
-    arrive(2)
-    for a, b, part in entries:
-        z_link = tile(links, (2, a, b, part)) * (-1.0 / 6.0)
-        for row, pick in rows:
-            u_z = pick(z_link, z_link, low)
-            inner[row, 1, a, b, part] = u_z
-            u_z = z_prev(u_z, z)
-            inner[row, 2, b, a, part] = u_z if part == 0 else -u_z
-    arrive(0)
+    pick = second_of if row else first_of
     for part in range(2):
-        x_link = [
-            [tile(links, (0, a, b, part)) * (-1.0 / 6.0) for b in range(3)] for a in range(3)
-        ]
+        x_link, y_link, z_link = (
+            [
+                [tile(links, (mu, a, b, part)) * (-1.0 / 6.0) for b in range(3)]
+                for a in range(3)
+            ]
+            for mu in range(3)
+        )
         for a in range(3):
             for b in range(3):
                 other = x_other(x_link[b][a], even)
                 both = x_link[a][b] + (other if part == 0 else -other)
-                for row, pick in rows:
-                    inner[row, 0, a, b, part] = pick(both, both, low)
-
-
-def add_inner(inner, row, pairs, field, sums):
+                inner[slot, 0, a, b, part] = pick(both, both, low)
+                u_z = pick(z_link[a][b], z_link[a][b], low)
+                inner[slot, 1, a, b, part] = u_z
+                u_z = z_prev(u_z, z)
+                inner[slot, 2, b, a, part] = u_z if part == 0 else -u_z
+                u_y = first_of(y_link[a][b], y_link[a][b], low)
+                if row == 0:
+                    inner[slot, 3, a, b, part] = u_y
+                else:
+                    inner[slot, 3, b, a, part] = u_y if part == 0 else -u_y
+
+
+def add_x_and_z(inner, slot, vectors, sums):
     z = lane_ids() % LS
     even = sublane_ids() % 2 == 0
-    here = take(field, row, pairs)
-    mat_vec(link_at(inner, row, 0), [[x_other(c, even) for c in vec] for vec in here], sums)
-    mat_vec(link_at(inner, row, 1), [[z_next(c, z) for c in vec] for vec in here], sums)
-    mat_vec(link_at(inner, row, 2), [[z_prev(c, z) for c in vec] for vec in here], sums)
-    mat_vec(link_at(inner, row, 3), take(field, 1 - row, pairs), sums)
+    mat_vec(link_at(inner, slot, 0), [[x_other(c, even) for c in vec] for vec in vectors], sums)
+    mat_vec(link_at(inner, slot, 1), [[z_next(c, z) for c in vec] for vec in vectors], sums)
+    mat_vec(link_at(inner, slot, 2), [[z_prev(c, z) for c in vec] for vec in vectors], sums)
+
+
+def add_inner(inner, slot, row, pairs, field, sums):
+    add_x_and_z(inner, slot, take(field, row, pairs), sums)
+    mat_vec(link_at(inner, slot, 3), take(field, 1 - row, pairs), sums)
 
 
 def scaled_rows(coeff, start, row, pairs):
@@ -170,44 +176,53 @@
     put(*out[part], pairs, vectors)
 
 
-def local_sums(coeff, pairs, row, rows, start, inner):
+def local_sums(coeff, pairs, row, rows, start, inner, slot):
     sums = scaled_rows(coeff, start, row, pairs)
-    add_inner(inner, row, pairs, rows, sums)
+    add_inner(inner, slot, row, pairs, rows, sums)
     return sums
 
 
 def open_round(coeff, pairs, rows, start, inner, edge, sums_out, down, up):
     for row, out in enumerate((down, up)):
-        sums = local_sums(coeff, pairs, row, rows, start, inner)
+        sums = local_sums(coeff, pairs, row, rows, start, inner, row)
         put(sums_out, row, pairs, sums)
         send(edge, pairs, 0, row, take(rows, row, pairs), out)
         send(edge, pairs, 1, row, sums, out)
 
 
+def plus(sums, more):
+    return [[s + m for s, m in zip(*both)] for both in zip(sums, more)]
+
+
+def add_message(edge, pairs, part, row, message, sums):
+    received = take(*message[part], pairs)
+    if row == 0:
+        return plus(sums, received)
+    mat_vec(link_at(edge), received, sums)
+    return sums
+
+
+def second_start(coeff, pairs, row, rows, start):
+    return [
+        [c + (1.0 / 36.0) * r for c, r in zip(*both)]
+        for both in zip(scaled_rows(coeff, start, row, pairs), take(rows, row, pairs))
+    ]
+
+
 def close_round(coeff, pairs, below, above, rows, sums_in, start, inner, edge, middle):
-    lower = [
-        [s + u for s, u in zip(*both)]
-        for both in zip(take(sums_in, 0, pairs), take(*below[0], pairs))
-    ]
-    put(middle, 0, pairs, lower)
-    upper = take(sums_in, 1, pairs)
-    mat_vec(link_at(edge), take(*above[0], pairs), upper)
-    put(middle, 1, pairs, upper)
+    for row, message in enumerate((below, above)):
+        sums = take(sums_in, row, pairs)
+        put(middle, row, pairs, add_message(edge, pairs, 0, row, message, sums))
     result = []
-    for row in range(2):
-        sums = [
-            [c + (1.0 / 36.0) * r for c, r in zip(*both)]
-            for both in zip(scaled_rows(coeff, start, row, pairs), take(rows, row, pairs))
-        ]
-        add_inner(inner, row, pairs, middle, sums)
-        if row == 0:
-            sums = [
-                [s + u for s, u in zip(*both)] for both in zip(sums, take(*below[1], pairs))
-            ]
-        else:
-            mat_vec(link_at(edge), take(*above[1], pairs), sums)
-        result.append(sums)
+    for row, message in enumerate((below, above)):
+        sums = second_start(coeff, pairs, row, rows, start)
+        add_inner(inner, row, row, pairs, middle, sums)
+        result.append(add_message(edge, pairs, 1, row, message, sums))
     return result
+
+
+def side(below, above):
+    return (0, below) if above is None else (1, above)
 
 
 def pack_rows(source, rows, arrive=lambda n: None):
@@ -235,7 +250,7 @@
     by_parity(run, parts(near_out), parts(far_out))
 
 
-def first_kernel(coeff, src, links, inner, edge, rows, far_sums, far_out, later, now, held, sems):
+def first_kernel(coeff, src, links, inner, edge, rows, far_sums, far_out, later, held, now, sems):
     count = now.shape[0]
     link_copies = [
         pltpu.make_async_copy(links.at[mu], held.at[mu], sems.at[mu]) for mu in range(3)
@@ -252,14 +267,18 @@
     for n in range(count // 2):
         first_copy(n).start()
     later_copy.start()
-    pack_links(held, inner, edge, lambda mu: link_copies[mu].wait())
+    link_copies[1].wait()
+    pack_edge(held, edge)
+    link_copies[2].wait()
+    link_copies[0].wait()
+    by_parity(lambda *sides: pack_links(held, inner, 0, side(*sides)[0]), None, True)
     pack_rows(lambda n, k: tile(now, (n, k)), rows, lambda n: first_copy(n).wait())
 
-    def run(down, up):
-        row, out = (0, down) if up is None else (1, up)
+    def run(*sides):
+        row, out = side(*sides)
 
         def body(pairs):
-            sums = local_sums(coeff, pairs, row, rows, rows, inner)
+            sums = local_sums(coeff, pairs, row, rows, rows, inner, 0)
             put(far_sums, 0, pairs, sums)
             send(edge, pairs, 0, row, take(rows, row, pairs), out)
             send(edge, pairs, 1, row, sums, out)
@@ -270,14 +289,20 @@
     later_copy.wait()
 
 
-def start_kernel(coeff, later, inner, edge, first_rows, far_sums, *refs):
+def start_kernel(coeff, later, links, far_inner, edge, first_rows, far_sums, inner, *refs):
     first_sums, *first_near, rows, sums, far_out, near_out = refs
 
-    def run(down, up):
-        row, out = (0, down) if up is None else (1, up)
+    def run(*sides):
+        row, out = side(*sides)
+        pack_links(links, inner, row, row)
+        for term in range(4):
+            for a in range(3):
+                for b in range(3):
+                    for part in range(2):
+                        inner[1 - row, term, a, b, part] = far_inner[0, term, a, b, part]
 
         def body(pairs):
-            ends = local_sums(coeff, pairs, row, first_rows, first_rows, inner)
+            ends = local_sums(coeff, pairs, row, first_rows, first_rows, inner, row)
             put(first_sums, row, pairs, ends)
             put(first_sums, 1 - row, pairs, take(far_sums, 0, pairs))
             send(edge, pairs, 0, row, take(first_rows, row, pairs), out)
@@ -312,7 +337,26 @@
     by_parity(run, near_side, (parts(far_in), parts(far_out)))
 
 
-def last_kernel(coeff, first, lead, far_in, near_in, rows, sums_in, start, inner, edge, *rest):
+def near_kernel(coeff, near_in, rows, sums_in, start, inner, edge, partial, middle):
+    def run(*sides):
+        row, message = side(*sides)
+
+        def body(pairs):
+            first = add_message(edge, pairs, 0, row, message, take(sums_in, row, pairs))
+            put(middle, row, pairs, first)
+            sums = second_start(coeff, pairs, row, rows, start)
+            add_x_and_z(inner, row, take(middle, row, pairs), sums)
+            put(partial, row, pairs, add_message(edge, pairs, 1, row, message, sums))
+            sums = second_start(coeff, pairs, 1 - row, rows, start)
+            mat_vec(link_at(inner, 1 - row, 3), take(middle, row, pairs), sums)
+            put(partial, 1 - row, pairs, sums)
+
+        each_group(rows, body)
+
+    by_parity(run, parts(near_in), None)
+
+
+def last_kernel(first, lead, far_in, partial, sums_in, inner, edge, *rest):
     out, middle, filled, sems = rest[-4:]
     low = low_half()
 
@@ -321,11 +365,19 @@
         there = pl.ds(first + 2 * n, 2)
         return pltpu.make_async_copy(filled.at[here], out.at[there], sems.at[n])
 
-    def run(below, above):
+    def run(*sides):
+        row, message = side(*sides)
+
         def body(pairs):
-            lower, upper = close_round(
-                coeff, pairs, below, above, rows, sums_in, start, inner, edge, middle
-            )
+            sums = add_message(edge, pairs, 0, row, message, take(sums_in, row, pairs))
+            put(middle, row, pairs, sums)
+            ends = [None, None]
+            ends[1 - row] = take(partial, 1 - row, pairs)
+            mat_vec(link_at(inner, 1 - row, 3), take(middle, row, pairs), ends[1 - row])
+            sums = take(partial, row, pairs)
+            add_x_and_z(inner, row, take(middle, row, pairs), sums)
+            ends[row] = add_message(edge, pairs, 1, row, message, sums)
+            lower, upper = ends
             for n, bottom, top in zip(pairs, lower, upper):
                 for k in range(6):
                     p = first_of(bottom[k], top[k], low) * lead
@@ -335,10 +387,10 @@
                         filled[m, k, 8:16] = value[:, 2 * LS :]
                 store(n).start()
 
-        each_group(rows, body)
-
-    by_parity(run, parts(near_in), parts(far_in))
-    for n in range(rows.shape[1]):
+        each_group(sums_in, body)
+
+    by_parity(run, None, parts(far_in))
+    for n in range(sums_in.shape[1]):
         store(n).wait()
 
 
@@ -401,31 +453,31 @@
     def to_near(value):
         return lax.ppermute(value, "space", near_pairs)
 
-    inner, edge, rows, far_sums, far_out, later = call(
+    far_inner, edge, rows, far_sums, far_out, later, held = call(
         functools.partial(first_kernel, steps[0]),
         [
-            f32((2, 4, 3, 3, 2, 8, 128)),
+            f32((1, 4, 3, 3, 2, 8, 128)),
             f32((3, 3, 2, 8, 128)),
             both[0],
             f32((1, *both[0].shape[1:])),
             both[0],
             f32((vectors - first[1], 6, planes, sites)),
+            f32(link_view.shape),
         ],
         [source_view, link_view],
         6 * work[0],
         [
             pltpu.VMEM(raw[0], jnp.float32),
-            pltpu.VMEM(link_view.shape, jnp.float32),
             pltpu.SemaphoreType.DMA((4 + sizes[0],)),
         ],
         (0, 1),
     )
     far = to_far(far_out)
     half = f32((1, *both[0].shape[1:]))
-    first_sums, *first_near, second_rows, second_sums, far_out, near_out = call(
+    inner, first_sums, *first_near, second_rows, second_sums, far_out, near_out = call(
         functools.partial(start_kernel, steps[0]),
-        [both[0], half, half] + [both[1]] * 4,
-        [later, inner, edge, rows, far_sums],
+        [f32((2, 4, 3, 3, 2, 8, 128)), both[0], half, half] + [both[1]] * 4,
+        [later, held, far_inner, edge, rows, far_sums],
         6 * work[1],
     )
     start = [rows, second_rows]
@@ -443,9 +495,17 @@
         halos[chunk] = (to_far(sends[0]), to_near(sends[1]))
     out = None
     for chunk in chunks:
-        args = [*halos[chunk], *fields[chunk], start[chunk], inner, edge]
+        far_in, near_in = halos[chunk]
+        (partial,) = call(
+            functools.partial(near_kernel, steps[3]),
+            [both[chunk]],
+            [near_in, *fields[chunk], start[chunk], inner, edge],
+            4 * work[chunk],
+            [middle[chunk]],
+        )
+        args = [far_in, partial, fields[chunk][1], inner, edge]
         (out,) = call(
-            functools.partial(last_kernel, steps[3], first[chunk], lead),
+            functools.partial(last_kernel, first[chunk], lead),
             [f32(source_view.shape)],
             args if out is None else args + [out],
             6 * work[chunk],

time: 34.7 us -> 35.5 us (1.023)
  starting transfers between devices: 11.5 us -> 12.5 us
  waiting for transfers between devices: 11.9 us -> 11.5 us
    ppermute x5, starting transfers between devices: 3.79 us -> 7.37 us  [to_near(): return lax.ppermute(value, 'space', near_pairs)]
    ppermute x4, starting transfers between devices: 7.69 us -> 5.16 us  [to_far(): return lax.ppermute(value, 'space', far_pairs)]
    ppermute x4, waiting for transfers between devices: 11.3 us -> 9.69 us  [to_far(): return lax.ppermute(value, 'space', far_pairs)]
    ppermute x5, waiting for transfers between devices: 0.68 us -> 1.81 us  [to_near(): return lax.ppermute(value, 'space', near_pairs)]
    pallas_call x6 -> x8, Pallas kernels: 11.1 us -> 11.3 us  [call(): pl.pallas_call(kernel, out_shape=outs, in_specs=[hbm if i in in_hbm else...]
  transfers between devices with their start and end apart: 9 -> 9, of which waited for: 6 -> 6; matrix products, arithmetic and copies ran while one was open for 0% -> 0% of each run, Pallas kernels for 19% -> 21%
where the time goes in v13:
time: 35.5 us; the launch traced here: 35.4 us
  starting transfers between devices  12.5 us (35%)
  waiting for transfers between devices  11.5 us (32%)
  Pallas kernels  11.3 us (32%)
    pallas_call x8, Pallas kernels, call(): pl.pallas_call(kernel, out_shape=outs, in_specs=[hbm if i in in_hbm else...  11.3 us
    ppermute x4, waiting for transfers between devices, to_far(): return lax.ppermute(value, 'space', far_pairs)  9.69 us
    ppermute x5, starting transfers between devices, to_near(): return lax.ppermute(value, 'space', near_pairs)  7.37 us
    ppermute x4, starting transfers between devices, to_far(): return lax.ppermute(value, 'space', far_pairs)  5.16 us
    ppermute x5, waiting for transfers between devices, to_near(): return lax.ppermute(value, 'space', near_pairs)  1.81 us
  transfers between devices with their start and end apart: 9, of which 6 were waited for; matrix products, arithmetic and copies ran while one was open for 0% of the time, Pallas kernels for 21%

profile of v13, /device:TPU:1, one launch (start us, length us, event | category | flops | bytes accessed | tf_op | source)
XLA Modules:
  0.0 35.4 jit_solution(10228290029508658302)
XLA Ops:
  0.0 2.7 %shard_map.28 = (f32[1,4,3,3,2,8,128]{6,5,4,3,2,1,0:T(8,128)S(1)}, f32[3,3,2,8,128]{4,3,2,1,0:T(8,128)S(1)}, f32[2,7,6,8,128]{4,3,2,1,0:T(8,128)S(1)}, f32[1,7,6...) custom-call(f32[24,6,16,64]{3,2,1,0:T(8,128)} %bitcast.7, ...), custom_call_target="tpu_custom_call" | custom-call | flops 6193152 | bytes 2506752 | tf_op jit(solution)/shard_map/pallas_call | solution.py:411
  2.7 2.6 %collective-permute-start.4 = (f32[2,7,6,8,128]{4,3,2,1,0:T(8,128)S(1)}, f32[2,7,6,8,128]{4,3,2,1,0:T(8,128)S(1)}, u32[]{:S(2)}, u32[]{:S(2)}) collective-permute-start(f32[2,7,6,8,128]{4,3,2,1,0:T(8,128)S(1)} %get-tuple-element.43), channel_id=1, source_target_pairs={{0,15},{1,2},{2,1},{3,4},{4,3},{5,6},{6,5},{7,8},{8,7},{9,10},{10,... | collective-permute-start | bytes 1032200 | tf_op jit(solution)/shard_map/ppermute | solution.py:451
  5.3 1.7 %shard_map.29 = (f32[2,4,3,3,2,8,128]{6,5,4,3,2,1,0:T(8,128)S(1)}, f32[2,7,6,8,128]{4,3,2,1,0:T(8,128)S(1)}, f32[1,7,6,8,128]{4,3,2,1,0:T(8,128)S(1)}, f32[1,7,6...) custom-call(f32[10,6,16,64]{3,2,1,0:T(8,128)S(1)} %get-tuple-element, ...), custom_call_target="tpu_custom_call" | custom-call | flops 4423680 | bytes 3612672 | tf_op jit(solution)/shard_map/pallas_call | solution.py:411
  7.0 3.0 %collective-permute-start.5 = (f32[1,7,6,8,128]{4,3,2,1,0:T(8,128)S(1)}, f32[1,7,6,8,128]{4,3,2,1,0:T(8,128)S(1)}, u32[]{:S(2)}, u32[]{:S(2)}) collective-permute-start(f32[1,7,6,8,128]{4,3,2,1,0:T(8,128)S(1)} %get-tuple-element.44), channel_id=1, source_target_pairs={{0,1},{1,0},{2,3},{3,2},{4,5},{5,4},{6,7},{7,6},{8,9},{9,8},{10,11... | collective-permute-start | bytes 516104 | tf_op jit(solution)/shard_map/ppermute | solution.py:454
  10.1 0.1 collective-permute-start.6
  10.1 0.7 %collective-permute-start.1 = (f32[2,5,6,8,128]{4,3,2,1,0:T(8,128)S(1)}, f32[2,5,6,8,128]{4,3,2,1,0:T(8,128)S(1)}, u32[]{:S(2)}, u32[]{:S(2)}) collective-permute-start(f32[2,5,6,8,128]{4,3,2,1,0:T(8,128)S(1)} %get-tuple-element.35), channel_id=1, source_target_pairs={{0,1},{1,0},{2,3},{3,2},{4,5},{5,4},{6,7},{7,6},{8,9},{9,8},{10,11... | collective-permute-start | bytes 737288 | tf_op jit(solution)/shard_map/ppermute | solution.py:454
  10.8 0.3 collective-permute-done.5.refs_0_
  11.1 0.4 %collective-permute-done.6.refs_1_ = f32[1,7,6,8,128]{4,3,2,1,0:T(8,128)S(1)} collective-permute-done((f32[1,7,6,8,128]{4,3,2,1,0:T(8,128)S(1)}, f32[1,7,6,8,128]{4,3,2,1,0:T(8,128)S(1)}, u32[]{:S(2)}, u32[]{:S(2)}) %collective-permute-start.6) | collective-permute-done | bytes 172064 | tf_op jit(solution)/shard_map/ppermute | solution.py:454
  11.5 4.4 %collective-permute-done.4.far_in = f32[2,7,6,8,128]{4,3,2,1,0:T(8,128)S(1)} collective-permute-done((f32[2,7,6,8,128]{4,3,2,1,0:T(8,128)S(1)}, f32[2,7,6,8,128]{4,3,2,1,0:T(8,128)S(1)}, u32[]{:S(2)}, u32[]{:S(2)}) %collective-permute-start.4) | collective-permute-done | bytes 344096 | tf_op jit(solution)/shard_map/ppermute | solution.py:451
  15.8 1.7 %shard_map.32 = (f32[2,7,6,8,128]{4,3,2,1,0:T(8,128)S(1)}, f32[2,7,6,8,128]{4,3,2,1,0:T(8,128)S(1)}, f32[2,7,6,8,128]{4,3,2,1,0:T(8,128)S(1)}, f32[2,7,6,8,128]{4,3,2,1,0:T(8,128)S(1)}) custom-call(f32[2,7,6,8,128]{4,3,2,1,0:T(8,128)S(1)} %collective-permute-done.4.far_in, f32[1,7,6,8,128]{4,3,2,1,0:T(8,128)S(1)} %collective-permute-done.5.refs_0_, ...), custom_call_target="tpu_custom_call" | custom-call | flops 12386304 | bytes 3760128 | tf_op jit(solution)/shard_map/pallas_call | solution.py:411
  17.6 0.1 collective-permute-start.8
  17.7 2.5 %collective-permute-start.7 = (f32[2,7,6,8,128]{4,3,2,1,0:T(8,128)S(1)}, f32[2,7,6,8,128]{4,3,2,1,0:T(8,128)S(1)}, u32[]{:S(2)}, u32[]{:S(2)}) collective-permute-start(f32[2,7,6,8,128]{4,3,2,1,0:T(8,128)S(1)} %get-tuple-element.47), channel_id=1, source_target_pairs={{0,15},{1,2},{2,1},{3,4},{4,3},{5,6},{6,5},{7,8},{8,7},{9,10},{10,... | collective-permute-start | bytes 1032200 | tf_op jit(solution)/shard_map/ppermute | solution.py:451
  20.2 0.0 collective-permute-done.far_in
  20.2 0.0 collective-permute-done.1.refs_0_
  20.2 1.2 %shard_map.30 = (f32[2,5,6,8,128]{4,3,2,1,0:T(8,128)S(1)}, f32[2,5,6,8,128]{4,3,2,1,0:T(8,128)S(1)}, f32[2,5,6,8,128]{4,3,2,1,0:T(8,128)S(1)}, f32[2,5,6,8,128]{4,3,2,1,0:T(8,128)S(1)}) custom-call(f32[2,5,6,8,128]{4,3,2,1,0:T(8,128)S(1)} %collective-permute-done.far_in, f32[2,5,6,8,128]{4,3,2,1,0:T(8,128)S(1)} %collective-permute-done.1.refs_0_, ...), custom_call_target="tpu_custom_call" | custom-call | flops 8847360 | bytes 2875392 | tf_op jit(solution)/shard_map/pallas_call | solution.py:411
  21.4 3.5 %collective-permute-start.3 = (f32[2,5,6,8,128]{4,3,2,1,0:T(8,128)S(1)}, f32[2,5,6,8,128]{4,3,2,1,0:T(8,128)S(1)}, u32[]{:S(2)}, u32[]{:S(2)}) collective-permute-start(f32[2,5,6,8,128]{4,3,2,1,0:T(8,128)S(1)} %get-tuple-element.40), channel_id=1, source_target_pairs={{0,1},{1,0},{2,3},{3,2},{4,5},{5,4},{6,7},{7,6},{8,9},{9,8},{10,11... | collective-permute-start | bytes 737288 | tf_op jit(solution)/shard_map/ppermute | solution.py:454
  24.9 1.1 %collective-permute-done.3.near_in = f32[2,5,6,8,128]{4,3,2,1,0:T(8,128)S(1)} collective-permute-done((f32[2,5,6,8,128]{4,3,2,1,0:T(8,128)S(1)}, f32[2,5,6,8,128]{4,3,2,1,0:T(8,128)S(1)}, u32[]{:S(2)}, u32[]{:S(2)}) %collective-permute-start.3) | collective-permute-done | bytes 245792 | tf_op jit(solution)/shard_map/ppermute | solution.py:454
  26.1 0.3 shard_map.31.partial
  26.4 0.0 collective-permute-done.8.near_in
  26.4 0.5 %shard_map.33.partial = f32[2,7,6,8,128]{4,3,2,1,0:T(8,128)S(1)} custom-call(f32[2,7,6,8,128]{4,3,2,1,0:T(8,128)S(1)} %collective-permute-done.8.near_in, f32[2,7,6,8,128]{4,3,2,1,0:T(8,128)S(1)} %get-tuple-element.49.rows, f32[2,7,6,8,128]{4,3,2,1,0:T(8,128)S(1)} %get-tuple-element.50.sums_in, ...), custom_call_target="tpu_custom_call" | custom-call | flops 4128768 | bytes 2383872 | tf_op jit(solution)/shard_map/pallas_call | solution.py:411
  26.9 3.8 %collective-permute-done.7.far_in = f32[2,7,6,8,128]{4,3,2,1,0:T(8,128)S(1)} collective-permute-done((f32[2,7,6,8,128]{4,3,2,1,0:T(8,128)S(1)}, f32[2,7,6,8,128]{4,3,2,1,0:T(8,128)S(1)}, u32[]{:S(2)}, u32[]{:S(2)}) %collective-permute-start.7) | collective-permute-done | bytes 344096 | tf_op jit(solution)/shard_map/ppermute | solution.py:451
  30.7 1.9 %shard_map.34.rest_0_ = f32[24,6,16,64]{3,2,1,0:T(8,128)} custom-call(f32[2,7,6,8,128]{4,3,2,1,0:T(8,128)S(1)} %collective-permute-done.7.far_in, f32[2,7,6,8,128]{4,3,2,1,0:T(8,128)S(1)} %shard_map.33.partial, f32[2,7,6,8,128]{4,3,2,1,0:T(8,128)S(1)} %get-tuple-element.50.sums_in, f32[2,4,3,3,2,8,128]{6,5,4,3,2,1,0:T(8,128)S(1)} %get-tuple-element.38.refs_4_.inner.refs_5_, ...), custom_call_target="tpu_custom_call" | custom-call | flops 6193152 | bytes 2285568 | tf_op jit(solution)/shard_map/pallas_call | solution.py:411
  32.6 1.5 %collective-permute-done.2.far_in = f32[2,5,6,8,128]{4,3,2,1,0:T(8,128)S(1)} collective-permute-done((f32[2,5,6,8,128]{4,3,2,1,0:T(8,128)S(1)}, f32[2,5,6,8,128]{4,3,2,1,0:T(8,128)S(1)}, u32[]{:S(2)}, u32[]{:S(2)}) %collective-permute-start.2) | collective-permute-done | bytes 245792 | tf_op jit(solution)/shard_map/ppermute | solution.py:451
  34.1 1.3 %shard_map.35 = f32[24,6,16,64]{3,2,1,0:T(8,128)} custom-call(f32[2,5,6,8,128]{4,3,2,1,0:T(8,128)S(1)} %collective-permute-done.2.far_in, f32[2,5,6,8,128]{4,3,2,1,0:T(8,128)S(1)} %shard_map.31.partial, f32[2,5,6,8,128]{4,3,2,1,0:T(8,128)S(1)} %get-tuple-element.42.sums_in, ...), custom_call_target="tpu_custom_call", output_to_operand_aliasing={{}: (5, {})} | custom-call | flops 4423680 | bytes 2580480 | tf_op jit(solution)/shard_map/pallas_call | solution.py:411
  (2 shorter events, 0.0 us)
Async XLA Ops:
  2.7 13.1 %collective-permute-start.4 = (f32[2,7,6,8,128]{4,3,2,1,0:T(8,128)S(1)}, f32[2,7,6,8,128]{4,3,2,1,0:T(8,128)S(1)}, u32[]{:S(2)}, u32[]{:S(2)}) collective-permute-start(f32[2,7,6,8,128]{4,3,2,1,0:T(8,128)S(1)} %get-tuple-element.43), channel_id=1, source_target_pairs={{0,15},{1,2},{2,1},{3,4},{4,3},{5,6},{6,5},{7,8},{8,7},{9,10},{10,... | collective-permute-start | bytes 1032200 | tf_op jit(solution)/shard_map/ppermute | solution.py:451
  7.0 4.1 %collective-permute-start.5 = (f32[1,7,6,8,128]{4,3,2,1,0:T(8,128)S(1)}, f32[1,7,6,8,128]{4,3,2,1,0:T(8,128)S(1)}, u32[]{:S(2)}, u32[]{:S(2)}) collective-permute-start(f32[1,7,6,8,128]{4,3,2,1,0:T(8,128)S(1)} %get-tuple-element.44), channel_id=1, source_target_pairs={{0,1},{1,0},{2,3},{3,2},{4,5},{5,4},{6,7},{7,6},{8,9},{9,8},{10,11... | collective-permute-start | bytes 516104 | tf_op jit(solution)/shard_map/ppermute | solution.py:454
  10.1 1.4 %collective-permute-start.6 = (f32[1,7,6,8,128]{4,3,2,1,0:T(8,128)S(1)}, f32[1,7,6,8,128]{4,3,2,1,0:T(8,128)S(1)}, u32[]{:S(2)}, u32[]{:S(2)}) collective-permute-start(f32[1,7,6,8,128]{4,3,2,1,0:T(8,128)S(1)} %get-tuple-element.45), channel_id=1, source_target_pairs={{0,1},{1,0},{2,3},{3,2},{4,5},{5,4},{6,7},{7,6},{8,9},{9,8},{10,11... | collective-permute-start | bytes 516104 | tf_op jit(solution)/shard_map/ppermute | solution.py:454
  10.1 10.1 %collective-permute-start = (f32[2,5,6,8,128]{4,3,2,1,0:T(8,128)S(1)}, f32[2,5,6,8,128]{4,3,2,1,0:T(8,128)S(1)}, u32[]{:S(2)}, u32[]{:S(2)}) collective-permute-start(f32[2,5,6,8,128]{4,3,2,1,0:T(8,128)S(1)} %get-tuple-element.34), channel_id=1, source_target_pairs={{0,15},{1,2},{2,1},{3,4},{4,3},{5,6},{6,5},{7,8},{8,7},{9,10},{10,... | collective-permute-start | bytes 737288 | tf_op jit(solution)/shard_map/ppermute | solution.py:451
  10.1 10.1 %collective-permute-start.1 = (f32[2,5,6,8,128]{4,3,2,1,0:T(8,128)S(1)}, f32[2,5,6,8,128]{4,3,2,1,0:T(8,128)S(1)}, u32[]{:S(2)}, u32[]{:S(2)}) collective-permute-start(f32[2,5,6,8,128]{4,3,2,1,0:T(8,128)S(1)} %get-tuple-element.35), channel_id=1, source_target_pairs={{0,1},{1,0},{2,3},{3,2},{4,5},{5,4},{6,7},{7,6},{8,9},{9,8},{10,11... | collective-permute-start | bytes 737288 | tf_op jit(solution)/shard_map/ppermute | solution.py:454
  17.6 8.8 %collective-permute-start.8 = (f32[2,7,6,8,128]{4,3,2,1,0:T(8,128)S(1)}, f32[2,7,6,8,128]{4,3,2,1,0:T(8,128)S(1)}, u32[]{:S(2)}, u32[]{:S(2)}) collective-permute-start(f32[2,7,6,8,128]{4,3,2,1,0:T(8,128)S(1)} %get-tuple-element.48), channel_id=1, source_target_pairs={{0,1},{1,0},{2,3},{3,2},{4,5},{5,4},{6,7},{7,6},{8,9},{9,8},{10,11... | collective-permute-start | bytes 1032200 | tf_op jit(solution)/shard_map/ppermute | solution.py:454
  17.7 13.1 %collective-permute-start.7 = (f32[2,7,6,8,128]{4,3,2,1,0:T(8,128)S(1)}, f32[2,7,6,8,128]{4,3,2,1,0:T(8,128)S(1)}, u32[]{:S(2)}, u32[]{:S(2)}) collective-permute-start(f32[2,7,6,8,128]{4,3,2,1,0:T(8,128)S(1)} %get-tuple-element.47), channel_id=1, source_target_pairs={{0,15},{1,2},{2,1},{3,4},{4,3},{5,6},{6,5},{7,8},{8,7},{9,10},{10,... | collective-permute-start | bytes 1032200 | tf_op jit(solution)/shard_map/ppermute | solution.py:451
  21.4 4.7 %collective-permute-start.3 = (f32[2,5,6,8,128]{4,3,2,1,0:T(8,128)S(1)}, f32[2,5,6,8,128]{4,3,2,1,0:T(8,128)S(1)}, u32[]{:S(2)}, u32[]{:S(2)}) collective-permute-start(f32[2,5,6,8,128]{4,3,2,1,0:T(8,128)S(1)} %get-tuple-element.40), channel_id=1, source_target_pairs={{0,1},{1,0},{2,3},{3,2},{4,5},{5,4},{6,7},{7,6},{8,9},{9,8},{10,11... | collective-permute-start | bytes 737288 | tf_op jit(solution)/shard_map/ppermute | solution.py:454
  24.9 9.1 %collective-permute-start.2 = (f32[2,5,6,8,128]{4,3,2,1,0:T(8,128)S(1)}, f32[2,5,6,8,128]{4,3,2,1,0:T(8,128)S(1)}, u32[]{:S(2)}, u32[]{:S(2)}) collective-permute-start(f32[2,5,6,8,128]{4,3,2,1,0:T(8,128)S(1)} %get-tuple-element.39), channel_id=1, source_target_pairs={{0,15},{1,2},{2,1},{3,4},{4,3},{5,6},{6,5},{7,8},{8,7},{9,10},{10,... | collective-permute-start | bytes 737288 | tf_op jit(solution)/shard_map/ppermute | solution.py:451

commit v14 on v13

--- a/solution.py
+++ b/solution.py
@@ -337,26 +337,7 @@
     by_parity(run, near_side, (parts(far_in), parts(far_out)))
 
 
-def near_kernel(coeff, near_in, rows, sums_in, start, inner, edge, partial, middle):
-    def run(*sides):
-        row, message = side(*sides)
-
-        def body(pairs):
-            first = add_message(edge, pairs, 0, row, message, take(sums_in, row, pairs))
-            put(middle, row, pairs, first)
-            sums = second_start(coeff, pairs, row, rows, start)
-            add_x_and_z(inner, row, take(middle, row, pairs), sums)
-            put(partial, row, pairs, add_message(edge, pairs, 1, row, message, sums))
-            sums = second_start(coeff, pairs, 1 - row, rows, start)
-            mat_vec(link_at(inner, 1 - row, 3), take(middle, row, pairs), sums)
-            put(partial, 1 - row, pairs, sums)
-
-        each_group(rows, body)
-
-    by_parity(run, parts(near_in), None)
-
-
-def last_kernel(first, lead, far_in, partial, sums_in, inner, edge, *rest):
+def last_kernel(coeff, first, lead, far_in, near_in, rows, sums_in, start, inner, edge, *rest):
     out, middle, filled, sems = rest[-4:]
     low = low_half()
 
@@ -365,19 +346,11 @@
         there = pl.ds(first + 2 * n, 2)
         return pltpu.make_async_copy(filled.at[here], out.at[there], sems.at[n])
 
-    def run(*sides):
-        row, message = side(*sides)
-
+    def run(below, above):
         def body(pairs):
-            sums = add_message(edge, pairs, 0, row, message, take(sums_in, row, pairs))
-            put(middle, row, pairs, sums)
-            ends = [None, None]
-            ends[1 - row] = take(partial, 1 - row, pairs)
-            mat_vec(link_at(inner, 1 - row, 3), take(middle, row, pairs), ends[1 - row])
-            sums = take(partial, row, pairs)
-            add_x_and_z(inner, row, take(middle, row, pairs), sums)
-            ends[row] = add_message(edge, pairs, 1, row, message, sums)
-            lower, upper = ends
+            lower, upper = close_round(
+                coeff, pairs, below, above, rows, sums_in, start, inner, edge, middle
+            )
             for n, bottom, top in zip(pairs, lower, upper):
                 for k in range(6):
                     p = first_of(bottom[k], top[k], low) * lead
@@ -387,10 +360,10 @@
                         filled[m, k, 8:16] = value[:, 2 * LS :]
                 store(n).start()
 
-        each_group(sums_in, body)
-
-    by_parity(run, None, parts(far_in))
-    for n in range(sums_in.shape[1]):
+        each_group(rows, body)
+
+    by_parity(run, parts(near_in), parts(far_in))
+    for n in range(rows.shape[1]):
         store(n).wait()
 
 
@@ -495,17 +468,9 @@
         halos[chunk] = (to_far(sends[0]), to_near(sends[1]))
     out = None
     for chunk in chunks:
-        far_in, near_in = halos[chunk]
-        (partial,) = call(
-            functools.partial(near_kernel, steps[3]),
-            [both[chunk]],
-            [near_in, *fields[chunk], start[chunk], inner, edge],
-            4 * work[chunk],
-            [middle[chunk]],
-        )
-        args = [far_in, partial, fields[chunk][1], inner, edge]
+        args = [*halos[chunk], *fields[chunk], start[chunk], inner, edge]
         (out,) = call(
-            functools.partial(last_kernel, first[chunk], lead),
+            functools.partial(last_kernel, steps[3], first[chunk], lead),
             [f32(source_view.shape)],
             args if out is None else args + [out],
             6 * work[chunk],

time: 35.5 us -> 34.4 us (0.969)
  starting transfers between devices: 12.5 us -> 11.5 us
    ppermute x5, starting transfers between devices: 7.37 us -> 3.78 us  [to_near(): return lax.ppermute(value, 'space', near_pairs)]
    ppermute x4, starting transfers between devices: 5.16 us -> 7.7 us  [to_far(): return lax.ppermute(value, 'space', far_pairs)]
    ppermute x4, waiting for transfers between devices: 9.69 us -> 11.1 us  [to_far(): return lax.ppermute(value, 'space', far_pairs)]
    ppermute x5, waiting for transfers between devices: 1.81 us -> 0.67 us  [to_near(): return lax.ppermute(value, 'space', near_pairs)]
    pallas_call x8 -> x6, Pallas kernels: 11.3 us -> 11 us  [call(): pl.pallas_call(kernel, out_shape=outs, in_specs=[hbm if i in in_hbm else...]
  transfers between devices with their start and end apart: 9 -> 9, of which waited for: 6 -> 6; matrix products, arithmetic and copies ran while one was open for 0% -> 0% of each run, Pallas kernels for 21% -> 20%
where the time goes in v14:
time: 34.4 us; the launch traced here: 34.3 us
  waiting for transfers between devices  11.7 us (34%)
  starting transfers between devices  11.5 us (33%)
  Pallas kernels  11 us (32%)
    ppermute x4, waiting for transfers between devices, to_far(): return lax.ppermute(value, 'space', far_pairs)  11.1 us
    pallas_call x6, Pallas kernels, call(): pl.pallas_call(kernel, out_shape=outs, in_specs=[hbm if i in in_hbm else...  11 us
    ppermute x4, starting transfers between devices, to_far(): return lax.ppermute(value, 'space', far_pairs)  7.7 us
    ppermute x5, starting transfers between devices, to_near(): return lax.ppermute(value, 'space', near_pairs)  3.78 us
  transfers between devices with their start and end apart: 9, of which 6 were waited for; matrix products, arithmetic and copies ran while one was open for 0% of the time, Pallas kernels for 20%

profile of v14, /device:TPU:1, one launch (start us, length us, event | category | flops | bytes accessed | tf_op | source)
XLA Modules:
  0.0 34.3 jit_solution(6447151127119870284)
XLA Ops:
  0.0 2.7 %shard_map.28 = (f32[1,4,3,3,2,8,128]{6,5,4,3,2,1,0:T(8,128)S(1)}, f32[3,3,2,8,128]{4,3,2,1,0:T(8,128)S(1)}, f32[2,7,6,8,128]{4,3,2,1,0:T(8,128)S(1)}, f32[1,7,6...) custom-call(f32[24,6,16,64]{3,2,1,0:T(8,128)} %bitcast.7, ...), custom_call_target="tpu_custom_call" | custom-call | flops 6193152 | bytes 2506752 | tf_op jit(solution)/shard_map/pallas_call | solution.py:384
  2.7 2.6 %collective-permute-start.4 = (f32[2,7,6,8,128]{4,3,2,1,0:T(8,128)S(1)}, f32[2,7,6,8,128]{4,3,2,1,0:T(8,128)S(1)}, u32[]{:S(2)}, u32[]{:S(2)}) collective-permute-start(f32[2,7,6,8,128]{4,3,2,1,0:T(8,128)S(1)} %get-tuple-element.43), channel_id=1, source_target_pairs={{0,15},{1,2},{2,1},{3,4},{4,3},{5,6},{6,5},{7,8},{8,7},{9,10},{10,... | collective-permute-start | bytes 1032200 | tf_op jit(solution)/shard_map/ppermute | solution.py:424
  5.3 1.7 %shard_map.29 = (f32[2,4,3,3,2,8,128]{6,5,4,3,2,1,0:T(8,128)S(1)}, f32[2,7,6,8,128]{4,3,2,1,0:T(8,128)S(1)}, f32[1,7,6,8,128]{4,3,2,1,0:T(8,128)S(1)}, f32[1,7,6...) custom-call(f32[10,6,16,64]{3,2,1,0:T(8,128)S(1)} %get-tuple-element, ...), custom_call_target="tpu_custom_call" | custom-call | flops 4423680 | bytes 3612672 | tf_op jit(solution)/shard_map/pallas_call | solution.py:384
  7.0 3.0 %collective-permute-start.5 = (f32[1,7,6,8,128]{4,3,2,1,0:T(8,128)S(1)}, f32[1,7,6,8,128]{4,3,2,1,0:T(8,128)S(1)}, u32[]{:S(2)}, u32[]{:S(2)}) collective-permute-start(f32[1,7,6,8,128]{4,3,2,1,0:T(8,128)S(1)} %get-tuple-element.44), channel_id=1, source_target_pairs={{0,1},{1,0},{2,3},{3,2},{4,5},{5,4},{6,7},{7,6},{8,9},{9,8},{10,11... | collective-permute-start | bytes 516104 | tf_op jit(solution)/shard_map/ppermute | solution.py:427
  10.1 0.1 collective-permute-start.6
  10.1 0.0 collective-permute-start
  10.1 0.7 %collective-permute-start.1 = (f32[2,5,6,8,128]{4,3,2,1,0:T(8,128)S(1)}, f32[2,5,6,8,128]{4,3,2,1,0:T(8,128)S(1)}, u32[]{:S(2)}, u32[]{:S(2)}) collective-permute-start(f32[2,5,6,8,128]{4,3,2,1,0:T(8,128)S(1)} %get-tuple-element.35), channel_id=1, source_target_pairs={{0,1},{1,0},{2,3},{3,2},{4,5},{5,4},{6,7},{7,6},{8,9},{9,8},{10,11... | collective-permute-start | bytes 737288 | tf_op jit(solution)/shard_map/ppermute | solution.py:427
  10.8 0.3 collective-permute-done.5.refs_0_
  11.1 0.4 %collective-permute-done.6.refs_1_ = f32[1,7,6,8,128]{4,3,2,1,0:T(8,128)S(1)} collective-permute-done((f32[1,7,6,8,128]{4,3,2,1,0:T(8,128)S(1)}, f32[1,7,6,8,128]{4,3,2,1,0:T(8,128)S(1)}, u32[]{:S(2)}, u32[]{:S(2)}) %collective-permute-start.6) | collective-permute-done | bytes 172064 | tf_op jit(solution)/shard_map/ppermute | solution.py:427
  11.5 4.4 %collective-permute-done.4.far_in = f32[2,7,6,8,128]{4,3,2,1,0:T(8,128)S(1)} collective-permute-done((f32[2,7,6,8,128]{4,3,2,1,0:T(8,128)S(1)}, f32[2,7,6,8,128]{4,3,2,1,0:T(8,128)S(1)}, u32[]{:S(2)}, u32[]{:S(2)}) %collective-permute-start.4) | collective-permute-done | bytes 344096 | tf_op jit(solution)/shard_map/ppermute | solution.py:424
  15.8 1.7 %shard_map.31 = (f32[2,7,6,8,128]{4,3,2,1,0:T(8,128)S(1)}, f32[2,7,6,8,128]{4,3,2,1,0:T(8,128)S(1)}, f32[2,7,6,8,128]{4,3,2,1,0:T(8,128)S(1)}, f32[2,7,6,8,128]{4,3,2,1,0:T(8,128)S(1)}) custom-call(f32[2,7,6,8,128]{4,3,2,1,0:T(8,128)S(1)} %collective-permute-done.4.far_in, f32[1,7,6,8,128]{4,3,2,1,0:T(8,128)S(1)} %collective-permute-done.5.refs_0_, ...), custom_call_target="tpu_custom_call" | custom-call | flops 12386304 | bytes 3760128 | tf_op jit(solution)/shard_map/pallas_call | solution.py:384
  17.6 2.5 %collective-permute-start.7 = (f32[2,7,6,8,128]{4,3,2,1,0:T(8,128)S(1)}, f32[2,7,6,8,128]{4,3,2,1,0:T(8,128)S(1)}, u32[]{:S(2)}, u32[]{:S(2)}) collective-permute-start(f32[2,7,6,8,128]{4,3,2,1,0:T(8,128)S(1)} %get-tuple-element.47), channel_id=1, source_target_pairs={{0,15},{1,2},{2,1},{3,4},{4,3},{5,6},{6,5},{7,8},{8,7},{9,10},{10,... | collective-permute-start | bytes 1032200 | tf_op jit(solution)/shard_map/ppermute | solution.py:424
  20.1 0.0 collective-permute-start.8
  20.1 2.0 %collective-permute-done.far_in = f32[2,5,6,8,128]{4,3,2,1,0:T(8,128)S(1)} collective-permute-done((f32[2,5,6,8,128]{4,3,2,1,0:T(8,128)S(1)}, f32[2,5,6,8,128]{4,3,2,1,0:T(8,128)S(1)}, u32[]{:S(2)}, u32[]{:S(2)}) %collective-permute-start) | collective-permute-done | bytes 245792 | tf_op jit(solution)/shard_map/ppermute | solution.py:424
  22.2 0.0 collective-permute-done.1.refs_0_
  22.2 1.2 %shard_map.30 = (f32[2,5,6,8,128]{4,3,2,1,0:T(8,128)S(1)}, f32[2,5,6,8,128]{4,3,2,1,0:T(8,128)S(1)}, f32[2,5,6,8,128]{4,3,2,1,0:T(8,128)S(1)}, f32[2,5,6,8,128]{4,3,2,1,0:T(8,128)S(1)}) custom-call(f32[2,5,6,8,128]{4,3,2,1,0:T(8,128)S(1)} %collective-permute-done.far_in, f32[2,5,6,8,128]{4,3,2,1,0:T(8,128)S(1)} %collective-permute-done.1.refs_0_, ...), custom_call_target="tpu_custom_call" | custom-call | flops 8847360 | bytes 2875392 | tf_op jit(solution)/shard_map/pallas_call | solution.py:384
  23.4 2.5 %collective-permute-start.2 = (f32[2,5,6,8,128]{4,3,2,1,0:T(8,128)S(1)}, f32[2,5,6,8,128]{4,3,2,1,0:T(8,128)S(1)}, u32[]{:S(2)}, u32[]{:S(2)}) collective-permute-start(f32[2,5,6,8,128]{4,3,2,1,0:T(8,128)S(1)} %get-tuple-element.39), channel_id=1, source_target_pairs={{0,15},{1,2},{2,1},{3,4},{4,3},{5,6},{6,5},{7,8},{8,7},{9,10},{10,... | collective-permute-start | bytes 737288 | tf_op jit(solution)/shard_map/ppermute | solution.py:424
  25.9 0.0 collective-permute-start.3
  25.9 4.2 %collective-permute-done.7.far_in = f32[2,7,6,8,128]{4,3,2,1,0:T(8,128)S(1)} collective-permute-done((f32[2,7,6,8,128]{4,3,2,1,0:T(8,128)S(1)}, f32[2,7,6,8,128]{4,3,2,1,0:T(8,128)S(1)}, u32[]{:S(2)}, u32[]{:S(2)}) %collective-permute-start.7) | collective-permute-done | bytes 344096 | tf_op jit(solution)/shard_map/ppermute | solution.py:424
  30.1 0.0 collective-permute-done.8.near_in
  30.1 2.2 %shard_map.32.rest_0_ = f32[24,6,16,64]{3,2,1,0:T(8,128)} custom-call(f32[2,7,6,8,128]{4,3,2,1,0:T(8,128)S(1)} %collective-permute-done.7.far_in, f32[2,7,6,8,128]{4,3,2,1,0:T(8,128)S(1)} %collective-permute-done.8.near_in, f32[2,7,6,8,128]{4,3,2,1,0:T(8,128)S(1)} %get-tuple-element.49.rows, f32[2,7,6,8,128]{4,3,2,1,0:T(8,128)S(1)} %get-tuple-element.50.sums_in, ...), custom_call_target="tpu_custom_call" | custom-call | flops 6193152 | bytes 2973696 | tf_op jit(solution)/shard_map/pallas_call | solution.py:384
  32.3 0.5 %collective-permute-done.2.far_in = f32[2,5,6,8,128]{4,3,2,1,0:T(8,128)S(1)} collective-permute-done((f32[2,5,6,8,128]{4,3,2,1,0:T(8,128)S(1)}, f32[2,5,6,8,128]{4,3,2,1,0:T(8,128)S(1)}, u32[]{:S(2)}, u32[]{:S(2)}) %collective-permute-start.2) | collective-permute-done | bytes 245792 | tf_op jit(solution)/shard_map/ppermute | solution.py:424
  32.7 0.0 collective-permute-done.3.near_in
  32.7 1.5 %shard_map.33 = f32[24,6,16,64]{3,2,1,0:T(8,128)} custom-call(f32[2,5,6,8,128]{4,3,2,1,0:T(8,128)S(1)} %collective-permute-done.2.far_in, f32[2,5,6,8,128]{4,3,2,1,0:T(8,128)S(1)} %collective-permute-done.3.near_in, f32[2,5,6,8,128]{4,3,2,1,0:T(8,128)S(1)} %get-tuple-element.41.rows, ...), custom_call_target="tpu_custom_call", output_to_operand_aliasing={{}: (7, {})} | custom-call | flops 4423680 | bytes 3072000 | tf_op jit(solution)/shard_map/pallas_call | solution.py:384
Async XLA Ops:
  2.7 13.1 %collective-permute-start.4 = (f32[2,7,6,8,128]{4,3,2,1,0:T(8,128)S(1)}, f32[2,7,6,8,128]{4,3,2,1,0:T(8,128)S(1)}, u32[]{:S(2)}, u32[]{:S(2)}) collective-permute-start(f32[2,7,6,8,128]{4,3,2,1,0:T(8,128)S(1)} %get-tuple-element.43), channel_id=1, source_target_pairs={{0,15},{1,2},{2,1},{3,4},{4,3},{5,6},{6,5},{7,8},{8,7},{9,10},{10,... | collective-permute-start | bytes 1032200 | tf_op jit(solution)/shard_map/ppermute | solution.py:424
  7.0 4.1 %collective-permute-start.5 = (f32[1,7,6,8,128]{4,3,2,1,0:T(8,128)S(1)}, f32[1,7,6,8,128]{4,3,2,1,0:T(8,128)S(1)}, u32[]{:S(2)}, u32[]{:S(2)}) collective-permute-start(f32[1,7,6,8,128]{4,3,2,1,0:T(8,128)S(1)} %get-tuple-element.44), channel_id=1, source_target_pairs={{0,1},{1,0},{2,3},{3,2},{4,5},{5,4},{6,7},{7,6},{8,9},{9,8},{10,11... | collective-permute-start | bytes 516104 | tf_op jit(solution)/shard_map/ppermute | solution.py:427
  10.1 1.4 %collective-permute-start.6 = (f32[1,7,6,8,128]{4,3,2,1,0:T(8,128)S(1)}, f32[1,7,6,8,128]{4,3,2,1,0:T(8,128)S(1)}, u32[]{:S(2)}, u32[]{:S(2)}) collective-permute-start(f32[1,7,6,8,128]{4,3,2,1,0:T(8,128)S(1)} %get-tuple-element.45), channel_id=1, source_target_pairs={{0,1},{1,0},{2,3},{3,2},{4,5},{5,4},{6,7},{7,6},{8,9},{9,8},{10,11... | collective-permute-start | bytes 516104 | tf_op jit(solution)/shard_map/ppermute | solution.py:427
  10.1 12.0 %collective-permute-start = (f32[2,5,6,8,128]{4,3,2,1,0:T(8,128)S(1)}, f32[2,5,6,8,128]{4,3,2,1,0:T(8,128)S(1)}, u32[]{:S(2)}, u32[]{:S(2)}) collective-permute-start(f32[2,5,6,8,128]{4,3,2,1,0:T(8,128)S(1)} %get-tuple-element.34), channel_id=1, source_target_pairs={{0,15},{1,2},{2,1},{3,4},{4,3},{5,6},{6,5},{7,8},{8,7},{9,10},{10,... | collective-permute-start | bytes 737288 | tf_op jit(solution)/shard_map/ppermute | solution.py:424
  10.1 12.0 %collective-permute-start.1 = (f32[2,5,6,8,128]{4,3,2,1,0:T(8,128)S(1)}, f32[2,5,6,8,128]{4,3,2,1,0:T(8,128)S(1)}, u32[]{:S(2)}, u32[]{:S(2)}) collective-permute-start(f32[2,5,6,8,128]{4,3,2,1,0:T(8,128)S(1)} %get-tuple-element.35), channel_id=1, source_target_pairs={{0,1},{1,0},{2,3},{3,2},{4,5},{5,4},{6,7},{7,6},{8,9},{9,8},{10,11... | collective-permute-start | bytes 737288 | tf_op jit(solution)/shard_map/ppermute | solution.py:427
  17.6 12.5 %collective-permute-start.7 = (f32[2,7,6,8,128]{4,3,2,1,0:T(8,128)S(1)}, f32[2,7,6,8,128]{4,3,2,1,0:T(8,128)S(1)}, u32[]{:S(2)}, u32[]{:S(2)}) collective-permute-start(f32[2,7,6,8,128]{4,3,2,1,0:T(8,128)S(1)} %get-tuple-element.47), channel_id=1, source_target_pairs={{0,15},{1,2},{2,1},{3,4},{4,3},{5,6},{6,5},{7,8},{8,7},{9,10},{10,... | collective-permute-start | bytes 1032200 | tf_op jit(solution)/shard_map/ppermute | solution.py:424
  20.1 10.0 %collective-permute-start.8 = (f32[2,7,6,8,128]{4,3,2,1,0:T(8,128)S(1)}, f32[2,7,6,8,128]{4,3,2,1,0:T(8,128)S(1)}, u32[]{:S(2)}, u32[]{:S(2)}) collective-permute-start(f32[2,7,6,8,128]{4,3,2,1,0:T(8,128)S(1)} %get-tuple-element.48), channel_id=1, source_target_pairs={{0,1},{1,0},{2,3},{3,2},{4,5},{5,4},{6,7},{7,6},{8,9},{9,8},{10,11... | collective-permute-start | bytes 1032200 | tf_op jit(solution)/shard_map/ppermute | solution.py:427
  23.4 9.4 %collective-permute-start.2 = (f32[2,5,6,8,128]{4,3,2,1,0:T(8,128)S(1)}, f32[2,5,6,8,128]{4,3,2,1,0:T(8,128)S(1)}, u32[]{:S(2)}, u32[]{:S(2)}) collective-permute-start(f32[2,5,6,8,128]{4,3,2,1,0:T(8,128)S(1)} %get-tuple-element.39), channel_id=1, source_target_pairs={{0,15},{1,2},{2,1},{3,4},{4,3},{5,6},{6,5},{7,8},{8,7},{9,10},{10,... | collective-permute-start | bytes 737288 | tf_op jit(solution)/shard_map/ppermute | solution.py:424
  25.9 6.8 %collective-permute-start.3 = (f32[2,5,6,8,128]{4,3,2,1,0:T(8,128)S(1)}, f32[2,5,6,8,128]{4,3,2,1,0:T(8,128)S(1)}, u32[]{:S(2)}, u32[]{:S(2)}) collective-permute-start(f32[2,5,6,8,128]{4,3,2,1,0:T(8,128)S(1)} %get-tuple-element.40), channel_id=1, source_target_pairs={{0,1},{1,0},{2,3},{3,2},{4,5},{5,4},{6,7},{7,6},{8,9},{9,8},{10,11... | collective-permute-start | bytes 737288 | tf_op jit(solution)/shard_map/ppermute | solution.py:427

commit v15 on v14

--- a/solution.py
+++ b/solution.py
@@ -262,17 +262,18 @@
 
     rest = src.at[pl.ds(count, later.shape[0])]
     later_copy = pltpu.make_async_copy(rest, later, sems.at[3])
-    for mu in (1, 2, 0):
-        link_copies[mu].start()
+    link_copies[1].start()
     for n in range(count // 2):
         first_copy(n).start()
+    link_copies[2].start()
+    link_copies[0].start()
     later_copy.start()
     link_copies[1].wait()
     pack_edge(held, edge)
+    pack_rows(lambda n, k: tile(now, (n, k)), rows, lambda n: first_copy(n).wait())
     link_copies[2].wait()
     link_copies[0].wait()
     by_parity(lambda *sides: pack_links(held, inner, 0, side(*sides)[0]), None, True)
-    pack_rows(lambda n, k: tile(now, (n, k)), rows, lambda n: first_copy(n).wait())
 
     def run(*sides):
         row, out = side(*sides)

time: 34.4 us -> 34.4 us (level)
  no operation moved by 1% of the time
where the time goes in v15:
time: 34.4 us; the launch traced here: 34.3 us
  waiting for transfers between devices  11.7 us (34%)
  starting transfers between devices  11.5 us (33%)
  Pallas kernels  11 us (32%)
    ppermute x4, waiting for transfers between devices, to_far(): return lax.ppermute(value, 'space', far_pairs)  11.1 us
    pallas_call x6, Pallas kernels, call(): pl.pallas_call(kernel, out_shape=outs, in_specs=[hbm if i in in_hbm else...  11 us
    ppermute x4, starting transfers between devices, to_far(): return lax.ppermute(value, 'space', far_pairs)  7.7 us
    ppermute x5, starting transfers between devices, to_near(): return lax.ppermute(value, 'space', near_pairs)  3.78 us
  transfers between devices with their start and end apart: 9, of which 6 were waited for; matrix products, arithmetic and copies ran while one was open for 0% of the time, Pallas kernels for 20%

profile of v15, /device:TPU:1, one launch (start us, length us, event | category | flops | bytes accessed | tf_op | source)
XLA Modules:
  0.0 34.3 jit_solution(13356157500713830370)
XLA Ops:
  0.0 2.7 %shard_map.28 = (f32[1,4,3,3,2,8,128]{6,5,4,3,2,1,0:T(8,128)S(1)}, f32[3,3,2,8,128]{4,3,2,1,0:T(8,128)S(1)}, f32[2,7,6,8,128]{4,3,2,1,0:T(8,128)S(1)}, f32[1,7,6...) custom-call(f32[24,6,16,64]{3,2,1,0:T(8,128)} %bitcast.7, ...), custom_call_target="tpu_custom_call" | custom-call | flops 6193152 | bytes 2506752 | tf_op jit(solution)/shard_map/pallas_call | solution.py:385
  2.7 2.6 %collective-permute-start.4 = (f32[2,7,6,8,128]{4,3,2,1,0:T(8,128)S(1)}, f32[2,7,6,8,128]{4,3,2,1,0:T(8,128)S(1)}, u32[]{:S(2)}, u32[]{:S(2)}) collective-permute-start(f32[2,7,6,8,128]{4,3,2,1,0:T(8,128)S(1)} %get-tuple-element.43), channel_id=1, source_target_pairs={{0,15},{1,2},{2,1},{3,4},{4,3},{5,6},{6,5},{7,8},{8,7},{9,10},{10,... | collective-permute-start | bytes 1032200 | tf_op jit(solution)/shard_map/ppermute | solution.py:425
  5.3 1.7 %shard_map.29 = (f32[2,4,3,3,2,8,128]{6,5,4,3,2,1,0:T(8,128)S(1)}, f32[2,7,6,8,128]{4,3,2,1,0:T(8,128)S(1)}, f32[1,7,6,8,128]{4,3,2,1,0:T(8,128)S(1)}, f32[1,7,6...) custom-call(f32[10,6,16,64]{3,2,1,0:T(8,128)S(1)} %get-tuple-element, ...), custom_call_target="tpu_custom_call" | custom-call | flops 4423680 | bytes 3612672 | tf_op jit(solution)/shard_map/pallas_call | solution.py:385
  7.0 3.0 %collective-permute-start.5 = (f32[1,7,6,8,128]{4,3,2,1,0:T(8,128)S(1)}, f32[1,7,6,8,128]{4,3,2,1,0:T(8,128)S(1)}, u32[]{:S(2)}, u32[]{:S(2)}) collective-permute-start(f32[1,7,6,8,128]{4,3,2,1,0:T(8,128)S(1)} %get-tuple-element.44), channel_id=1, source_target_pairs={{0,1},{1,0},{2,3},{3,2},{4,5},{5,4},{6,7},{7,6},{8,9},{9,8},{10,11... | collective-permute-start | bytes 516104 | tf_op jit(solution)/shard_map/ppermute | solution.py:428
  10.0 0.1 collective-permute-start.6
  10.1 0.0 collective-permute-start
  10.1 0.7 %collective-permute-start.1 = (f32[2,5,6,8,128]{4,3,2,1,0:T(8,128)S(1)}, f32[2,5,6,8,128]{4,3,2,1,0:T(8,128)S(1)}, u32[]{:S(2)}, u32[]{:S(2)}) collective-permute-start(f32[2,5,6,8,128]{4,3,2,1,0:T(8,128)S(1)} %get-tuple-element.35), channel_id=1, source_target_pairs={{0,1},{1,0},{2,3},{3,2},{4,5},{5,4},{6,7},{7,6},{8,9},{9,8},{10,11... | collective-permute-start | bytes 737288 | tf_op jit(solution)/shard_map/ppermute | solution.py:428
  10.8 0.3 collective-permute-done.5.refs_0_
  11.1 0.4 %collective-permute-done.6.refs_1_ = f32[1,7,6,8,128]{4,3,2,1,0:T(8,128)S(1)} collective-permute-done((f32[1,7,6,8,128]{4,3,2,1,0:T(8,128)S(1)}, f32[1,7,6,8,128]{4,3,2,1,0:T(8,128)S(1)}, u32[]{:S(2)}, u32[]{:S(2)}) %collective-permute-start.6) | collective-permute-done | bytes 172064 | tf_op jit(solution)/shard_map/ppermute | solution.py:428
  11.5 4.4 %collective-permute-done.4.far_in = f32[2,7,6,8,128]{4,3,2,1,0:T(8,128)S(1)} collective-permute-done((f32[2,7,6,8,128]{4,3,2,1,0:T(8,128)S(1)}, f32[2,7,6,8,128]{4,3,2,1,0:T(8,128)S(1)}, u32[]{:S(2)}, u32[]{:S(2)}) %collective-permute-start.4) | collective-permute-done | bytes 344096 | tf_op jit(solution)/shard_map/ppermute | solution.py:425
  15.8 1.7 %shard_map.31 = (f32[2,7,6,8,128]{4,3,2,1,0:T(8,128)S(1)}, f32[2,7,6,8,128]{4,3,2,1,0:T(8,128)S(1)}, f32[2,7,6,8,128]{4,3,2,1,0:T(8,128)S(1)}, f32[2,7,6,8,128]{4,3,2,1,0:T(8,128)S(1)}) custom-call(f32[2,7,6,8,128]{4,3,2,1,0:T(8,128)S(1)} %collective-permute-done.4.far_in, f32[1,7,6,8,128]{4,3,2,1,0:T(8,128)S(1)} %collective-permute-done.5.refs_0_, ...), custom_call_target="tpu_custom_call" | custom-call | flops 12386304 | bytes 3760128 | tf_op jit(solution)/shard_map/pallas_call | solution.py:385
  17.6 2.5 %collective-permute-start.7 = (f32[2,7,6,8,128]{4,3,2,1,0:T(8,128)S(1)}, f32[2,7,6,8,128]{4,3,2,1,0:T(8,128)S(1)}, u32[]{:S(2)}, u32[]{:S(2)}) collective-permute-start(f32[2,7,6,8,128]{4,3,2,1,0:T(8,128)S(1)} %get-tuple-element.47), channel_id=1, source_target_pairs={{0,15},{1,2},{2,1},{3,4},{4,3},{5,6},{6,5},{7,8},{8,7},{9,10},{10,... | collective-permute-start | bytes 1032200 | tf_op jit(solution)/shard_map/ppermute | solution.py:425
  20.1 0.0 collective-permute-start.8
  20.1 2.0 %collective-permute-done.far_in = f32[2,5,6,8,128]{4,3,2,1,0:T(8,128)S(1)} collective-permute-done((f32[2,5,6,8,128]{4,3,2,1,0:T(8,128)S(1)}, f32[2,5,6,8,128]{4,3,2,1,0:T(8,128)S(1)}, u32[]{:S(2)}, u32[]{:S(2)}) %collective-permute-start) | collective-permute-done | bytes 245792 | tf_op jit(solution)/shard_map/ppermute | solution.py:425
  22.2 0.0 collective-permute-done.1.refs_0_
  22.2 1.2 %shard_map.30 = (f32[2,5,6,8,128]{4,3,2,1,0:T(8,128)S(1)}, f32[2,5,6,8,128]{4,3,2,1,0:T(8,128)S(1)}, f32[2,5,6,8,128]{4,3,2,1,0:T(8,128)S(1)}, f32[2,5,6,8,128]{4,3,2,1,0:T(8,128)S(1)}) custom-call(f32[2,5,6,8,128]{4,3,2,1,0:T(8,128)S(1)} %collective-permute-done.far_in, f32[2,5,6,8,128]{4,3,2,1,0:T(8,128)S(1)} %collective-permute-done.1.refs_0_, ...), custom_call_target="tpu_custom_call" | custom-call | flops 8847360 | bytes 2875392 | tf_op jit(solution)/shard_map/pallas_call | solution.py:385
  23.4 2.5 %collective-permute-start.2 = (f32[2,5,6,8,128]{4,3,2,1,0:T(8,128)S(1)}, f32[2,5,6,8,128]{4,3,2,1,0:T(8,128)S(1)}, u32[]{:S(2)}, u32[]{:S(2)}) collective-permute-start(f32[2,5,6,8,128]{4,3,2,1,0:T(8,128)S(1)} %get-tuple-element.39), channel_id=1, source_target_pairs={{0,15},{1,2},{2,1},{3,4},{4,3},{5,6},{6,5},{7,8},{8,7},{9,10},{10,... | collective-permute-start | bytes 737288 | tf_op jit(solution)/shard_map/ppermute | solution.py:425
  25.9 0.0 collective-permute-start.3
  25.9 4.2 %collective-permute-done.7.far_in = f32[2,7,6,8,128]{4,3,2,1,0:T(8,128)S(1)} collective-permute-done((f32[2,7,6,8,128]{4,3,2,1,0:T(8,128)S(1)}, f32[2,7,6,8,128]{4,3,2,1,0:T(8,128)S(1)}, u32[]{:S(2)}, u32[]{:S(2)}) %collective-permute-start.7) | collective-permute-done | bytes 344096 | tf_op jit(solution)/shard_map/ppermute | solution.py:425
  30.1 0.0 collective-permute-done.8.near_in
  30.1 2.2 %shard_map.32.rest_0_ = f32[24,6,16,64]{3,2,1,0:T(8,128)} custom-call(f32[2,7,6,8,128]{4,3,2,1,0:T(8,128)S(1)} %collective-permute-done.7.far_in, f32[2,7,6,8,128]{4,3,2,1,0:T(8,128)S(1)} %collective-permute-done.8.near_in, f32[2,7,6,8,128]{4,3,2,1,0:T(8,128)S(1)} %get-tuple-element.49.rows, f32[2,7,6,8,128]{4,3,2,1,0:T(8,128)S(1)} %get-tuple-element.50.sums_in, ...), custom_call_target="tpu_custom_call" | custom-call | flops 6193152 | bytes 2973696 | tf_op jit(solution)/shard_map/pallas_call | solution.py:385
  32.3 0.5 %collective-permute-done.2.far_in = f32[2,5,6,8,128]{4,3,2,1,0:T(8,128)S(1)} collective-permute-done((f32[2,5,6,8,128]{4,3,2,1,0:T(8,128)S(1)}, f32[2,5,6,8,128]{4,3,2,1,0:T(8,128)S(1)}, u32[]{:S(2)}, u32[]{:S(2)}) %collective-permute-start.2) | collective-permute-done | bytes 245792 | tf_op jit(solution)/shard_map/ppermute | solution.py:425
  32.7 0.0 collective-permute-done.3.near_in
  32.7 1.5 %shard_map.33 = f32[24,6,16,64]{3,2,1,0:T(8,128)} custom-call(f32[2,5,6,8,128]{4,3,2,1,0:T(8,128)S(1)} %collective-permute-done.2.far_in, f32[2,5,6,8,128]{4,3,2,1,0:T(8,128)S(1)} %collective-permute-done.3.near_in, f32[2,5,6,8,128]{4,3,2,1,0:T(8,128)S(1)} %get-tuple-element.41.rows, ...), custom_call_target="tpu_custom_call", output_to_operand_aliasing={{}: (7, {})} | custom-call | flops 4423680 | bytes 3072000 | tf_op jit(solution)/shard_map/pallas_call | solution.py:385
Async XLA Ops:
  2.7 13.1 %collective-permute-start.4 = (f32[2,7,6,8,128]{4,3,2,1,0:T(8,128)S(1)}, f32[2,7,6,8,128]{4,3,2,1,0:T(8,128)S(1)}, u32[]{:S(2)}, u32[]{:S(2)}) collective-permute-start(f32[2,7,6,8,128]{4,3,2,1,0:T(8,128)S(1)} %get-tuple-element.43), channel_id=1, source_target_pairs={{0,15},{1,2},{2,1},{3,4},{4,3},{5,6},{6,5},{7,8},{8,7},{9,10},{10,... | collective-permute-start | bytes 1032200 | tf_op jit(solution)/shard_map/ppermute | solution.py:425
  7.0 4.1 %collective-permute-start.5 = (f32[1,7,6,8,128]{4,3,2,1,0:T(8,128)S(1)}, f32[1,7,6,8,128]{4,3,2,1,0:T(8,128)S(1)}, u32[]{:S(2)}, u32[]{:S(2)}) collective-permute-start(f32[1,7,6,8,128]{4,3,2,1,0:T(8,128)S(1)} %get-tuple-element.44), channel_id=1, source_target_pairs={{0,1},{1,0},{2,3},{3,2},{4,5},{5,4},{6,7},{7,6},{8,9},{9,8},{10,11... | collective-permute-start | bytes 516104 | tf_op jit(solution)/shard_map/ppermute | solution.py:428
  10.0 1.4 %collective-permute-start.6 = (f32[1,7,6,8,128]{4,3,2,1,0:T(8,128)S(1)}, f32[1,7,6,8,128]{4,3,2,1,0:T(8,128)S(1)}, u32[]{:S(2)}, u32[]{:S(2)}) collective-permute-start(f32[1,7,6,8,128]{4,3,2,1,0:T(8,128)S(1)} %get-tuple-element.45), channel_id=1, source_target_pairs={{0,1},{1,0},{2,3},{3,2},{4,5},{5,4},{6,7},{7,6},{8,9},{9,8},{10,11... | collective-permute-start | bytes 516104 | tf_op jit(solution)/shard_map/ppermute | solution.py:428
  10.1 12.0 %collective-permute-start = (f32[2,5,6,8,128]{4,3,2,1,0:T(8,128)S(1)}, f32[2,5,6,8,128]{4,3,2,1,0:T(8,128)S(1)}, u32[]{:S(2)}, u32[]{:S(2)}) collective-permute-start(f32[2,5,6,8,128]{4,3,2,1,0:T(8,128)S(1)} %get-tuple-element.34), channel_id=1, source_target_pairs={{0,15},{1,2},{2,1},{3,4},{4,3},{5,6},{6,5},{7,8},{8,7},{9,10},{10,... | collective-permute-start | bytes 737288 | tf_op jit(solution)/shard_map/ppermute | solution.py:425
  10.1 12.0 %collective-permute-start.1 = (f32[2,5,6,8,128]{4,3,2,1,0:T(8,128)S(1)}, f32[2,5,6,8,128]{4,3,2,1,0:T(8,128)S(1)}, u32[]{:S(2)}, u32[]{:S(2)}) collective-permute-start(f32[2,5,6,8,128]{4,3,2,1,0:T(8,128)S(1)} %get-tuple-element.35), channel_id=1, source_target_pairs={{0,1},{1,0},{2,3},{3,2},{4,5},{5,4},{6,7},{7,6},{8,9},{9,8},{10,11... | collective-permute-start | bytes 737288 | tf_op jit(solution)/shard_map/ppermute | solution.py:428
  17.6 12.5 %collective-permute-start.7 = (f32[2,7,6,8,128]{4,3,2,1,0:T(8,128)S(1)}, f32[2,7,6,8,128]{4,3,2,1,0:T(8,128)S(1)}, u32[]{:S(2)}, u32[]{:S(2)}) collective-permute-start(f32[2,7,6,8,128]{4,3,2,1,0:T(8,128)S(1)} %get-tuple-element.47), channel_id=1, source_target_pairs={{0,15},{1,2},{2,1},{3,4},{4,3},{5,6},{6,5},{7,8},{8,7},{9,10},{10,... | collective-permute-start | bytes 1032200 | tf_op jit(solution)/shard_map/ppermute | solution.py:425
  20.1 10.0 %collective-permute-start.8 = (f32[2,7,6,8,128]{4,3,2,1,0:T(8,128)S(1)}, f32[2,7,6,8,128]{4,3,2,1,0:T(8,128)S(1)}, u32[]{:S(2)}, u32[]{:S(2)}) collective-permute-start(f32[2,7,6,8,128]{4,3,2,1,0:T(8,128)S(1)} %get-tuple-element.48), channel_id=1, source_target_pairs={{0,1},{1,0},{2,3},{3,2},{4,5},{5,4},{6,7},{7,6},{8,9},{9,8},{10,11... | collective-permute-start | bytes 1032200 | tf_op jit(solution)/shard_map/ppermute | solution.py:428
  23.4 9.4 %collective-permute-start.2 = (f32[2,5,6,8,128]{4,3,2,1,0:T(8,128)S(1)}, f32[2,5,6,8,128]{4,3,2,1,0:T(8,128)S(1)}, u32[]{:S(2)}, u32[]{:S(2)}) collective-permute-start(f32[2,5,6,8,128]{4,3,2,1,0:T(8,128)S(1)} %get-tuple-element.39), channel_id=1, source_target_pairs={{0,15},{1,2},{2,1},{3,4},{4,3},{5,6},{6,5},{7,8},{8,7},{9,10},{10,... | collective-permute-start | bytes 737288 | tf_op jit(solution)/shard_map/ppermute | solution.py:425
  25.9 6.8 %collective-permute-start.3 = (f32[2,5,6,8,128]{4,3,2,1,0:T(8,128)S(1)}, f32[2,5,6,8,128]{4,3,2,1,0:T(8,128)S(1)}, u32[]{:S(2)}, u32[]{:S(2)}) collective-permute-start(f32[2,5,6,8,128]{4,3,2,1,0:T(8,128)S(1)} %get-tuple-element.40), channel_id=1, source_target_pairs={{0,1},{1,0},{2,3},{3,2},{4,5},{5,4},{6,7},{7,6},{8,9},{9,8},{10,11... | collective-permute-start | bytes 737288 | tf_op jit(solution)/shard_map/ppermute | solution.py:428
